TPU v7x, 32 devices: a whole 2x2x4 slice. The times are simulated.
32 devices in a mesh: rows: 4 (over x, core), feat: 8 (over z, y).
Axes of the slice: x: 2, y: 2, z: 4, core: 2. Of those that a mesh axis runs over, the one named last changes fastest.
Arguments:
- design: bfloat16 [3072, 65536], P('rows', 'feat'), may hold values from -0.0234375 to 0.0234375
- labels: int32 [64, 3072], P(None, 'rows'), may hold values from -1 to 1, as said below
- local_x: float32 [4, 64, 65536], P('rows', None, 'feat'), may hold values from -6 to 6
- dual_u: float32 [4, 64, 65536], P('rows', None, 'feat'), may hold values from -3 to 3
- consensus_z: float32 [64, 65536], P(None, 'feat'), may hold values from -6 to 6
- step_size: float32 [64], replicated, may hold values from 0.5 to 1
- rho: float32 [64], replicated, may hold values from 0.5 to 1.5
- penalty: float32 [64], replicated, may hold values from 0.5 to 4
Outputs:
- new_x: float32 [4, 64, 65536], P('rows', None, 'feat')
- new_z: float32 [64, 65536], P(None, 'feat')
- new_u: float32 [4, 64, 65536], P('rows', None, 'feat')
Inputs may be any that keep to these rules, and one draw needn't show every extreme that they name: `labels`: each entry is -1 or 1.
All inputs are finite; a program needn't handle non-finite values.
Results may differ from a plain program's by a relative error of at most 0.0023.
Values may be sent and summed in bfloat16 or wider, within the bound.
No kernel may reach another device: no remote copies, remote signals or barrier semaphores. Data moves between devices by JAX's collectives and lax.ppermute only.
A program may use at most 64 MiB of HBM per device.

v0:
```python
import jax
import jax.numpy as jnp
from jax import lax
from jax.sharding import PartitionSpec as P


def per_device(design, labels, local_x, dual_u, consensus_z, step_size, rho, penalty):
    x = local_x[0]
    dual = dual_u[0]
    sign = labels.astype(jnp.float32)
    eta = step_size[:, None]
    weight = rho[:, None]
    for turn in range(2):
        xb = x.astype(jnp.bfloat16)
        partial_margin = lax.dot_general(
            xb, design, (((1,), (1,)), ((), ())), preferred_element_type=jnp.float32
        )
        margin = lax.psum(partial_margin, "feat")
        resid = (sign * jax.nn.sigmoid(-sign * margin)).astype(jnp.bfloat16)
        grad = jnp.dot(resid, design, preferred_element_type=jnp.float32)
        x = x - eta * (weight * (x - consensus_z + dual) - grad)
    blocks_count = lax.axis_size("rows")
    limit = (penalty / (rho * blocks_count))[:, None]
    total = lax.psum(x + dual, "rows")
    mean = total / blocks_count
    new_z = mean - jnp.clip(mean, -limit, limit)
    new_u = dual + x - new_z
    return (x[None], new_z, new_u[None])


def solution(mesh):
    in_specs = (
        P("rows", "feat"),
        P(None, "rows"),
        P("rows", None, "feat"),
        P("rows", None, "feat"),
        P(None, "feat"),
        P(),
        P(),
        P(),
    )
    out_specs = (P("rows", None, "feat"), P(None, "feat"), P("rows", None, "feat"))
    return jax.shard_map(
        per_device, mesh=mesh, in_specs=in_specs, out_specs=out_specs, check_vma=False
    )
```

profile of v0, /device:TPU:0, one launch (start us, length us, event | category | flops | bytes accessed | tf_op | source)
XLA Modules:
  0.0 245.9 jit_solution(14331785148566467952)
XLA Ops:
  7.2 0.0 copy-start.3
  7.2 0.0 copy-start.4
  7.2 0.0 copy-start.2
  7.2 0.0 all-reduce.4.cloned.1.call-start
  7.2 9.9 %fusion.15 = f32[64,768]{1,0:T(8,128)} fusion(bf16[768,8192]{1,0:T(8,128)(2,1)} %param.8, f32[1,64,8192]{2,1,0:T(8,128)} %param.10), kind=kOutput, calls=%fused_computation.27 | convolution fusion | flops 805306368 | bytes 14876672 | tf_op jit(solution)/shard_map/dot_general | solution.py:15
  17.1 0.0 all-reduce.4.cloned.1.call-update
  17.1 0.0 all-reduce.6.cloned.1.call-start
  17.2 72.8 %all-reduce.4.cloned.1.call-done = f32[64,768]{1,0:T(8,128)} async-done(((f32[64,768]{1,0:T(8,128)}), f32[64,768]{1,0:T(8,128)}) %all-reduce.4.cloned.1.call-update) | async-done | bytes 196624 | tf_op jit(solution)/shard_map/psum | solution.py:18
  90.0 0.0 copy-done.3
  90.0 0.0 copy-done.4
  90.0 0.0 copy-done.2
  90.0 9.1 %fusion.2 = f32[64,8192]{1,0:T(8,128)S(1)} fusion(bf16[768,8192]{1,0:T(8,128)(2,1)} %param.8, f32[1,64,8192]{2,1,0:T(8,128)} %param.11, f32[1,64,8192]{2,1,0:T(8,128)} %param.10, f32[64,8192]{1,0:T(8,128)} %param.12, f32[64]{0:T(128)S(1)} %copy-done.3, f32[64]{0:T(128)S(1)} %copy-done.4, f32[64,768]{1,0:T(8,128)} %all-reduce.4.cloned.1.call-done, ...), kind=kOutput, calls=%fused_computation.4 | convolution fusion | flops 808845312 | bytes 21365248 | tf_op jit(solution)/shard_map/dot_general | solution.py:20
  99.1 0.9 copy-done
  100.0 4.6 %fusion.7 = f32[64,768]{1,0:T(8,128)} fusion(bf16[768,8192]{1,0:T(8,128)(2,1)S(1)} %copy-done, f32[64,8192]{1,0:T(8,128)S(1)} %fusion.2), kind=kOutput, calls=%fused_computation.16 | convolution fusion | flops 805830656 | bytes 14876672 | tf_op jit(solution)/shard_map/dot_general | solution.py:15
  104.7 0.0 all-reduce.6.cloned.1.call-update
  104.7 0.0 all-reduce.8.cloned.1.call-start
  104.7 69.2 %all-reduce.6.cloned.1.call-done = f32[64,768]{1,0:T(8,128)} async-done(((f32[64,768]{1,0:T(8,128)}), f32[64,768]{1,0:T(8,128)}) %all-reduce.6.cloned.1.call-update) | async-done | bytes 196624 | tf_op jit(solution)/shard_map/psum | solution.py:18
  174.0 10.6 %bitcast_add_fusion = (f32[64,8192]{1,0:T(8,128)}, f32[64,8192]{1,0:T(8,128)}) fusion(f32[1,64,8192]{2,1,0:T(8,128)} %param.11, f32[64,8192]{1,0:T(8,128)S(1)} %fusion.2, bf16[768,8192]{1,0:T(8,128)(2,1)} %param.8, f32[64,768]{1,0:T(8,128)} %all-reduce.6.cloned.1.call-done, s32[64,768]{1,0:T(8,128)S(1)} %copy-done.2, f32[64,8192]{1,0:T(8,128)} %param.12, ...), kind=kOutput, calls=%fused_computation.6 | convolution fusion | flops 809369600 | bytes 23462400 | tf_op jit(solution)/shard_map/dot_general | solution.py:20
  184.5 0.0 copy-start.5
  184.5 0.0 all-reduce.8.cloned.1.call-update
  184.6 0.6 copy-done.5
  185.2 50.0 %all-reduce.8.cloned.1.call-done = f32[64,8192]{1,0:T(8,128)} async-done(((f32[64,8192]{1,0:T(8,128)}), f32[64,8192]{1,0:T(8,128)}) %all-reduce.8.cloned.1.call-update) | async-done | bytes 2097168 | tf_op jit(solution)/shard_map/psum | solution.py:24
  235.2 0.0 copy-done.1
  235.2 4.2 %subtract_bitcast_fusion = (f32[1,64,8192]{2,1,0:T(8,128)}, f32[64,8192]{1,0:T(8,128)}) fusion(f32[64,8192]{1,0:T(8,128)S(1)} %copy-done.1, f32[64]{0:T(128)S(1)} %get-tuple-element.5, f32[64]{0:T(128)S(1)} %get-tuple-element.6, f32[64,8192]{1,0:T(8,128)} %all-reduce.8.cloned.1.call-done), kind=kLoop, calls=%fused_computation.13 | loop fusion | flops 2621440 | bytes 8389120 | tf_op jit(solution)/shard_map/broadcast_in_dim | solution.py:28
  (3 shorter events, 0.0 us)
Async XLA Ops:
  7.2 82.8 %copy-start.3 = (f32[64]{0:T(128)S(1)}, f32[64]{0:T(128)}, u32[]{:S(2)}) copy-start(f32[64]{0:T(128)} %param.14) | copy-start | bytes 772
  7.2 82.8 %copy-start.4 = (f32[64]{0:T(128)S(1)}, f32[64]{0:T(128)}, u32[]{:S(2)}) copy-start(f32[64]{0:T(128)} %param.13) | copy-start | bytes 772
  7.2 82.8 %copy-start.2 = (s32[64,768]{1,0:T(8,128)S(1)}, s32[64,768]{1,0:T(8,128)}, u32[]{:S(2)}) copy-start(s32[64,768]{1,0:T(8,128)} %param.9) | copy-start | bytes 589828
  7.2 82.8 %all-reduce.4.cloned.1.call-start = ((), (), s32[]{:S(2)}) async-start(), calls=%async_computation | async-start | bytes 393216 | tf_op jit(solution)/shard_map/psum | solution.py:18
  17.1 156.8 %all-reduce.6.cloned.1.call-start = ((), (), s32[]{:S(2)}) async-start(), calls=%async_computation.1 | async-start | bytes 393216 | tf_op jit(solution)/shard_map/psum | solution.py:18
  90.0 10.0 %copy-start = (bf16[768,8192]{1,0:T(8,128)(2,1)S(1)}, bf16[768,8192]{1,0:T(8,128)(2,1)}, u32[]{:S(2)}) copy-start(bf16[768,8192]{1,0:T(8,128)(2,1)} %param.8) | copy-start | bytes 37748740
  104.7 130.5 %all-reduce.8.cloned.1.call-start = ((), (), s32[]{:S(2)}) async-start(), calls=%async_computation.2 | async-start | bytes 4194304 | tf_op jit(solution)/shard_map/psum | solution.py:24
  184.5 0.7 copy-start.5
  184.5 50.6 %copy-start.1 = (f32[64,8192]{1,0:T(8,128)S(1)}, f32[64,8192]{1,0:T(8,128)}, u32[]{:S(2)}) copy-start(f32[64,8192]{1,0:T(8,128)} %get-tuple-element.7) | copy-start | bytes 6291460
Sparse Core Ops, SparseCore 0:
  17.2 72.7 all-reduce.3
  104.8 69.1 all-reduce.5
  184.7 50.4 all-reduce.7
where the time goes:
time: 246 us
  waiting for transfers between devices  192 us (78%)
  matrix products  34.2 us (14%)
  between operations  13.8 us (6%)
  other arithmetic  4.17 us (2%)
    psum x2, waiting for transfers between devices, per_device(): margin = lax.psum(partial_margin, 'feat')  142 us
    psum x1, waiting for transfers between devices, per_device(): total = lax.psum(x + dual, 'rows')  50 us
    dot_general x2, matrix products, per_device(): grad = jnp.dot(resid, design, preferred_element_type=jnp.float32)  19.7 us
    dot_general x2, matrix products, per_device(): lax.dot_general(xb, design, (((1,), (1,)), ((), ())), preferred_element_t...  14.5 us
  transfers between devices with their start and end apart: 3, of which 3 were waited for; matrix products, arithmetic and copies ran while one was open for 0% of the time, Pallas kernels for 0%

commit v1 on v0

v1 whole, which is shorter than its diff:
```python
import jax
import jax.numpy as jnp
from jax import lax
from jax.sharding import PartitionSpec as P

CHUNKS = 4


def exchange(value, axis, mask):
    n = lax.axis_size(axis)
    return lax.ppermute(value, axis, [(i, i ^ mask) for i in range(n)])


def sum_over_rows(value, wire):
    n = lax.axis_size("rows")
    if n & (n - 1):
        return lax.psum(value, "rows")
    half = value.shape[1] // 2
    odd = (lax.axis_index("rows") & 1) == 1
    low, high = value[:, :half], value[:, half:]
    mine = jnp.where(odd, high, low)
    other = jnp.where(odd, low, high)
    mine = mine + exchange(other.astype(wire), "rows", 1).astype(jnp.float32)
    mask = 2
    while mask < n:
        sent = mine.astype(wire)
        mine = sent.astype(jnp.float32) + exchange(sent, "rows", mask).astype(jnp.float32)
        mask *= 2
    sent = mine.astype(wire)
    theirs = exchange(sent, "rows", 1).astype(jnp.float32)
    mine = sent.astype(jnp.float32)
    return jnp.concatenate(
        [jnp.where(odd, theirs, mine), jnp.where(odd, mine, theirs)], axis=1
    )


def per_device(design, labels, local_x, dual_u, consensus_z, step_size, rho, penalty):
    x0 = local_x[0]
    dual = dual_u[0]
    z = consensus_z
    tasks, width = x0.shape
    samples = design.shape[0]
    shards = lax.axis_size("feat")
    blocks_count = lax.axis_size("rows")
    part = tasks // shards
    sign = lax.dynamic_slice_in_dim(
        labels, lax.axis_index("feat") * part, part, 0
    ).astype(jnp.float32)
    eta = step_size[:, None]
    pull = eta * rho[:, None]
    keep = 1.0 - pull

    def residual(xb):
        partial = lax.dot_general(
            xb, design, (((1,), (1,)), ((), ())), preferred_element_type=jnp.float32
        )
        got = lax.all_to_all(partial.reshape(shards, part, samples), "feat", 0, 0)
        margin = jnp.sum(got, axis=0)
        resid = (sign * jax.nn.sigmoid(-sign * margin)).astype(jnp.bfloat16)
        spread = jnp.broadcast_to(resid[None], (shards, part, samples))
        return lax.all_to_all(spread, "feat", 0, 0).reshape(tasks, samples)

    start = sum_over_rows(x0 + dual, jnp.float32) / blocks_count

    resid1 = residual(x0.astype(jnp.bfloat16))
    grad1 = jnp.dot(resid1, design, preferred_element_type=jnp.float32)
    x1 = x0 - pull * (x0 - z + dual) + eta * grad1
    resid2 = residual(x1.astype(jnp.bfloat16))

    limit = (penalty / (rho * blocks_count))[:, None]
    step = width // CHUNKS
    xs, zs, us = [], [], []
    for c in range(CHUNKS):
        cut = slice(c * step, (c + 1) * step)
        grad2 = jnp.dot(resid2, design[:, cut], preferred_element_type=jnp.float32)
        x2 = x1[:, cut] - pull * (x1[:, cut] - z[:, cut] + dual[:, cut]) + eta * grad2
        pushed = sum_over_rows(eta * (keep * grad1[:, cut] + grad2), jnp.bfloat16) / blocks_count
        mean = keep * keep * start[:, cut] + pull * (1.0 + keep) * z[:, cut] + pushed
        new_z = mean - jnp.clip(mean, -limit, limit)
        xs.append(x2)
        zs.append(new_z)
        us.append(dual[:, cut] + x2 - new_z)
    cat = lambda parts: jnp.concatenate(parts, axis=1)
    return (cat(xs)[None], cat(zs), cat(us)[None])


def solution(mesh):
    in_specs = (
        P("rows", "feat"),
        P(None, "rows"),
        P("rows", None, "feat"),
        P("rows", None, "feat"),
        P(None, "feat"),
        P(),
        P(),
        P(),
    )
    out_specs = (P("rows", None, "feat"), P(None, "feat"), P("rows", None, "feat"))
    return jax.shard_map(
        per_device, mesh=mesh, in_specs=in_specs, out_specs=out_specs, check_vma=False
    )
```

time: 246 us -> 141 us (0.57)
  waiting for transfers between devices: 192 us -> 57.4 us
  starting transfers between devices: 0.12 us -> 25.5 us
  between operations: 13.8 us -> 1.02 us
  other arithmetic: 4.17 us -> 11.5 us
  matrix products: 34.2 us -> 41 us
    psum x3 -> x0, waiting for transfers between devices: 192 us -> none  [the longest x2 142 us: per_device(): margin = lax.psum(partial_margin, 'feat')]
    ppermute x0 -> x15, waiting for transfers between devices: none -> 30.5 us  [exchange(): return lax.ppermute(value, axis, [(i, i ^ mask) for i in range(n)])]
    all_to_all x0 -> x4, waiting for transfers between devices: none -> 26.9 us  [the longest x2 15.7 us: residual(): got = lax.all_to_all(partial.reshape(shards, part, samples), 'feat', 0, 0)]
    all_to_all x0 -> x4, starting transfers between devices: none -> 17.6 us  [the longest x2 10.7 us: residual(): got = lax.all_to_all(partial.reshape(shards, part, samples), 'feat', 0, 0)]
    ppermute x0 -> x15, starting transfers between devices: none -> 7.97 us  [exchange(): return lax.ppermute(value, axis, [(i, i ^ mask) for i in range(n)])]
    dot_general x4 -> x7, matrix products: 34.2 us -> 41 us  [the longest x2 19 us: residual(): lax.dot_general(xb, design, (((1,), (1,)), ((), ())), preferred_element_t...]
    select_n x0 -> x6, other arithmetic: none -> 2.99 us  [the longest x1 2.62 us: sum_over_rows(): other = jnp.where(odd, low, high)]
  transfers between devices with their start and end apart: 3 -> 19, of which waited for: 3 -> 9; matrix products, arithmetic and copies ran while one was open for 0% -> 10% of each run, Pallas kernels for 0% -> 0%
where the time goes in v1:
time: 141 us; the launch traced here: 140 us
  waiting for transfers between devices  57.4 us (41%)
  matrix products  41 us (29%)
  starting transfers between devices  25.5 us (18%)
  other arithmetic  11.5 us (8%)
  local copies, waits for them, and re-layouts  3.35 us (2%)
    ppermute x15, waiting for transfers between devices, exchange(): return lax.ppermute(value, axis, [(i, i ^ mask) for i in range(n)])  30.5 us
    dot_general x2, matrix products, residual(): lax.dot_general(xb, design, (((1,), (1,)), ((), ())), preferred_element_t...  19 us
    all_to_all x2, waiting for transfers between devices, residual(): got = lax.all_to_all(partial.reshape(shards, part, samples), 'feat', 0, 0)  15.7 us
    all_to_all x2, waiting for transfers between devices, residual(): return lax.all_to_all(spread, 'feat', 0, 0).reshape(tasks, samples)  11.3 us
    dot_general x4, matrix products, per_device(): grad2 = jnp.dot(resid2, design[:, cut], preferred_element_type=jnp.float32)  11.1 us
    dot_general x1, matrix products, per_device(): grad1 = jnp.dot(resid1, design, preferred_element_type=jnp.float32)  10.9 us
    all_to_all x2, starting transfers between devices, residual(): got = lax.all_to_all(partial.reshape(shards, part, samples), 'feat', 0, 0)  10.7 us
    ppermute x15, starting transfers between devices, exchange(): return lax.ppermute(value, axis, [(i, i ^ mask) for i in range(n)])  7.97 us
  transfers between devices with their start and end apart: 19, of which 9 were waited for; matrix products, arithmetic and copies ran while one was open for 10% of the time, Pallas kernels for 0%

profile of v1, /device:TPU:0, one launch (start us, length us, event | category | flops | bytes accessed | tf_op | source)
XLA Modules:
  0.0 139.8 jit_solution(7079306394807142871)
XLA Ops:
  0.7 9.8 %fusion = f32[8,8,768]{2,1,0:T(8,128)} fusion(bf16[768,8192]{1,0:T(8,128)(2,1)} %param.8, f32[1,64,8192]{2,1,0:T(8,128)} %param.10), kind=kOutput, calls=%fused_computation | convolution fusion | flops 805830656 | bytes 14876672 | tf_op jit(solution)/shard_map/dot_general | solution.py:54
  10.5 7.3 %all-to-all-start = ((f32[8,8,768]{2,1,0:T(8,128)}), f32[8,8,768]{2,1,0:T(8,128)S(1)}, u32[]{:S(2)}, u32[]{:S(2)}) async-start(f32[8,8,768]{2,1,0:T(8,128)} %fusion), calls=%async_computation | async-start | bytes 393216 | tf_op jit(solution)/shard_map/all_to_all | solution.py:57
  17.8 8.0 %all-to-all-done = f32[8,8,768]{2,1,0:T(8,128)S(1)} async-done(((f32[8,8,768]{2,1,0:T(8,128)}), f32[8,8,768]{2,1,0:T(8,128)S(1)}, u32[]{:S(2)}, u32[]{:S(2)}) %all-to-all-start) | async-done | bytes 196640 | tf_op jit(solution)/shard_map/all_to_all | solution.py:57
  27.2 3.4 %all-to-all-start.1 = ((bf16[8,8,768]{2,1,0:T(8,128)(2,1)}), bf16[8,8,768]{2,1,0:T(8,128)(2,1)S(1)}, u32[]{:S(2)}, u32[]{:S(2)}) async-start(bf16[8,8,768]{2,1,0:T(8,128)(2,1)} %broadcast_in_dim.8), calls=%async_computation.1 | async-start | bytes 196608 | tf_op jit(solution)/shard_map/all_to_all | solution.py:61
  30.6 7.0 %all-to-all-done.1 = bf16[8,8,768]{2,1,0:T(8,128)(2,1)S(1)} async-done(((bf16[8,8,768]{2,1,0:T(8,128)(2,1)}), bf16[8,8,768]{2,1,0:T(8,128)(2,1)S(1)}, u32[]{:S(2)}, u32[]{:S(2)}) %all-to-all-start.1) | async-done | bytes 98336 | tf_op jit(solution)/shard_map/all_to_all | solution.py:61
  37.6 10.9 %bitcast_add_fusion = (f32[64,8192]{1,0:T(8,128)}, f32[64,8192]{1,0:T(8,128)S(1)}, f32[64,8192]{1,0:T(8,128)}) fusion(f32[1,64,8192]{2,1,0:T(8,128)} %param.10, f32[1,64,8192]{2,1,0:T(8,128)} %param.11, f32[64]{0:T(128)S(1)} %copy-done.3, f32[64,8192]{1,0:T(8,128)} %param.12, f32[64]{0:T(128)S(1)} %get-tuple-element.16, bf16[768,8192]{1,0:T(8,128)(2,1)} %param.8, ...), kind=kOutput, calls=%fused_computation.14 | convolution fusion | flops 808976384 | bytes 25264640 | tf_op jit(solution)/shard_map/dot_general | solution.py:66
  48.5 9.2 %convolution_bitcast_fusion = f32[8,8,768]{2,1,0:T(8,128)} fusion(bf16[768,8192]{1,0:T(8,128)(2,1)} %param.8, f32[64,8192]{1,0:T(8,128)S(1)} %get-tuple-element.20), kind=kOutput, calls=%fused_computation.20 | convolution fusion | flops 805830656 | bytes 14876672 | tf_op jit(solution)/shard_map/dot_general | solution.py:54
  57.7 3.4 %all-to-all-start.2 = ((f32[8,8,768]{2,1,0:T(8,128)}), f32[8,8,768]{2,1,0:T(8,128)S(1)}, u32[]{:S(2)}, u32[]{:S(2)}) async-start(f32[8,8,768]{2,1,0:T(8,128)} %convolution_bitcast_fusion), calls=%async_computation.2 | async-start | bytes 393216 | tf_op jit(solution)/shard_map/all_to_all | solution.py:57
  61.1 7.7 %all-to-all-done.2 = f32[8,8,768]{2,1,0:T(8,128)S(1)} async-done(((f32[8,8,768]{2,1,0:T(8,128)}), f32[8,8,768]{2,1,0:T(8,128)S(1)}, u32[]{:S(2)}, u32[]{:S(2)}) %all-to-all-start.2) | async-done | bytes 196640 | tf_op jit(solution)/shard_map/all_to_all | solution.py:57
  70.2 3.5 %all-to-all-start.3 = ((bf16[8,8,768]{2,1,0:T(8,128)(2,1)}), bf16[8,8,768]{2,1,0:T(8,128)(2,1)S(1)}, u32[]{:S(2)}, u32[]{:S(2)}) async-start(bf16[8,8,768]{2,1,0:T(8,128)(2,1)} %broadcast_in_dim.9), calls=%async_computation.3 | async-start | bytes 196608 | tf_op jit(solution)/shard_map/all_to_all | solution.py:61
  73.8 2.6 %slice_select_fusion = f32[64,4096]{1,0:T(8,128)} fusion(f32[64,8192]{1,0:T(8,128)} %get-tuple-element.19, pred[]{:T(512)S(6)} %eq.2), kind=kLoop, calls=%fused_computation.25 | loop fusion | flops 262144 | bytes 3145729 | tf_op jit(solution)/shard_map/jit(_where)/select_n | solution.py:22
  76.4 4.3 %all-to-all-done.3 = bf16[8,8,768]{2,1,0:T(8,128)(2,1)S(1)} async-done(((bf16[8,8,768]{2,1,0:T(8,128)(2,1)}), bf16[8,8,768]{2,1,0:T(8,128)(2,1)S(1)}, u32[]{:S(2)}, u32[]{:S(2)}) %all-to-all-start.3) | async-done | bytes 98336 | tf_op jit(solution)/shard_map/all_to_all | solution.py:61
  80.6 2.5 %fusion.2 = f32[64,2048]{1,0:T(8,128)S(1)} fusion(bf16[768,8192]{1,0:T(8,128)(2,1)} %param.8, bf16[8,8,768]{2,1,0:T(8,128)(2,1)S(1)} %all-to-all-done.3), kind=kOutput, calls=%fused_computation.2 | convolution fusion | flops 201326592 | bytes 3768320 | tf_op jit(solution)/shard_map/dot_general | solution.py:75
  83.2 2.5 %fusion.4 = f32[64,2048]{1,0:T(8,128)S(1)} fusion(bf16[768,8192]{1,0:T(8,128)(2,1)} %param.8, bf16[8,8,768]{2,1,0:T(8,128)(2,1)S(1)} %all-to-all-done.3), kind=kOutput, calls=%fused_computation.4 | convolution fusion | flops 201326592 | bytes 3768320 | tf_op jit(solution)/shard_map/dot_general | solution.py:75
  85.8 2.5 %fusion.6 = f32[64,2048]{1,0:T(8,128)S(1)} fusion(bf16[768,8192]{1,0:T(8,128)(2,1)} %param.8, bf16[8,8,768]{2,1,0:T(8,128)(2,1)S(1)} %all-to-all-done.3), kind=kOutput, calls=%fused_computation.6 | convolution fusion | flops 201326592 | bytes 3768320 | tf_op jit(solution)/shard_map/dot_general | solution.py:75
  88.3 3.5 %fusion.29 = (f32[64,2048]{1,0:T(8,128)S(1)}, f32[64,2048]{1,0:T(8,128)S(1)}, f32[64,2048]{1,0:T(8,128)S(1)}, f32[64,2048]{1,0:T(8,128)S(1)}, f32[64,2048]{1,0:T(8,128)S(1)}) fusion(f32[64,8192]{1,0:T(8,128)} %get-tuple-element.39, f32[64]{0:T(128)S(1)} %get-tuple-element.36, f32[64]{0:T(128)S(1)} %copy-done.3, f32[64,2048]{1,0:T(8,128)S(1)} %fusion.2, ...), kind=kOutput, calls=%fused_computation.46 | convolution fusion | flops 202899456 | bytes 9536000 | tf_op jit(solution)/shard_map/dot_general | solution.py:75
  93.3 1.6 %collective-permute-start.4 = (bf16[64,1024]{1,0:T(8,128)(2,1)S(1)}, bf16[64,1024]{1,0:T(8,128)(2,1)S(1)}, u32[]{:S(2)}, u32[]{:S(2)}) collective-permute-start(bf16[64,1024]{1,0:T(8,128)(2,1)S(1)} %add_convert_fusion.7), channel_id=1, source_target_pairs={{0,16},{8,24},{16,0},{24,8},{1,17},{9,25},{17,1},{25,9},{2,18},{10... | collective-permute-start | bytes 393224 | tf_op jit(solution)/shard_map/ppermute | solution.py:11
  95.7 1.6 %collective-permute-start.1 = (f32[64,4096]{1,0:T(8,128)S(1)}, f32[64,4096]{1,0:T(8,128)S(1)}, u32[]{:S(2)}, u32[]{:S(2)}) collective-permute-start(f32[64,4096]{1,0:T(8,128)S(1)} %select_add_fusion), channel_id=1, source_target_pairs={{0,16},{8,24},{16,0},{24,8},{1,17},{9,25},{17,1},{25,9},{2,18},{10... | collective-permute-start | bytes 3145736 | tf_op jit(solution)/shard_map/ppermute | solution.py:11
  97.9 1.6 %collective-permute-start.13 = (bf16[64,1024]{1,0:T(8,128)(2,1)S(1)}, bf16[64,1024]{1,0:T(8,128)(2,1)S(1)}, u32[]{:S(2)}, u32[]{:S(2)}) collective-permute-start(bf16[64,1024]{1,0:T(8,128)(2,1)S(1)} %add_convert_fusion.1), channel_id=1, source_target_pairs={{0,16},{8,24},{16,0},{24,8},{1,17},{9,25},{17,1},{25,9},{2,18},{10... | collective-permute-start | bytes 393224 | tf_op jit(solution)/shard_map/ppermute | solution.py:11
  99.8 2.7 %collective-permute-done.7 = bf16[64,1024]{1,0:T(8,128)(2,1)S(1)} collective-permute-done((bf16[64,1024]{1,0:T(8,128)(2,1)S(1)}, bf16[64,1024]{1,0:T(8,128)(2,1)S(1)}, u32[]{:S(2)}, u32[]{:S(2)}) %collective-permute-start.7) | collective-permute-done | bytes 131104 | tf_op jit(solution)/shard_map/ppermute | solution.py:11
  102.6 25.2 %collective-permute-done.10 = bf16[64,1024]{1,0:T(8,128)(2,1)S(1)} collective-permute-done((bf16[64,1024]{1,0:T(8,128)(2,1)S(1)}, bf16[64,1024]{1,0:T(8,128)(2,1)S(1)}, u32[]{:S(2)}, u32[]{:S(2)}) %collective-permute-start.10) | collective-permute-done | bytes 131104 | tf_op jit(solution)/shard_map/ppermute | solution.py:11
  131.7 1.4 copy-done.1
  135.9 1.5 %pad_maximum_fusion = f32[64,8192]{1,0:T(8,128)} fusion(f32[64,2048]{1,0:T(8,128)S(1)} %get-tuple-element.13, f32[64,2048]{1,0:T(8,128)S(1)} %get-tuple-element.10, f32[64,2048]{1,0:T(8,128)S(1)} %get-tuple-element.7, f32[64,2048]{1,0:T(8,128)S(1)} %get-tuple-element.4), kind=kLoop, calls=%fused_computation.12 | loop fusion | flops 1572864 | bytes 4194304 | tf_op jit(solution)/shard_map/concatenate | solution.py:83
  137.4 2.4 %maximum_bitcast_fusion = (f32[1,64,8192]{2,1,0:T(8,128)}, f32[1,64,8192]{2,1,0:T(8,128)}) fusion(f32[64,2048]{1,0:T(8,128)S(1)} %get-tuple-element.14, f32[64,2048]{1,0:T(8,128)S(1)} %get-tuple-element.11, f32[64,2048]{1,0:T(8,128)S(1)} %get-tuple-element.8, f32[64,2048]{1,0:T(8,128)S(1)} %get-tuple-element.5, f32[64,2048]{1,0:T(8,128)S(1)} %get-tuple-element.12, ...), kind=kLoop, calls=%fused_computation.10 | loop fusion | flops 3145728 | bytes 8388608 | tf_op jit(solution)/shard_map/broadcast_in_dim | solution.py:84
  (68 shorter events, 12.9 us)
Async XLA Ops:
  0.6 29.9 %copy-start.3 = (f32[64]{0:T(128)S(1)}, f32[64]{0:T(128)}, u32[]{:S(2)}) copy-start(f32[64]{0:T(128)} %param.13) | copy-start | bytes 772
  0.6 29.9 %copy-start.4 = (f32[64]{0:T(128)S(1)}, f32[64]{0:T(128)}, u32[]{:S(2)}) copy-start(f32[64]{0:T(128)} %param.14) | copy-start | bytes 772
  0.7 29.9 %copy-start.5 = (f32[64]{0:T(128)S(1)}, f32[64]{0:T(128)}, u32[]{:S(2)}) copy-start(f32[64]{0:T(128)} %param.15) | copy-start | bytes 772
  10.5 15.2 %all-to-all-start = ((f32[8,8,768]{2,1,0:T(8,128)}), f32[8,8,768]{2,1,0:T(8,128)S(1)}, u32[]{:S(2)}, u32[]{:S(2)}) async-start(f32[8,8,768]{2,1,0:T(8,128)} %fusion), calls=%async_computation | async-start | bytes 393216 | tf_op jit(solution)/shard_map/all_to_all | solution.py:57
  27.2 10.4 %all-to-all-start.1 = ((bf16[8,8,768]{2,1,0:T(8,128)(2,1)}), bf16[8,8,768]{2,1,0:T(8,128)(2,1)S(1)}, u32[]{:S(2)}, u32[]{:S(2)}) async-start(bf16[8,8,768]{2,1,0:T(8,128)(2,1)} %broadcast_in_dim.8), calls=%async_computation.1 | async-start | bytes 196608 | tf_op jit(solution)/shard_map/all_to_all | solution.py:61
  57.7 11.1 %all-to-all-start.2 = ((f32[8,8,768]{2,1,0:T(8,128)}), f32[8,8,768]{2,1,0:T(8,128)S(1)}, u32[]{:S(2)}, u32[]{:S(2)}) async-start(f32[8,8,768]{2,1,0:T(8,128)} %convolution_bitcast_fusion), calls=%async_computation.2 | async-start | bytes 393216 | tf_op jit(solution)/shard_map/all_to_all | solution.py:57
  70.2 10.4 %all-to-all-start.3 = ((bf16[8,8,768]{2,1,0:T(8,128)(2,1)}), bf16[8,8,768]{2,1,0:T(8,128)(2,1)S(1)}, u32[]{:S(2)}, u32[]{:S(2)}) async-start(bf16[8,8,768]{2,1,0:T(8,128)(2,1)} %broadcast_in_dim.9), calls=%async_computation.3 | async-start | bytes 196608 | tf_op jit(solution)/shard_map/all_to_all | solution.py:61
  76.4 19.1 %collective-permute-start = (f32[64,4096]{1,0:T(8,128)}, f32[64,4096]{1,0:T(8,128)S(1)}, u32[]{:S(2)}, u32[]{:S(2)}) collective-permute-start(f32[64,4096]{1,0:T(8,128)} %slice_select_fusion), channel_id=1, source_target_pairs={{0,8},{8,0},{16,24},{24,16},{1,9},{9,1},{17,25},{25,17},{2,10},{10... | collective-permute-start | bytes 3145736 | tf_op jit(solution)/shard_map/ppermute | solution.py:11
  91.8 3.7 %copy-start = (f32[64,8192]{1,0:T(8,128)S(1)}, f32[64,8192]{1,0:T(8,128)}, u32[]{:S(2)}) copy-start(f32[64,8192]{1,0:T(8,128)} %get-tuple-element.19) | copy-start | bytes 6291460
  91.8 1.4 %collective-permute-start.3 = (bf16[64,1024]{1,0:T(8,128)(2,1)S(1)}, bf16[64,1024]{1,0:T(8,128)(2,1)S(1)}, u32[]{:S(2)}, u32[]{:S(2)}) collective-permute-start(bf16[64,1024]{1,0:T(8,128)(2,1)S(1)} %select_convert_fusion.3), channel_id=1, source_target_pairs={{0,8},{8,0},{16,24},{24,16},{1,9},{9,1},{17,25},{25,17},{2,10},{10... | collective-permute-start | bytes 393224 | tf_op jit(solution)/shard_map/ppermute | solution.py:11
  91.9 2.9 %collective-permute-start.6 = (bf16[64,1024]{1,0:T(8,128)(2,1)S(1)}, bf16[64,1024]{1,0:T(8,128)(2,1)S(1)}, u32[]{:S(2)}, u32[]{:S(2)}) collective-permute-start(bf16[64,1024]{1,0:T(8,128)(2,1)S(1)} %select_convert_fusion.2), channel_id=1, source_target_pairs={{0,8},{8,0},{16,24},{24,16},{1,9},{9,1},{17,25},{25,17},{2,10},{10... | collective-permute-start | bytes 393224 | tf_op jit(solution)/shard_map/ppermute | solution.py:11
  92.5 4.7 %collective-permute-start.9 = (bf16[64,1024]{1,0:T(8,128)(2,1)S(1)}, bf16[64,1024]{1,0:T(8,128)(2,1)S(1)}, u32[]{:S(2)}, u32[]{:S(2)}) collective-permute-start(bf16[64,1024]{1,0:T(8,128)(2,1)S(1)} %select_convert_fusion.1), channel_id=1, source_target_pairs={{0,8},{8,0},{16,24},{24,16},{1,9},{9,1},{17,25},{25,17},{2,10},{10... | collective-permute-start | bytes 393224 | tf_op jit(solution)/shard_map/ppermute | solution.py:11
  92.6 5.3 %collective-permute-start.12 = (bf16[64,1024]{1,0:T(8,128)(2,1)S(1)}, bf16[64,1024]{1,0:T(8,128)(2,1)S(1)}, u32[]{:S(2)}, u32[]{:S(2)}) collective-permute-start(bf16[64,1024]{1,0:T(8,128)(2,1)S(1)} %select_convert_fusion), channel_id=1, source_target_pairs={{0,8},{8,0},{16,24},{24,16},{1,9},{9,1},{17,25},{25,17},{2,10},{10... | collective-permute-start | bytes 393224 | tf_op jit(solution)/shard_map/ppermute | solution.py:11
  93.3 6.4 %collective-permute-start.4 = (bf16[64,1024]{1,0:T(8,128)(2,1)S(1)}, bf16[64,1024]{1,0:T(8,128)(2,1)S(1)}, u32[]{:S(2)}, u32[]{:S(2)}) collective-permute-start(bf16[64,1024]{1,0:T(8,128)(2,1)S(1)} %add_convert_fusion.7), channel_id=1, source_target_pairs={{0,16},{8,24},{16,0},{24,8},{1,17},{9,25},{17,1},{25,9},{2,18},{10... | collective-permute-start | bytes 393224 | tf_op jit(solution)/shard_map/ppermute | solution.py:11
  94.9 7.6 %collective-permute-start.7 = (bf16[64,1024]{1,0:T(8,128)(2,1)S(1)}, bf16[64,1024]{1,0:T(8,128)(2,1)S(1)}, u32[]{:S(2)}, u32[]{:S(2)}) collective-permute-start(bf16[64,1024]{1,0:T(8,128)(2,1)S(1)} %add_convert_fusion.5), channel_id=1, source_target_pairs={{0,16},{8,24},{16,0},{24,8},{1,17},{9,25},{17,1},{25,9},{2,18},{10... | collective-permute-start | bytes 393224 | tf_op jit(solution)/shard_map/ppermute | solution.py:11
  95.7 32.2 %collective-permute-start.1 = (f32[64,4096]{1,0:T(8,128)S(1)}, f32[64,4096]{1,0:T(8,128)S(1)}, u32[]{:S(2)}, u32[]{:S(2)}) collective-permute-start(f32[64,4096]{1,0:T(8,128)S(1)} %select_add_fusion), channel_id=1, source_target_pairs={{0,16},{8,24},{16,0},{24,8},{1,17},{9,25},{17,1},{25,9},{2,18},{10... | collective-permute-start | bytes 3145736 | tf_op jit(solution)/shard_map/ppermute | solution.py:11
  97.3 30.5 %collective-permute-start.10 = (bf16[64,1024]{1,0:T(8,128)(2,1)S(1)}, bf16[64,1024]{1,0:T(8,128)(2,1)S(1)}, u32[]{:S(2)}, u32[]{:S(2)}) collective-permute-start(bf16[64,1024]{1,0:T(8,128)(2,1)S(1)} %add_convert_fusion.3), channel_id=1, source_target_pairs={{0,16},{8,24},{16,0},{24,8},{1,17},{9,25},{17,1},{25,9},{2,18},{10... | collective-permute-start | bytes 393224 | tf_op jit(solution)/shard_map/ppermute | solution.py:11
  97.9 31.9 %collective-permute-start.13 = (bf16[64,1024]{1,0:T(8,128)(2,1)S(1)}, bf16[64,1024]{1,0:T(8,128)(2,1)S(1)}, u32[]{:S(2)}, u32[]{:S(2)}) collective-permute-start(bf16[64,1024]{1,0:T(8,128)(2,1)S(1)} %add_convert_fusion.1), channel_id=1, source_target_pairs={{0,16},{8,24},{16,0},{24,8},{1,17},{9,25},{17,1},{25,9},{2,18},{10... | collective-permute-start | bytes 393224 | tf_op jit(solution)/shard_map/ppermute | solution.py:11
  99.7 30.2 %collective-permute-start.5 = (bf16[64,1024]{1,0:T(8,128)(2,1)S(1)}, bf16[64,1024]{1,0:T(8,128)(2,1)S(1)}, u32[]{:S(2)}, u32[]{:S(2)}) collective-permute-start(bf16[64,1024]{1,0:T(8,128)(2,1)S(1)} %add_convert_fusion.6), channel_id=1, source_target_pairs={{0,8},{8,0},{16,24},{24,16},{1,9},{9,1},{17,25},{25,17},{2,10},{10... | collective-permute-start | bytes 393224 | tf_op jit(solution)/shard_map/ppermute | solution.py:11
  102.5 27.4 %collective-permute-start.8 = (bf16[64,1024]{1,0:T(8,128)(2,1)S(1)}, bf16[64,1024]{1,0:T(8,128)(2,1)S(1)}, u32[]{:S(2)}, u32[]{:S(2)}) collective-permute-start(bf16[64,1024]{1,0:T(8,128)(2,1)S(1)} %add_convert_fusion.4), channel_id=1, source_target_pairs={{0,8},{8,0},{16,24},{24,16},{1,9},{9,1},{17,25},{25,17},{2,10},{10... | collective-permute-start | bytes 393224 | tf_op jit(solution)/shard_map/ppermute | solution.py:11
  127.8 2.2 %collective-permute-start.11 = (bf16[64,1024]{1,0:T(8,128)(2,1)S(1)}, bf16[64,1024]{1,0:T(8,128)(2,1)S(1)}, u32[]{:S(2)}, u32[]{:S(2)}) collective-permute-start(bf16[64,1024]{1,0:T(8,128)(2,1)S(1)} %add_convert_fusion.2), channel_id=1, source_target_pairs={{0,8},{8,0},{16,24},{24,16},{1,9},{9,1},{17,25},{25,17},{2,10},{10... | collective-permute-start | bytes 393224 | tf_op jit(solution)/shard_map/ppermute | solution.py:11
  128.0 3.3 %collective-permute-start.2 = (f32[64,4096]{1,0:T(8,128)S(1)}, f32[64,4096]{1,0:T(8,128)S(1)}, u32[]{:S(2)}, u32[]{:S(2)}) collective-permute-start(f32[64,4096]{1,0:T(8,128)S(1)} %add.144), channel_id=1, source_target_pairs={{0,8},{8,0},{16,24},{24,16},{1,9},{9,1},{17,25},{25,17},{2,10},{10... | collective-permute-start | bytes 3145736 | tf_op jit(solution)/shard_map/ppermute | solution.py:11
  129.8 1.4 %collective-permute-start.14 = (bf16[64,1024]{1,0:T(8,128)(2,1)S(1)}, bf16[64,1024]{1,0:T(8,128)(2,1)S(1)}, u32[]{:S(2)}, u32[]{:S(2)}) collective-permute-start(bf16[64,1024]{1,0:T(8,128)(2,1)S(1)} %add_convert_fusion), channel_id=1, source_target_pairs={{0,8},{8,0},{16,24},{24,16},{1,9},{9,1},{17,25},{25,17},{2,10},{10... | collective-permute-start | bytes 393224 | tf_op jit(solution)/shard_map/ppermute | solution.py:11
  131.5 2.2 %copy-start.2 = (f32[64,8192]{1,0:T(8,128)S(1)}, f32[64,8192]{1,0:T(8,128)}, u32[]{:S(2)}) copy-start(f32[64,8192]{1,0:T(8,128)} %param.12) | copy-start | bytes 6291460
  (1 other events, 1.6 us)

commit v2 on v0

v2 whole, which is shorter than its diff:
```python
import functools

import jax
import jax.numpy as jnp
from jax import lax
from jax.experimental import pallas as pl
from jax.experimental.pallas import tpu as pltpu
from jax.sharding import PartitionSpec as P

BF16 = jnp.bfloat16
F32 = jnp.float32
CHUNKS = 4
PARAMS = pltpu.CompilerParams(vmem_limit_bytes=32 * 1024 * 1024)


def exchange(value, axis, mask):
    n = lax.axis_size(axis)
    return lax.ppermute(value, axis, [(i, i ^ mask) for i in range(n)])


def sum_over(value, axis, first=1):
    n = lax.axis_size(axis)
    mask = first
    total = value.astype(F32)
    while mask < n:
        sent = total.astype(value.dtype)
        total = sent.astype(F32) + exchange(sent, axis, mask).astype(F32)
        mask *= 2
    return total


def nt(a, b):
    return lax.dot_general(a, b, (((1,), (1,)), ((), ())), preferred_element_type=F32)


def cost(flops, nbytes):
    return pl.CostEstimate(flops=flops // 64, bytes_accessed=nbytes // 64, transcendentals=0)


def margin_kernel(x_ref, a_ref, out_ref, acc_ref):
    @pl.when(pl.program_id(0) == 0)
    def _():
        acc_ref[...] = jnp.zeros_like(acc_ref)

    acc_ref[...] += nt(x_ref[...].astype(BF16), a_ref[...])

    @pl.when(pl.program_id(0) == pl.num_programs(0) - 1)
    def _():
        out_ref[...] = acc_ref[...].astype(BF16)


def margins(x, design, block):
    tasks, width = x.shape
    samples = design.shape[0]
    return pl.pallas_call(
        margin_kernel,
        grid=(width // block,),
        in_specs=[
            pl.BlockSpec((tasks, block), lambda i: (0, i)),
            pl.BlockSpec((samples, block), lambda i: (0, i)),
        ],
        out_specs=pl.BlockSpec((tasks, samples), lambda i: (0, 0)),
        out_shape=jax.ShapeDtypeStruct((tasks, samples), BF16),
        scratch_shapes=[pltpu.VMEM((tasks, samples), F32)],
        compiler_params=PARAMS,
        cost_estimate=cost(2 * tasks * samples * width, 2 * samples * width + 4 * tasks * width),
        name="margins",
    )(x, design)


def turn_kernel(r_ref, eta_ref, pull_ref, x_ref, u_ref, z_ref, a_ref, q_ref, out_ref, acc_ref):
    @pl.when(pl.program_id(0) == 0)
    def _():
        acc_ref[...] = jnp.zeros_like(acc_ref)

    pull = pull_ref[...]
    push = eta_ref[...] * jnp.dot(r_ref[...], a_ref[...], preferred_element_type=F32)
    x = x_ref[...]
    x = x - pull * (x - z_ref[...] + u_ref[...]) + push
    q_ref[...] = (1.0 - pull) * push
    acc_ref[...] += nt(x.astype(BF16), a_ref[...])

    @pl.when(pl.program_id(0) == pl.num_programs(0) - 1)
    def _():
        out_ref[...] = acc_ref[...].astype(BF16)


def turn(resid, eta, pull, x, u, z, design, block):
    tasks, width = x.shape
    samples = design.shape[0]
    column = pl.BlockSpec((tasks, block), lambda i: (0, i))
    scale = pl.BlockSpec((tasks, 1), lambda i: (0, 0))
    whole = pl.BlockSpec((tasks, samples), lambda i: (0, 0))
    return pl.pallas_call(
        turn_kernel,
        grid=(width // block,),
        in_specs=[whole, scale, scale, column, column, column, pl.BlockSpec((samples, block), lambda i: (0, i))],
        out_specs=(column, whole),
        out_shape=(jax.ShapeDtypeStruct((tasks, width), F32), jax.ShapeDtypeStruct((tasks, samples), BF16)),
        scratch_shapes=[pltpu.VMEM((tasks, samples), F32)],
        compiler_params=PARAMS,
        cost_estimate=cost(4 * tasks * samples * width, 2 * samples * width + 16 * tasks * width),
        name="turn",
    )(resid, eta, pull, x, u, z, design)


def push_kernel(has_buffer, has_sum, *refs):
    refs = list(refs[1:])
    if has_buffer:
        refs.pop(0)
    r_ref, eta_ref, pull_ref, x_ref, u_ref, z_ref, q_ref, a_ref = refs[:8]
    rest = refs[8:]
    x_out, h_out = rest[-2:]
    keep = 1.0 - pull_ref[...]
    push = q_ref[...] + eta_ref[...] * jnp.dot(r_ref[...], a_ref[...], preferred_element_type=F32)
    u, z = u_ref[...], z_ref[...]
    x_out[...] = z - u + keep * keep * (x_ref[...] - z + u) + push
    if has_sum:
        push = push + rest[0][...].astype(F32)
    h_out[...] = push.astype(BF16)


def push(parity, buffer, resid, eta, pull, x, u, z, q, design, received, mine, chunk, count, block):
    tasks, width = x.shape
    samples = design.shape[0]
    chunk_width = width // 2 // count
    steps = chunk_width // block
    half_blocks = width // 2 // block

    def place(i, p):
        side = p[0] if mine else 1 - p[0]
        return (0, side * half_blocks + chunk * steps + i)

    column = pl.BlockSpec((tasks, block), place)
    local = pl.BlockSpec((tasks, block), lambda i, p: (0, i))
    scale = pl.BlockSpec((tasks, 1), lambda i, p: (0, 0))
    whole = pl.BlockSpec((tasks, samples), lambda i, p: (0, 0))
    in_specs = [whole, scale, scale, column, column, column, column, pl.BlockSpec((samples, block), place)]
    args = [resid, eta, pull, x, u, z, q, design]
    aliases = {}
    if buffer is not None:
        in_specs.insert(0, pl.BlockSpec(memory_space=pl.ANY))
        args.insert(0, buffer)
        aliases = {1: 0}
    if received is not None:
        in_specs.append(local)
        args.append(received)
    return pl.pallas_call(
        functools.partial(push_kernel, buffer is not None, received is not None),
        grid_spec=pltpu.PrefetchScalarGridSpec(
            num_scalar_prefetch=1,
            grid=(steps,),
            in_specs=in_specs,
            out_specs=(column, local),
        ),
        out_shape=(jax.ShapeDtypeStruct((tasks, width), F32), jax.ShapeDtypeStruct((tasks, chunk_width), BF16)),
        input_output_aliases=aliases,
        compiler_params=PARAMS,
        cost_estimate=cost(2 * tasks * samples * chunk_width, 2 * samples * chunk_width + 24 * tasks * chunk_width),
        name="push",
    )(parity, *args)


def final_kernel(blocks_count, has_buffers, *refs):
    refs = list(refs[1:])
    if has_buffers:
        refs = refs[2:]
    pull_ref, limit_ref, x_ref, u_ref, z_ref, s_mine, s_theirs, h_mine, h_theirs, z_out, u_out = refs
    pull, limit = pull_ref[...], limit_ref[...]
    keep = 1.0 - pull
    first = pl.program_id(0) == 0
    start = jnp.where(first, s_mine[...], s_theirs[...])
    pushed = jnp.where(first, h_mine[...].astype(F32), h_theirs[...].astype(F32))
    mean = (keep * keep * start + pushed) * (1.0 / blocks_count) + pull * (1.0 + keep) * z_ref[...]
    new_z = mean - jnp.clip(mean, -limit, limit)
    z_out[...] = new_z
    u_out[...] = u_ref[...] + x_ref[...] - new_z


def final(parity, buffers, pull, limit, x, u, z, starts, pushes, chunk, count, blocks_count):
    tasks, width = x.shape
    block = width // 2 // count
    half_blocks = count

    def place(i, p):
        return (0, (p[0] + i - 2 * p[0] * i) * half_blocks + chunk)

    column = pl.BlockSpec((tasks, block), place)
    half = pl.BlockSpec((tasks, block), lambda i, p: (0, chunk))
    local = pl.BlockSpec((tasks, block), lambda i, p: (0, 0))
    scale = pl.BlockSpec((tasks, 1), lambda i, p: (0, 0))
    in_specs = [scale, scale, column, column, column, half, half, local, local]
    args = [pull, limit, x, u, z, *starts, *pushes]
    aliases = {}
    if buffers is not None:
        in_specs = [pl.BlockSpec(memory_space=pl.ANY)] * 2 + in_specs
        args = list(buffers) + args
        aliases = {1: 0, 2: 1}
    out = jax.ShapeDtypeStruct((tasks, width), F32)
    return pl.pallas_call(
        functools.partial(final_kernel, blocks_count, buffers is not None),
        grid_spec=pltpu.PrefetchScalarGridSpec(
            num_scalar_prefetch=1, grid=(2,), in_specs=in_specs, out_specs=(column, column)
        ),
        out_shape=(out, out),
        input_output_aliases=aliases,
        compiler_params=PARAMS,
        cost_estimate=cost(20 * tasks * block, 60 * tasks * block),
        name="final",
    )(parity, *args)


def per_device(design, labels, local_x, dual_u, consensus_z, step_size, rho, penalty):
    x0 = local_x[0]
    dual = dual_u[0]
    z = consensus_z
    tasks, width = x0.shape
    half = width // 2
    blocks_count = lax.axis_size("rows")
    side = lax.axis_index("rows") & 1
    parity = side.astype(jnp.int32)[None]
    sign = labels.astype(F32)
    eta = step_size[:, None]
    pull = eta * rho[:, None]
    limit = (penalty / (rho * blocks_count))[:, None]

    def residual(margin):
        return (sign * jax.nn.sigmoid(-sign * margin)).astype(BF16)

    def side_of(which):
        cut = lambda v: lax.dynamic_slice_in_dim(v, which * half, half, 1)
        return cut(x0) + cut(dual)

    margin1 = margins(x0, design, 1024)
    margin1, here = lax.optimization_barrier((margin1, side))
    start_mine = side_of(here) + exchange(side_of(1 - here), "rows", 1)
    resid1 = residual(sum_over(margin1, "feat"))
    resid1, start_mine = lax.optimization_barrier((resid1, start_mine))

    carried, margin2 = turn(resid1, eta, pull, x0, dual, z, design, 1024)
    start_mine = sum_over(start_mine, "rows", 2)
    resid2 = residual(sum_over(margin2, "feat"))
    resid2, start_mine = lax.optimization_barrier((resid2, start_mine))
    start_theirs = exchange(start_mine, "rows", 1)

    new_x = None
    args = (resid2, eta, pull, x0, dual, z, carried, design)
    block = min(1024, half // CHUNKS)
    received = []
    pieces = []
    for c in range(CHUNKS + 1):
        if c < CHUNKS:
            new_x, other = push(parity, new_x, *args, None, False, c, CHUNKS, block)
            received.append(exchange(other, "rows", 1))
        if c > 0:
            new_x, mine = push(parity, new_x, *args, received[c - 1], True, c - 1, CHUNKS, block)
            pieces.append(sum_over(mine, "rows", 2).astype(BF16))
    results = None
    for c in range(CHUNKS):
        piece = pieces[c]
        if results is not None:
            piece, results = lax.optimization_barrier((piece, results))
        pushes = (piece, exchange(piece, "rows", 1))
        results = final(
            parity, results, pull, limit, new_x, dual, z, (start_mine, start_theirs), pushes, c, CHUNKS, blocks_count
        )
    new_z, new_u = results
    return (new_x[None], new_z, new_u[None])


def solution(mesh):
    in_specs = (
        P("rows", "feat"),
        P(None, "rows"),
        P("rows", None, "feat"),
        P("rows", None, "feat"),
        P(None, "feat"),
        P(),
        P(),
        P(),
    )
    out_specs = (P("rows", None, "feat"), P(None, "feat"), P("rows", None, "feat"))
    return jax.shard_map(
        per_device, mesh=mesh, in_specs=in_specs, out_specs=out_specs, check_vma=False
    )
```

time: 246 us -> 114 us (0.46)
  waiting for transfers between devices: 192 us -> 24.2 us
  matrix products: 34.2 us -> 0 us
  Pallas kernels: 0 us -> 33.9 us
  local copies, waits for them, and re-layouts: 1.54 us -> 25.2 us
  starting transfers between devices: 0.12 us -> 20.8 us
  between operations: 13.8 us -> 0.85 us
  other arithmetic: 4.17 us -> 8.07 us
    psum x3 -> x0, waiting for transfers between devices: 192 us -> none  [the longest x2 142 us: per_device(): margin = lax.psum(partial_margin, 'feat')]
    dot_general x4 -> x0, matrix products: 34.2 us -> none  [the longest x2 19.7 us: per_device(): grad = jnp.dot(resid, design, preferred_element_type=jnp.float32)]
    pallas_call x0 -> x14, Pallas kernels: none -> 33.9 us  [the longest x8 10 us: push(): pl.pallas_call(functools.partial(push_kernel, buffer is not None, receive...]
    ppermute x0 -> x21, waiting for transfers between devices: none -> 24.2 us  [exchange(): return lax.ppermute(value, axis, [(i, i ^ mask) for i in range(n)])]
    unnamed x12 -> x36, local copies, waits for them, and re-layouts: 1.54 us -> 24.9 us
    ppermute x0 -> x21, starting transfers between devices: none -> 20.8 us  [exchange(): return lax.ppermute(value, axis, [(i, i ^ mask) for i in range(n)])]
    add x0 -> x3, other arithmetic: none -> 6.68 us  [the longest x1 2.67 us: per_device(): start_mine = side_of(here) + exchange(side_of(1 - here), 'rows', 1)]
    broadcast_in_dim x1, other arithmetic: 4.16 us -> 0.01 us  [per_device(): limit = (penalty / (rho * blocks_count))[:, None]]
  transfers between devices with their start and end apart: 3 -> 21, of which waited for: 3 -> 11; matrix products, arithmetic and copies ran while one was open for 0% -> 1% of each run, Pallas kernels for 0% -> 21%
where the time goes in v2:
time: 114 us; the launch traced here: 113 us
  Pallas kernels  33.9 us (30%)
  local copies, waits for them, and re-layouts  25.2 us (22%)
  waiting for transfers between devices  24.2 us (21%)
  starting transfers between devices  20.8 us (18%)
  other arithmetic  8.07 us (7%)
    unnamed x36, local copies, waits for them, and re-layouts  24.9 us
    ppermute x21, waiting for transfers between devices, exchange(): return lax.ppermute(value, axis, [(i, i ^ mask) for i in range(n)])  24.2 us
    ppermute x21, starting transfers between devices, exchange(): return lax.ppermute(value, axis, [(i, i ^ mask) for i in range(n)])  20.8 us
    pallas_call x8, Pallas kernels, push(): pl.pallas_call(functools.partial(push_kernel, buffer is not None, receive...  10 us
    pallas_call x4, Pallas kernels, final(): pl.pallas_call(functools.partial(final_kernel, blocks_count, buffers is n...  9.28 us
    pallas_call x1, Pallas kernels, turn(): pl.pallas_call(turn_kernel, grid=(width // block,), in_specs=[whole, scal...  8.69 us
    pallas_call x1, Pallas kernels, margins(): pl.pallas_call(margin_kernel, grid=(width // block,), in_specs=[pl.BlockS...  5.85 us
    add x1, other arithmetic, per_device(): start_mine = side_of(here) + exchange(side_of(1 - here), 'rows', 1)  2.67 us
  transfers between devices with their start and end apart: 21, of which 11 were waited for; matrix products, arithmetic and copies ran while one was open for 1% of the time, Pallas kernels for 21%

profile of v2, /device:TPU:0, one launch (start us, length us, event | category | flops | bytes accessed | tf_op | source)
XLA Modules:
  0.0 113.0 jit_solution(9100041527161986322)
XLA Ops:
  0.6 4.6 %copy-done = bf16[768,8192]{1,0:T(8,128)(2,1)S(1)} copy-done((bf16[768,8192]{1,0:T(8,128)(2,1)S(1)}, bf16[768,8192]{1,0:T(8,128)(2,1)}, u32[]{:S(2)}) %copy-start) | copy-done | bytes 12582936
  6.8 5.8 %margins.1 = bf16[64,768]{1,0:T(8,128)(2,1)S(1)} custom-call(f32[64,8192]{1,0:T(8,128)S(1)} %bitcast.27, bf16[768,8192]{1,0:T(8,128)(2,1)S(1)} %copy-done), custom_call_target="tpu_custom_call" | custom-call | flops 12582912 | bytes 229376 | tf_op jit(solution)/shard_map/margins/pallas_call | solution.py:55
  12.7 2.4 %add_bitcast_fusion = f32[64,4096]{1,0:T(8,128)} fusion(f32[1,64,8192]{2,1,0:T(8,128)S(1)} %copy-done.3, s32[]{:T(128)S(6)} %select_n.9, f32[1,64,8192]{2,1,0:T(8,128)} %param.10), kind=kLoop, calls=%fused_computation.1 | loop fusion | flops 262144 | bytes 3145732 | tf_op jit(solution)/shard_map/add | solution.py:232
  15.5 2.5 %collective-permute-start = (bf16[64,768]{1,0:T(8,128)(2,1)S(1)}, bf16[64,768]{1,0:T(8,128)(2,1)S(1)}, u32[]{:S(2)}, u32[]{:S(2)}) collective-permute-start(bf16[64,768]{1,0:T(8,128)(2,1)S(1)} %margins.1), channel_id=1, source_target_pairs={{0,1},{1,0},{2,3},{3,2},{4,5},{5,4},{6,7},{7,6},{8,9},{9,8},{10,11... | collective-permute-start | bytes 294920 | tf_op jit(solution)/shard_map/ppermute | solution.py:18
  18.0 3.5 %collective-permute-done = bf16[64,768]{1,0:T(8,128)(2,1)S(1)} collective-permute-done((bf16[64,768]{1,0:T(8,128)(2,1)S(1)}, bf16[64,768]{1,0:T(8,128)(2,1)S(1)}, u32[]{:S(2)}, u32[]{:S(2)}) %collective-permute-start) | collective-permute-done | bytes 98336 | tf_op jit(solution)/shard_map/ppermute | solution.py:18
  21.5 1.9 %collective-permute-start.1 = (bf16[64,768]{1,0:T(8,128)(2,1)S(1)}, bf16[64,768]{1,0:T(8,128)(2,1)S(1)}, u32[]{:S(2)}, u32[]{:S(2)}) collective-permute-start(bf16[64,768]{1,0:T(8,128)(2,1)S(1)} %add_convert_fusion.7), channel_id=1, source_target_pairs={{0,2},{1,3},{2,0},{3,1},{4,6},{5,7},{6,4},{7,5},{8,10},{9,11},{10,... | collective-permute-start | bytes 294920 | tf_op jit(solution)/shard_map/ppermute | solution.py:18
  23.4 2.8 %collective-permute-done.1 = bf16[64,768]{1,0:T(8,128)(2,1)S(1)} collective-permute-done((bf16[64,768]{1,0:T(8,128)(2,1)S(1)}, bf16[64,768]{1,0:T(8,128)(2,1)S(1)}, u32[]{:S(2)}, u32[]{:S(2)}) %collective-permute-start.1) | collective-permute-done | bytes 98336 | tf_op jit(solution)/shard_map/ppermute | solution.py:18
  26.2 2.9 %collective-permute-start.2 = (bf16[64,768]{1,0:T(8,128)(2,1)S(1)}, bf16[64,768]{1,0:T(8,128)(2,1)S(1)}, u32[]{:S(2)}, u32[]{:S(2)}) collective-permute-start(bf16[64,768]{1,0:T(8,128)(2,1)S(1)} %add_convert_fusion.6), channel_id=1, source_target_pairs={{0,4},{1,5},{2,6},{3,7},{4,0},{5,1},{6,2},{7,3},{8,12},{9,13},{10,... | collective-permute-start | bytes 294920 | tf_op jit(solution)/shard_map/ppermute | solution.py:18
  29.1 2.9 %collective-permute-done.2 = bf16[64,768]{1,0:T(8,128)(2,1)S(1)} collective-permute-done((bf16[64,768]{1,0:T(8,128)(2,1)S(1)}, bf16[64,768]{1,0:T(8,128)(2,1)S(1)}, u32[]{:S(2)}, u32[]{:S(2)}) %collective-permute-start.2) | collective-permute-done | bytes 98336 | tf_op jit(solution)/shard_map/ppermute | solution.py:18
  32.2 2.7 %bitcast_add_fusion = f32[64,4096]{1,0:T(8,128)} fusion(f32[64,4096]{1,0:T(8,128)} %collective-permute-done.3, f32[1,64,8192]{2,1,0:T(8,128)S(1)} %copy-done.3, s32[]{:T(128)S(6)} %select_n.8, f32[1,64,8192]{2,1,0:T(8,128)} %param.10), kind=kLoop, calls=%fused_computation | loop fusion | flops 524288 | bytes 4194308 | tf_op jit(solution)/shard_map/add | solution.py:236
  36.6 4.6 %copy-done.1 = bf16[768,8192]{1,0:T(8,128)(2,1)S(1)} copy-done((bf16[768,8192]{1,0:T(8,128)(2,1)S(1)}, bf16[768,8192]{1,0:T(8,128)(2,1)}, u32[]{:S(2)}) %copy-start.1) | copy-done | bytes 12582936
  44.3 8.7 %turn.1 = (f32[64,8192]{1,0:T(8,128)S(1)}, bf16[64,768]{1,0:T(8,128)(2,1)S(1)}) custom-call(bf16[64,768]{1,0:T(8,128)(2,1)S(1)} %multiply_convert_fusion.1.r_ref, f32[64,1]{1,0:T(8,128)S(1)} %copy.24.eta_ref.refs_2_.refs_3_, f32[64,1]{1,0:T(8,128)S(1)} %copy.25.pull_ref.refs_3_.refs_4_.refs_1_, f32[64,8192]{1,0:T(8,128)S(1)} %bitcast.28, ...), custom_call_target="tpu_custom_call" | custom-call | flops 25165824 | bytes 327680 | tf_op jit(solution)/shard_map/turn/pallas_call | solution.py:94
  54.6 3.1 %collective-permute-done.4 = bf16[64,768]{1,0:T(8,128)(2,1)S(1)} collective-permute-done((bf16[64,768]{1,0:T(8,128)(2,1)S(1)}, bf16[64,768]{1,0:T(8,128)(2,1)S(1)}, u32[]{:S(2)}, u32[]{:S(2)}) %collective-permute-start.4) | collective-permute-done | bytes 98336 | tf_op jit(solution)/shard_map/ppermute | solution.py:18
  57.7 1.8 %collective-permute-start.5 = (bf16[64,768]{1,0:T(8,128)(2,1)S(1)}, bf16[64,768]{1,0:T(8,128)(2,1)S(1)}, u32[]{:S(2)}, u32[]{:S(2)}) collective-permute-start(bf16[64,768]{1,0:T(8,128)(2,1)S(1)} %add_convert_fusion.5), channel_id=1, source_target_pairs={{0,2},{1,3},{2,0},{3,1},{4,6},{5,7},{6,4},{7,5},{8,10},{9,11},{10,... | collective-permute-start | bytes 294920 | tf_op jit(solution)/shard_map/ppermute | solution.py:18
  59.5 4.0 %collective-permute-done.5 = bf16[64,768]{1,0:T(8,128)(2,1)S(1)} collective-permute-done((bf16[64,768]{1,0:T(8,128)(2,1)S(1)}, bf16[64,768]{1,0:T(8,128)(2,1)S(1)}, u32[]{:S(2)}, u32[]{:S(2)}) %collective-permute-start.5) | collective-permute-done | bytes 98336 | tf_op jit(solution)/shard_map/ppermute | solution.py:18
  63.5 2.6 %collective-permute-start.6 = (bf16[64,768]{1,0:T(8,128)(2,1)S(1)}, bf16[64,768]{1,0:T(8,128)(2,1)S(1)}, u32[]{:S(2)}, u32[]{:S(2)}) collective-permute-start(bf16[64,768]{1,0:T(8,128)(2,1)S(1)} %add_convert_fusion.4), channel_id=1, source_target_pairs={{0,4},{1,5},{2,6},{3,7},{4,0},{5,1},{6,2},{7,3},{8,12},{9,13},{10,... | collective-permute-start | bytes 294920 | tf_op jit(solution)/shard_map/ppermute | solution.py:18
  66.1 3.0 %collective-permute-done.6 = bf16[64,768]{1,0:T(8,128)(2,1)S(1)} collective-permute-done((bf16[64,768]{1,0:T(8,128)(2,1)S(1)}, bf16[64,768]{1,0:T(8,128)(2,1)S(1)}, u32[]{:S(2)}, u32[]{:S(2)}) %collective-permute-start.6) | collective-permute-done | bytes 98336 | tf_op jit(solution)/shard_map/ppermute | solution.py:18
  69.2 1.7 %add.77.refs_6_.refs_8_ = f32[64,4096]{1,0:T(8,128)S(1)} add(f32[64,4096]{1,0:T(8,128)} %bitcast_add_fusion, f32[64,4096]{1,0:T(8,128)} %collective-permute-done.7) | non-fusion elementwise | flops 262144 | bytes 3145728 | tf_op jit(solution)/shard_map/add | solution.py:27
  81.0 4.6 %copy-done.2 = bf16[768,8192]{1,0:T(8,128)(2,1)S(1)} copy-done((bf16[768,8192]{1,0:T(8,128)(2,1)S(1)}, bf16[768,8192]{1,0:T(8,128)(2,1)}, u32[]{:S(2)}) %copy-start.2) | copy-done | bytes 12582936
  91.5 2.2 %push.15 = (f32[64,8192]{1,0:T(8,128)}, bf16[64,1024]{1,0:T(8,128)(2,1)S(1)}) custom-call(s32[1]{0:T(128)} %bitcast.refs_0_, f32[64,8192]{1,0:T(8,128)} %get-tuple-element.60.refs_1_, bf16[64,768]{1,0:T(8,128)(2,1)S(1)} %multiply_convert_fusion.refs_1_.refs_2_, f32[64,1]{1,0:T(8,128)S(1)} %copy.24.eta_ref.refs_2_.refs_3_, ...), custom_call_target="tpu_custom_call", output_to_operand_aliasing={{0}: (1, {})} | custom-call | flops 1572864 | bytes 49152 | tf_op jit(solution)/shard_map/push/pallas_call | solution.py:148
  99.7 2.3 %final.4 = (f32[64,8192]{1,0:T(8,128)}, f32[64,8192]{1,0:T(8,128)}) custom-call(s32[1]{0:T(128)} %bitcast.refs_0_, f32[64,1]{1,0:T(8,128)S(1)} %copy.25.pull_ref.refs_3_.refs_4_.refs_1_, f32[64,1]{1,0:T(8,128)S(1)} %copy.43.refs_2_.refs_4_, f32[64,8192]{1,0:T(8,128)S(1)} %copy-done.9, f32[64,8192]{1,0:T(8,128)S(1)} %bitcast.23, f32[64,8192]{1,0:T(8,128)S(1)} %copy-done.5, ...), custom_call_target="tpu_custom_call" | custom-call | flops 20480 | bytes 61440 | tf_op jit(solution)/shard_map/final/pallas_call | solution.py:200
  103.3 2.3 %final.5 = (f32[64,8192]{1,0:T(8,128)}, f32[64,8192]{1,0:T(8,128)}) custom-call(s32[1]{0:T(128)} %bitcast.refs_0_, f32[64,8192]{1,0:T(8,128)} %get-tuple-element.70.refs_1_, f32[64,8192]{1,0:T(8,128)} %get-tuple-element.71.refs_2_, f32[64,1]{1,0:T(8,128)S(1)} %copy.25.pull_ref.refs_3_.refs_4_.refs_1_, ...), custom_call_target="tpu_custom_call", output_to_operand_aliasing={{0}: (1, {}), {1}: (2, {})} | custom-call | flops 20480 | bytes 61440 | tf_op jit(solution)/shard_map/final/pallas_call | solution.py:200
  107.0 2.3 %final.6 = (f32[64,8192]{1,0:T(8,128)}, f32[64,8192]{1,0:T(8,128)}) custom-call(s32[1]{0:T(128)} %bitcast.refs_0_, f32[64,8192]{1,0:T(8,128)} %get-tuple-element.75.refs_1_, f32[64,8192]{1,0:T(8,128)} %get-tuple-element.76.refs_2_, f32[64,1]{1,0:T(8,128)S(1)} %copy.25.pull_ref.refs_3_.refs_4_.refs_1_, ...), custom_call_target="tpu_custom_call", output_to_operand_aliasing={{0}: (1, {}), {1}: (2, {})} | custom-call | flops 20480 | bytes 61440 | tf_op jit(solution)/shard_map/final/pallas_call | solution.py:200
  110.7 2.3 %final.7 = (f32[64,8192]{1,0:T(8,128)}, f32[64,8192]{1,0:T(8,128)}) custom-call(s32[1]{0:T(128)} %bitcast.refs_0_, f32[64,8192]{1,0:T(8,128)} %get-tuple-element.80.refs_1_, f32[64,8192]{1,0:T(8,128)} %get-tuple-element.81.refs_2_, f32[64,1]{1,0:T(8,128)S(1)} %copy.25.pull_ref.refs_3_.refs_4_.refs_1_, ...), custom_call_target="tpu_custom_call", output_to_operand_aliasing={{0}: (1, {}), {1}: (2, {})} | custom-call | flops 20480 | bytes 61440 | tf_op jit(solution)/shard_map/final/pallas_call | solution.py:200
  (85 shorter events, 34.9 us)
Async XLA Ops:
  6.8 5.9 %copy-start.3 = (f32[1,64,8192]{2,1,0:T(8,128)S(1)}, f32[1,64,8192]{2,1,0:T(8,128)}, u32[]{:S(2)}) copy-start(f32[1,64,8192]{2,1,0:T(8,128)} %param.11) | copy-start | bytes 6291460
  12.7 19.4 %copy-start.14 = (s32[64,768]{1,0:T(8,128)S(1)}, s32[64,768]{1,0:T(8,128)}, u32[]{:S(2)}) copy-start(s32[64,768]{1,0:T(8,128)} %param.9) | copy-start | bytes 589828
  15.0 17.1 %collective-permute-start.3 = (f32[64,4096]{1,0:T(8,128)}, f32[64,4096]{1,0:T(8,128)}, u32[]{:S(2)}, u32[]{:S(2)}) collective-permute-start(f32[64,4096]{1,0:T(8,128)} %add_bitcast_fusion), channel_id=1, source_target_pairs={{0,8},{8,0},{16,24},{24,16},{1,9},{9,1},{17,25},{25,17},{2,10},{10... | collective-permute-start | bytes 3145736 | tf_op jit(solution)/shard_map/ppermute | solution.py:18
  15.5 6.0 %collective-permute-start = (bf16[64,768]{1,0:T(8,128)(2,1)S(1)}, bf16[64,768]{1,0:T(8,128)(2,1)S(1)}, u32[]{:S(2)}, u32[]{:S(2)}) collective-permute-start(bf16[64,768]{1,0:T(8,128)(2,1)S(1)} %margins.1), channel_id=1, source_target_pairs={{0,1},{1,0},{2,3},{3,2},{4,5},{5,4},{6,7},{7,6},{8,9},{9,8},{10,11... | collective-permute-start | bytes 294920 | tf_op jit(solution)/shard_map/ppermute | solution.py:18
  21.5 4.7 %collective-permute-start.1 = (bf16[64,768]{1,0:T(8,128)(2,1)S(1)}, bf16[64,768]{1,0:T(8,128)(2,1)S(1)}, u32[]{:S(2)}, u32[]{:S(2)}) collective-permute-start(bf16[64,768]{1,0:T(8,128)(2,1)S(1)} %add_convert_fusion.7), channel_id=1, source_target_pairs={{0,2},{1,3},{2,0},{3,1},{4,6},{5,7},{6,4},{7,5},{8,10},{9,11},{10,... | collective-permute-start | bytes 294920 | tf_op jit(solution)/shard_map/ppermute | solution.py:18
  26.2 5.8 %collective-permute-start.2 = (bf16[64,768]{1,0:T(8,128)(2,1)S(1)}, bf16[64,768]{1,0:T(8,128)(2,1)S(1)}, u32[]{:S(2)}, u32[]{:S(2)}) collective-permute-start(bf16[64,768]{1,0:T(8,128)(2,1)S(1)} %add_convert_fusion.6), channel_id=1, source_target_pairs={{0,4},{1,5},{2,6},{3,7},{4,0},{5,1},{6,2},{7,3},{8,12},{9,13},{10,... | collective-permute-start | bytes 294920 | tf_op jit(solution)/shard_map/ppermute | solution.py:18
  34.8 34.3 %collective-permute-start.7 = (f32[64,4096]{1,0:T(8,128)}, f32[64,4096]{1,0:T(8,128)}, u32[]{:S(2)}, u32[]{:S(2)}) collective-permute-start(f32[64,4096]{1,0:T(8,128)} %bitcast_add_fusion), channel_id=1, source_target_pairs={{0,16},{8,24},{16,0},{24,8},{1,17},{9,25},{17,1},{25,9},{2,18},{10... | collective-permute-start | bytes 3145736 | tf_op jit(solution)/shard_map/ppermute | solution.py:18
  53.0 24.5 %copy-start.10 = (f32[64,8192]{1,0:T(8,128)}, f32[64,8192]{1,0:T(8,128)S(1)}, u32[]{:S(2)}) copy-start(f32[64,8192]{1,0:T(8,128)S(1)} %get-tuple-element.50.refs_7_.refs_8_) | copy-start | bytes 6291460
  53.0 4.7 %collective-permute-start.4 = (bf16[64,768]{1,0:T(8,128)(2,1)S(1)}, bf16[64,768]{1,0:T(8,128)(2,1)S(1)}, u32[]{:S(2)}, u32[]{:S(2)}) collective-permute-start(bf16[64,768]{1,0:T(8,128)(2,1)S(1)} %get-tuple-element.47), channel_id=1, source_target_pairs={{0,1},{1,0},{2,3},{3,2},{4,5},{5,4},{6,7},{7,6},{8,9},{9,8},{10,11... | collective-permute-start | bytes 294920 | tf_op jit(solution)/shard_map/ppermute | solution.py:18
  57.7 5.7 %collective-permute-start.5 = (bf16[64,768]{1,0:T(8,128)(2,1)S(1)}, bf16[64,768]{1,0:T(8,128)(2,1)S(1)}, u32[]{:S(2)}, u32[]{:S(2)}) collective-permute-start(bf16[64,768]{1,0:T(8,128)(2,1)S(1)} %add_convert_fusion.5), channel_id=1, source_target_pairs={{0,2},{1,3},{2,0},{3,1},{4,6},{5,7},{6,4},{7,5},{8,10},{9,11},{10,... | collective-permute-start | bytes 294920 | tf_op jit(solution)/shard_map/ppermute | solution.py:18
  63.5 5.6 %collective-permute-start.6 = (bf16[64,768]{1,0:T(8,128)(2,1)S(1)}, bf16[64,768]{1,0:T(8,128)(2,1)S(1)}, u32[]{:S(2)}, u32[]{:S(2)}) collective-permute-start(bf16[64,768]{1,0:T(8,128)(2,1)S(1)} %add_convert_fusion.4), channel_id=1, source_target_pairs={{0,4},{1,5},{2,6},{3,7},{4,0},{5,1},{6,2},{7,3},{8,12},{9,13},{10,... | collective-permute-start | bytes 294920 | tf_op jit(solution)/shard_map/ppermute | solution.py:18
  70.8 27.2 %collective-permute-start.15 = (f32[64,4096]{1,0:T(8,128)S(1)}, f32[64,4096]{1,0:T(8,128)}, u32[]{:S(2)}, u32[]{:S(2)}) collective-permute-start(f32[64,4096]{1,0:T(8,128)S(1)} %add.77.refs_6_.refs_8_), channel_id=1, source_target_pairs={{0,8},{8,0},{16,24},{24,16},{1,9},{9,1},{17,25},{25,17},{2,10},{10... | collective-permute-start | bytes 3145736 | tf_op jit(solution)/shard_map/ppermute | solution.py:18
  72.0 1.7 %collective-permute-start.8 = (bf16[64,1024]{1,0:T(8,128)(2,1)S(1)}, bf16[64,1024]{1,0:T(8,128)(2,1)S(1)}, u32[]{:S(2)}, u32[]{:S(2)}) collective-permute-start(bf16[64,1024]{1,0:T(8,128)(2,1)S(1)} %get-tuple-element.53), channel_id=1, source_target_pairs={{0,8},{8,0},{16,24},{24,16},{1,9},{9,1},{17,25},{25,17},{2,10},{10... | collective-permute-start | bytes 393224 | tf_op jit(solution)/shard_map/ppermute | solution.py:18
  73.6 2.8 %collective-permute-start.9 = (bf16[64,1024]{1,0:T(8,128)(2,1)S(1)}, bf16[64,1024]{1,0:T(8,128)(2,1)S(1)}, u32[]{:S(2)}, u32[]{:S(2)}) collective-permute-start(bf16[64,1024]{1,0:T(8,128)(2,1)S(1)} %get-tuple-element.56), channel_id=1, source_target_pairs={{0,8},{8,0},{16,24},{24,16},{1,9},{9,1},{17,25},{25,17},{2,10},{10... | collective-permute-start | bytes 393224 | tf_op jit(solution)/shard_map/ppermute | solution.py:18
  76.0 5.0 %collective-permute-start.10 = (bf16[64,1024]{1,0:T(8,128)(2,1)}, bf16[64,1024]{1,0:T(8,128)(2,1)S(1)}, u32[]{:S(2)}, u32[]{:S(2)}) collective-permute-start(bf16[64,1024]{1,0:T(8,128)(2,1)} %get-tuple-element.59), channel_id=1, source_target_pairs={{0,8},{8,0},{16,24},{24,16},{1,9},{9,1},{17,25},{25,17},{2,10},{10... | collective-permute-start | bytes 393224 | tf_op jit(solution)/shard_map/ppermute | solution.py:18
  78.7 12.8 %collective-permute-start.11 = (bf16[64,1024]{1,0:T(8,128)(2,1)}, bf16[64,1024]{1,0:T(8,128)(2,1)}, u32[]{:S(2)}, u32[]{:S(2)}) collective-permute-start(bf16[64,1024]{1,0:T(8,128)(2,1)} %get-tuple-element.61), channel_id=1, source_target_pairs={{0,8},{8,0},{16,24},{24,16},{1,9},{9,1},{17,25},{25,17},{2,10},{10... | collective-permute-start | bytes 393224 | tf_op jit(solution)/shard_map/ppermute | solution.py:18
  78.8 16.8 %collective-permute-start.16 = (bf16[64,1024]{1,0:T(8,128)(2,1)}, bf16[64,1024]{1,0:T(8,128)(2,1)}, u32[]{:S(2)}, u32[]{:S(2)}) collective-permute-start(bf16[64,1024]{1,0:T(8,128)(2,1)} %get-tuple-element.67), channel_id=1, source_target_pairs={{0,16},{8,24},{16,0},{24,8},{1,17},{9,25},{17,1},{25,9},{2,18},{10... | collective-permute-start | bytes 393224 | tf_op jit(solution)/shard_map/ppermute | solution.py:18
  80.4 16.4 %collective-permute-start.14 = (bf16[64,1024]{1,0:T(8,128)(2,1)}, bf16[64,1024]{1,0:T(8,128)(2,1)S(1)}, u32[]{:S(2)}, u32[]{:S(2)}) collective-permute-start(bf16[64,1024]{1,0:T(8,128)(2,1)} %copy-done.12), channel_id=1, source_target_pairs={{0,16},{8,24},{16,0},{24,8},{1,17},{9,25},{17,1},{25,9},{2,18},{10... | collective-permute-start | bytes 393224 | tf_op jit(solution)/shard_map/ppermute | solution.py:18
  93.6 12.2 %collective-permute-start.12 = (bf16[64,1024]{1,0:T(8,128)(2,1)S(1)}, bf16[64,1024]{1,0:T(8,128)(2,1)S(1)}, u32[]{:S(2)}, u32[]{:S(2)}) collective-permute-start(bf16[64,1024]{1,0:T(8,128)(2,1)S(1)} %get-tuple-element.63), channel_id=1, source_target_pairs={{0,16},{8,24},{16,0},{24,8},{1,17},{9,25},{17,1},{25,9},{2,18},{10... | collective-permute-start | bytes 393224 | tf_op jit(solution)/shard_map/ppermute | solution.py:18
  95.0 7.1 %collective-permute-start.13 = (bf16[64,1024]{1,0:T(8,128)(2,1)S(1)}, bf16[64,1024]{1,0:T(8,128)(2,1)S(1)}, u32[]{:S(2)}, u32[]{:S(2)}) collective-permute-start(bf16[64,1024]{1,0:T(8,128)(2,1)S(1)} %get-tuple-element.64), channel_id=1, source_target_pairs={{0,16},{8,24},{16,0},{24,8},{1,17},{9,25},{17,1},{25,9},{2,18},{10... | collective-permute-start | bytes 393224 | tf_op jit(solution)/shard_map/ppermute | solution.py:18
  96.7 1.4 %collective-permute-start.17 = (bf16[64,1024]{1,0:T(8,128)(2,1)S(1)}, bf16[64,1024]{1,0:T(8,128)(2,1)S(1)}, u32[]{:S(2)}, u32[]{:S(2)}) collective-permute-start(bf16[64,1024]{1,0:T(8,128)(2,1)S(1)} %add_convert_fusion.refs_8_), channel_id=1, source_target_pairs={{0,8},{8,0},{16,24},{24,16},{1,9},{9,1},{17,25},{25,17},{2,10},{10... | collective-permute-start | bytes 393224 | tf_op jit(solution)/shard_map/ppermute | solution.py:18
  102.0 1.3 %collective-permute-start.18 = (bf16[64,1024]{1,0:T(8,128)(2,1)S(1)}, bf16[64,1024]{1,0:T(8,128)(2,1)S(1)}, u32[]{:S(2)}, u32[]{:S(2)}) collective-permute-start(bf16[64,1024]{1,0:T(8,128)(2,1)S(1)} %add_convert_fusion.1.refs_10_), channel_id=1, source_target_pairs={{0,8},{8,0},{16,24},{24,16},{1,9},{9,1},{17,25},{25,17},{2,10},{10... | collective-permute-start | bytes 393224 | tf_op jit(solution)/shard_map/ppermute | solution.py:18
  105.7 1.3 %collective-permute-start.19 = (bf16[64,1024]{1,0:T(8,128)(2,1)S(1)}, bf16[64,1024]{1,0:T(8,128)(2,1)S(1)}, u32[]{:S(2)}, u32[]{:S(2)}) collective-permute-start(bf16[64,1024]{1,0:T(8,128)(2,1)S(1)} %add_convert_fusion.2.refs_10_), channel_id=1, source_target_pairs={{0,8},{8,0},{16,24},{24,16},{1,9},{9,1},{17,25},{25,17},{2,10},{10... | collective-permute-start | bytes 393224 | tf_op jit(solution)/shard_map/ppermute | solution.py:18
  109.3 1.3 %collective-permute-start.20 = (bf16[64,1024]{1,0:T(8,128)(2,1)S(1)}, bf16[64,1024]{1,0:T(8,128)(2,1)S(1)}, u32[]{:S(2)}, u32[]{:S(2)}) collective-permute-start(bf16[64,1024]{1,0:T(8,128)(2,1)S(1)} %add_convert_fusion.3.refs_10_), channel_id=1, source_target_pairs={{0,8},{8,0},{16,24},{24,16},{1,9},{9,1},{17,25},{25,17},{2,10},{10... | collective-permute-start | bytes 393224 | tf_op jit(solution)/shard_map/ppermute | solution.py:18
  (15 other events, 44.0 us)

commit v3 on v0

v3 whole, which is shorter than its diff:
```python
import functools

import jax
import jax.numpy as jnp
from jax import lax
from jax.experimental import pallas as pl
from jax.experimental.pallas import tpu as pltpu
from jax.sharding import PartitionSpec as P

BF16 = jnp.bfloat16
F32 = jnp.float32
CHUNKS = 4
STEP = 1024
HBM = pl.BlockSpec(memory_space=pltpu.HBM)
VMEM = pl.BlockSpec(memory_space=pltpu.VMEM)
SMEM = pl.BlockSpec(memory_space=pltpu.SMEM)


def exchange(value, axis, mask):
    n = lax.axis_size(axis)
    return lax.ppermute(value, axis, [(i, i ^ mask) for i in range(n)])


def doubling(value, axis, first=1):
    n = lax.axis_size(axis)
    mask = first
    other = exchange(value, axis, mask)
    while 2 * mask < n:
        mask *= 2
        value = (value.astype(F32) + other.astype(F32)).astype(value.dtype)
        other = exchange(value, axis, mask)
    return value, other


def nt(a, b):
    return lax.dot_general(a, b, (((1,), (1,)), ((), ())), preferred_element_type=F32)


def call(kernel, name, in_specs, out_shape, out_specs, scratch=(), aliases=None, limit=16, work=1000):
    return pl.pallas_call(
        kernel,
        in_specs=in_specs,
        out_shape=out_shape,
        out_specs=out_specs,
        scratch_shapes=list(scratch),
        input_output_aliases=aliases or {},
        compiler_params=pltpu.CompilerParams(vmem_limit_bytes=limit * 1024 * 1024),
        cost_estimate=pl.CostEstimate(flops=work, bytes_accessed=work, transcendentals=0),
        name=name,
    )


def pin(space, *values):
    return [pltpu.with_memory_space_constraint(v, space) for v in values]


def columns(start, size):
    return pl.ds(pl.multiple_of(start, 128), size)


def load_kernel(side, x_hbm, u_hbm, z_hbm, a_hbm, m_out, a_out, x_out, u_out, z_out, mine_out, other_out, acc, sems):
    width = x_hbm.shape[1]
    steps = width // STEP

    def pair(j):
        cut = columns(j * STEP, STEP)
        return (
            pltpu.make_async_copy(x_hbm.at[:, cut], x_out.at[:, cut], sems.at[0, j]),
            pltpu.make_async_copy(a_hbm.at[:, cut], a_out.at[:, cut], sems.at[1, j]),
        )

    rest = (
        pltpu.make_async_copy(u_hbm, u_out, sems.at[2, 0]),
        pltpu.make_async_copy(z_hbm, z_out, sems.at[2, 1]),
    )
    for j in range(steps):
        for copy in pair(j):
            copy.start()
    for copy in rest:
        copy.start()
    acc[...] = jnp.zeros_like(acc)

    @pl.loop(0, steps)
    def _(j):
        for copy in pair(j):
            copy.wait()
        cut = columns(j * STEP, STEP)
        acc[...] += nt(x_out[:, cut].astype(BF16), a_out[:, cut])

    m_out[...] = acc[...].astype(BF16)
    for copy in rest:
        copy.wait()
    half = width // 2
    mine = columns(side[0] * half, half)
    other = columns((1 - side[0]) * half, half)
    mine_out[...] = x_out[:, mine] + u_out[:, mine]
    other_out[...] = x_out[:, other] + u_out[:, other]


def load(side, x, u, z, design):
    tasks, width = x.shape
    samples = design.shape[0]
    steps = width // STEP
    full = pltpu.VMEM((tasks, width), F32)
    half = pltpu.VMEM((tasks, width // 2), F32)
    return call(
        load_kernel,
        "load_and_margins",
        [SMEM] + [HBM] * 4,
        (pltpu.VMEM((tasks, samples), BF16), pltpu.VMEM(design.shape, BF16), full, full, full, half, half),
        [VMEM] * 7,
        [pltpu.VMEM((tasks, samples), F32), pltpu.SemaphoreType.DMA((3, max(steps, 2)))],
    )(side, *pin(pltpu.HBM, x, u, z, design))


def residual(sign, own, other):
    margin = own.astype(F32) + other.astype(F32)
    sign = sign.astype(F32)
    return (sign * jax.nn.sigmoid(-sign * margin)).astype(BF16)


def turn_kernel(sign, own, other, scale, x_ref, u_ref, z_ref, a_ref, q_out, m_out, resid, acc):
    resid[...] = residual(sign[...], own[...], other[...])
    acc[...] = jnp.zeros_like(acc)
    eta, pull = scale[:, 0:1], scale[:, 1:2]

    @pl.loop(0, x_ref.shape[1] // STEP)
    def _(j):
        cut = columns(j * STEP, STEP)
        push = eta * jnp.dot(resid[...], a_ref[:, cut], preferred_element_type=F32)
        x = x_ref[:, cut]
        x = x - pull * (x - z_ref[:, cut] + u_ref[:, cut]) + push
        q_out[:, cut] = (1.0 - pull) * push
        acc[...] += nt(x.astype(BF16), a_ref[:, cut])

    m_out[...] = acc[...].astype(BF16)


def turn(sign, pair, scale, x, u, z, design):
    tasks, width = x.shape
    samples = design.shape[0]
    return call(
        turn_kernel,
        "turn",
        [VMEM] * 8,
        (pltpu.VMEM((tasks, width), F32), pltpu.VMEM((tasks, samples), BF16)),
        [VMEM] * 2,
        [pltpu.VMEM((tasks, samples), BF16), pltpu.VMEM((tasks, samples), F32)],
    )(*pin(pltpu.VMEM, sign, *pair, scale, x, u, z, design))


def push_kernel(mine, chunk, size, side, sign, own, other, scale, q_ref, a_ref, *rest):
    received = rest[0] if mine else None
    h_out, sent_out = rest[-2:]
    half = q_ref.shape[1] // 2
    eta = scale[:, 0:1]
    resid = residual(sign[...], own[...], other[...])
    base = (side[0] if mine else 1 - side[0]) * half + chunk * size
    step = min(STEP, size)
    for j in range(size // step):
        cut = columns(base + j * step, step)
        here = pl.ds(j * step, step)
        push = q_ref[:, cut] + eta * jnp.dot(resid, a_ref[:, cut], preferred_element_type=F32)
        h_out[:, here] = push
        if mine:
            push = push + received[:, here].astype(F32)
        sent_out[:, here] = push.astype(BF16)


def push(side, sign, pair, scale, q, design, received, chunk, size):
    tasks = q.shape[0]
    mine = received is not None
    args = [sign, *pair, scale, q, design] + ([received] if mine else [])
    return call(
        functools.partial(push_kernel, mine, chunk, size),
        "push_mine" if mine else "push_other",
        [SMEM] + [VMEM] * len(args),
        (pltpu.VMEM((tasks, size), F32), pltpu.VMEM((tasks, size), BF16)),
        [VMEM] * 2,
    )(side, *pin(pltpu.VMEM, *args))


def final_kernel(blocks_count, chunk, size, buffered, side, scale, x_ref, u_ref, z_ref, *rest):
    starts, hs, pushes = rest[0:2], rest[2:4], rest[4:6]
    outs = rest[6 + 3 * buffered : 9 + 3 * buffered]
    stage, sems = rest[-2:]
    half = x_ref.shape[1] // 2
    pull, limit = scale[:, 1:2], scale[:, 2:3]
    keep = 1.0 - pull
    copies = []
    for k in range(2):
        base = (side[0] if k == 0 else 1 - side[0]) * half + chunk * size
        cut = columns(base, size)
        u, z = u_ref[:, cut], z_ref[:, cut]
        new_x = z - u + keep * keep * (x_ref[:, cut] - z + u) + hs[k][...]
        start = starts[k][:, pl.ds(chunk * size, size)]
        mean = (keep * keep * start + pushes[k][...].astype(F32)) * (1.0 / blocks_count) + pull * (1.0 + keep) * z
        new_z = mean - jnp.clip(mean, -limit, limit)
        for o, value in enumerate((new_x, new_z, u + new_x - new_z)):
            stage[k, o] = value
            copy = pltpu.make_async_copy(stage.at[k, o], outs[o].at[:, cut], sems.at[k, o])
            copy.start()
            copies.append(copy)
    for copy in copies:
        copy.wait()


def final(side, scale, x, u, z, starts, hs, pushes, buffers, chunk, size, blocks_count):
    tasks, width = x.shape
    buffered = buffers is not None
    args = pin(pltpu.VMEM, scale, x, u, z, *starts, *hs, *pushes)
    out = pltpu.HBM((tasks, width), F32)
    aliases = {}
    if buffered:
        aliases = {1 + len(args) + o: o for o in range(3)}
        args += pin(pltpu.HBM, *buffers)
    return call(
        functools.partial(final_kernel, blocks_count, chunk, size, buffered),
        "final",
        [SMEM] + [VMEM] * 10 + [HBM] * (3 * buffered),
        (out, out, out),
        [HBM] * 3,
        [pltpu.VMEM((2, 3, tasks, size), F32), pltpu.SemaphoreType.DMA((2, 3))],
        aliases,
    )(side, *args)


def per_device(design, labels, local_x, dual_u, consensus_z, step_size, rho, penalty):
    tasks, width = consensus_z.shape
    blocks_count = lax.axis_size("rows")
    side = (lax.axis_index("rows") & 1).astype(jnp.int32)[None]
    scale = jnp.stack([step_size, step_size * rho, penalty / (rho * blocks_count)], axis=1)

    margin1, design, x0, dual, z, start_mine, start_other = load(side, local_x[0], dual_u[0], consensus_z, design)
    start_mine = start_mine + exchange(start_other, "rows", 1)
    pair = doubling(margin1, "feat")
    pair, start_mine = lax.optimization_barrier((pair, start_mine))

    carried, margin2 = turn(labels, pair, scale, x0, dual, z, design)
    pair = doubling(margin2, "feat")
    mask = 2
    while mask < blocks_count:
        start_mine = start_mine + exchange(start_mine, "rows", mask)
        mask *= 2
    pair, start_mine = lax.optimization_barrier((pair, start_mine))
    start_theirs = exchange(start_mine, "rows", 1)

    size = width // 2 // CHUNKS
    args = (side, labels, pair, scale, carried, design)
    others, mines, received, pieces = [], [], [], []
    for c in range(CHUNKS + 1):
        if c < CHUNKS:
            value, other = push(*args, None, c, size)
            others.append(value)
            received.append(exchange(other, "rows", 1))
        if c > 0:
            value, mine = push(*args, received[c - 1], c - 1, size)
            mines.append(value)
            a, b = doubling(mine, "rows", 2)
            pieces.append((a.astype(F32) + b.astype(F32)).astype(BF16))
    results = None
    for c in range(CHUNKS):
        piece = pieces[c]
        if results is not None:
            piece, results = lax.optimization_barrier((piece, results))
        pushes = (piece, exchange(piece, "rows", 1))
        results = final(
            side, scale, x0, dual, z, (start_mine, start_theirs), (mines[c], others[c]), pushes, results, c, size, blocks_count
        )
    new_x, new_z, new_u = results
    return (new_x[None], new_z, new_u[None])


def solution(mesh):
    in_specs = (
        P("rows", "feat"),
        P(None, "rows"),
        P("rows", None, "feat"),
        P("rows", None, "feat"),
        P(None, "feat"),
        P(),
        P(),
        P(),
    )
    out_specs = (P("rows", None, "feat"), P(None, "feat"), P("rows", None, "feat"))
    return jax.shard_map(
        per_device, mesh=mesh, in_specs=in_specs, out_specs=out_specs, check_vma=False
    )
```

time: 246 us -> 88.9 us (0.36)
  waiting for transfers between devices: 192 us -> 24.3 us
  matrix products: 34.2 us -> 0 us
  Pallas kernels: 0 us -> 23.6 us
  starting transfers between devices: 0.12 us -> 21.9 us
  local copies, waits for them, and re-layouts: 1.54 us -> 15.1 us
  between operations: 13.8 us -> 0.88 us
    psum x3 -> x0, waiting for transfers between devices: 192 us -> none  [the longest x2 142 us: per_device(): margin = lax.psum(partial_margin, 'feat')]
    dot_general x4 -> x0, matrix products: 34.2 us -> none  [the longest x2 19.7 us: per_device(): grad = jnp.dot(resid, design, preferred_element_type=jnp.float32)]
    ppermute x0 -> x21, waiting for transfers between devices: none -> 24.3 us  [exchange(): return lax.ppermute(value, axis, [(i, i ^ mask) for i in range(n)])]
    pallas_call x0 -> x14, Pallas kernels: none -> 23.6 us  [the longest x1 7.19 us: turn(): call(turn_kernel, 'turn', [VMEM] * 8, (pltpu.VMEM((tasks, width), F32), p...]
    ppermute x0 -> x21, starting transfers between devices: none -> 21.9 us  [exchange(): return lax.ppermute(value, axis, [(i, i ^ mask) for i in range(n)])]
    unnamed x12 -> x26, local copies, waits for them, and re-layouts: 1.54 us -> 15 us
    broadcast_in_dim x1 -> x0, other arithmetic: 4.16 us -> none  [per_device(): return (x[None], new_z, new_u[None])]
    add x0 -> x2, other arithmetic: none -> 2.73 us  [the longest x1 1.65 us: per_device(): start_mine = start_mine + exchange(start_mine, 'rows', mask)]
  transfers between devices with their start and end apart: 3 -> 21, of which waited for: 3 -> 13; matrix products, arithmetic and copies ran while one was open for 0% -> 3% of each run, Pallas kernels for 0% -> 15%
where the time goes in v3:
time: 88.9 us; the launch traced here: 88.7 us
  waiting for transfers between devices  24.3 us (27%)
  Pallas kernels  23.6 us (27%)
  starting transfers between devices  21.9 us (25%)
  local copies, waits for them, and re-layouts  15.1 us (17%)
  other arithmetic  2.98 us (3%)
    ppermute x21, waiting for transfers between devices, exchange(): return lax.ppermute(value, axis, [(i, i ^ mask) for i in range(n)])  24.3 us
    ppermute x21, starting transfers between devices, exchange(): return lax.ppermute(value, axis, [(i, i ^ mask) for i in range(n)])  21.9 us
    unnamed x26, local copies, waits for them, and re-layouts  15 us
    pallas_call x1, Pallas kernels, turn(): call(turn_kernel, 'turn', [VMEM] * 8, (pltpu.VMEM((tasks, width), F32), p...  7.19 us
    pallas_call x1, Pallas kernels, load(): call(load_kernel, 'load_and_margins', [SMEM] + [HBM] * 4, (pltpu.VMEM((ta...  7.03 us
    pallas_call x4, Pallas kernels, final(): call(functools.partial(final_kernel, blocks_count, chunk, size, buffered)...  6.16 us
    pallas_call x8, Pallas kernels, push(): call(functools.partial(push_kernel, mine, chunk, size), 'push_mine' if mi...  3.2 us
  transfers between devices with their start and end apart: 21, of which 13 were waited for; matrix products, arithmetic and copies ran while one was open for 3% of the time, Pallas kernels for 15%

profile of v3, /device:TPU:0, one launch (start us, length us, event | category | flops | bytes accessed | tf_op | source)
XLA Modules:
  0.0 88.7 jit_solution(8934690945831195560)
XLA Ops:
  0.6 7.0 %load_and_margins.1 = (bf16[64,768]{1,0:T(8,128)(2,1)S(1)}, bf16[768,8192]{1,0:T(8,128)(2,1)S(1)}, f32[64,8192]{1,0:T(8,128)S(1)}, f32[64,8192]{1,0:T(8,128)S(1)...) custom-call(s32[1]{0:T(128)} %bitcast.side, f32[64,8192]{1,0:T(8,128)} %bitcast.12, ...), custom_call_target="tpu_custom_call" | custom-call | flops 1000 | bytes 1000 | tf_op jit(solution)/shard_map/load_and_margins/pallas_call | solution.py:106
  7.7 4.5 %copy-done = bf16[768,8192]{1,0:T(8,128)(2,1)} copy-done((bf16[768,8192]{1,0:T(8,128)(2,1)}, bf16[768,8192]{1,0:T(8,128)(2,1)S(1)}, u32[]{:S(2)}) %copy-start) | copy-done | bytes 12582936
  15.4 2.6 %collective-permute-start = (bf16[64,768]{1,0:T(8,128)(2,1)S(1)}, bf16[64,768]{1,0:T(8,128)(2,1)S(1)}, u32[]{:S(2)}, u32[]{:S(2)}) collective-permute-start(bf16[64,768]{1,0:T(8,128)(2,1)S(1)} %get-tuple-element.61), channel_id=1, source_target_pairs={{0,1},{1,0},{2,3},{3,2},{4,5},{5,4},{6,7},{7,6},{8,9},{9,8},{10,11... | collective-permute-start | bytes 294920 | tf_op jit(solution)/shard_map/ppermute | solution.py:21
  18.0 3.4 %collective-permute-done = bf16[64,768]{1,0:T(8,128)(2,1)S(1)} collective-permute-done((bf16[64,768]{1,0:T(8,128)(2,1)S(1)}, bf16[64,768]{1,0:T(8,128)(2,1)S(1)}, u32[]{:S(2)}, u32[]{:S(2)}) %collective-permute-start) | collective-permute-done | bytes 98336 | tf_op jit(solution)/shard_map/ppermute | solution.py:21
  21.4 1.9 %collective-permute-start.1 = (bf16[64,768]{1,0:T(8,128)(2,1)S(1)}, bf16[64,768]{1,0:T(8,128)(2,1)S(1)}, u32[]{:S(2)}, u32[]{:S(2)}) collective-permute-start(bf16[64,768]{1,0:T(8,128)(2,1)S(1)} %add_convert_fusion.7), channel_id=1, source_target_pairs={{0,2},{1,3},{2,0},{3,1},{4,6},{5,7},{6,4},{7,5},{8,10},{9,11},{10,... | collective-permute-start | bytes 294920 | tf_op jit(solution)/shard_map/ppermute | solution.py:21
  23.3 2.8 %collective-permute-done.1 = bf16[64,768]{1,0:T(8,128)(2,1)S(1)} collective-permute-done((bf16[64,768]{1,0:T(8,128)(2,1)S(1)}, bf16[64,768]{1,0:T(8,128)(2,1)S(1)}, u32[]{:S(2)}, u32[]{:S(2)}) %collective-permute-start.1) | collective-permute-done | bytes 98336 | tf_op jit(solution)/shard_map/ppermute | solution.py:21
  26.1 2.9 %collective-permute-start.2 = (bf16[64,768]{1,0:T(8,128)(2,1)S(1)}, bf16[64,768]{1,0:T(8,128)(2,1)S(1)}, u32[]{:S(2)}, u32[]{:S(2)}) collective-permute-start(bf16[64,768]{1,0:T(8,128)(2,1)S(1)} %add_convert_fusion.6.own), channel_id=1, source_target_pairs={{0,4},{1,5},{2,6},{3,7},{4,0},{5,1},{6,2},{7,3},{8,12},{9,13},{10,... | collective-permute-start | bytes 294920 | tf_op jit(solution)/shard_map/ppermute | solution.py:21
  30.1 1.6 %collective-permute-done.2.other = bf16[64,768]{1,0:T(8,128)(2,1)S(1)} collective-permute-done((bf16[64,768]{1,0:T(8,128)(2,1)S(1)}, bf16[64,768]{1,0:T(8,128)(2,1)S(1)}, u32[]{:S(2)}, u32[]{:S(2)}) %collective-permute-start.2) | collective-permute-done | bytes 98336 | tf_op jit(solution)/shard_map/ppermute | solution.py:21
  31.7 1.7 %collective-permute-start.7 = (f32[64,4096]{1,0:T(8,128)}, f32[64,4096]{1,0:T(8,128)}, u32[]{:S(2)}, u32[]{:S(2)}) collective-permute-start(f32[64,4096]{1,0:T(8,128)} %add.32), channel_id=1, source_target_pairs={{0,16},{8,24},{16,0},{24,8},{1,17},{9,25},{17,1},{25,9},{2,18},{10... | collective-permute-start | bytes 3145736 | tf_op jit(solution)/shard_map/ppermute | solution.py:21
  33.6 4.6 %copy-done.1 = bf16[768,8192]{1,0:T(8,128)(2,1)S(1)} copy-done((bf16[768,8192]{1,0:T(8,128)(2,1)S(1)}, bf16[768,8192]{1,0:T(8,128)(2,1)}, u32[]{:S(2)}) %copy-start.1) | copy-done | bytes 12582936
  38.2 1.6 %copy-done.4 = f32[64,8192]{1,0:T(8,128)S(1)} copy-done((f32[64,8192]{1,0:T(8,128)S(1)}, f32[64,8192]{1,0:T(8,128)}, u32[]{:S(2)}) %copy-start.4) | copy-done | bytes 2097176
  39.8 1.6 %copy-done.7 = f32[64,8192]{1,0:T(8,128)S(1)} copy-done((f32[64,8192]{1,0:T(8,128)S(1)}, f32[64,8192]{1,0:T(8,128)}, u32[]{:S(2)}) %copy-start.7) | copy-done | bytes 2097176
  41.3 7.2 %turn.1 = (f32[64,8192]{1,0:T(8,128)S(1)}, bf16[64,768]{1,0:T(8,128)(2,1)S(1)}) custom-call(s32[64,768]{1,0:T(8,128)S(1)} %copy-done.9, bf16[64,768]{1,0:T(8,128)(2,1)S(1)} %add_convert_fusion.6.own, bf16[64,768]{1,0:T(8,128)(2,1)S(1)} %collective-permute-done.2.other, f32[64,3]{1,0:T(8,128)S(1)} %copy.35.scale, f32[64,8192]{1,0:T(8,128)S(1)} %get-tuple-element.58.x_ref, ...), custom_call_target="tpu_custom_call" | custom-call | flops 1000 | bytes 1000 | tf_op jit(solution)/shard_map/turn/pallas_call | solution.py:142
  48.5 1.6 %collective-permute-start.4 = (bf16[64,768]{1,0:T(8,128)(2,1)S(1)}, bf16[64,768]{1,0:T(8,128)(2,1)S(1)}, u32[]{:S(2)}, u32[]{:S(2)}) collective-permute-start(bf16[64,768]{1,0:T(8,128)(2,1)S(1)} %get-tuple-element.67), channel_id=1, source_target_pairs={{0,1},{1,0},{2,3},{3,2},{4,5},{5,4},{6,7},{7,6},{8,9},{9,8},{10,11... | collective-permute-start | bytes 294920 | tf_op jit(solution)/shard_map/ppermute | solution.py:21
  50.1 3.1 %collective-permute-done.4 = bf16[64,768]{1,0:T(8,128)(2,1)S(1)} collective-permute-done((bf16[64,768]{1,0:T(8,128)(2,1)S(1)}, bf16[64,768]{1,0:T(8,128)(2,1)S(1)}, u32[]{:S(2)}, u32[]{:S(2)}) %collective-permute-start.4) | collective-permute-done | bytes 98336 | tf_op jit(solution)/shard_map/ppermute | solution.py:21
  53.3 1.8 %collective-permute-start.5 = (bf16[64,768]{1,0:T(8,128)(2,1)S(1)}, bf16[64,768]{1,0:T(8,128)(2,1)S(1)}, u32[]{:S(2)}, u32[]{:S(2)}) collective-permute-start(bf16[64,768]{1,0:T(8,128)(2,1)S(1)} %add_convert_fusion.5), channel_id=1, source_target_pairs={{0,2},{1,3},{2,0},{3,1},{4,6},{5,7},{6,4},{7,5},{8,10},{9,11},{10,... | collective-permute-start | bytes 294920 | tf_op jit(solution)/shard_map/ppermute | solution.py:21
  55.0 4.0 %collective-permute-done.5 = bf16[64,768]{1,0:T(8,128)(2,1)S(1)} collective-permute-done((bf16[64,768]{1,0:T(8,128)(2,1)S(1)}, bf16[64,768]{1,0:T(8,128)(2,1)S(1)}, u32[]{:S(2)}, u32[]{:S(2)}) %collective-permute-start.5) | collective-permute-done | bytes 98336 | tf_op jit(solution)/shard_map/ppermute | solution.py:21
  59.0 2.7 %collective-permute-start.6 = (bf16[64,768]{1,0:T(8,128)(2,1)S(1)}, bf16[64,768]{1,0:T(8,128)(2,1)S(1)}, u32[]{:S(2)}, u32[]{:S(2)}) collective-permute-start(bf16[64,768]{1,0:T(8,128)(2,1)S(1)} %add_convert_fusion.4.own), channel_id=1, source_target_pairs={{0,4},{1,5},{2,6},{3,7},{4,0},{5,1},{6,2},{7,3},{8,12},{9,13},{10,... | collective-permute-start | bytes 294920 | tf_op jit(solution)/shard_map/ppermute | solution.py:21
  61.8 1.6 %add.35.rest_0_ = f32[64,4096]{1,0:T(8,128)S(1)} add(f32[64,4096]{1,0:T(8,128)} %add.32, f32[64,4096]{1,0:T(8,128)} %collective-permute-done.7) | non-fusion elementwise | flops 262144 | bytes 3145728 | tf_op jit(solution)/shard_map/add | solution.py:243
  63.4 2.2 %collective-permute-done.6.other = bf16[64,768]{1,0:T(8,128)(2,1)S(1)} collective-permute-done((bf16[64,768]{1,0:T(8,128)(2,1)S(1)}, bf16[64,768]{1,0:T(8,128)(2,1)S(1)}, u32[]{:S(2)}, u32[]{:S(2)}) %collective-permute-start.6) | collective-permute-done | bytes 98336 | tf_op jit(solution)/shard_map/ppermute | solution.py:21
  69.8 1.8 %collective-permute-start.14 = (bf16[64,1024]{1,0:T(8,128)(2,1)S(1)}, bf16[64,1024]{1,0:T(8,128)(2,1)S(1)}, u32[]{:S(2)}, u32[]{:S(2)}) collective-permute-start(bf16[64,1024]{1,0:T(8,128)(2,1)S(1)} %get-tuple-element.84), channel_id=1, source_target_pairs={{0,16},{8,24},{16,0},{24,8},{1,17},{9,25},{17,1},{25,9},{2,18},{10... | collective-permute-start | bytes 393224 | tf_op jit(solution)/shard_map/ppermute | solution.py:21
  72.8 1.8 %collective-permute-start.10 = (bf16[64,1024]{1,0:T(8,128)(2,1)S(1)}, bf16[64,1024]{1,0:T(8,128)(2,1)S(1)}, u32[]{:S(2)}, u32[]{:S(2)}) collective-permute-start(bf16[64,1024]{1,0:T(8,128)(2,1)S(1)} %get-tuple-element.76), channel_id=1, source_target_pairs={{0,16},{8,24},{16,0},{24,8},{1,17},{9,25},{17,1},{25,9},{2,18},{10... | collective-permute-start | bytes 393224 | tf_op jit(solution)/shard_map/ppermute | solution.py:21
  75.5 2.7 %collective-permute-done.14 = bf16[64,1024]{1,0:T(8,128)(2,1)S(1)} collective-permute-done((bf16[64,1024]{1,0:T(8,128)(2,1)S(1)}, bf16[64,1024]{1,0:T(8,128)(2,1)S(1)}, u32[]{:S(2)}, u32[]{:S(2)}) %collective-permute-start.14) | collective-permute-done | bytes 131104 | tf_op jit(solution)/shard_map/ppermute | solution.py:21
  78.2 1.5 %final.4 = (f32[64,8192]{1,0:T(8,128)}, f32[64,8192]{1,0:T(8,128)}, f32[64,8192]{1,0:T(8,128)}) custom-call(s32[1]{0:T(128)} %bitcast.side, f32[64,3]{1,0:T(8,128)S(1)} %copy.35.scale, f32[64,8192]{1,0:T(8,128)S(1)} %get-tuple-element.58.x_ref, f32[64,8192]{1,0:T(8,128)S(1)} %copy-done.5, f32[64,8192]{1,0:T(8,128)S(1)} %copy-done.8, ...), custom_call_target="tpu_custom_call" | custom-call | flops 1000 | bytes 1000 | tf_op jit(solution)/shard_map/final/pallas_call | solution.py:217
  (71 shorter events, 19.5 us)
Async XLA Ops:
  14.9 18.6 %copy-start.12 = (f32[64]{0:T(128)S(1)}, f32[64]{0:T(128)}, u32[]{:S(2)}) copy-start(f32[64]{0:T(128)} %param.15) | copy-start | bytes 772
  14.9 18.7 %copy-start.9 = (s32[64,768]{1,0:T(8,128)S(1)}, s32[64,768]{1,0:T(8,128)}, u32[]{:S(2)}) copy-start(s32[64,768]{1,0:T(8,128)} %sign.17) | copy-start | bytes 589828
  14.9 14.1 %collective-permute-start.3 = (f32[64,4096]{1,0:T(8,128)S(1)}, f32[64,4096]{1,0:T(8,128)S(1)}, u32[]{:S(2)}, u32[]{:S(2)}) collective-permute-start(f32[64,4096]{1,0:T(8,128)S(1)} %get-tuple-element.63), channel_id=1, source_target_pairs={{0,8},{8,0},{16,24},{24,16},{1,9},{9,1},{17,25},{25,17},{2,10},{10... | collective-permute-start | bytes 3145736 | tf_op jit(solution)/shard_map/ppermute | solution.py:21
  15.4 6.0 %collective-permute-start = (bf16[64,768]{1,0:T(8,128)(2,1)S(1)}, bf16[64,768]{1,0:T(8,128)(2,1)S(1)}, u32[]{:S(2)}, u32[]{:S(2)}) collective-permute-start(bf16[64,768]{1,0:T(8,128)(2,1)S(1)} %get-tuple-element.61), channel_id=1, source_target_pairs={{0,1},{1,0},{2,3},{3,2},{4,5},{5,4},{6,7},{7,6},{8,9},{9,8},{10,11... | collective-permute-start | bytes 294920 | tf_op jit(solution)/shard_map/ppermute | solution.py:21
  21.4 4.7 %collective-permute-start.1 = (bf16[64,768]{1,0:T(8,128)(2,1)S(1)}, bf16[64,768]{1,0:T(8,128)(2,1)S(1)}, u32[]{:S(2)}, u32[]{:S(2)}) collective-permute-start(bf16[64,768]{1,0:T(8,128)(2,1)S(1)} %add_convert_fusion.7), channel_id=1, source_target_pairs={{0,2},{1,3},{2,0},{3,1},{4,6},{5,7},{6,4},{7,5},{8,10},{9,11},{10,... | collective-permute-start | bytes 294920 | tf_op jit(solution)/shard_map/ppermute | solution.py:21
  26.1 5.6 %collective-permute-start.2 = (bf16[64,768]{1,0:T(8,128)(2,1)S(1)}, bf16[64,768]{1,0:T(8,128)(2,1)S(1)}, u32[]{:S(2)}, u32[]{:S(2)}) collective-permute-start(bf16[64,768]{1,0:T(8,128)(2,1)S(1)} %add_convert_fusion.6.own), channel_id=1, source_target_pairs={{0,4},{1,5},{2,6},{3,7},{4,0},{5,1},{6,2},{7,3},{8,12},{9,13},{10,... | collective-permute-start | bytes 294920 | tf_op jit(solution)/shard_map/ppermute | solution.py:21
  31.7 30.1 %collective-permute-start.7 = (f32[64,4096]{1,0:T(8,128)}, f32[64,4096]{1,0:T(8,128)}, u32[]{:S(2)}, u32[]{:S(2)}) collective-permute-start(f32[64,4096]{1,0:T(8,128)} %add.32), channel_id=1, source_target_pairs={{0,16},{8,24},{16,0},{24,8},{1,17},{9,25},{17,1},{25,9},{2,18},{10... | collective-permute-start | bytes 3145736 | tf_op jit(solution)/shard_map/ppermute | solution.py:21
  41.3 24.3 %copy-start.2 = (bf16[768,8192]{1,0:T(8,128)(2,1)S(1)}, bf16[768,8192]{1,0:T(8,128)(2,1)}, u32[]{:S(2)}) copy-start(bf16[768,8192]{1,0:T(8,128)(2,1)} %copy-done) | copy-start | bytes 37748740
  48.5 4.7 %collective-permute-start.4 = (bf16[64,768]{1,0:T(8,128)(2,1)S(1)}, bf16[64,768]{1,0:T(8,128)(2,1)S(1)}, u32[]{:S(2)}, u32[]{:S(2)}) collective-permute-start(bf16[64,768]{1,0:T(8,128)(2,1)S(1)} %get-tuple-element.67), channel_id=1, source_target_pairs={{0,1},{1,0},{2,3},{3,2},{4,5},{5,4},{6,7},{7,6},{8,9},{9,8},{10,11... | collective-permute-start | bytes 294920 | tf_op jit(solution)/shard_map/ppermute | solution.py:21
  53.3 5.7 %collective-permute-start.5 = (bf16[64,768]{1,0:T(8,128)(2,1)S(1)}, bf16[64,768]{1,0:T(8,128)(2,1)S(1)}, u32[]{:S(2)}, u32[]{:S(2)}) collective-permute-start(bf16[64,768]{1,0:T(8,128)(2,1)S(1)} %add_convert_fusion.5), channel_id=1, source_target_pairs={{0,2},{1,3},{2,0},{3,1},{4,6},{5,7},{6,4},{7,5},{8,10},{9,11},{10,... | collective-permute-start | bytes 294920 | tf_op jit(solution)/shard_map/ppermute | solution.py:21
  59.0 6.6 %collective-permute-start.6 = (bf16[64,768]{1,0:T(8,128)(2,1)S(1)}, bf16[64,768]{1,0:T(8,128)(2,1)S(1)}, u32[]{:S(2)}, u32[]{:S(2)}) collective-permute-start(bf16[64,768]{1,0:T(8,128)(2,1)S(1)} %add_convert_fusion.4.own), channel_id=1, source_target_pairs={{0,4},{1,5},{2,6},{3,7},{4,0},{5,1},{6,2},{7,3},{8,12},{9,13},{10,... | collective-permute-start | bytes 294920 | tf_op jit(solution)/shard_map/ppermute | solution.py:21
  65.7 12.6 %collective-permute-start.8 = (f32[64,4096]{1,0:T(8,128)S(1)}, f32[64,4096]{1,0:T(8,128)S(1)}, u32[]{:S(2)}, u32[]{:S(2)}) collective-permute-start(f32[64,4096]{1,0:T(8,128)S(1)} %add.35.rest_0_), channel_id=1, source_target_pairs={{0,8},{8,0},{16,24},{24,16},{1,9},{9,1},{17,25},{25,17},{2,10},{10... | collective-permute-start | bytes 3145736 | tf_op jit(solution)/shard_map/ppermute | solution.py:21
  66.1 2.5 %collective-permute-start.15 = (bf16[64,1024]{1,0:T(8,128)(2,1)S(1)}, bf16[64,1024]{1,0:T(8,128)(2,1)S(1)}, u32[]{:S(2)}, u32[]{:S(2)}) collective-permute-start(bf16[64,1024]{1,0:T(8,128)(2,1)S(1)} %get-tuple-element.85), channel_id=1, source_target_pairs={{0,8},{8,0},{16,24},{24,16},{1,9},{9,1},{17,25},{25,17},{2,10},{10... | collective-permute-start | bytes 393224 | tf_op jit(solution)/shard_map/ppermute | solution.py:21
  67.0 2.3 %collective-permute-start.13 = (bf16[64,1024]{1,0:T(8,128)(2,1)S(1)}, bf16[64,1024]{1,0:T(8,128)(2,1)S(1)}, u32[]{:S(2)}, u32[]{:S(2)}) collective-permute-start(bf16[64,1024]{1,0:T(8,128)(2,1)S(1)} %get-tuple-element.81), channel_id=1, source_target_pairs={{0,8},{8,0},{16,24},{24,16},{1,9},{9,1},{17,25},{25,17},{2,10},{10... | collective-permute-start | bytes 393224 | tf_op jit(solution)/shard_map/ppermute | solution.py:21
  67.5 4.0 %collective-permute-start.11 = (bf16[64,1024]{1,0:T(8,128)(2,1)S(1)}, bf16[64,1024]{1,0:T(8,128)(2,1)S(1)}, u32[]{:S(2)}, u32[]{:S(2)}) collective-permute-start(bf16[64,1024]{1,0:T(8,128)(2,1)S(1)} %get-tuple-element.77), channel_id=1, source_target_pairs={{0,8},{8,0},{16,24},{24,16},{1,9},{9,1},{17,25},{25,17},{2,10},{10... | collective-permute-start | bytes 393224 | tf_op jit(solution)/shard_map/ppermute | solution.py:21
  68.5 3.8 %collective-permute-start.9 = (bf16[64,1024]{1,0:T(8,128)(2,1)S(1)}, bf16[64,1024]{1,0:T(8,128)(2,1)S(1)}, u32[]{:S(2)}, u32[]{:S(2)}) collective-permute-start(bf16[64,1024]{1,0:T(8,128)(2,1)S(1)} %get-tuple-element.73), channel_id=1, source_target_pairs={{0,8},{8,0},{16,24},{24,16},{1,9},{9,1},{17,25},{25,17},{2,10},{10... | collective-permute-start | bytes 393224 | tf_op jit(solution)/shard_map/ppermute | solution.py:21
  69.0 6.4 %collective-permute-start.16 = (bf16[64,1024]{1,0:T(8,128)(2,1)S(1)}, bf16[64,1024]{1,0:T(8,128)(2,1)S(1)}, u32[]{:S(2)}, u32[]{:S(2)}) collective-permute-start(bf16[64,1024]{1,0:T(8,128)(2,1)S(1)} %get-tuple-element.88), channel_id=1, source_target_pairs={{0,16},{8,24},{16,0},{24,8},{1,17},{9,25},{17,1},{25,9},{2,18},{10... | collective-permute-start | bytes 393224 | tf_op jit(solution)/shard_map/ppermute | solution.py:21
  69.8 8.4 %collective-permute-start.14 = (bf16[64,1024]{1,0:T(8,128)(2,1)S(1)}, bf16[64,1024]{1,0:T(8,128)(2,1)S(1)}, u32[]{:S(2)}, u32[]{:S(2)}) collective-permute-start(bf16[64,1024]{1,0:T(8,128)(2,1)S(1)} %get-tuple-element.84), channel_id=1, source_target_pairs={{0,16},{8,24},{16,0},{24,8},{1,17},{9,25},{17,1},{25,9},{2,18},{10... | collective-permute-start | bytes 393224 | tf_op jit(solution)/shard_map/ppermute | solution.py:21
  72.0 9.0 %collective-permute-start.12 = (bf16[64,1024]{1,0:T(8,128)(2,1)S(1)}, bf16[64,1024]{1,0:T(8,128)(2,1)S(1)}, u32[]{:S(2)}, u32[]{:S(2)}) collective-permute-start(bf16[64,1024]{1,0:T(8,128)(2,1)S(1)} %get-tuple-element.80), channel_id=1, source_target_pairs={{0,16},{8,24},{16,0},{24,8},{1,17},{9,25},{17,1},{25,9},{2,18},{10... | collective-permute-start | bytes 393224 | tf_op jit(solution)/shard_map/ppermute | solution.py:21
  72.8 10.6 %collective-permute-start.10 = (bf16[64,1024]{1,0:T(8,128)(2,1)S(1)}, bf16[64,1024]{1,0:T(8,128)(2,1)S(1)}, u32[]{:S(2)}, u32[]{:S(2)}) collective-permute-start(bf16[64,1024]{1,0:T(8,128)(2,1)S(1)} %get-tuple-element.76), channel_id=1, source_target_pairs={{0,16},{8,24},{16,0},{24,8},{1,17},{9,25},{17,1},{25,9},{2,18},{10... | collective-permute-start | bytes 393224 | tf_op jit(solution)/shard_map/ppermute | solution.py:21
  75.4 2.8 %collective-permute-start.17 = (bf16[64,1024]{1,0:T(8,128)(2,1)S(1)}, bf16[64,1024]{1,0:T(8,128)(2,1)S(1)}, u32[]{:S(2)}, u32[]{:S(2)}) collective-permute-start(bf16[64,1024]{1,0:T(8,128)(2,1)S(1)} %add_convert_fusion.rest_4_), channel_id=1, source_target_pairs={{0,8},{8,0},{16,24},{24,16},{1,9},{9,1},{17,25},{25,17},{2,10},{10... | collective-permute-start | bytes 393224 | tf_op jit(solution)/shard_map/ppermute | solution.py:21
  79.8 1.4 %collective-permute-start.18 = (bf16[64,1024]{1,0:T(8,128)(2,1)S(1)}, bf16[64,1024]{1,0:T(8,128)(2,1)S(1)}, u32[]{:S(2)}, u32[]{:S(2)}) collective-permute-start(bf16[64,1024]{1,0:T(8,128)(2,1)S(1)} %add_convert_fusion.1.rest_4_), channel_id=1, source_target_pairs={{0,8},{8,0},{16,24},{24,16},{1,9},{9,1},{17,25},{25,17},{2,10},{10... | collective-permute-start | bytes 393224 | tf_op jit(solution)/shard_map/ppermute | solution.py:21
  82.8 1.4 %collective-permute-start.19 = (bf16[64,1024]{1,0:T(8,128)(2,1)S(1)}, bf16[64,1024]{1,0:T(8,128)(2,1)S(1)}, u32[]{:S(2)}, u32[]{:S(2)}) collective-permute-start(bf16[64,1024]{1,0:T(8,128)(2,1)S(1)} %add_convert_fusion.2.rest_4_), channel_id=1, source_target_pairs={{0,8},{8,0},{16,24},{24,16},{1,9},{9,1},{17,25},{25,17},{2,10},{10... | collective-permute-start | bytes 393224 | tf_op jit(solution)/shard_map/ppermute | solution.py:21
  85.7 1.4 %collective-permute-start.20 = (bf16[64,1024]{1,0:T(8,128)(2,1)S(1)}, bf16[64,1024]{1,0:T(8,128)(2,1)S(1)}, u32[]{:S(2)}, u32[]{:S(2)}) collective-permute-start(bf16[64,1024]{1,0:T(8,128)(2,1)S(1)} %add_convert_fusion.3.rest_4_), channel_id=1, source_target_pairs={{0,8},{8,0},{16,24},{24,16},{1,9},{9,1},{17,25},{25,17},{2,10},{10... | collective-permute-start | bytes 393224 | tf_op jit(solution)/shard_map/ppermute | solution.py:21
  (10 other events, 63.9 us)

commit v4 on v3

v4 whole, which is shorter than its diff:
```python
import functools
import math

import jax
import jax.numpy as jnp
from jax import lax
from jax.experimental import pallas as pl
from jax.experimental.pallas import tpu as pltpu
from jax.sharding import PartitionSpec as P

BF16 = jnp.bfloat16
F32 = jnp.float32
EIGHTHS = (3, 3, 2)
STEP = 1024
AHEAD = 3
HBM = pl.BlockSpec(memory_space=pltpu.HBM)
VMEM = pl.BlockSpec(memory_space=pltpu.VMEM)
SMEM = pl.BlockSpec(memory_space=pltpu.SMEM)


def exchange(value, axis, mask):
    n = lax.axis_size(axis)
    return lax.ppermute(value, axis, [(i, i ^ mask) for i in range(n)])


def doubling(value, axis, first=1, other=None):
    n = lax.axis_size(axis)
    mask = first
    if other is None:
        other = exchange(value, axis, mask)
    while 2 * mask < n:
        mask *= 2
        value = (value.astype(F32) + other.astype(F32)).astype(value.dtype)
        other = exchange(value, axis, mask)
    return value, other


def nt(a, b):
    return lax.dot_general(a, b, (((1,), (1,)), ((), ())), preferred_element_type=F32)


def call(kernel, name, in_specs, out_shape, out_specs, scratch=(), aliases=None, limit=16, work=1000):
    return pl.pallas_call(
        kernel,
        in_specs=in_specs,
        out_shape=out_shape,
        out_specs=out_specs,
        scratch_shapes=list(scratch),
        input_output_aliases=aliases or {},
        compiler_params=pltpu.CompilerParams(vmem_limit_bytes=limit * 1024 * 1024),
        cost_estimate=pl.CostEstimate(flops=work, bytes_accessed=work, transcendentals=0),
        name=name,
    )


def pin(space, *values):
    return [pltpu.with_memory_space_constraint(v, space) for v in values]


def columns(start, size):
    return pl.ds(pl.multiple_of(start, 128), size)


def load_kernel(side, x_hbm, u_hbm, a_hbm, m_out, a_out, x_out, u_out, mine_out, other_out, acc, sems):
    width = x_hbm.shape[1]
    steps = width // STEP

    def pair(j):
        cut = columns(j * STEP, STEP)
        return (
            pltpu.make_async_copy(x_hbm.at[:, cut], x_out.at[:, cut], sems.at[0, j]),
            pltpu.make_async_copy(a_hbm.at[:, cut], a_out.at[:, cut], sems.at[1, j]),
        )

    def begin(j):
        for copy in pair(j):
            copy.start()

    dual = pltpu.make_async_copy(u_hbm, u_out, sems.at[2, 0])
    for j in range(min(AHEAD, steps)):
        begin(j)
    acc[...] = jnp.zeros_like(acc)

    @pl.loop(0, steps)
    def _(j):
        for copy in pair(j):
            copy.wait()

        @pl.when(j + AHEAD < steps)
        def _():
            begin(j + AHEAD)

        @pl.when(j == max(steps - AHEAD, 0))
        def _():
            dual.start()

        cut = columns(j * STEP, STEP)
        acc[...] += nt(x_out[:, cut].astype(BF16), a_out[:, cut])

    m_out[...] = acc[...].astype(BF16)
    dual.wait()
    half = width // 2
    mine = columns(side[0] * half, half)
    other = columns((1 - side[0]) * half, half)
    mine_out[...] = x_out[:, mine] + u_out[:, mine]
    other_out[...] = x_out[:, other] + u_out[:, other]


def load(side, x, u, design):
    tasks, width = x.shape
    samples = design.shape[0]
    full = pltpu.VMEM((tasks, width), F32)
    half = pltpu.VMEM((tasks, width // 2), F32)
    return call(
        load_kernel,
        "load_and_margins",
        [SMEM] + [HBM] * 3,
        (pltpu.VMEM((tasks, samples), BF16), pltpu.VMEM(design.shape, BF16), full, full, half, half),
        [VMEM] * 6,
        [pltpu.VMEM((tasks, samples), F32), pltpu.SemaphoreType.DMA((3, width // STEP))],
    )(side, *pin(pltpu.HBM, x, u, design))


def rest_kernel(blocks_count, z_hbm, sign_hbm, eta_hbm, rho_hbm, lam_hbm, *refs):
    z_out, sign_out, scale_out, eta_row, rho_row, lam_row, sems = refs
    pairs = ((eta_hbm, eta_row), (rho_hbm, rho_row), (lam_hbm, lam_row), (z_hbm, z_out), (sign_hbm, sign_out))
    copies = [pltpu.make_async_copy(a, b, sems.at[k]) for k, (a, b) in enumerate(pairs)]
    for copy in copies:
        copy.start()
    for copy in copies[:3]:
        copy.wait()
    tasks = z_out.shape[0]
    one = lax.broadcasted_iota(jnp.int32, (tasks, tasks), 0) == lax.broadcasted_iota(jnp.int32, (tasks, tasks), 1)
    eta, rho, lam = eta_row[...], rho_row[...], lam_row[...]
    for k, row in enumerate((eta, eta * rho, lam / (rho * blocks_count))):
        upright = jnp.where(one, jnp.broadcast_to(row, (tasks, tasks)), 0.0)
        scale_out[:, k : k + 1] = jnp.sum(upright, axis=1, keepdims=True)
    for copy in copies[3:]:
        copy.wait()


def load_rest(z, sign, step_size, rho, penalty, blocks_count):
    tasks, width = z.shape
    rows = [v.reshape(1, tasks) for v in (step_size, rho, penalty)]
    return call(
        functools.partial(rest_kernel, blocks_count),
        "load_rest",
        [HBM] * 5,
        (pltpu.VMEM((tasks, width), F32), pltpu.VMEM(sign.shape, jnp.int32), pltpu.VMEM((tasks, 128), F32)),
        [VMEM] * 3,
        [pltpu.VMEM((1, tasks), F32)] * 3 + [pltpu.SemaphoreType.DMA((5,))],
    )(*pin(pltpu.HBM, z, sign, *rows))


def residual(sign, own, other):
    margin = own.astype(F32) + other.astype(F32)
    sign = sign.astype(F32)
    return (sign * jax.nn.sigmoid(-sign * margin)).astype(BF16)


def turn_kernel(sign, own, other, scale, x_ref, u_ref, z_ref, a_ref, q_out, m_out, resid, acc):
    resid[...] = residual(sign[...], own[...], other[...])
    acc[...] = jnp.zeros_like(acc)
    eta, pull = scale[:, 0:1], scale[:, 1:2]

    @pl.loop(0, x_ref.shape[1] // STEP)
    def _(j):
        cut = columns(j * STEP, STEP)
        push = eta * jnp.dot(resid[...], a_ref[:, cut], preferred_element_type=F32)
        x = x_ref[:, cut]
        x = x - pull * (x - z_ref[:, cut] + u_ref[:, cut]) + push
        q_out[:, cut] = (1.0 - pull) * push
        acc[...] += nt(x.astype(BF16), a_ref[:, cut])

    m_out[...] = acc[...].astype(BF16)


def turn(sign, pair, scale, x, u, z, design):
    tasks, width = x.shape
    samples = design.shape[0]
    return call(
        turn_kernel,
        "turn",
        [VMEM] * 8,
        (pltpu.VMEM((tasks, width), F32), pltpu.VMEM((tasks, samples), BF16)),
        [VMEM] * 2,
        [pltpu.VMEM((tasks, samples), BF16), pltpu.VMEM((tasks, samples), F32)],
    )(*pin(pltpu.VMEM, sign, *pair, scale, x, u, z, design))


def push_kernel(mine, begin, size, side, sign, own, other, scale, q_ref, a_ref, *rest):
    received = rest[0] if mine else None
    h_out, sent_out = rest[-2:]
    half = q_ref.shape[1] // 2
    eta = scale[:, 0:1]
    resid = residual(sign[...], own[...], other[...])
    base = (side[0] if mine else 1 - side[0]) * half + begin
    step = math.gcd(512, size)
    for j in range(size // step):
        cut = columns(base + j * step, step)
        here = pl.ds(j * step, step)
        push = q_ref[:, cut] + eta * jnp.dot(resid, a_ref[:, cut], preferred_element_type=F32)
        h_out[:, here] = push
        if mine:
            push = push + received[:, here].astype(F32)
        sent_out[:, here] = push.astype(BF16)


def push(side, sign, pair, scale, q, design, received, begin, size):
    tasks = q.shape[0]
    mine = received is not None
    args = [sign, *pair, scale, q, design] + ([received] if mine else [])
    return call(
        functools.partial(push_kernel, mine, begin, size),
        "push_mine" if mine else "push_other",
        [SMEM] + [VMEM] * len(args),
        (pltpu.VMEM((tasks, size), F32), pltpu.VMEM((tasks, size), BF16)),
        [VMEM] * 2,
    )(side, *pin(pltpu.VMEM, *args))


def store_kernel(sizes, side, scale, x_ref, u_ref, z_ref, *rest):
    count = len(sizes)
    hs = (rest[:count], rest[count : 2 * count])
    x_out, stage, sems = rest[2 * count :]
    half = x_ref.shape[1] // 2
    keep = 1.0 - scale[:, 1:2]
    copies = []
    for k in range(2):
        begin = 0
        for c, size in enumerate(sizes):
            cut = columns((side[0] if k == 0 else 1 - side[0]) * half + begin, size)
            u, z = u_ref[:, cut], z_ref[:, cut]
            stage[:, cut] = z - u + keep * keep * (x_ref[:, cut] - z + u) + hs[k][c][...]
            copy = pltpu.make_async_copy(stage.at[:, cut], x_out.at[:, cut], sems.at[k, c])
            copy.start()
            copies.append(copy)
            begin += size
    for copy in copies:
        copy.wait()


def store_x(side, scale, x, u, z, mines, others, sizes):
    tasks, width = x.shape
    return call(
        functools.partial(store_kernel, sizes),
        "store_x",
        [SMEM] + [VMEM] * (4 + 2 * len(sizes)),
        pltpu.HBM((tasks, width), F32),
        HBM,
        [pltpu.VMEM((tasks, width), F32), pltpu.SemaphoreType.DMA((2, len(sizes)))],
    )(side, *pin(pltpu.VMEM, scale, x, u, z, *mines, *others))


def final_kernel(blocks_count, begin, size, buffered, side, scale, x_ref, u_ref, z_ref, *rest):
    starts, hs, pushes = rest[0:2], rest[2:4], rest[4:6]
    outs = rest[6 + 2 * buffered : 8 + 2 * buffered]
    stage, sems = rest[-2:]
    half = x_ref.shape[1] // 2
    pull, limit = scale[:, 1:2], scale[:, 2:3]
    keep = 1.0 - pull
    copies = []
    for k in range(2):
        cut = columns((side[0] if k == 0 else 1 - side[0]) * half + begin, size)
        z = z_ref[:, cut]
        start = starts[k][:, pl.ds(begin, size)]
        mean = (keep * keep * start + pushes[k][...].astype(F32)) * (1.0 / blocks_count) + pull * (1.0 + keep) * z
        new_z = mean - jnp.clip(mean, -limit, limit)
        moved = z + keep * keep * (x_ref[:, cut] - z + u_ref[:, cut]) + hs[k][...]
        for o, value in enumerate((new_z, moved - new_z)):
            stage[k, o] = value
            copy = pltpu.make_async_copy(stage.at[k, o], outs[o].at[:, cut], sems.at[k, o])
            copy.start()
            copies.append(copy)
    for copy in copies:
        copy.wait()


def final(side, scale, x, u, z, starts, hs, pushes, buffers, begin, size, blocks_count):
    tasks, width = x.shape
    buffered = buffers is not None
    args = pin(pltpu.VMEM, scale, x, u, z, *starts, *hs, *pushes)
    out = pltpu.HBM((tasks, width), F32)
    aliases = {}
    if buffered:
        aliases = {1 + len(args) + o: o for o in range(2)}
        args += pin(pltpu.HBM, *buffers)
    return call(
        functools.partial(final_kernel, blocks_count, begin, size, buffered),
        "final",
        [SMEM] + [VMEM] * 10 + [HBM] * (2 * buffered),
        (out, out),
        [HBM] * 2,
        [pltpu.VMEM((2, 2, tasks, size), F32), pltpu.SemaphoreType.DMA((2, 2))],
        aliases,
    )(side, *args)


def tie(value, *after):
    return lax.optimization_barrier((value, after))[0]


def per_device(design, labels, local_x, dual_u, consensus_z, step_size, rho, penalty):
    tasks, width = consensus_z.shape
    half = width // 2
    blocks_count = lax.axis_size("rows")
    side = (lax.axis_index("rows") & 1).astype(jnp.int32)[None]

    margin1, design, x0, dual, start_mine, start_other = load(side, local_x[0], dual_u[0], design)
    start_mine = start_mine + exchange(start_other, "rows", 1)
    other = exchange(margin1, "feat", 1)
    z, sign, scale = load_rest(consensus_z, labels, tie(step_size, other), rho, penalty, blocks_count)
    pair = doubling(margin1, "feat", 1, other)
    pair = tie(pair, start_mine)

    carried, margin2 = turn(sign, pair, scale, x0, dual, z, design)
    pair = doubling(margin2, "feat")
    mask = 2
    while mask < blocks_count:
        start_mine = start_mine + exchange(start_mine, "rows", mask)
        mask *= 2
    pair = tie(pair, start_mine)
    start_theirs = exchange(start_mine, "rows", 1)

    sizes = [half * part // sum(EIGHTHS) for part in EIGHTHS]
    begins = [sum(sizes[:c]) for c in range(len(sizes))]
    count = len(sizes)
    args = (sign, pair, scale, carried, design)
    others, mines, received, sums = [], [], [], []
    token = side
    for c in range(count + 1):
        if c < count:
            value, other = push(token, *args, None, begins[c], sizes[c])
            others.append(value)
            received.append(exchange(other, "rows", 1))
        if c > 0:
            value, sent = push(token, *args, received[c - 1], begins[c - 1], sizes[c - 1])
            mines.append(value)
            sums.append(doubling(sent, "rows", 2))
            token = tie(side, sent)
    new_x = store_x(side, scale, x0, dual, z, mines, others, sizes)

    results, pushes = None, []
    for c in range(count + 1):
        if c < count:
            a, b = sums[c]
            if c == 0:
                b = tie(b, new_x)
            if c > 1:
                b = tie(b, results)
            piece = (a.astype(F32) + b.astype(F32)).astype(BF16)
            pushes.append((piece, exchange(piece, "rows", 1)))
        if c > 0:
            results = final(
                side, scale, x0, dual, z, (start_mine, start_theirs), (mines[c - 1], others[c - 1]), pushes[c - 1],
                results, begins[c - 1], sizes[c - 1], blocks_count,
            )
    new_z, new_u = results
    return (new_x[None], new_z, new_u[None])


def solution(mesh):
    in_specs = (
        P("rows", "feat"),
        P(None, "rows"),
        P("rows", None, "feat"),
        P("rows", None, "feat"),
        P(None, "feat"),
        P(),
        P(),
        P(),
    )
    out_specs = (P("rows", None, "feat"), P(None, "feat"), P("rows", None, "feat"))
    return jax.shard_map(
        per_device, mesh=mesh, in_specs=in_specs, out_specs=out_specs, check_vma=False
    )
```

time: 88.9 us -> 69 us (0.78)
  local copies, waits for them, and re-layouts: 15.1 us -> 0 us
  waiting for transfers between devices: 24.3 us -> 19.3 us
  other arithmetic: 2.98 us -> 0.45 us
  Pallas kernels: 23.6 us -> 25.5 us
  starting transfers between devices: 21.9 us -> 22.8 us
    unnamed x26 -> x0, local copies, waits for them, and re-layouts: 15 us -> none
    ppermute x21 -> x18, waiting for transfers between devices: 24.3 us -> 19.3 us  [exchange(): return lax.ppermute(value, axis, [(i, i ^ mask) for i in range(n)])]
    pallas_call x13 -> x12, Pallas kernels: 16.4 us -> 18.2 us  [the longest x1 6.82 us: load(): call(load_kernel, 'load_and_margins', [SMEM] + [HBM] * 3, (pltpu.VMEM((ta...]
    add x1, other arithmetic: 1.65 us -> 0.11 us  [per_device(): start_mine = start_mine + exchange(start_mine, 'rows', mask)]
    add x1, other arithmetic: 1.08 us -> 0.11 us  [per_device(): start_mine = start_mine + exchange(start_other, 'rows', 1)]
    ppermute x21 -> x18, starting transfers between devices: 21.9 us -> 22.8 us  [exchange(): return lax.ppermute(value, axis, [(i, i ^ mask) for i in range(n)])]
  transfers between devices with their start and end apart: 21 -> 18, of which waited for: 13 -> 10; matrix products, arithmetic and copies ran while one was open for 3% -> 1% of each run, Pallas kernels for 15% -> 24%
where the time goes in v4:
time: 69 us; the launch traced here: 68.8 us
  Pallas kernels  25.5 us (37%)
  starting transfers between devices  22.8 us (33%)
  waiting for transfers between devices  19.3 us (28%)
  between operations  0.81 us (1%)
    ppermute x18, starting transfers between devices, exchange(): return lax.ppermute(value, axis, [(i, i ^ mask) for i in range(n)])  22.8 us
    ppermute x18, waiting for transfers between devices, exchange(): return lax.ppermute(value, axis, [(i, i ^ mask) for i in range(n)])  19.3 us
    pallas_call x1, Pallas kernels, turn(): call(turn_kernel, 'turn', [VMEM] * 8, (pltpu.VMEM((tasks, width), F32), p...  7.28 us
    pallas_call x1, Pallas kernels, load(): call(load_kernel, 'load_and_margins', [SMEM] + [HBM] * 3, (pltpu.VMEM((ta...  6.82 us
    pallas_call x3, Pallas kernels, final(): call(functools.partial(final_kernel, blocks_count, begin, size, buffered)...  4.65 us
    pallas_call x6, Pallas kernels, push(): call(functools.partial(push_kernel, mine, begin, size), 'push_mine' if mi...  3.05 us
    pallas_call x1, Pallas kernels, store_x(): call(functools.partial(store_kernel, sizes), 'store_x', [SMEM] + [VMEM] *...  1.98 us
    pallas_call x1, Pallas kernels, load_rest(): call(functools.partial(rest_kernel, blocks_count), 'load_rest', [HBM] * 5...  1.68 us
  transfers between devices with their start and end apart: 18, of which 10 were waited for; matrix products, arithmetic and copies ran while one was open for 1% of the time, Pallas kernels for 24%

profile of v4, /device:TPU:0, one launch (start us, length us, event | category | flops | bytes accessed | tf_op | source)
XLA Modules:
  0.0 68.8 jit_solution(2733216553555073529)
XLA Ops:
  0.6 6.8 %load_and_margins.1 = (bf16[64,768]{1,0:T(8,128)(2,1)S(1)}, bf16[768,8192]{1,0:T(8,128)(2,1)S(1)}, f32[64,8192]{1,0:T(8,128)S(1)}, f32[64,8192]{1,0:T(8,128)S(1)...) custom-call(s32[1]{0:T(128)} %bitcast.side, f32[64,8192]{1,0:T(8,128)} %bitcast.9, f32[64,8192]{1,0:T(8,128)} %bitcast.10, ...), custom_call_target="tpu_custom_call" | custom-call | flops 1000 | bytes 1000 | tf_op jit(solution)/shard_map/load_and_margins/pallas_call | solution.py:114
  8.0 2.6 %collective-permute-start = (bf16[64,768]{1,0:T(8,128)(2,1)S(1)}, bf16[64,768]{1,0:T(8,128)(2,1)S(1)}, u32[]{:S(2)}, u32[]{:S(2)}) collective-permute-start(bf16[64,768]{1,0:T(8,128)(2,1)S(1)} %get-tuple-element.41), channel_id=1, source_target_pairs={{0,1},{1,0},{2,3},{3,2},{4,5},{5,4},{6,7},{7,6},{8,9},{9,8},{10,11... | collective-permute-start | bytes 294920 | tf_op jit(solution)/shard_map/ppermute | solution.py:23
  10.6 3.4 %collective-permute-done = bf16[64,768]{1,0:T(8,128)(2,1)S(1)} collective-permute-done((bf16[64,768]{1,0:T(8,128)(2,1)S(1)}, bf16[64,768]{1,0:T(8,128)(2,1)S(1)}, u32[]{:S(2)}, u32[]{:S(2)}) %collective-permute-start) | collective-permute-done | bytes 98336 | tf_op jit(solution)/shard_map/ppermute | solution.py:23
  14.0 1.9 %collective-permute-start.1 = (bf16[64,768]{1,0:T(8,128)(2,1)S(1)}, bf16[64,768]{1,0:T(8,128)(2,1)S(1)}, u32[]{:S(2)}, u32[]{:S(2)}) collective-permute-start(bf16[64,768]{1,0:T(8,128)(2,1)S(1)} %add_convert_fusion.6), channel_id=1, source_target_pairs={{0,2},{1,3},{2,0},{3,1},{4,6},{5,7},{6,4},{7,5},{8,10},{9,11},{10,... | collective-permute-start | bytes 294920 | tf_op jit(solution)/shard_map/ppermute | solution.py:23
  16.0 1.6 %collective-permute-start.7 = (f32[64,4096]{1,0:T(8,128)S(1)}, f32[64,4096]{1,0:T(8,128)S(1)}, u32[]{:S(2)}, u32[]{:S(2)}) collective-permute-start(f32[64,4096]{1,0:T(8,128)S(1)} %add.29), channel_id=1, source_target_pairs={{0,16},{8,24},{16,0},{24,8},{1,17},{9,25},{17,1},{25,9},{2,18},{10... | collective-permute-start | bytes 3145736 | tf_op jit(solution)/shard_map/ppermute | solution.py:23
  17.5 1.1 %collective-permute-done.1 = bf16[64,768]{1,0:T(8,128)(2,1)S(1)} collective-permute-done((bf16[64,768]{1,0:T(8,128)(2,1)S(1)}, bf16[64,768]{1,0:T(8,128)(2,1)S(1)}, u32[]{:S(2)}, u32[]{:S(2)}) %collective-permute-start.1) | collective-permute-done | bytes 98336 | tf_op jit(solution)/shard_map/ppermute | solution.py:23
  18.7 2.9 %collective-permute-start.2 = (bf16[64,768]{1,0:T(8,128)(2,1)S(1)}, bf16[64,768]{1,0:T(8,128)(2,1)S(1)}, u32[]{:S(2)}, u32[]{:S(2)}) collective-permute-start(bf16[64,768]{1,0:T(8,128)(2,1)S(1)} %add_convert_fusion.5.own), channel_id=1, source_target_pairs={{0,4},{1,5},{2,6},{3,7},{4,0},{5,1},{6,2},{7,3},{8,12},{9,13},{10,... | collective-permute-start | bytes 294920 | tf_op jit(solution)/shard_map/ppermute | solution.py:23
  21.6 1.7 %load_rest.1 = (f32[64,8192]{1,0:T(8,128)S(1)}, s32[64,768]{1,0:T(8,128)S(1)}, f32[64,128]{1,0:T(8,128)S(1)}) custom-call(f32[64,8192]{1,0:T(8,128)} %z_hbm.1, s32[64,768]{1,0:T(8,128)} %sign_hbm.1, f32[1,64]{1,0:T(1,128)} %bitcast.12, f32[1,64]{1,0:T(1,128)} %bitcast.13, f32[1,64]{1,0:T(1,128)} %bitcast.14), custom_call_target="tpu_custom_call" | custom-call | flops 1000 | bytes 1000 | tf_op jit(solution)/shard_map/load_rest/pallas_call | solution.py:145
  23.3 1.0 %collective-permute-done.2.other = bf16[64,768]{1,0:T(8,128)(2,1)S(1)} collective-permute-done((bf16[64,768]{1,0:T(8,128)(2,1)S(1)}, bf16[64,768]{1,0:T(8,128)(2,1)S(1)}, u32[]{:S(2)}, u32[]{:S(2)}) %collective-permute-start.2) | collective-permute-done | bytes 98336 | tf_op jit(solution)/shard_map/ppermute | solution.py:23
  24.3 7.3 %turn.1 = (f32[64,8192]{1,0:T(8,128)S(1)}, bf16[64,768]{1,0:T(8,128)(2,1)S(1)}) custom-call(s32[64,768]{1,0:T(8,128)S(1)} %get-tuple-element.47.sign, bf16[64,768]{1,0:T(8,128)(2,1)S(1)} %add_convert_fusion.5.own, bf16[64,768]{1,0:T(8,128)(2,1)S(1)} %collective-permute-done.2.other, f32[64,128]{1,0:T(8,128)S(1)} %get-tuple-element.43.scale, ...), custom_call_target="tpu_custom_call" | custom-call | flops 1000 | bytes 1000 | tf_op jit(solution)/shard_map/turn/pallas_call | solution.py:181
  31.6 1.8 %collective-permute-start.4 = (bf16[64,768]{1,0:T(8,128)(2,1)S(1)}, bf16[64,768]{1,0:T(8,128)(2,1)S(1)}, u32[]{:S(2)}, u32[]{:S(2)}) collective-permute-start(bf16[64,768]{1,0:T(8,128)(2,1)S(1)} %get-tuple-element.53), channel_id=1, source_target_pairs={{0,1},{1,0},{2,3},{3,2},{4,5},{5,4},{6,7},{7,6},{8,9},{9,8},{10,11... | collective-permute-start | bytes 294920 | tf_op jit(solution)/shard_map/ppermute | solution.py:23
  33.4 2.9 %collective-permute-done.4 = bf16[64,768]{1,0:T(8,128)(2,1)S(1)} collective-permute-done((bf16[64,768]{1,0:T(8,128)(2,1)S(1)}, bf16[64,768]{1,0:T(8,128)(2,1)S(1)}, u32[]{:S(2)}, u32[]{:S(2)}) %collective-permute-start.4) | collective-permute-done | bytes 98336 | tf_op jit(solution)/shard_map/ppermute | solution.py:23
  36.3 2.0 %collective-permute-start.5 = (bf16[64,768]{1,0:T(8,128)(2,1)S(1)}, bf16[64,768]{1,0:T(8,128)(2,1)S(1)}, u32[]{:S(2)}, u32[]{:S(2)}) collective-permute-start(bf16[64,768]{1,0:T(8,128)(2,1)S(1)} %add_convert_fusion.4), channel_id=1, source_target_pairs={{0,2},{1,3},{2,0},{3,1},{4,6},{5,7},{6,4},{7,5},{8,10},{9,11},{10,... | collective-permute-start | bytes 294920 | tf_op jit(solution)/shard_map/ppermute | solution.py:23
  38.3 2.7 %collective-permute-done.5 = bf16[64,768]{1,0:T(8,128)(2,1)S(1)} collective-permute-done((bf16[64,768]{1,0:T(8,128)(2,1)S(1)}, bf16[64,768]{1,0:T(8,128)(2,1)S(1)}, u32[]{:S(2)}, u32[]{:S(2)}) %collective-permute-start.5) | collective-permute-done | bytes 98336 | tf_op jit(solution)/shard_map/ppermute | solution.py:23
  41.0 4.1 %collective-permute-start.6 = (bf16[64,768]{1,0:T(8,128)(2,1)S(1)}, bf16[64,768]{1,0:T(8,128)(2,1)S(1)}, u32[]{:S(2)}, u32[]{:S(2)}) collective-permute-start(bf16[64,768]{1,0:T(8,128)(2,1)S(1)} %add_convert_fusion.3.own), channel_id=1, source_target_pairs={{0,4},{1,5},{2,6},{3,7},{4,0},{5,1},{6,2},{7,3},{8,12},{9,13},{10,... | collective-permute-start | bytes 294920 | tf_op jit(solution)/shard_map/ppermute | solution.py:23
  45.2 3.5 %collective-permute-done.6.other = bf16[64,768]{1,0:T(8,128)(2,1)S(1)} collective-permute-done((bf16[64,768]{1,0:T(8,128)(2,1)S(1)}, bf16[64,768]{1,0:T(8,128)(2,1)S(1)}, u32[]{:S(2)}, u32[]{:S(2)}) %collective-permute-start.6) | collective-permute-done | bytes 98336 | tf_op jit(solution)/shard_map/ppermute | solution.py:23
  51.4 1.6 %collective-permute-start.13 = (bf16[64,1536]{1,0:T(8,128)(2,1)S(1)}, bf16[64,1536]{1,0:T(8,128)(2,1)S(1)}, u32[]{:S(2)}, u32[]{:S(2)}) collective-permute-start(bf16[64,1536]{1,0:T(8,128)(2,1)S(1)} %get-tuple-element.59), channel_id=1, source_target_pairs={{0,16},{8,24},{16,0},{24,8},{1,17},{9,25},{17,1},{25,9},{2,18},{10... | collective-permute-start | bytes 589832 | tf_op jit(solution)/shard_map/ppermute | solution.py:23
  54.5 0.6 collective-permute-start.16
  55.5 1.6 %collective-permute-start.12 = (bf16[64,1024]{1,0:T(8,128)(2,1)S(1)}, bf16[64,1024]{1,0:T(8,128)(2,1)S(1)}, u32[]{:S(2)}, u32[]{:S(2)}) collective-permute-start(bf16[64,1024]{1,0:T(8,128)(2,1)S(1)} %get-tuple-element.70), channel_id=1, source_target_pairs={{0,16},{8,24},{16,0},{24,8},{1,17},{9,25},{17,1},{25,9},{2,18},{10... | collective-permute-start | bytes 393224 | tf_op jit(solution)/shard_map/ppermute | solution.py:23
  57.1 2.0 %store_x.1 = f32[64,8192]{1,0:T(8,128)} custom-call(s32[1]{0:T(128)} %bitcast.side, f32[64,128]{1,0:T(8,128)S(1)} %get-tuple-element.43.scale, f32[64,8192]{1,0:T(8,128)S(1)} %get-tuple-element.44.x_ref, f32[64,8192]{1,0:T(8,128)S(1)} %get-tuple-element.45.u_ref, f32[64,8192]{1,0:T(8,128)S(1)} %get-tuple-element.46.z_ref, ...), custom_call_target="tpu_custom_call" | custom-call | flops 1000 | bytes 1000 | tf_op jit(solution)/shard_map/store_x/pallas_call | solution.py:245
  59.3 4.1 %collective-permute-done.16 = bf16[64,1536]{1,0:T(8,128)(2,1)S(1)} collective-permute-done((bf16[64,1536]{1,0:T(8,128)(2,1)S(1)}, bf16[64,1536]{1,0:T(8,128)(2,1)S(1)}, u32[]{:S(2)}, u32[]{:S(2)}) %collective-permute-start.16) | collective-permute-done | bytes 196640 | tf_op jit(solution)/shard_map/ppermute | solution.py:23
  63.5 1.7 %final.3 = (f32[64,8192]{1,0:T(8,128)}, f32[64,8192]{1,0:T(8,128)}) custom-call(s32[1]{0:T(128)} %bitcast.side, f32[64,128]{1,0:T(8,128)S(1)} %get-tuple-element.43.scale, f32[64,8192]{1,0:T(8,128)S(1)} %get-tuple-element.44.x_ref, f32[64,8192]{1,0:T(8,128)S(1)} %get-tuple-element.45.u_ref, f32[64,8192]{1,0:T(8,128)S(1)} %get-tuple-element.46.z_ref, ...), custom_call_target="tpu_custom_call" | custom-call | flops 1000 | bytes 1000 | tf_op jit(solution)/shard_map/final/pallas_call | solution.py:288
  65.8 1.7 %final.4 = (f32[64,8192]{1,0:T(8,128)}, f32[64,8192]{1,0:T(8,128)}) custom-call(s32[1]{0:T(128)} %bitcast.side, f32[64,128]{1,0:T(8,128)S(1)} %get-tuple-element.43.scale, f32[64,8192]{1,0:T(8,128)S(1)} %get-tuple-element.44.x_ref, f32[64,8192]{1,0:T(8,128)S(1)} %get-tuple-element.45.u_ref, ...), custom_call_target="tpu_custom_call", output_to_operand_aliasing={{0}: (11, {}), {1}: (12, {})} | custom-call | flops 1000 | bytes 1000 | tf_op jit(solution)/shard_map/final/pallas_call | solution.py:288
  67.5 1.3 %final.5 = (f32[64,8192]{1,0:T(8,128)}, f32[64,8192]{1,0:T(8,128)}) custom-call(s32[1]{0:T(128)} %bitcast.side, f32[64,128]{1,0:T(8,128)S(1)} %get-tuple-element.43.scale, f32[64,8192]{1,0:T(8,128)S(1)} %get-tuple-element.44.x_ref, f32[64,8192]{1,0:T(8,128)S(1)} %get-tuple-element.45.u_ref, ...), custom_call_target="tpu_custom_call", output_to_operand_aliasing={{0}: (11, {}), {1}: (12, {})} | custom-call | flops 1000 | bytes 1000 | tf_op jit(solution)/shard_map/final/pallas_call | solution.py:288
  (34 shorter events, 6.4 us)
Async XLA Ops:
  7.5 8.4 %collective-permute-start.3 = (f32[64,4096]{1,0:T(8,128)S(1)}, f32[64,4096]{1,0:T(8,128)S(1)}, u32[]{:S(2)}, u32[]{:S(2)}) collective-permute-start(f32[64,4096]{1,0:T(8,128)S(1)} %get-tuple-element.49), channel_id=1, source_target_pairs={{0,8},{8,0},{16,24},{24,16},{1,9},{9,1},{17,25},{25,17},{2,10},{10... | collective-permute-start | bytes 3145736 | tf_op jit(solution)/shard_map/ppermute | solution.py:23
  8.0 6.0 %collective-permute-start = (bf16[64,768]{1,0:T(8,128)(2,1)S(1)}, bf16[64,768]{1,0:T(8,128)(2,1)S(1)}, u32[]{:S(2)}, u32[]{:S(2)}) collective-permute-start(bf16[64,768]{1,0:T(8,128)(2,1)S(1)} %get-tuple-element.41), channel_id=1, source_target_pairs={{0,1},{1,0},{2,3},{3,2},{4,5},{5,4},{6,7},{7,6},{8,9},{9,8},{10,11... | collective-permute-start | bytes 294920 | tf_op jit(solution)/shard_map/ppermute | solution.py:23
  14.0 4.7 %collective-permute-start.1 = (bf16[64,768]{1,0:T(8,128)(2,1)S(1)}, bf16[64,768]{1,0:T(8,128)(2,1)S(1)}, u32[]{:S(2)}, u32[]{:S(2)}) collective-permute-start(bf16[64,768]{1,0:T(8,128)(2,1)S(1)} %add_convert_fusion.6), channel_id=1, source_target_pairs={{0,2},{1,3},{2,0},{3,1},{4,6},{5,7},{6,4},{7,5},{8,10},{9,11},{10,... | collective-permute-start | bytes 294920 | tf_op jit(solution)/shard_map/ppermute | solution.py:23
  16.0 29.1 %collective-permute-start.7 = (f32[64,4096]{1,0:T(8,128)S(1)}, f32[64,4096]{1,0:T(8,128)S(1)}, u32[]{:S(2)}, u32[]{:S(2)}) collective-permute-start(f32[64,4096]{1,0:T(8,128)S(1)} %add.29), channel_id=1, source_target_pairs={{0,16},{8,24},{16,0},{24,8},{1,17},{9,25},{17,1},{25,9},{2,18},{10... | collective-permute-start | bytes 3145736 | tf_op jit(solution)/shard_map/ppermute | solution.py:23
  18.7 5.6 %collective-permute-start.2 = (bf16[64,768]{1,0:T(8,128)(2,1)S(1)}, bf16[64,768]{1,0:T(8,128)(2,1)S(1)}, u32[]{:S(2)}, u32[]{:S(2)}) collective-permute-start(bf16[64,768]{1,0:T(8,128)(2,1)S(1)} %add_convert_fusion.5.own), channel_id=1, source_target_pairs={{0,4},{1,5},{2,6},{3,7},{4,0},{5,1},{6,2},{7,3},{8,12},{9,13},{10,... | collective-permute-start | bytes 294920 | tf_op jit(solution)/shard_map/ppermute | solution.py:23
  31.6 4.7 %collective-permute-start.4 = (bf16[64,768]{1,0:T(8,128)(2,1)S(1)}, bf16[64,768]{1,0:T(8,128)(2,1)S(1)}, u32[]{:S(2)}, u32[]{:S(2)}) collective-permute-start(bf16[64,768]{1,0:T(8,128)(2,1)S(1)} %get-tuple-element.53), channel_id=1, source_target_pairs={{0,1},{1,0},{2,3},{3,2},{4,5},{5,4},{6,7},{7,6},{8,9},{9,8},{10,11... | collective-permute-start | bytes 294920 | tf_op jit(solution)/shard_map/ppermute | solution.py:23
  36.3 4.7 %collective-permute-start.5 = (bf16[64,768]{1,0:T(8,128)(2,1)S(1)}, bf16[64,768]{1,0:T(8,128)(2,1)S(1)}, u32[]{:S(2)}, u32[]{:S(2)}) collective-permute-start(bf16[64,768]{1,0:T(8,128)(2,1)S(1)} %add_convert_fusion.4), channel_id=1, source_target_pairs={{0,2},{1,3},{2,0},{3,1},{4,6},{5,7},{6,4},{7,5},{8,10},{9,11},{10,... | collective-permute-start | bytes 294920 | tf_op jit(solution)/shard_map/ppermute | solution.py:23
  41.0 7.8 %collective-permute-start.6 = (bf16[64,768]{1,0:T(8,128)(2,1)S(1)}, bf16[64,768]{1,0:T(8,128)(2,1)S(1)}, u32[]{:S(2)}, u32[]{:S(2)}) collective-permute-start(bf16[64,768]{1,0:T(8,128)(2,1)S(1)} %add_convert_fusion.3.own), channel_id=1, source_target_pairs={{0,4},{1,5},{2,6},{3,7},{4,0},{5,1},{6,2},{7,3},{8,12},{9,13},{10,... | collective-permute-start | bytes 294920 | tf_op jit(solution)/shard_map/ppermute | solution.py:23
  49.3 1.5 %collective-permute-start.8 = (bf16[64,1536]{1,0:T(8,128)(2,1)S(1)}, bf16[64,1536]{1,0:T(8,128)(2,1)S(1)}, u32[]{:S(2)}, u32[]{:S(2)}) collective-permute-start(bf16[64,1536]{1,0:T(8,128)(2,1)S(1)} %get-tuple-element.57), channel_id=1, source_target_pairs={{0,8},{8,0},{16,24},{24,16},{1,9},{9,1},{17,25},{25,17},{2,10},{10... | collective-permute-start | bytes 589832 | tf_op jit(solution)/shard_map/ppermute | solution.py:23
  49.9 4.0 %collective-permute-start.9 = (bf16[64,1536]{1,0:T(8,128)(2,1)S(1)}, bf16[64,1536]{1,0:T(8,128)(2,1)S(1)}, u32[]{:S(2)}, u32[]{:S(2)}) collective-permute-start(bf16[64,1536]{1,0:T(8,128)(2,1)S(1)} %get-tuple-element.61), channel_id=1, source_target_pairs={{0,8},{8,0},{16,24},{24,16},{1,9},{9,1},{17,25},{25,17},{2,10},{10... | collective-permute-start | bytes 589832 | tf_op jit(solution)/shard_map/ppermute | solution.py:23
  51.4 7.8 %collective-permute-start.13 = (bf16[64,1536]{1,0:T(8,128)(2,1)S(1)}, bf16[64,1536]{1,0:T(8,128)(2,1)S(1)}, u32[]{:S(2)}, u32[]{:S(2)}) collective-permute-start(bf16[64,1536]{1,0:T(8,128)(2,1)S(1)} %get-tuple-element.59), channel_id=1, source_target_pairs={{0,16},{8,24},{16,0},{24,8},{1,17},{9,25},{17,1},{25,9},{2,18},{10... | collective-permute-start | bytes 589832 | tf_op jit(solution)/shard_map/ppermute | solution.py:23
  53.3 1.7 %collective-permute-start.10 = (bf16[64,1024]{1,0:T(8,128)(2,1)S(1)}, bf16[64,1024]{1,0:T(8,128)(2,1)S(1)}, u32[]{:S(2)}, u32[]{:S(2)}) collective-permute-start(bf16[64,1024]{1,0:T(8,128)(2,1)S(1)} %get-tuple-element.65), channel_id=1, source_target_pairs={{0,8},{8,0},{16,24},{24,16},{1,9},{9,1},{17,25},{25,17},{2,10},{10... | collective-permute-start | bytes 393224 | tf_op jit(solution)/shard_map/ppermute | solution.py:23
  53.4 10.1 %collective-permute-start.11 = (f32[64,4096]{1,0:T(8,128)S(1)}, f32[64,4096]{1,0:T(8,128)S(1)}, u32[]{:S(2)}, u32[]{:S(2)}) collective-permute-start(f32[64,4096]{1,0:T(8,128)S(1)} %add.32.rest_0_), channel_id=1, source_target_pairs={{0,8},{8,0},{16,24},{24,16},{1,9},{9,1},{17,25},{25,17},{2,10},{10... | collective-permute-start | bytes 3145736 | tf_op jit(solution)/shard_map/ppermute | solution.py:23
  54.5 8.9 %collective-permute-start.16 = (bf16[64,1536]{1,0:T(8,128)(2,1)S(1)}, bf16[64,1536]{1,0:T(8,128)(2,1)S(1)}, u32[]{:S(2)}, u32[]{:S(2)}) collective-permute-start(bf16[64,1536]{1,0:T(8,128)(2,1)S(1)} %get-tuple-element.63), channel_id=1, source_target_pairs={{0,16},{8,24},{16,0},{24,8},{1,17},{9,25},{17,1},{25,9},{2,18},{10... | collective-permute-start | bytes 589832 | tf_op jit(solution)/shard_map/ppermute | solution.py:23
  55.5 9.9 %collective-permute-start.12 = (bf16[64,1024]{1,0:T(8,128)(2,1)S(1)}, bf16[64,1024]{1,0:T(8,128)(2,1)S(1)}, u32[]{:S(2)}, u32[]{:S(2)}) collective-permute-start(bf16[64,1024]{1,0:T(8,128)(2,1)S(1)} %get-tuple-element.70), channel_id=1, source_target_pairs={{0,16},{8,24},{16,0},{24,8},{1,17},{9,25},{17,1},{25,9},{2,18},{10... | collective-permute-start | bytes 393224 | tf_op jit(solution)/shard_map/ppermute | solution.py:23
  59.2 4.3 %collective-permute-start.14 = (bf16[64,1536]{1,0:T(8,128)(2,1)S(1)}, bf16[64,1536]{1,0:T(8,128)(2,1)S(1)}, u32[]{:S(2)}, u32[]{:S(2)}) collective-permute-start(bf16[64,1536]{1,0:T(8,128)(2,1)S(1)} %add_convert_fusion.1.rest_4_), channel_id=1, source_target_pairs={{0,8},{8,0},{16,24},{24,16},{1,9},{9,1},{17,25},{25,17},{2,10},{10... | collective-permute-start | bytes 589832 | tf_op jit(solution)/shard_map/ppermute | solution.py:23
  63.4 2.4 %collective-permute-start.17 = (bf16[64,1536]{1,0:T(8,128)(2,1)S(1)}, bf16[64,1536]{1,0:T(8,128)(2,1)S(1)}, u32[]{:S(2)}, u32[]{:S(2)}) collective-permute-start(bf16[64,1536]{1,0:T(8,128)(2,1)S(1)} %add_convert_fusion.rest_4_), channel_id=1, source_target_pairs={{0,8},{8,0},{16,24},{24,16},{1,9},{9,1},{17,25},{25,17},{2,10},{10... | collective-permute-start | bytes 589832 | tf_op jit(solution)/shard_map/ppermute | solution.py:23
  65.4 2.1 %collective-permute-start.15 = (bf16[64,1024]{1,0:T(8,128)(2,1)S(1)}, bf16[64,1024]{1,0:T(8,128)(2,1)S(1)}, u32[]{:S(2)}, u32[]{:S(2)}) collective-permute-start(bf16[64,1024]{1,0:T(8,128)(2,1)S(1)} %add_convert_fusion.2.rest_4_), channel_id=1, source_target_pairs={{0,8},{8,0},{16,24},{24,16},{1,9},{9,1},{17,25},{25,17},{2,10},{10... | collective-permute-start | bytes 393224 | tf_op jit(solution)/shard_map/ppermute | solution.py:23

commit v5 on v4

--- a/solution.py
+++ b/solution.py
@@ -10,9 +10,10 @@
 
 BF16 = jnp.bfloat16
 F32 = jnp.float32
-EIGHTHS = (3, 3, 2)
+EIGHTHS = (2, 4, 2)
 STEP = 1024
-AHEAD = 3
+AHEAD = 4
+NARROW = 256
 HBM = pl.BlockSpec(memory_space=pltpu.HBM)
 VMEM = pl.BlockSpec(memory_space=pltpu.VMEM)
 SMEM = pl.BlockSpec(memory_space=pltpu.SMEM)
@@ -23,15 +24,36 @@
     return lax.ppermute(value, axis, [(i, i ^ mask) for i in range(n)])
 
 
-def doubling(value, axis, first=1, other=None):
+def doubling(value, axis, first=1):
     n = lax.axis_size(axis)
     mask = first
-    if other is None:
-        other = exchange(value, axis, mask)
+    other = exchange(value, axis, mask)
     while 2 * mask < n:
         mask *= 2
         value = (value.astype(F32) + other.astype(F32)).astype(value.dtype)
         other = exchange(value, axis, mask)
+    return value, other
+
+
+def feat_orders():
+    n = lax.axis_size("feat")
+    masks = [1 << k for k in range(n.bit_length() - 1)]
+    return list(zip(masks[:1] + masks[:0:-1], masks[1:2] + masks[:1] + masks[2:]))
+
+
+def feat_exchange(value, pair):
+    n = lax.axis_size("feat")
+    moves = [(r * n + f, r * n + (f ^ pair[r & 1])) for r in range(lax.axis_size("rows")) for f in range(n)]
+    return lax.ppermute(value, ("rows", "feat"), moves)
+
+
+def feat_doubling(value, other=None):
+    pairs = feat_orders()
+    for k, pair in enumerate(pairs):
+        if k > 0:
+            value = (value.astype(F32) + other.astype(F32)).astype(value.dtype)
+        if k > 0 or other is None:
+            other = feat_exchange(value, pair)
     return value, other
 
 
@@ -163,9 +185,9 @@
     acc[...] = jnp.zeros_like(acc)
     eta, pull = scale[:, 0:1], scale[:, 1:2]
 
-    @pl.loop(0, x_ref.shape[1] // STEP)
+    @pl.loop(0, x_ref.shape[1] // 512)
     def _(j):
-        cut = columns(j * STEP, STEP)
+        cut = columns(j * 512, 512)
         push = eta * jnp.dot(resid[...], a_ref[:, cut], preferred_element_type=F32)
         x = x_ref[:, cut]
         x = x - pull * (x - z_ref[:, cut] + u_ref[:, cut]) + push
@@ -188,34 +210,40 @@
     )(*pin(pltpu.VMEM, sign, *pair, scale, x, u, z, design))
 
 
-def push_kernel(mine, begin, size, side, sign, own, other, scale, q_ref, a_ref, *rest):
-    received = rest[0] if mine else None
-    h_out, sent_out = rest[-2:]
+def push_kernel(mine, begin, size, side, *refs):
+    if mine is None:
+        sign, own, other, scale, q_ref, a_ref, h_out, sent_out, resid = refs
+        resid[...] = residual(sign[...], own[...], other[...])
+    else:
+        resid, scale, q_ref, a_ref, *received, h_out, sent_out = refs
     half = q_ref.shape[1] // 2
     eta = scale[:, 0:1]
-    resid = residual(sign[...], own[...], other[...])
     base = (side[0] if mine else 1 - side[0]) * half + begin
     step = math.gcd(512, size)
     for j in range(size // step):
         cut = columns(base + j * step, step)
         here = pl.ds(j * step, step)
-        push = q_ref[:, cut] + eta * jnp.dot(resid, a_ref[:, cut], preferred_element_type=F32)
+        push = q_ref[:, cut] + eta * jnp.dot(resid[...], a_ref[:, cut], preferred_element_type=F32)
         h_out[:, here] = push
         if mine:
-            push = push + received[:, here].astype(F32)
+            push = push + received[0][:, here].astype(F32)
         sent_out[:, here] = push.astype(BF16)
 
 
-def push(side, sign, pair, scale, q, design, received, begin, size):
+def push(side, resid, scale, q, design, received, begin, size):
     tasks = q.shape[0]
     mine = received is not None
-    args = [sign, *pair, scale, q, design] + ([received] if mine else [])
-    return call(
-        functools.partial(push_kernel, mine, begin, size),
+    first = isinstance(resid, tuple)
+    args = [*(resid if first else [resid]), scale, q, design] + ([received] if mine else [])
+    out = [pltpu.VMEM((tasks, size), F32), pltpu.VMEM((tasks, size), BF16)]
+    if first:
+        out.append(pltpu.VMEM((tasks, design.shape[0]), BF16))
+    return call(
+        functools.partial(push_kernel, None if first else mine, begin, size),
         "push_mine" if mine else "push_other",
         [SMEM] + [VMEM] * len(args),
-        (pltpu.VMEM((tasks, size), F32), pltpu.VMEM((tasks, size), BF16)),
-        [VMEM] * 2,
+        tuple(out),
+        [VMEM] * len(out),
     )(side, *pin(pltpu.VMEM, *args))
 
 
@@ -229,9 +257,13 @@
     for k in range(2):
         begin = 0
         for c, size in enumerate(sizes):
-            cut = columns((side[0] if k == 0 else 1 - side[0]) * half + begin, size)
-            u, z = u_ref[:, cut], z_ref[:, cut]
-            stage[:, cut] = z - u + keep * keep * (x_ref[:, cut] - z + u) + hs[k][c][...]
+            base = (side[0] if k == 0 else 1 - side[0]) * half + begin
+            for j in range(0, size, NARROW):
+                cut = columns(base + j, NARROW)
+                u, z = u_ref[:, cut], z_ref[:, cut]
+                h = hs[k][c][:, pl.ds(j, NARROW)]
+                stage[:, cut] = z - u + keep * keep * (x_ref[:, cut] - z + u) + h
+            cut = columns(base, size)
             copy = pltpu.make_async_copy(stage.at[:, cut], x_out.at[:, cut], sems.at[k, c])
             copy.start()
             copies.append(copy)
@@ -261,14 +293,18 @@
     keep = 1.0 - pull
     copies = []
     for k in range(2):
-        cut = columns((side[0] if k == 0 else 1 - side[0]) * half + begin, size)
-        z = z_ref[:, cut]
-        start = starts[k][:, pl.ds(begin, size)]
-        mean = (keep * keep * start + pushes[k][...].astype(F32)) * (1.0 / blocks_count) + pull * (1.0 + keep) * z
-        new_z = mean - jnp.clip(mean, -limit, limit)
-        moved = z + keep * keep * (x_ref[:, cut] - z + u_ref[:, cut]) + hs[k][...]
-        for o, value in enumerate((new_z, moved - new_z)):
-            stage[k, o] = value
+        base = (side[0] if k == 0 else 1 - side[0]) * half + begin
+        for j in range(0, size, NARROW):
+            cut, here = columns(base + j, NARROW), pl.ds(j, NARROW)
+            z = z_ref[:, cut]
+            start = starts[k][:, pl.ds(begin + j, NARROW)]
+            mean = (keep * keep * start + pushes[k][:, here].astype(F32)) * (1.0 / blocks_count) + pull * (1.0 + keep) * z
+            new_z = mean - jnp.clip(mean, -limit, limit)
+            moved = z + keep * keep * (x_ref[:, cut] - z + u_ref[:, cut]) + hs[k][:, here]
+            stage[k, 0, :, here] = new_z
+            stage[k, 1, :, here] = moved - new_z
+        cut = columns(base, size)
+        for o in range(2):
             copy = pltpu.make_async_copy(stage.at[k, o], outs[o].at[:, cut], sems.at[k, o])
             copy.start()
             copies.append(copy)
@@ -308,13 +344,13 @@
 
     margin1, design, x0, dual, start_mine, start_other = load(side, local_x[0], dual_u[0], design)
     start_mine = start_mine + exchange(start_other, "rows", 1)
-    other = exchange(margin1, "feat", 1)
+    other = feat_exchange(margin1, feat_orders()[0])
     z, sign, scale = load_rest(consensus_z, labels, tie(step_size, other), rho, penalty, blocks_count)
-    pair = doubling(margin1, "feat", 1, other)
+    pair = feat_doubling(margin1, other)
     pair = tie(pair, start_mine)
 
     carried, margin2 = turn(sign, pair, scale, x0, dual, z, design)
-    pair = doubling(margin2, "feat")
+    pair = feat_doubling(margin2)
     mask = 2
     while mask < blocks_count:
         start_mine = start_mine + exchange(start_mine, "rows", mask)
@@ -325,37 +361,41 @@
     sizes = [half * part // sum(EIGHTHS) for part in EIGHTHS]
     begins = [sum(sizes[:c]) for c in range(len(sizes))]
     count = len(sizes)
-    args = (sign, pair, scale, carried, design)
     others, mines, received, sums = [], [], [], []
-    token = side
+    resid, token = (sign, *pair), side
     for c in range(count + 1):
         if c < count:
-            value, other = push(token, *args, None, begins[c], sizes[c])
+            value, other, *made = push(token, resid, scale, carried, design, None, begins[c], sizes[c])
+            if made:
+                resid = made[0]
             others.append(value)
             received.append(exchange(other, "rows", 1))
         if c > 0:
-            value, sent = push(token, *args, received[c - 1], begins[c - 1], sizes[c - 1])
+            value, sent = push(token, resid, scale, carried, design, received[c - 1], begins[c - 1], sizes[c - 1])
             mines.append(value)
             sums.append(doubling(sent, "rows", 2))
             token = tie(side, sent)
     new_x = store_x(side, scale, x0, dual, z, mines, others, sizes)
 
-    results, pushes = None, []
-    for c in range(count + 1):
-        if c < count:
-            a, b = sums[c]
-            if c == 0:
-                b = tie(b, new_x)
-            if c > 1:
-                b = tie(b, results)
-            piece = (a.astype(F32) + b.astype(F32)).astype(BF16)
-            pushes.append((piece, exchange(piece, "rows", 1)))
-        if c > 0:
-            results = final(
-                side, scale, x0, dual, z, (start_mine, start_theirs), (mines[c - 1], others[c - 1]), pushes[c - 1],
-                results, begins[c - 1], sizes[c - 1], blocks_count,
+    results, pushes = [None], []
+
+    def finish(c):
+        results.append(
+            final(
+                side, scale, x0, dual, z, (start_mine, start_theirs), (mines[c], others[c]), pushes[c],
+                results[-1], begins[c], sizes[c], blocks_count,
             )
-    new_z, new_u = results
+        )
+
+    for c, (a, b) in enumerate(sums):
+        if 0 < c < count - 1:
+            finish(c - 1)
+        b = tie(b, new_x, results[-1])
+        piece = (a.astype(F32) + b.astype(F32)).astype(BF16)
+        pushes.append((piece, exchange(piece, "rows", 1)))
+    for c in range(len(results) - 1, count):
+        finish(c)
+    new_z, new_u = results[-1]
     return (new_x[None], new_z, new_u[None])
 
 

time: 69 us -> 72.7 us (1.054)
  starting transfers between devices: 22.8 us -> 25.5 us
  Pallas kernels: 25.5 us -> 26.5 us
    ppermute x0 -> x6, starting transfers between devices: none -> 17.2 us  [feat_exchange(): return lax.ppermute(value, ('rows', 'feat'), moves)]
    ppermute x18 -> x12, starting transfers between devices: 22.8 us -> 8.39 us  [exchange(): return lax.ppermute(value, axis, [(i, i ^ mask) for i in range(n)])]
    ppermute x18 -> x12, waiting for transfers between devices: 19.3 us -> 7.38 us  [exchange(): return lax.ppermute(value, axis, [(i, i ^ mask) for i in range(n)])]
    ppermute x0 -> x6, waiting for transfers between devices: none -> 11.8 us  [feat_exchange(): return lax.ppermute(value, ('rows', 'feat'), moves)]
    pallas_call x1, Pallas kernels: 7.28 us -> 9.03 us  [turn(): call(turn_kernel, 'turn', [VMEM] * 8, (pltpu.VMEM((tasks, width), F32), p...]
  transfers between devices with their start and end apart: 18 -> 18, of which waited for: 10 -> 9; matrix products, arithmetic and copies ran while one was open for 1% -> 1% of each run, Pallas kernels for 24% -> 25%
where the time goes in v5:
time: 72.7 us; the launch traced here: 72.4 us
  Pallas kernels  26.5 us (36%)
  starting transfers between devices  25.5 us (35%)
  waiting for transfers between devices  19.2 us (26%)
  between operations  0.81 us (1%)
    ppermute x6, starting transfers between devices, feat_exchange(): return lax.ppermute(value, ('rows', 'feat'), moves)  17.2 us
    ppermute x6, waiting for transfers between devices, feat_exchange(): return lax.ppermute(value, ('rows', 'feat'), moves)  11.8 us
    pallas_call x1, Pallas kernels, turn(): call(turn_kernel, 'turn', [VMEM] * 8, (pltpu.VMEM((tasks, width), F32), p...  9.03 us
    ppermute x12, starting transfers between devices, exchange(): return lax.ppermute(value, axis, [(i, i ^ mask) for i in range(n)])  8.39 us
    ppermute x12, waiting for transfers between devices, exchange(): return lax.ppermute(value, axis, [(i, i ^ mask) for i in range(n)])  7.38 us
    pallas_call x1, Pallas kernels, load(): call(load_kernel, 'load_and_margins', [SMEM] + [HBM] * 3, (pltpu.VMEM((ta...  6.75 us
    pallas_call x3, Pallas kernels, final(): call(functools.partial(final_kernel, blocks_count, begin, size, buffered)...  4.44 us
    pallas_call x6, Pallas kernels, push(): call(functools.partial(push_kernel, None if first else mine, begin, size)...  3 us
  transfers between devices with their start and end apart: 18, of which 9 were waited for; matrix products, arithmetic and copies ran while one was open for 1% of the time, Pallas kernels for 25%

profile of v5, /device:TPU:0, one launch (start us, length us, event | category | flops | bytes accessed | tf_op | source)
XLA Modules:
  0.0 72.4 jit_solution(12802045953899130705)
XLA Ops:
  0.6 6.8 %load_and_margins.1 = (bf16[64,768]{1,0:T(8,128)(2,1)S(1)}, bf16[768,8192]{1,0:T(8,128)(2,1)S(1)}, f32[64,8192]{1,0:T(8,128)S(1)}, f32[64,8192]{1,0:T(8,128)S(1)...) custom-call(s32[1]{0:T(128)} %bitcast.side, f32[64,8192]{1,0:T(8,128)} %bitcast.9, f32[64,8192]{1,0:T(8,128)} %bitcast.10, ...), custom_call_target="tpu_custom_call" | custom-call | flops 1000 | bytes 1000 | tf_op jit(solution)/shard_map/load_and_margins/pallas_call | solution.py:136
  7.9 2.6 %collective-permute-start = (bf16[64,768]{1,0:T(8,128)(2,1)S(1)}, bf16[64,768]{1,0:T(8,128)(2,1)S(1)}, u32[]{:S(2)}, u32[]{:S(2)}) collective-permute-start(bf16[64,768]{1,0:T(8,128)(2,1)S(1)} %get-tuple-element.43), channel_id=1, source_target_pairs={{0,1},{1,0},{2,3},{3,2},{4,5},{5,4},{6,7},{7,6},{8,10},{9,11},{10,... | collective-permute-start | bytes 294920 | tf_op jit(solution)/shard_map/ppermute | solution.py:47
  10.6 2.6 %collective-permute-start.7 = (f32[64,4096]{1,0:T(8,128)S(1)}, f32[64,4096]{1,0:T(8,128)S(1)}, u32[]{:S(2)}, u32[]{:S(2)}) collective-permute-start(f32[64,4096]{1,0:T(8,128)S(1)} %add.29), channel_id=1, source_target_pairs={{0,16},{8,24},{16,0},{24,8},{1,17},{9,25},{17,1},{25,9},{2,18},{10... | collective-permute-start | bytes 3145736 | tf_op jit(solution)/shard_map/ppermute | solution.py:24
  13.3 3.0 %collective-permute-start.1 = (bf16[64,768]{1,0:T(8,128)(2,1)S(1)}, bf16[64,768]{1,0:T(8,128)(2,1)S(1)}, u32[]{:S(2)}, u32[]{:S(2)}) collective-permute-start(bf16[64,768]{1,0:T(8,128)(2,1)S(1)} %add_convert_fusion.6), channel_id=1, source_target_pairs={{0,4},{1,5},{2,6},{3,7},{4,0},{5,1},{6,2},{7,3},{8,9},{9,8},{10,11... | collective-permute-start | bytes 294920 | tf_op jit(solution)/shard_map/ppermute | solution.py:47
  16.3 2.6 %collective-permute-done.1 = bf16[64,768]{1,0:T(8,128)(2,1)S(1)} collective-permute-done((bf16[64,768]{1,0:T(8,128)(2,1)S(1)}, bf16[64,768]{1,0:T(8,128)(2,1)S(1)}, u32[]{:S(2)}, u32[]{:S(2)}) %collective-permute-start.1) | collective-permute-done | bytes 98336 | tf_op jit(solution)/shard_map/ppermute | solution.py:47
  18.9 2.1 %collective-permute-start.2 = (bf16[64,768]{1,0:T(8,128)(2,1)S(1)}, bf16[64,768]{1,0:T(8,128)(2,1)S(1)}, u32[]{:S(2)}, u32[]{:S(2)}) collective-permute-start(bf16[64,768]{1,0:T(8,128)(2,1)S(1)} %add_convert_fusion.5.own), channel_id=1, source_target_pairs={{0,2},{1,3},{2,0},{3,1},{4,6},{5,7},{6,4},{7,5},{8,12},{9,13},{10,... | collective-permute-start | bytes 294920 | tf_op jit(solution)/shard_map/ppermute | solution.py:47
  21.0 1.7 %load_rest.1 = (f32[64,8192]{1,0:T(8,128)S(1)}, s32[64,768]{1,0:T(8,128)S(1)}, f32[64,128]{1,0:T(8,128)S(1)}) custom-call(f32[64,8192]{1,0:T(8,128)} %z_hbm.1, s32[64,768]{1,0:T(8,128)} %sign_hbm.1, f32[1,64]{1,0:T(1,128)} %bitcast.12, f32[1,64]{1,0:T(1,128)} %bitcast.13, f32[1,64]{1,0:T(1,128)} %bitcast.14), custom_call_target="tpu_custom_call" | custom-call | flops 1000 | bytes 1000 | tf_op jit(solution)/shard_map/load_rest/pallas_call | solution.py:167
  22.7 0.9 %collective-permute-done.2.other = bf16[64,768]{1,0:T(8,128)(2,1)S(1)} collective-permute-done((bf16[64,768]{1,0:T(8,128)(2,1)S(1)}, bf16[64,768]{1,0:T(8,128)(2,1)S(1)}, u32[]{:S(2)}, u32[]{:S(2)}) %collective-permute-start.2) | collective-permute-done | bytes 98336 | tf_op jit(solution)/shard_map/ppermute | solution.py:47
  23.6 9.0 %turn.1 = (f32[64,8192]{1,0:T(8,128)S(1)}, bf16[64,768]{1,0:T(8,128)(2,1)S(1)}) custom-call(s32[64,768]{1,0:T(8,128)S(1)} %get-tuple-element.49.sign.refs_0_, bf16[64,768]{1,0:T(8,128)(2,1)S(1)} %add_convert_fusion.5.own, bf16[64,768]{1,0:T(8,128)(2,1)S(1)} %collective-permute-done.2.other, f32[64,128]{1,0:T(8,128)S(1)} %get-tuple-element.45.scale.refs_3_.refs_1_, ...), custom_call_target="tpu_custom_call" | custom-call | flops 1000 | bytes 1000 | tf_op jit(solution)/shard_map/turn/pallas_call | solution.py:203
  32.7 1.9 %collective-permute-start.4 = (bf16[64,768]{1,0:T(8,128)(2,1)S(1)}, bf16[64,768]{1,0:T(8,128)(2,1)S(1)}, u32[]{:S(2)}, u32[]{:S(2)}) collective-permute-start(bf16[64,768]{1,0:T(8,128)(2,1)S(1)} %get-tuple-element.55), channel_id=1, source_target_pairs={{0,1},{1,0},{2,3},{3,2},{4,5},{5,4},{6,7},{7,6},{8,10},{9,11},{10,... | collective-permute-start | bytes 294920 | tf_op jit(solution)/shard_map/ppermute | solution.py:47
  34.6 2.8 %collective-permute-done.4 = bf16[64,768]{1,0:T(8,128)(2,1)S(1)} collective-permute-done((bf16[64,768]{1,0:T(8,128)(2,1)S(1)}, bf16[64,768]{1,0:T(8,128)(2,1)S(1)}, u32[]{:S(2)}, u32[]{:S(2)}) %collective-permute-start.4) | collective-permute-done | bytes 98336 | tf_op jit(solution)/shard_map/ppermute | solution.py:47
  37.4 3.8 %collective-permute-start.5 = (bf16[64,768]{1,0:T(8,128)(2,1)S(1)}, bf16[64,768]{1,0:T(8,128)(2,1)S(1)}, u32[]{:S(2)}, u32[]{:S(2)}) collective-permute-start(bf16[64,768]{1,0:T(8,128)(2,1)S(1)} %add_convert_fusion.4), channel_id=1, source_target_pairs={{0,4},{1,5},{2,6},{3,7},{4,0},{5,1},{6,2},{7,3},{8,9},{9,8},{10,11... | collective-permute-start | bytes 294920 | tf_op jit(solution)/shard_map/ppermute | solution.py:47
  41.4 2.9 %collective-permute-done.5 = bf16[64,768]{1,0:T(8,128)(2,1)S(1)} collective-permute-done((bf16[64,768]{1,0:T(8,128)(2,1)S(1)}, bf16[64,768]{1,0:T(8,128)(2,1)S(1)}, u32[]{:S(2)}, u32[]{:S(2)}) %collective-permute-start.5) | collective-permute-done | bytes 98336 | tf_op jit(solution)/shard_map/ppermute | solution.py:47
  44.3 3.7 %collective-permute-start.6 = (bf16[64,768]{1,0:T(8,128)(2,1)S(1)}, bf16[64,768]{1,0:T(8,128)(2,1)S(1)}, u32[]{:S(2)}, u32[]{:S(2)}) collective-permute-start(bf16[64,768]{1,0:T(8,128)(2,1)S(1)} %add_convert_fusion.3.refs_1_), channel_id=1, source_target_pairs={{0,2},{1,3},{2,0},{3,1},{4,6},{5,7},{6,4},{7,5},{8,12},{9,13},{10,... | collective-permute-start | bytes 294920 | tf_op jit(solution)/shard_map/ppermute | solution.py:47
  48.0 2.6 %collective-permute-done.6.refs_2_ = bf16[64,768]{1,0:T(8,128)(2,1)S(1)} collective-permute-done((bf16[64,768]{1,0:T(8,128)(2,1)S(1)}, bf16[64,768]{1,0:T(8,128)(2,1)S(1)}, u32[]{:S(2)}, u32[]{:S(2)}) %collective-permute-start.6) | collective-permute-done | bytes 98336 | tf_op jit(solution)/shard_map/ppermute | solution.py:47
  53.5 1.5 %collective-permute-start.13 = (bf16[64,1024]{1,0:T(8,128)(2,1)S(1)}, bf16[64,1024]{1,0:T(8,128)(2,1)S(1)}, u32[]{:S(2)}, u32[]{:S(2)}) collective-permute-start(bf16[64,1024]{1,0:T(8,128)(2,1)S(1)} %get-tuple-element.62), channel_id=1, source_target_pairs={{0,16},{8,24},{16,0},{24,8},{1,17},{9,25},{17,1},{25,9},{2,18},{10... | collective-permute-start | bytes 393224 | tf_op jit(solution)/shard_map/ppermute | solution.py:24
  56.7 1.6 %store_x.1 = f32[64,8192]{1,0:T(8,128)} custom-call(s32[1]{0:T(128)} %bitcast.side, f32[64,128]{1,0:T(8,128)S(1)} %get-tuple-element.45.scale.refs_3_.refs_1_, f32[64,8192]{1,0:T(8,128)S(1)} %get-tuple-element.46.x_ref, f32[64,8192]{1,0:T(8,128)S(1)} %get-tuple-element.47.u_ref, f32[64,8192]{1,0:T(8,128)S(1)} %get-tuple-element.48.z_ref, ...), custom_call_target="tpu_custom_call" | custom-call | flops 1000 | bytes 1000 | tf_op jit(solution)/shard_map/store_x/pallas_call | solution.py:277
  58.3 1.5 %collective-permute-done.13 = bf16[64,1024]{1,0:T(8,128)(2,1)S(1)} collective-permute-done((bf16[64,1024]{1,0:T(8,128)(2,1)S(1)}, bf16[64,1024]{1,0:T(8,128)(2,1)S(1)}, u32[]{:S(2)}, u32[]{:S(2)}) %collective-permute-start.13) | collective-permute-done | bytes 131104 | tf_op jit(solution)/shard_map/ppermute | solution.py:24
  59.9 1.6 %collective-permute-start.12 = (bf16[64,1024]{1,0:T(8,128)(2,1)S(1)}, bf16[64,1024]{1,0:T(8,128)(2,1)S(1)}, u32[]{:S(2)}, u32[]{:S(2)}) collective-permute-start(bf16[64,1024]{1,0:T(8,128)(2,1)S(1)} %get-tuple-element.73), channel_id=1, source_target_pairs={{0,16},{8,24},{16,0},{24,8},{1,17},{9,25},{17,1},{25,9},{2,18},{10... | collective-permute-start | bytes 393224 | tf_op jit(solution)/shard_map/ppermute | solution.py:24
  61.5 1.4 %final.3 = (f32[64,8192]{1,0:T(8,128)}, f32[64,8192]{1,0:T(8,128)}) custom-call(s32[1]{0:T(128)} %bitcast.side, f32[64,128]{1,0:T(8,128)S(1)} %get-tuple-element.45.scale.refs_3_.refs_1_, f32[64,8192]{1,0:T(8,128)S(1)} %get-tuple-element.46.x_ref, f32[64,8192]{1,0:T(8,128)S(1)} %get-tuple-element.47.u_ref, f32[64,8192]{1,0:T(8,128)S(1)} %get-tuple-element.48.z_ref, ...), custom_call_target="tpu_custom_call" | custom-call | flops 1000 | bytes 1000 | tf_op jit(solution)/shard_map/final/pallas_call | solution.py:324
  62.8 4.8 %collective-permute-done.12 = bf16[64,1024]{1,0:T(8,128)(2,1)S(1)} collective-permute-done((bf16[64,1024]{1,0:T(8,128)(2,1)S(1)}, bf16[64,1024]{1,0:T(8,128)(2,1)S(1)}, u32[]{:S(2)}, u32[]{:S(2)}) %collective-permute-start.12) | collective-permute-done | bytes 131104 | tf_op jit(solution)/shard_map/ppermute | solution.py:24
  68.4 0.9 %collective-permute-done.17.rest_5_ = bf16[64,2048]{1,0:T(8,128)(2,1)S(1)} collective-permute-done((bf16[64,2048]{1,0:T(8,128)(2,1)S(1)}, bf16[64,2048]{1,0:T(8,128)(2,1)S(1)}, u32[]{:S(2)}, u32[]{:S(2)}) %collective-permute-start.17) | collective-permute-done | bytes 262176 | tf_op jit(solution)/shard_map/ppermute | solution.py:24
  69.3 1.7 %final.4 = (f32[64,8192]{1,0:T(8,128)}, f32[64,8192]{1,0:T(8,128)}) custom-call(s32[1]{0:T(128)} %bitcast.side, f32[64,128]{1,0:T(8,128)S(1)} %get-tuple-element.45.scale.refs_3_.refs_1_, f32[64,8192]{1,0:T(8,128)S(1)} %get-tuple-element.46.x_ref, f32[64,8192]{1,0:T(8,128)S(1)} %get-tuple-element.47.u_ref, ...), custom_call_target="tpu_custom_call", output_to_operand_aliasing={{0}: (11, {}), {1}: (12, {})} | custom-call | flops 1000 | bytes 1000 | tf_op jit(solution)/shard_map/final/pallas_call | solution.py:324
  71.1 1.4 %final.5 = (f32[64,8192]{1,0:T(8,128)}, f32[64,8192]{1,0:T(8,128)}) custom-call(s32[1]{0:T(128)} %bitcast.side, f32[64,128]{1,0:T(8,128)S(1)} %get-tuple-element.45.scale.refs_3_.refs_1_, f32[64,8192]{1,0:T(8,128)S(1)} %get-tuple-element.46.x_ref, f32[64,8192]{1,0:T(8,128)S(1)} %get-tuple-element.47.u_ref, ...), custom_call_target="tpu_custom_call", output_to_operand_aliasing={{0}: (11, {}), {1}: (12, {})} | custom-call | flops 1000 | bytes 1000 | tf_op jit(solution)/shard_map/final/pallas_call | solution.py:324
  (34 shorter events, 6.3 us)
Async XLA Ops:
  7.4 3.1 %collective-permute-start.3 = (f32[64,4096]{1,0:T(8,128)S(1)}, f32[64,4096]{1,0:T(8,128)S(1)}, u32[]{:S(2)}, u32[]{:S(2)}) collective-permute-start(f32[64,4096]{1,0:T(8,128)S(1)} %get-tuple-element.51), channel_id=1, source_target_pairs={{0,8},{8,0},{16,24},{24,16},{1,9},{9,1},{17,25},{25,17},{2,10},{10... | collective-permute-start | bytes 3145736 | tf_op jit(solution)/shard_map/ppermute | solution.py:24
  7.9 5.3 %collective-permute-start = (bf16[64,768]{1,0:T(8,128)(2,1)S(1)}, bf16[64,768]{1,0:T(8,128)(2,1)S(1)}, u32[]{:S(2)}, u32[]{:S(2)}) collective-permute-start(bf16[64,768]{1,0:T(8,128)(2,1)S(1)} %get-tuple-element.43), channel_id=1, source_target_pairs={{0,1},{1,0},{2,3},{3,2},{4,5},{5,4},{6,7},{7,6},{8,10},{9,11},{10,... | collective-permute-start | bytes 294920 | tf_op jit(solution)/shard_map/ppermute | solution.py:47
  10.6 30.6 %collective-permute-start.7 = (f32[64,4096]{1,0:T(8,128)S(1)}, f32[64,4096]{1,0:T(8,128)S(1)}, u32[]{:S(2)}, u32[]{:S(2)}) collective-permute-start(f32[64,4096]{1,0:T(8,128)S(1)} %add.29), channel_id=1, source_target_pairs={{0,16},{8,24},{16,0},{24,8},{1,17},{9,25},{17,1},{25,9},{2,18},{10... | collective-permute-start | bytes 3145736 | tf_op jit(solution)/shard_map/ppermute | solution.py:24
  13.3 5.6 %collective-permute-start.1 = (bf16[64,768]{1,0:T(8,128)(2,1)S(1)}, bf16[64,768]{1,0:T(8,128)(2,1)S(1)}, u32[]{:S(2)}, u32[]{:S(2)}) collective-permute-start(bf16[64,768]{1,0:T(8,128)(2,1)S(1)} %add_convert_fusion.6), channel_id=1, source_target_pairs={{0,4},{1,5},{2,6},{3,7},{4,0},{5,1},{6,2},{7,3},{8,9},{9,8},{10,11... | collective-permute-start | bytes 294920 | tf_op jit(solution)/shard_map/ppermute | solution.py:47
  18.9 4.7 %collective-permute-start.2 = (bf16[64,768]{1,0:T(8,128)(2,1)S(1)}, bf16[64,768]{1,0:T(8,128)(2,1)S(1)}, u32[]{:S(2)}, u32[]{:S(2)}) collective-permute-start(bf16[64,768]{1,0:T(8,128)(2,1)S(1)} %add_convert_fusion.5.own), channel_id=1, source_target_pairs={{0,2},{1,3},{2,0},{3,1},{4,6},{5,7},{6,4},{7,5},{8,12},{9,13},{10,... | collective-permute-start | bytes 294920 | tf_op jit(solution)/shard_map/ppermute | solution.py:47
  32.7 4.7 %collective-permute-start.4 = (bf16[64,768]{1,0:T(8,128)(2,1)S(1)}, bf16[64,768]{1,0:T(8,128)(2,1)S(1)}, u32[]{:S(2)}, u32[]{:S(2)}) collective-permute-start(bf16[64,768]{1,0:T(8,128)(2,1)S(1)} %get-tuple-element.55), channel_id=1, source_target_pairs={{0,1},{1,0},{2,3},{3,2},{4,5},{5,4},{6,7},{7,6},{8,10},{9,11},{10,... | collective-permute-start | bytes 294920 | tf_op jit(solution)/shard_map/ppermute | solution.py:47
  37.4 6.9 %collective-permute-start.5 = (bf16[64,768]{1,0:T(8,128)(2,1)S(1)}, bf16[64,768]{1,0:T(8,128)(2,1)S(1)}, u32[]{:S(2)}, u32[]{:S(2)}) collective-permute-start(bf16[64,768]{1,0:T(8,128)(2,1)S(1)} %add_convert_fusion.4), channel_id=1, source_target_pairs={{0,4},{1,5},{2,6},{3,7},{4,0},{5,1},{6,2},{7,3},{8,9},{9,8},{10,11... | collective-permute-start | bytes 294920 | tf_op jit(solution)/shard_map/ppermute | solution.py:47
  41.3 20.2 %collective-permute-start.11 = (f32[64,4096]{1,0:T(8,128)S(1)}, f32[64,4096]{1,0:T(8,128)S(1)}, u32[]{:S(2)}, u32[]{:S(2)}) collective-permute-start(f32[64,4096]{1,0:T(8,128)S(1)} %add.32.rest_0_), channel_id=1, source_target_pairs={{0,8},{8,0},{16,24},{24,16},{1,9},{9,1},{17,25},{25,17},{2,10},{10... | collective-permute-start | bytes 3145736 | tf_op jit(solution)/shard_map/ppermute | solution.py:24
  44.3 6.3 %collective-permute-start.6 = (bf16[64,768]{1,0:T(8,128)(2,1)S(1)}, bf16[64,768]{1,0:T(8,128)(2,1)S(1)}, u32[]{:S(2)}, u32[]{:S(2)}) collective-permute-start(bf16[64,768]{1,0:T(8,128)(2,1)S(1)} %add_convert_fusion.3.refs_1_), channel_id=1, source_target_pairs={{0,2},{1,3},{2,0},{3,1},{4,6},{5,7},{6,4},{7,5},{8,12},{9,13},{10,... | collective-permute-start | bytes 294920 | tf_op jit(solution)/shard_map/ppermute | solution.py:47
  51.0 1.4 %collective-permute-start.8 = (bf16[64,1024]{1,0:T(8,128)(2,1)S(1)}, bf16[64,1024]{1,0:T(8,128)(2,1)S(1)}, u32[]{:S(2)}, u32[]{:S(2)}) collective-permute-start(bf16[64,1024]{1,0:T(8,128)(2,1)S(1)} %get-tuple-element.60), channel_id=1, source_target_pairs={{0,8},{8,0},{16,24},{24,16},{1,9},{9,1},{17,25},{25,17},{2,10},{10... | collective-permute-start | bytes 393224 | tf_op jit(solution)/shard_map/ppermute | solution.py:24
  51.8 3.2 %collective-permute-start.9 = (bf16[64,2048]{1,0:T(8,128)(2,1)S(1)}, bf16[64,2048]{1,0:T(8,128)(2,1)S(1)}, u32[]{:S(2)}, u32[]{:S(2)}) collective-permute-start(bf16[64,2048]{1,0:T(8,128)(2,1)S(1)} %get-tuple-element.64), channel_id=1, source_target_pairs={{0,8},{8,0},{16,24},{24,16},{1,9},{9,1},{17,25},{25,17},{2,10},{10... | collective-permute-start | bytes 786440 | tf_op jit(solution)/shard_map/ppermute | solution.py:24
  53.3 3.0 %collective-permute-start.10 = (bf16[64,1024]{1,0:T(8,128)(2,1)S(1)}, bf16[64,1024]{1,0:T(8,128)(2,1)S(1)}, u32[]{:S(2)}, u32[]{:S(2)}) collective-permute-start(bf16[64,1024]{1,0:T(8,128)(2,1)S(1)} %get-tuple-element.68), channel_id=1, source_target_pairs={{0,8},{8,0},{16,24},{24,16},{1,9},{9,1},{17,25},{25,17},{2,10},{10... | collective-permute-start | bytes 393224 | tf_op jit(solution)/shard_map/ppermute | solution.py:24
  53.5 6.3 %collective-permute-start.13 = (bf16[64,1024]{1,0:T(8,128)(2,1)S(1)}, bf16[64,1024]{1,0:T(8,128)(2,1)S(1)}, u32[]{:S(2)}, u32[]{:S(2)}) collective-permute-start(bf16[64,1024]{1,0:T(8,128)(2,1)S(1)} %get-tuple-element.62), channel_id=1, source_target_pairs={{0,16},{8,24},{16,0},{24,8},{1,17},{9,25},{17,1},{25,9},{2,18},{10... | collective-permute-start | bytes 393224 | tf_op jit(solution)/shard_map/ppermute | solution.py:24
  55.7 12.0 %collective-permute-start.16 = (bf16[64,2048]{1,0:T(8,128)(2,1)S(1)}, bf16[64,2048]{1,0:T(8,128)(2,1)S(1)}, u32[]{:S(2)}, u32[]{:S(2)}) collective-permute-start(bf16[64,2048]{1,0:T(8,128)(2,1)S(1)} %get-tuple-element.66), channel_id=1, source_target_pairs={{0,16},{8,24},{16,0},{24,8},{1,17},{9,25},{17,1},{25,9},{2,18},{10... | collective-permute-start | bytes 786440 | tf_op jit(solution)/shard_map/ppermute | solution.py:24
  59.8 1.6 %collective-permute-start.14 = (bf16[64,1024]{1,0:T(8,128)(2,1)S(1)}, bf16[64,1024]{1,0:T(8,128)(2,1)S(1)}, u32[]{:S(2)}, u32[]{:S(2)}) collective-permute-start(bf16[64,1024]{1,0:T(8,128)(2,1)S(1)} %add_convert_fusion.2.rest_4_), channel_id=1, source_target_pairs={{0,8},{8,0},{16,24},{24,16},{1,9},{9,1},{17,25},{25,17},{2,10},{10... | collective-permute-start | bytes 393224 | tf_op jit(solution)/shard_map/ppermute | solution.py:24
  59.9 7.7 %collective-permute-start.12 = (bf16[64,1024]{1,0:T(8,128)(2,1)S(1)}, bf16[64,1024]{1,0:T(8,128)(2,1)S(1)}, u32[]{:S(2)}, u32[]{:S(2)}) collective-permute-start(bf16[64,1024]{1,0:T(8,128)(2,1)S(1)} %get-tuple-element.73), channel_id=1, source_target_pairs={{0,16},{8,24},{16,0},{24,8},{1,17},{9,25},{17,1},{25,9},{2,18},{10... | collective-permute-start | bytes 393224 | tf_op jit(solution)/shard_map/ppermute | solution.py:24
  67.7 1.6 %collective-permute-start.17 = (bf16[64,2048]{1,0:T(8,128)(2,1)S(1)}, bf16[64,2048]{1,0:T(8,128)(2,1)S(1)}, u32[]{:S(2)}, u32[]{:S(2)}) collective-permute-start(bf16[64,2048]{1,0:T(8,128)(2,1)S(1)} %add_convert_fusion.rest_4_), channel_id=1, source_target_pairs={{0,8},{8,0},{16,24},{24,16},{1,9},{9,1},{17,25},{25,17},{2,10},{10... | collective-permute-start | bytes 786440 | tf_op jit(solution)/shard_map/ppermute | solution.py:24
  67.9 3.2 %collective-permute-start.15 = (bf16[64,1024]{1,0:T(8,128)(2,1)S(1)}, bf16[64,1024]{1,0:T(8,128)(2,1)S(1)}, u32[]{:S(2)}, u32[]{:S(2)}) collective-permute-start(bf16[64,1024]{1,0:T(8,128)(2,1)S(1)} %add_convert_fusion.1.rest_4_), channel_id=1, source_target_pairs={{0,8},{8,0},{16,24},{24,16},{1,9},{9,1},{17,25},{25,17},{2,10},{10... | collective-permute-start | bytes 393224 | tf_op jit(solution)/shard_map/ppermute | solution.py:24

commit v6 on v4

v6 whole, which is shorter than its diff:
```python
import functools
import math

import jax
import jax.numpy as jnp
from jax import lax
from jax.experimental import pallas as pl
from jax.experimental.pallas import tpu as pltpu
from jax.sharding import PartitionSpec as P

BF16 = jnp.bfloat16
F32 = jnp.float32
MINE = (2, 3, 3)
OTHER = (2, 6)
STEP = 1024
WIDE = 2048
AHEAD = 4
NARROW = 256
HBM = pl.BlockSpec(memory_space=pltpu.HBM)
VMEM = pl.BlockSpec(memory_space=pltpu.VMEM)
SMEM = pl.BlockSpec(memory_space=pltpu.SMEM)


def exchange(value, axis, mask):
    n = lax.axis_size(axis)
    return lax.ppermute(value, axis, [(i, i ^ mask) for i in range(n)])


def doubling(value, axis, first=1):
    n = lax.axis_size(axis)
    mask = first
    other = exchange(value, axis, mask)
    while 2 * mask < n:
        mask *= 2
        value = (value.astype(F32) + other.astype(F32)).astype(value.dtype)
        other = exchange(value, axis, mask)
    return value, other


def two_doublings(first, second):
    n = lax.axis_size("feat")
    values, gots, begun = [first, second], [None, None], [None, None]
    mask = 1
    while mask < n:
        for k in range(2):
            if mask > 1:
                got = gots[k] if k == 0 else tie(gots[k], values[0])
                values[k] = (values[k].astype(F32) + got.astype(F32)).astype(BF16)
            gots[k] = exchange(values[k], "feat", mask)
            if mask == 1:
                begun[k] = gots[k]
        mask *= 2
    return tuple(((v, g), b) for v, g, b in zip(values, gots, begun))


def nt(a, b):
    return lax.dot_general(a, b, (((1,), (1,)), ((), ())), preferred_element_type=F32)


def call(kernel, name, in_specs, out_shape, out_specs, scratch=(), aliases=None, limit=16, work=1000):
    return pl.pallas_call(
        kernel,
        in_specs=in_specs,
        out_shape=out_shape,
        out_specs=out_specs,
        scratch_shapes=list(scratch),
        input_output_aliases=aliases or {},
        compiler_params=pltpu.CompilerParams(vmem_limit_bytes=limit * 1024 * 1024),
        cost_estimate=pl.CostEstimate(flops=work, bytes_accessed=work, transcendentals=0),
        name=name,
    )


def pin(space, *values):
    return [pltpu.with_memory_space_constraint(v, space) for v in values]


def columns(start, size):
    return pl.ds(pl.multiple_of(start, 128), size)


def parts(tasks, samples):
    cut = samples - samples // 3
    return pltpu.VMEM((tasks, cut), BF16), pltpu.VMEM((tasks, samples - cut), BF16)


def load_kernel(side, x_hbm, u_hbm, a_hbm, first_out, second_out, a_out, x_out, u_out, mine_out, other_out, acc, sems):
    width = x_hbm.shape[1]
    steps = width // STEP

    def pair(j):
        cut = columns(j * STEP, STEP)
        return (
            pltpu.make_async_copy(x_hbm.at[:, cut], x_out.at[:, cut], sems.at[0, j]),
            pltpu.make_async_copy(a_hbm.at[:, cut], a_out.at[:, cut], sems.at[1, j]),
        )

    def begin(j):
        for copy in pair(j):
            copy.start()

    dual = pltpu.make_async_copy(u_hbm, u_out, sems.at[2, 0])
    for j in range(min(AHEAD, steps)):
        begin(j)
    acc[...] = jnp.zeros_like(acc)

    @pl.loop(0, steps)
    def _(j):
        for copy in pair(j):
            copy.wait()

        @pl.when(j + AHEAD < steps)
        def _():
            begin(j + AHEAD)

        @pl.when(j == max(steps - AHEAD, 0))
        def _():
            dual.start()

        cut = columns(j * STEP, STEP)
        acc[...] += nt(x_out[:, cut].astype(BF16), a_out[:, cut])

    cut = first_out.shape[1]
    first_out[...] = acc[:, :cut].astype(BF16)
    second_out[...] = acc[:, cut:].astype(BF16)
    dual.wait()
    half = width // 2
    mine = columns(side[0] * half, half)
    other = columns((1 - side[0]) * half, half)
    mine_out[...] = x_out[:, mine] + u_out[:, mine]
    other_out[...] = x_out[:, other] + u_out[:, other]


def load(side, x, u, design):
    tasks, width = x.shape
    samples = design.shape[0]
    full = pltpu.VMEM((tasks, width), F32)
    half = pltpu.VMEM((tasks, width // 2), F32)
    return call(
        load_kernel,
        "load_and_margins",
        [SMEM] + [HBM] * 3,
        (*parts(tasks, samples), pltpu.VMEM(design.shape, BF16), full, full, half, half),
        [VMEM] * 7,
        [pltpu.VMEM((tasks, samples), F32), pltpu.SemaphoreType.DMA((3, width // STEP))],
    )(side, *pin(pltpu.HBM, x, u, design))


def rest_kernel(blocks_count, z_hbm, sign_hbm, eta_hbm, rho_hbm, lam_hbm, *refs):
    z_out, sign_out, scale_out, eta_row, rho_row, lam_row, sems = refs
    pairs = ((eta_hbm, eta_row), (rho_hbm, rho_row), (lam_hbm, lam_row), (z_hbm, z_out), (sign_hbm, sign_out))
    copies = [pltpu.make_async_copy(a, b, sems.at[k]) for k, (a, b) in enumerate(pairs)]
    for copy in copies:
        copy.start()
    for copy in copies[:3]:
        copy.wait()
    tasks = z_out.shape[0]
    one = lax.broadcasted_iota(jnp.int32, (tasks, tasks), 0) == lax.broadcasted_iota(jnp.int32, (tasks, tasks), 1)
    eta, rho, lam = eta_row[...], rho_row[...], lam_row[...]
    for k, row in enumerate((eta, eta * rho, lam / (rho * blocks_count))):
        upright = jnp.where(one, jnp.broadcast_to(row, (tasks, tasks)), 0.0)
        scale_out[:, k : k + 1] = jnp.sum(upright, axis=1, keepdims=True)
    for copy in copies[3:]:
        copy.wait()


def load_rest(z, sign, step_size, rho, penalty, blocks_count):
    tasks, width = z.shape
    rows = [v.reshape(1, tasks) for v in (step_size, rho, penalty)]
    return call(
        functools.partial(rest_kernel, blocks_count),
        "load_rest",
        [HBM] * 5,
        (pltpu.VMEM((tasks, width), F32), pltpu.VMEM(sign.shape, jnp.int32), pltpu.VMEM((tasks, 128), F32)),
        [VMEM] * 3,
        [pltpu.VMEM((1, tasks), F32)] * 3 + [pltpu.SemaphoreType.DMA((5,))],
    )(*pin(pltpu.HBM, z, sign, *rows))


def residual(sign, own, other):
    margin = own.astype(F32) + other.astype(F32)
    sign = sign.astype(F32)
    return (sign * jax.nn.sigmoid(-sign * margin)).astype(BF16)


def first_kernel(sign, own, other, scale, a_ref, *rest):
    before, out, resid = rest[:-2], rest[-2], rest[-1]
    cut = own.shape[1]
    eta = scale[:, 0:1]
    resid[...] = residual(sign[:, :cut], own[...], other[...])

    @pl.loop(0, out.shape[1] // STEP)
    def _(j):
        at = columns(j * STEP, STEP)
        push = eta * jnp.dot(resid[...], a_ref[:cut, at], preferred_element_type=F32)
        out[:, at] = push + before[0][:, at] if before else push


def first_push(sign, pair, scale, design, before=None):
    tasks = sign.shape[0]
    args = [sign, *pair, scale, design] + ([] if before is None else [before])
    return call(
        first_kernel,
        "first_push",
        [VMEM] * len(args),
        pltpu.VMEM((tasks, design.shape[1]), F32),
        VMEM,
        [pltpu.VMEM(pair[0].shape, BF16)],
    )(*pin(pltpu.VMEM, *args))


def margin_loop(x_ref, a_ref, rows, acc, out):
    width = x_ref.shape[1]
    wide = math.gcd(WIDE, width)
    for j in range(width // wide):
        at = pl.ds(j * wide, wide)
        product = nt(x_ref[:, at], a_ref[rows, at])
        if j == 0:
            acc[...] = product
        else:
            acc[...] += product
    out[...] = acc[...].astype(BF16)


def turn_kernel(sign, own, other, scale, x_ref, u_ref, z_ref, p_ref, a_ref, q_out, x_out, m_out, resid, acc):
    cut = m_out.shape[1]
    resid[...] = residual(sign[:, cut:], own[...], other[...])
    eta, pull = scale[:, 0:1], scale[:, 1:2]

    @pl.loop(0, x_ref.shape[1] // STEP)
    def _(j):
        at = columns(j * STEP, STEP)
        push = p_ref[:, at] + eta * jnp.dot(resid[...], a_ref[cut:, at], preferred_element_type=F32)
        x = x_ref[:, at]
        x_out[:, at] = (x - pull * (x - z_ref[:, at] + u_ref[:, at]) + push).astype(BF16)
        q_out[:, at] = (1.0 - pull) * push

    margin_loop(x_out, a_ref, pl.ds(0, cut), acc, m_out)


def turn(sign, pair, scale, x, u, z, pushed, design):
    tasks, width = x.shape
    first, second = parts(tasks, design.shape[0])
    return call(
        turn_kernel,
        "turn",
        [VMEM] * 9,
        (pltpu.VMEM((tasks, width), F32), pltpu.VMEM((tasks, width), BF16), first),
        [VMEM] * 3,
        [pltpu.VMEM(second.shape, BF16), pltpu.VMEM(first.shape, F32)],
    )(*pin(pltpu.VMEM, sign, *pair, scale, x, u, z, pushed, design))


def margin_kernel(x_ref, a_ref, out, acc):
    rows = out.shape[1]
    margin_loop(x_ref, a_ref, pl.ds(a_ref.shape[0] - rows, rows), acc, out)


def rest_margins(x, design):
    tasks = x.shape[0]
    _, second = parts(tasks, design.shape[0])
    return call(
        margin_kernel, "rest_margins", [VMEM] * 2, second, VMEM, [pltpu.VMEM(second.shape, F32)]
    )(*pin(pltpu.VMEM, x, design))


def push_kernel(first, mine, begin, offset, size, side, *refs):
    if first:
        sign, own, other, scale, q_ref, a_ref, h_out, sent_out, resid = refs
        resid[...] = residual(sign[:, sign.shape[1] - own.shape[1] :], own[...], other[...])
    else:
        resid, scale, q_ref, a_ref, *received, h_out, sent_out = refs
    half = q_ref.shape[1] // 2
    cut = a_ref.shape[0] - resid.shape[1]
    eta = scale[:, 0:1]
    base = (side[0] if mine else 1 - side[0]) * half + begin
    step = math.gcd(512, size)
    for j in range(size // step):
        at = columns(base + j * step, step)
        here = pl.ds(j * step, step)
        push = q_ref[:, at] + eta * jnp.dot(resid[...], a_ref[cut:, at], preferred_element_type=F32)
        h_out[:, here] = push
        if mine:
            push = push + received[0][:, pl.ds(offset + j * step, step)].astype(F32)
        sent_out[:, here] = push.astype(BF16)


def push(side, resid, scale, q, design, received, begin, offset, size):
    tasks = q.shape[0]
    mine = received is not None
    first = isinstance(resid, tuple)
    args = [*(resid if first else [resid]), scale, q, design] + ([received] if mine else [])
    out = [pltpu.VMEM((tasks, size), F32), pltpu.VMEM((tasks, size), BF16)]
    if first:
        out.append(parts(tasks, design.shape[0])[1])
    return call(
        functools.partial(push_kernel, first, mine, begin, offset, size),
        "push_mine" if mine else "push_other",
        [SMEM] + [VMEM] * len(args),
        tuple(out),
        [VMEM] * len(out),
    )(side, *pin(pltpu.VMEM, *args))


def store_kernel(side, scale, x_ref, u_ref, z_ref, *rest):
    *hs, x_out, stage, sems = rest
    half = x_ref.shape[1] // 2
    keep = 1.0 - scale[:, 1:2]
    copies = []
    done = 0
    for c, h_ref in enumerate(hs):
        size = h_ref.shape[1]
        base = (side[0] if done < half else 1 - side[0]) * half + done % half
        done += size
        for j in range(0, size, NARROW):
            at = columns(base + j, NARROW)
            u, z = u_ref[:, at], z_ref[:, at]
            stage[:, at] = z - u + keep * keep * (x_ref[:, at] - z + u) + h_ref[:, pl.ds(j, NARROW)]
        at = columns(base, size)
        copy = pltpu.make_async_copy(stage.at[:, at], x_out.at[:, at], sems.at[c])
        copy.start()
        copies.append(copy)
    for copy in copies:
        copy.wait()


def store_x(side, scale, x, u, z, mines, others):
    tasks, width = x.shape
    args = [scale, x, u, z, *mines, *others]
    return call(
        store_kernel,
        "store_x",
        [SMEM] + [VMEM] * len(args),
        pltpu.HBM((tasks, width), F32),
        HBM,
        [pltpu.VMEM((tasks, width), F32), pltpu.SemaphoreType.DMA((len(mines) + len(others),))],
    )(side, *pin(pltpu.VMEM, *args))


def final_kernel(blocks_count, mine, begin, offset, size, buffered, side, scale, x_ref, u_ref, z_ref, *rest):
    start, h, pushed = rest[:3]
    outs = rest[3 + 2 * buffered : 5 + 2 * buffered]
    stage, sems = rest[-2:]
    half = x_ref.shape[1] // 2
    pull, limit = scale[:, 1:2], scale[:, 2:3]
    keep = 1.0 - pull
    base = (side[0] if mine else 1 - side[0]) * half + begin
    for j in range(0, size, NARROW):
        cut, here = columns(base + j, NARROW), pl.ds(j, NARROW)
        z = z_ref[:, cut]
        total = keep * keep * start[:, pl.ds(begin + j, NARROW)] + pushed[:, here].astype(F32)
        mean = total * (1.0 / blocks_count) + pull * (1.0 + keep) * z
        new_z = mean - jnp.clip(mean, -limit, limit)
        moved = z + keep * keep * (x_ref[:, cut] - z + u_ref[:, cut]) + h[:, pl.ds(offset + j, NARROW)]
        stage[0, :, here] = new_z
        stage[1, :, here] = moved - new_z
    cut = columns(base, size)
    copies = [pltpu.make_async_copy(stage.at[o], outs[o].at[:, cut], sems.at[o]) for o in range(2)]
    for copy in copies:
        copy.start()
    for copy in copies:
        copy.wait()


def final(side, scale, x, u, z, start, h, pushed, buffers, mine, begin, offset, blocks_count):
    tasks, width = x.shape
    size = pushed.shape[1]
    buffered = buffers is not None
    args = pin(pltpu.VMEM, scale, x, u, z, start, h, pushed)
    out = pltpu.HBM((tasks, width), F32)
    aliases = {}
    if buffered:
        aliases = {1 + len(args) + o: o for o in range(2)}
        args += pin(pltpu.HBM, *buffers)
    return call(
        functools.partial(final_kernel, blocks_count, mine, begin, offset, size, buffered),
        "final_mine" if mine else "final_other",
        [SMEM] + [VMEM] * 7 + [HBM] * (2 * buffered),
        (out, out),
        [HBM] * 2,
        [pltpu.VMEM((2, tasks, size), F32), pltpu.SemaphoreType.DMA((2,))],
        aliases,
    )(side, *args)


def tie(value, *after):
    return lax.optimization_barrier((value, after))[0]


def per_device(design, labels, local_x, dual_u, consensus_z, step_size, rho, penalty):
    tasks, width = consensus_z.shape
    half = width // 2
    blocks_count = lax.axis_size("rows")
    side = (lax.axis_index("rows") & 1).astype(jnp.int32)[None]

    first, second, design, x0, dual, start_mine, start_other = load(side, local_x[0], dual_u[0], design)
    start_mine = start_mine + exchange(start_other, "rows", 1)
    (pair_first, other_first), (pair_second, _) = two_doublings(first, second)
    z, sign, scale = load_rest(consensus_z, labels, tie(step_size, other_first), rho, penalty, blocks_count)
    pushed = first_push(sign, pair_first, scale, design)
    pair_second = tie(pair_second, pushed, start_mine)

    carried, x1, first = turn(sign, pair_second, scale, x0, dual, z, pushed, design)
    second = rest_margins(x1, design)
    mask = 2
    while mask < blocks_count:
        start_mine = start_mine + exchange(start_mine, "rows", mask)
        mask *= 2
    (pair_first, _), (pair_second, _) = two_doublings(first, second)
    pushed = first_push(sign, pair_first, scale, design, carried)
    pair_second = tie(pair_second, pushed, start_mine)

    sizes = [half * part // sum(MINE) for part in MINE]
    begins = [sum(sizes[:c]) for c in range(len(sizes))]
    other_sizes = [half * part // sum(OTHER) for part in OTHER]
    other_begins = [sum(other_sizes[:c]) for c in range(len(other_sizes))]
    count = len(sizes)
    others, received = [], []
    resid = (sign, *pair_second)
    for begin, size in zip(other_begins, other_sizes):
        value, other, *made = push(side, resid, scale, pushed, design, None, begin, 0, size)
        resid = made[0] if made else resid
        others.append(value)
        received.append(exchange(other, "rows", 1))
    mines, sums, places = [], [], []
    token = tie(side, others[-1])
    for begin, size in zip(begins, sizes):
        source = max(k for k, b in enumerate(other_begins) if b <= begin)
        places.append((source, begin - other_begins[source]))
        value, sent = push(token, resid, scale, pushed, design, received[source], begin, places[-1][1], size)
        mines.append(value)
        sums.append(doubling(sent, "rows", 2))
        token = tie(side, sent)
    new_x = store_x(side, scale, x0, dual, z, mines, others)

    start_theirs = exchange(tie(start_mine, mines[0]), "rows", 1)

    pieces, results = [], None

    def finish(c, mine):
        source, offset = places[c]
        return final(
            side, scale, x0, dual, z, start_mine if mine else start_theirs, mines[c] if mine else others[source],
            pieces[c][0 if mine else 1], results, mine, begins[c], 0 if mine else offset, blocks_count,
        )

    for c, (a, b) in enumerate(sums):
        b = tie(b, new_x, results)
        piece = (a.astype(F32) + b.astype(F32)).astype(BF16)
        if c == count - 1:
            results = tie(results, piece)
            results = finish(c - 1, False)
        pieces.append((piece, exchange(piece, "rows", 1)))
        results = finish(c, True)
        if c != count - 2:
            results = finish(c, False)
    new_z, new_u = results
    return (new_x[None], new_z, new_u[None])


def solution(mesh):
    in_specs = (
        P("rows", "feat"),
        P(None, "rows"),
        P("rows", None, "feat"),
        P("rows", None, "feat"),
        P(None, "feat"),
        P(),
        P(),
        P(),
    )
    out_specs = (P("rows", None, "feat"), P(None, "feat"), P("rows", None, "feat"))
    return jax.shard_map(
        per_device, mesh=mesh, in_specs=in_specs, out_specs=out_specs, check_vma=False
    )
```

time: 69 us -> 70.7 us (1.025)
  Pallas kernels: 25.5 us -> 29.3 us
  waiting for transfers between devices: 19.3 us -> 16.9 us
    pallas_call x12 -> x17, Pallas kernels: 23.8 us -> 27.6 us  [the longest x6 6.87 us: final(): call(functools.partial(final_kernel, blocks_count, mine, begin, offset, s...]
    ppermute x18 -> x23, waiting for transfers between devices: 19.3 us -> 16.9 us  [exchange(): return lax.ppermute(value, axis, [(i, i ^ mask) for i in range(n)])]
    ppermute x18 -> x23, starting transfers between devices: 22.8 us -> 22.9 us  [exchange(): return lax.ppermute(value, axis, [(i, i ^ mask) for i in range(n)])]
  transfers between devices with their start and end apart: 18 -> 23, of which waited for: 10 -> 11; matrix products, arithmetic and copies ran while one was open for 1% -> 1% of each run, Pallas kernels for 24% -> 30%
where the time goes in v6:
time: 70.7 us; the launch traced here: 70.5 us
  Pallas kernels  29.3 us (41%)
  starting transfers between devices  22.9 us (32%)
  waiting for transfers between devices  16.9 us (24%)
  between operations  0.91 us (1%)
    ppermute x23, starting transfers between devices, exchange(): return lax.ppermute(value, axis, [(i, i ^ mask) for i in range(n)])  22.9 us
    ppermute x23, waiting for transfers between devices, exchange(): return lax.ppermute(value, axis, [(i, i ^ mask) for i in range(n)])  16.9 us
    pallas_call x6, Pallas kernels, final(): call(functools.partial(final_kernel, blocks_count, mine, begin, offset, s...  6.87 us
    pallas_call x1, Pallas kernels, load(): call(load_kernel, 'load_and_margins', [SMEM] + [HBM] * 3, (*parts(tasks,...  6.82 us
    pallas_call x2, Pallas kernels, first_push(): call(first_kernel, 'first_push', [VMEM] * len(args), pltpu.VMEM((tasks, d...  4.93 us
    pallas_call x1, Pallas kernels, turn(): call(turn_kernel, 'turn', [VMEM] * 9, (pltpu.VMEM((tasks, width), F32), p...  4.58 us
    pallas_call x1, Pallas kernels, load_rest(): call(functools.partial(rest_kernel, blocks_count), 'load_rest', [HBM] * 5...  1.68 us
    pallas_call x1, Pallas kernels, store_x(): call(store_kernel, 'store_x', [SMEM] + [VMEM] * len(args), pltpu.HBM((tas...  1.66 us
  transfers between devices with their start and end apart: 23, of which 11 were waited for; matrix products, arithmetic and copies ran while one was open for 1% of the time, Pallas kernels for 30%

profile of v6, /device:TPU:0, one launch (start us, length us, event | category | flops | bytes accessed | tf_op | source)
XLA Modules:
  0.0 70.5 jit_solution(10735917269500982448)
XLA Ops:
  0.6 6.8 %load_and_margins.1 = (bf16[64,512]{1,0:T(8,128)(2,1)S(1)}, bf16[64,256]{1,0:T(8,128)(2,1)S(1)}, bf16[768,8192]{1,0:T(8,128)(2,1)S(1)}, f32[64,8192]{1,0:T(8,128...) custom-call(s32[1]{0:T(128)} %bitcast.side, f32[64,8192]{1,0:T(8,128)} %bitcast.9, ...), custom_call_target="tpu_custom_call" | custom-call | flops 1000 | bytes 1000 | tf_op jit(solution)/shard_map/load_and_margins/pallas_call | solution.py:139
  8.0 2.6 %collective-permute-start = (bf16[64,512]{1,0:T(8,128)(2,1)S(1)}, bf16[64,512]{1,0:T(8,128)(2,1)S(1)}, u32[]{:S(2)}, u32[]{:S(2)}) collective-permute-start(bf16[64,512]{1,0:T(8,128)(2,1)S(1)} %get-tuple-element.57), channel_id=1, source_target_pairs={{0,1},{1,0},{2,3},{3,2},{4,5},{5,4},{6,7},{7,6},{8,9},{9,8},{10,11... | collective-permute-start | bytes 196616 | tf_op jit(solution)/shard_map/ppermute | solution.py:26
  10.7 2.6 %collective-permute-done = bf16[64,512]{1,0:T(8,128)(2,1)S(1)} collective-permute-done((bf16[64,512]{1,0:T(8,128)(2,1)S(1)}, bf16[64,512]{1,0:T(8,128)(2,1)S(1)}, u32[]{:S(2)}, u32[]{:S(2)}) %collective-permute-start) | collective-permute-done | bytes 65568 | tf_op jit(solution)/shard_map/ppermute | solution.py:26
  13.3 2.1 %collective-permute-start.3 = (bf16[64,512]{1,0:T(8,128)(2,1)S(1)}, bf16[64,512]{1,0:T(8,128)(2,1)S(1)}, u32[]{:S(2)}, u32[]{:S(2)}) collective-permute-start(bf16[64,512]{1,0:T(8,128)(2,1)S(1)} %add_convert_fusion.6), channel_id=1, source_target_pairs={{0,2},{1,3},{2,0},{3,1},{4,6},{5,7},{6,4},{7,5},{8,10},{9,11},{10,... | collective-permute-start | bytes 196616 | tf_op jit(solution)/shard_map/ppermute | solution.py:26
  16.1 1.8 %collective-permute-done.3 = bf16[64,512]{1,0:T(8,128)(2,1)S(1)} collective-permute-done((bf16[64,512]{1,0:T(8,128)(2,1)S(1)}, bf16[64,512]{1,0:T(8,128)(2,1)S(1)}, u32[]{:S(2)}, u32[]{:S(2)}) %collective-permute-start.3) | collective-permute-done | bytes 65568 | tf_op jit(solution)/shard_map/ppermute | solution.py:26
  18.0 3.0 %collective-permute-start.5 = (bf16[64,512]{1,0:T(8,128)(2,1)S(1)}, bf16[64,512]{1,0:T(8,128)(2,1)S(1)}, u32[]{:S(2)}, u32[]{:S(2)}) collective-permute-start(bf16[64,512]{1,0:T(8,128)(2,1)S(1)} %add_convert_fusion.5.own), channel_id=1, source_target_pairs={{0,4},{1,5},{2,6},{3,7},{4,0},{5,1},{6,2},{7,3},{8,12},{9,13},{10,... | collective-permute-start | bytes 196616 | tf_op jit(solution)/shard_map/ppermute | solution.py:26
  21.1 1.6 %collective-permute-start.13 = (f32[64,4096]{1,0:T(8,128)S(1)}, f32[64,4096]{1,0:T(8,128)S(1)}, u32[]{:S(2)}, u32[]{:S(2)}) collective-permute-start(f32[64,4096]{1,0:T(8,128)S(1)} %add.43), channel_id=1, source_target_pairs={{0,16},{8,24},{16,0},{24,8},{1,17},{9,25},{17,1},{25,9},{2,18},{10... | collective-permute-start | bytes 3145736 | tf_op jit(solution)/shard_map/ppermute | solution.py:26
  22.6 1.4 %collective-permute-start.4 = (bf16[64,256]{1,0:T(8,128)(2,1)S(1)}, bf16[64,256]{1,0:T(8,128)(2,1)S(1)}, u32[]{:S(2)}, u32[]{:S(2)}) collective-permute-start(bf16[64,256]{1,0:T(8,128)(2,1)S(1)} %add_convert_fusion.9.own), channel_id=1, source_target_pairs={{0,4},{1,5},{2,6},{3,7},{4,0},{5,1},{6,2},{7,3},{8,12},{9,13},{10,... | collective-permute-start | bytes 98312 | tf_op jit(solution)/shard_map/ppermute | solution.py:26
  24.1 1.7 %load_rest.1 = (f32[64,8192]{1,0:T(8,128)S(1)}, s32[64,768]{1,0:T(8,128)S(1)}, f32[64,128]{1,0:T(8,128)S(1)}) custom-call(f32[64,8192]{1,0:T(8,128)} %z_hbm.1, s32[64,768]{1,0:T(8,128)} %sign_hbm.1, f32[1,64]{1,0:T(1,128)} %bitcast.12, f32[1,64]{1,0:T(1,128)} %bitcast.13, f32[1,64]{1,0:T(1,128)} %bitcast.14), custom_call_target="tpu_custom_call" | custom-call | flops 1000 | bytes 1000 | tf_op jit(solution)/shard_map/load_rest/pallas_call | solution.py:170
  25.8 2.5 %first_push.2.p_ref = f32[64,8192]{1,0:T(8,128)S(1)} custom-call(s32[64,768]{1,0:T(8,128)S(1)} %get-tuple-element.63.sign.refs_0_, bf16[64,512]{1,0:T(8,128)(2,1)S(1)} %add_convert_fusion.5.own, bf16[64,512]{1,0:T(8,128)(2,1)S(1)} %collective-permute-done.5.other, f32[64,128]{1,0:T(8,128)S(1)} %get-tuple-element.59.scale.refs_3_.refs_1_, ...), custom_call_target="tpu_custom_call" | custom-call | flops 1000 | bytes 1000 | tf_op jit(solution)/shard_map/first_push/pallas_call | solution.py:202
  28.2 4.6 %turn.1 = (f32[64,8192]{1,0:T(8,128)S(1)}, bf16[64,8192]{1,0:T(8,128)(2,1)S(1)}, bf16[64,512]{1,0:T(8,128)(2,1)S(1)}) custom-call(s32[64,768]{1,0:T(8,128)S(1)} %get-tuple-element.63.sign.refs_0_, bf16[64,256]{1,0:T(8,128)(2,1)S(1)} %add_convert_fusion.9.own, bf16[64,256]{1,0:T(8,128)(2,1)S(1)} %collective-permute-done.4.other, ...), custom_call_target="tpu_custom_call" | custom-call | flops 1000 | bytes 1000 | tf_op jit(solution)/shard_map/turn/pallas_call | solution.py:244
  32.8 1.7 %collective-permute-start.8 = (bf16[64,512]{1,0:T(8,128)(2,1)S(1)}, bf16[64,512]{1,0:T(8,128)(2,1)S(1)}, u32[]{:S(2)}, u32[]{:S(2)}) collective-permute-start(bf16[64,512]{1,0:T(8,128)(2,1)S(1)} %get-tuple-element.73), channel_id=1, source_target_pairs={{0,1},{1,0},{2,3},{3,2},{4,5},{5,4},{6,7},{7,6},{8,9},{9,8},{10,11... | collective-permute-start | bytes 196616 | tf_op jit(solution)/shard_map/ppermute | solution.py:26
  34.6 1.4 %rest_margins.1 = bf16[64,256]{1,0:T(8,128)(2,1)S(1)} custom-call(bf16[64,8192]{1,0:T(8,128)(2,1)S(1)} %get-tuple-element.72.x_ref, bf16[768,8192]{1,0:T(8,128)(2,1)S(1)} %get-tuple-element.67.a_ref.refs_5_.refs_3_), custom_call_target="tpu_custom_call" | custom-call | flops 1000 | bytes 1000 | tf_op jit(solution)/shard_map/rest_margins/pallas_call | solution.py:262
  37.9 2.0 %collective-permute-done.7 = bf16[64,256]{1,0:T(8,128)(2,1)S(1)} collective-permute-done((bf16[64,256]{1,0:T(8,128)(2,1)S(1)}, bf16[64,256]{1,0:T(8,128)(2,1)S(1)}, u32[]{:S(2)}, u32[]{:S(2)}) %collective-permute-start.7) | collective-permute-done | bytes 32800 | tf_op jit(solution)/shard_map/ppermute | solution.py:26
  41.6 1.6 %collective-permute-start.12 = (bf16[64,512]{1,0:T(8,128)(2,1)S(1)}, bf16[64,512]{1,0:T(8,128)(2,1)S(1)}, u32[]{:S(2)}, u32[]{:S(2)}) collective-permute-start(bf16[64,512]{1,0:T(8,128)(2,1)S(1)} %add_convert_fusion.3.own), channel_id=1, source_target_pairs={{0,4},{1,5},{2,6},{3,7},{4,0},{5,1},{6,2},{7,3},{8,12},{9,13},{10,... | collective-permute-start | bytes 196616 | tf_op jit(solution)/shard_map/ppermute | solution.py:26
  43.9 1.5 %collective-permute-start.11 = (bf16[64,256]{1,0:T(8,128)(2,1)S(1)}, bf16[64,256]{1,0:T(8,128)(2,1)S(1)}, u32[]{:S(2)}, u32[]{:S(2)}) collective-permute-start(bf16[64,256]{1,0:T(8,128)(2,1)S(1)} %add_convert_fusion.7.refs_1_), channel_id=1, source_target_pairs={{0,4},{1,5},{2,6},{3,7},{4,0},{5,1},{6,2},{7,3},{8,12},{9,13},{10,... | collective-permute-start | bytes 98312 | tf_op jit(solution)/shard_map/ppermute | solution.py:26
  45.4 1.4 %collective-permute-done.12.other = bf16[64,512]{1,0:T(8,128)(2,1)S(1)} collective-permute-done((bf16[64,512]{1,0:T(8,128)(2,1)S(1)}, bf16[64,512]{1,0:T(8,128)(2,1)S(1)}, u32[]{:S(2)}, u32[]{:S(2)}) %collective-permute-start.12) | collective-permute-done | bytes 65568 | tf_op jit(solution)/shard_map/ppermute | solution.py:26
  46.8 2.5 %first_push.3.refs_4_.refs_2_ = f32[64,8192]{1,0:T(8,128)S(1)} custom-call(s32[64,768]{1,0:T(8,128)S(1)} %get-tuple-element.63.sign.refs_0_, bf16[64,512]{1,0:T(8,128)(2,1)S(1)} %add_convert_fusion.3.own, bf16[64,512]{1,0:T(8,128)(2,1)S(1)} %collective-permute-done.12.other, f32[64,128]{1,0:T(8,128)S(1)} %get-tuple-element.59.scale.refs_3_.refs_1_, ...), custom_call_target="tpu_custom_call" | custom-call | flops 1000 | bytes 1000 | tf_op jit(solution)/shard_map/first_push/pallas_call | solution.py:202
  51.9 1.3 %collective-permute-start.19 = (bf16[64,1024]{1,0:T(8,128)(2,1)S(1)}, bf16[64,1024]{1,0:T(8,128)(2,1)S(1)}, u32[]{:S(2)}, u32[]{:S(2)}) collective-permute-start(bf16[64,1024]{1,0:T(8,128)(2,1)S(1)} %get-tuple-element.84), channel_id=1, source_target_pairs={{0,16},{8,24},{16,0},{24,8},{1,17},{9,25},{17,1},{25,9},{2,18},{10... | collective-permute-start | bytes 393224 | tf_op jit(solution)/shard_map/ppermute | solution.py:26
  53.2 1.4 %collective-permute-done.15.refs_4_ = bf16[64,3072]{1,0:T(8,128)(2,1)S(1)} collective-permute-done((bf16[64,3072]{1,0:T(8,128)(2,1)S(1)}, bf16[64,3072]{1,0:T(8,128)(2,1)S(1)}, u32[]{:S(2)}, u32[]{:S(2)}) %collective-permute-start.15) | collective-permute-done | bytes 393248 | tf_op jit(solution)/shard_map/ppermute | solution.py:26
  54.9 1.4 %collective-permute-start.18 = (bf16[64,1536]{1,0:T(8,128)(2,1)S(1)}, bf16[64,1536]{1,0:T(8,128)(2,1)S(1)}, u32[]{:S(2)}, u32[]{:S(2)}) collective-permute-start(bf16[64,1536]{1,0:T(8,128)(2,1)S(1)} %get-tuple-element.88), channel_id=1, source_target_pairs={{0,16},{8,24},{16,0},{24,8},{1,17},{9,25},{17,1},{25,9},{2,18},{10... | collective-permute-start | bytes 589832 | tf_op jit(solution)/shard_map/ppermute | solution.py:26
  56.5 1.7 %store_x.1 = f32[64,8192]{1,0:T(8,128)} custom-call(s32[1]{0:T(128)} %bitcast.side, f32[64,128]{1,0:T(8,128)S(1)} %get-tuple-element.59.scale.refs_3_.refs_1_, f32[64,8192]{1,0:T(8,128)S(1)} %get-tuple-element.60.x_ref, f32[64,8192]{1,0:T(8,128)S(1)} %get-tuple-element.61.u_ref, f32[64,8192]{1,0:T(8,128)S(1)} %get-tuple-element.62.z_ref, ...), custom_call_target="tpu_custom_call" | custom-call | flops 1000 | bytes 1000 | tf_op jit(solution)/shard_map/store_x/pallas_call | solution.py:330
  63.3 3.5 %collective-permute-done.17 = bf16[64,1536]{1,0:T(8,128)(2,1)S(1)} collective-permute-done((bf16[64,1536]{1,0:T(8,128)(2,1)S(1)}, bf16[64,1536]{1,0:T(8,128)(2,1)S(1)}, u32[]{:S(2)}, u32[]{:S(2)}) %collective-permute-start.17) | collective-permute-done | bytes 196640 | tf_op jit(solution)/shard_map/ppermute | solution.py:26
  68.1 1.2 %final_mine.5 = (f32[64,8192]{1,0:T(8,128)}, f32[64,8192]{1,0:T(8,128)}) custom-call(s32[1]{0:T(128)} %bitcast.side, f32[64,128]{1,0:T(8,128)S(1)} %get-tuple-element.59.scale.refs_3_.refs_1_, f32[64,8192]{1,0:T(8,128)S(1)} %get-tuple-element.60.x_ref, f32[64,8192]{1,0:T(8,128)S(1)} %get-tuple-element.61.u_ref, ...), custom_call_target="tpu_custom_call", output_to_operand_aliasing={{0}: (8, {}), {1}: (9, {})} | custom-call | flops 1000 | bytes 1000 | tf_op jit(solution)/shard_map/final_mine/pallas_call | solution.py:375
  (53 shorter events, 16.5 us)
Async XLA Ops:
  7.5 13.5 %collective-permute-start.6 = (f32[64,4096]{1,0:T(8,128)S(1)}, f32[64,4096]{1,0:T(8,128)S(1)}, u32[]{:S(2)}, u32[]{:S(2)}) collective-permute-start(f32[64,4096]{1,0:T(8,128)S(1)} %get-tuple-element.69), channel_id=1, source_target_pairs={{0,8},{8,0},{16,24},{24,16},{1,9},{9,1},{17,25},{25,17},{2,10},{10... | collective-permute-start | bytes 3145736 | tf_op jit(solution)/shard_map/ppermute | solution.py:26
  8.0 5.3 %collective-permute-start = (bf16[64,512]{1,0:T(8,128)(2,1)S(1)}, bf16[64,512]{1,0:T(8,128)(2,1)S(1)}, u32[]{:S(2)}, u32[]{:S(2)}) collective-permute-start(bf16[64,512]{1,0:T(8,128)(2,1)S(1)} %get-tuple-element.57), channel_id=1, source_target_pairs={{0,1},{1,0},{2,3},{3,2},{4,5},{5,4},{6,7},{7,6},{8,9},{9,8},{10,11... | collective-permute-start | bytes 196616 | tf_op jit(solution)/shard_map/ppermute | solution.py:26
  10.6 4.8 %collective-permute-start.1 = (bf16[64,256]{1,0:T(8,128)(2,1)S(1)}, bf16[64,256]{1,0:T(8,128)(2,1)S(1)}, u32[]{:S(2)}, u32[]{:S(2)}) collective-permute-start(bf16[64,256]{1,0:T(8,128)(2,1)S(1)} %get-tuple-element.64), channel_id=1, source_target_pairs={{0,1},{1,0},{2,3},{3,2},{4,5},{5,4},{6,7},{7,6},{8,9},{9,8},{10,11... | collective-permute-start | bytes 98312 | tf_op jit(solution)/shard_map/ppermute | solution.py:26
  13.3 4.7 %collective-permute-start.3 = (bf16[64,512]{1,0:T(8,128)(2,1)S(1)}, bf16[64,512]{1,0:T(8,128)(2,1)S(1)}, u32[]{:S(2)}, u32[]{:S(2)}) collective-permute-start(bf16[64,512]{1,0:T(8,128)(2,1)S(1)} %add_convert_fusion.6), channel_id=1, source_target_pairs={{0,2},{1,3},{2,0},{3,1},{4,6},{5,7},{6,4},{7,5},{8,10},{9,11},{10,... | collective-permute-start | bytes 196616 | tf_op jit(solution)/shard_map/ppermute | solution.py:26
  15.4 5.6 %collective-permute-start.2 = (bf16[64,256]{1,0:T(8,128)(2,1)S(1)}, bf16[64,256]{1,0:T(8,128)(2,1)S(1)}, u32[]{:S(2)}, u32[]{:S(2)}) collective-permute-start(bf16[64,256]{1,0:T(8,128)(2,1)S(1)} %add_convert_fusion.10), channel_id=1, source_target_pairs={{0,2},{1,3},{2,0},{3,1},{4,6},{5,7},{6,4},{7,5},{8,10},{9,11},{10,... | collective-permute-start | bytes 98312 | tf_op jit(solution)/shard_map/ppermute | solution.py:26
  18.0 7.8 %collective-permute-start.5 = (bf16[64,512]{1,0:T(8,128)(2,1)S(1)}, bf16[64,512]{1,0:T(8,128)(2,1)S(1)}, u32[]{:S(2)}, u32[]{:S(2)}) collective-permute-start(bf16[64,512]{1,0:T(8,128)(2,1)S(1)} %add_convert_fusion.5.own), channel_id=1, source_target_pairs={{0,4},{1,5},{2,6},{3,7},{4,0},{5,1},{6,2},{7,3},{8,12},{9,13},{10,... | collective-permute-start | bytes 196616 | tf_op jit(solution)/shard_map/ppermute | solution.py:26
  21.1 28.2 %collective-permute-start.13 = (f32[64,4096]{1,0:T(8,128)S(1)}, f32[64,4096]{1,0:T(8,128)S(1)}, u32[]{:S(2)}, u32[]{:S(2)}) collective-permute-start(f32[64,4096]{1,0:T(8,128)S(1)} %add.43), channel_id=1, source_target_pairs={{0,16},{8,24},{16,0},{24,8},{1,17},{9,25},{17,1},{25,9},{2,18},{10... | collective-permute-start | bytes 3145736 | tf_op jit(solution)/shard_map/ppermute | solution.py:26
  22.6 5.6 %collective-permute-start.4 = (bf16[64,256]{1,0:T(8,128)(2,1)S(1)}, bf16[64,256]{1,0:T(8,128)(2,1)S(1)}, u32[]{:S(2)}, u32[]{:S(2)}) collective-permute-start(bf16[64,256]{1,0:T(8,128)(2,1)S(1)} %add_convert_fusion.9.own), channel_id=1, source_target_pairs={{0,4},{1,5},{2,6},{3,7},{4,0},{5,1},{6,2},{7,3},{8,12},{9,13},{10,... | collective-permute-start | bytes 98312 | tf_op jit(solution)/shard_map/ppermute | solution.py:26
  32.8 4.3 %collective-permute-start.8 = (bf16[64,512]{1,0:T(8,128)(2,1)S(1)}, bf16[64,512]{1,0:T(8,128)(2,1)S(1)}, u32[]{:S(2)}, u32[]{:S(2)}) collective-permute-start(bf16[64,512]{1,0:T(8,128)(2,1)S(1)} %get-tuple-element.73), channel_id=1, source_target_pairs={{0,1},{1,0},{2,3},{3,2},{4,5},{5,4},{6,7},{7,6},{8,9},{9,8},{10,11... | collective-permute-start | bytes 196616 | tf_op jit(solution)/shard_map/ppermute | solution.py:26
  35.9 4.0 %collective-permute-start.7 = (bf16[64,256]{1,0:T(8,128)(2,1)S(1)}, bf16[64,256]{1,0:T(8,128)(2,1)S(1)}, u32[]{:S(2)}, u32[]{:S(2)}) collective-permute-start(bf16[64,256]{1,0:T(8,128)(2,1)S(1)} %rest_margins.1), channel_id=1, source_target_pairs={{0,1},{1,0},{2,3},{3,2},{4,5},{5,4},{6,7},{7,6},{8,9},{9,8},{10,11... | collective-permute-start | bytes 98312 | tf_op jit(solution)/shard_map/ppermute | solution.py:26
  37.2 4.4 %collective-permute-start.10 = (bf16[64,512]{1,0:T(8,128)(2,1)S(1)}, bf16[64,512]{1,0:T(8,128)(2,1)S(1)}, u32[]{:S(2)}, u32[]{:S(2)}) collective-permute-start(bf16[64,512]{1,0:T(8,128)(2,1)S(1)} %add_convert_fusion.4), channel_id=1, source_target_pairs={{0,2},{1,3},{2,0},{3,1},{4,6},{5,7},{6,4},{7,5},{8,10},{9,11},{10,... | collective-permute-start | bytes 196616 | tf_op jit(solution)/shard_map/ppermute | solution.py:26
  39.9 4.0 %collective-permute-start.9 = (bf16[64,256]{1,0:T(8,128)(2,1)S(1)}, bf16[64,256]{1,0:T(8,128)(2,1)S(1)}, u32[]{:S(2)}, u32[]{:S(2)}) collective-permute-start(bf16[64,256]{1,0:T(8,128)(2,1)S(1)} %add_convert_fusion.8), channel_id=1, source_target_pairs={{0,2},{1,3},{2,0},{3,1},{4,6},{5,7},{6,4},{7,5},{8,10},{9,11},{10,... | collective-permute-start | bytes 98312 | tf_op jit(solution)/shard_map/ppermute | solution.py:26
  41.6 5.2 %collective-permute-start.12 = (bf16[64,512]{1,0:T(8,128)(2,1)S(1)}, bf16[64,512]{1,0:T(8,128)(2,1)S(1)}, u32[]{:S(2)}, u32[]{:S(2)}) collective-permute-start(bf16[64,512]{1,0:T(8,128)(2,1)S(1)} %add_convert_fusion.3.own), channel_id=1, source_target_pairs={{0,4},{1,5},{2,6},{3,7},{4,0},{5,1},{6,2},{7,3},{8,12},{9,13},{10,... | collective-permute-start | bytes 196616 | tf_op jit(solution)/shard_map/ppermute | solution.py:26
  43.9 5.5 %collective-permute-start.11 = (bf16[64,256]{1,0:T(8,128)(2,1)S(1)}, bf16[64,256]{1,0:T(8,128)(2,1)S(1)}, u32[]{:S(2)}, u32[]{:S(2)}) collective-permute-start(bf16[64,256]{1,0:T(8,128)(2,1)S(1)} %add_convert_fusion.7.refs_1_), channel_id=1, source_target_pairs={{0,4},{1,5},{2,6},{3,7},{4,0},{5,1},{6,2},{7,3},{8,12},{9,13},{10,... | collective-permute-start | bytes 98312 | tf_op jit(solution)/shard_map/ppermute | solution.py:26
  49.7 1.4 %collective-permute-start.14 = (bf16[64,1024]{1,0:T(8,128)(2,1)S(1)}, bf16[64,1024]{1,0:T(8,128)(2,1)S(1)}, u32[]{:S(2)}, u32[]{:S(2)}) collective-permute-start(bf16[64,1024]{1,0:T(8,128)(2,1)S(1)} %get-tuple-element.82), channel_id=1, source_target_pairs={{0,8},{8,0},{16,24},{24,16},{1,9},{9,1},{17,25},{25,17},{2,10},{10... | collective-permute-start | bytes 393224 | tf_op jit(solution)/shard_map/ppermute | solution.py:26
  51.3 8.8 %collective-permute-start.16 = (f32[64,4096]{1,0:T(8,128)S(1)}, f32[64,4096]{1,0:T(8,128)S(1)}, u32[]{:S(2)}, u32[]{:S(2)}) collective-permute-start(f32[64,4096]{1,0:T(8,128)S(1)} %add.48.rest_0_), channel_id=1, source_target_pairs={{0,8},{8,0},{16,24},{24,16},{1,9},{9,1},{17,25},{25,17},{2,10},{10... | collective-permute-start | bytes 3145736 | tf_op jit(solution)/shard_map/ppermute | solution.py:26
  51.6 3.1 %collective-permute-start.15 = (bf16[64,3072]{1,0:T(8,128)(2,1)S(1)}, bf16[64,3072]{1,0:T(8,128)(2,1)S(1)}, u32[]{:S(2)}, u32[]{:S(2)}) collective-permute-start(bf16[64,3072]{1,0:T(8,128)(2,1)S(1)} %get-tuple-element.86), channel_id=1, source_target_pairs={{0,8},{8,0},{16,24},{24,16},{1,9},{9,1},{17,25},{25,17},{2,10},{10... | collective-permute-start | bytes 1179656 | tf_op jit(solution)/shard_map/ppermute | solution.py:26
  51.9 6.3 %collective-permute-start.19 = (bf16[64,1024]{1,0:T(8,128)(2,1)S(1)}, bf16[64,1024]{1,0:T(8,128)(2,1)S(1)}, u32[]{:S(2)}, u32[]{:S(2)}) collective-permute-start(bf16[64,1024]{1,0:T(8,128)(2,1)S(1)} %get-tuple-element.84), channel_id=1, source_target_pairs={{0,16},{8,24},{16,0},{24,8},{1,17},{9,25},{17,1},{25,9},{2,18},{10... | collective-permute-start | bytes 393224 | tf_op jit(solution)/shard_map/ppermute | solution.py:26
  54.9 7.0 %collective-permute-start.18 = (bf16[64,1536]{1,0:T(8,128)(2,1)S(1)}, bf16[64,1536]{1,0:T(8,128)(2,1)S(1)}, u32[]{:S(2)}, u32[]{:S(2)}) collective-permute-start(bf16[64,1536]{1,0:T(8,128)(2,1)S(1)} %get-tuple-element.88), channel_id=1, source_target_pairs={{0,16},{8,24},{16,0},{24,8},{1,17},{9,25},{17,1},{25,9},{2,18},{10... | collective-permute-start | bytes 589832 | tf_op jit(solution)/shard_map/ppermute | solution.py:26
  58.3 1.9 %collective-permute-start.20 = (bf16[64,1024]{1,0:T(8,128)(2,1)S(1)}, bf16[64,1024]{1,0:T(8,128)(2,1)S(1)}, u32[]{:S(2)}, u32[]{:S(2)}) collective-permute-start(bf16[64,1024]{1,0:T(8,128)(2,1)S(1)} %add_convert_fusion.2.rest_2_), channel_id=1, source_target_pairs={{0,8},{8,0},{16,24},{24,16},{1,9},{9,1},{17,25},{25,17},{2,10},{10... | collective-permute-start | bytes 393224 | tf_op jit(solution)/shard_map/ppermute | solution.py:26
  59.4 7.4 %collective-permute-start.17 = (bf16[64,1536]{1,0:T(8,128)(2,1)S(1)}, bf16[64,1536]{1,0:T(8,128)(2,1)S(1)}, u32[]{:S(2)}, u32[]{:S(2)}) collective-permute-start(bf16[64,1536]{1,0:T(8,128)(2,1)S(1)} %get-tuple-element.93), channel_id=1, source_target_pairs={{0,16},{8,24},{16,0},{24,8},{1,17},{9,25},{17,1},{25,9},{2,18},{10... | collective-permute-start | bytes 589832 | tf_op jit(solution)/shard_map/ppermute | solution.py:26
  63.2 3.7 %collective-permute-start.22 = (bf16[64,1536]{1,0:T(8,128)(2,1)S(1)}, bf16[64,1536]{1,0:T(8,128)(2,1)S(1)}, u32[]{:S(2)}, u32[]{:S(2)}) collective-permute-start(bf16[64,1536]{1,0:T(8,128)(2,1)S(1)} %add_convert_fusion.1.rest_2_), channel_id=1, source_target_pairs={{0,8},{8,0},{16,24},{24,16},{1,9},{9,1},{17,25},{25,17},{2,10},{10... | collective-permute-start | bytes 589832 | tf_op jit(solution)/shard_map/ppermute | solution.py:26
  66.8 2.5 %collective-permute-start.21 = (bf16[64,1536]{1,0:T(8,128)(2,1)S(1)}, bf16[64,1536]{1,0:T(8,128)(2,1)S(1)}, u32[]{:S(2)}, u32[]{:S(2)}) collective-permute-start(bf16[64,1536]{1,0:T(8,128)(2,1)S(1)} %add_convert_fusion.rest_2_), channel_id=1, source_target_pairs={{0,8},{8,0},{16,24},{24,16},{1,9},{9,1},{17,25},{25,17},{2,10},{10... | collective-permute-start | bytes 589832 | tf_op jit(solution)/shard_map/ppermute | solution.py:26

commit v7 on v6

v7 whole, which is shorter than its diff:
```python
import functools
import math

import jax
import jax.numpy as jnp
from jax import lax
from jax.experimental import pallas as pl
from jax.experimental.pallas import tpu as pltpu
from jax.sharding import PartitionSpec as P

BF16 = jnp.bfloat16
F32 = jnp.float32
MINE = (2, 3, 3)
OTHER = (2, 6)
STEP = 1024
WIDE = 2048
AHEAD = 4
NARROW = 256
TURN_BYTES = 150_000_000
HBM = pl.BlockSpec(memory_space=pltpu.HBM)
VMEM = pl.BlockSpec(memory_space=pltpu.VMEM)
SMEM = pl.BlockSpec(memory_space=pltpu.SMEM)


def exchange(value, axis, mask):
    n = lax.axis_size(axis)
    return lax.ppermute(value, axis, [(i, i ^ mask) for i in range(n)])


def doubling(value, axis, first=1):
    n = lax.axis_size(axis)
    mask = first
    other = exchange(value, axis, mask)
    while 2 * mask < n:
        mask *= 2
        value = (value.astype(F32) + other.astype(F32)).astype(value.dtype)
        other = exchange(value, axis, mask)
    return value, other


def square_sum(value, axis):
    n = lax.axis_size(axis)
    terms = [value]
    mask = 1
    while mask < n:
        if len(terms) > 1:
            terms = [sum(t.astype(F32) for t in terms).astype(value.dtype)]
        steps = [mask, 2 * mask, 3 * mask] if 2 * mask < n else [mask]
        terms += [exchange(terms[0], axis, step) for step in steps]
        mask *= 4
    return terms


def nt(a, b):
    return lax.dot_general(a, b, (((1,), (1,)), ((), ())), preferred_element_type=F32)


def call(kernel, name, in_specs, out_shape, out_specs, scratch=(), aliases=None, limit=16, work=1000):
    return pl.pallas_call(
        kernel,
        in_specs=in_specs,
        out_shape=out_shape,
        out_specs=out_specs,
        scratch_shapes=list(scratch),
        input_output_aliases=aliases or {},
        compiler_params=pltpu.CompilerParams(vmem_limit_bytes=limit * 1024 * 1024),
        cost_estimate=pl.CostEstimate(flops=1000, bytes_accessed=work, transcendentals=0),
        name=name,
    )


def pin(space, *values):
    return [pltpu.with_memory_space_constraint(v, space) for v in values]


def columns(start, size):
    return pl.ds(pl.multiple_of(start, 128), size)


def load_kernel(side, x_hbm, u_hbm, a_hbm, m_out, a_out, x_out, u_out, mine_out, other_out, acc, sems):
    width = x_hbm.shape[1]
    steps = width // STEP

    def pair(j):
        cut = columns(j * STEP, STEP)
        return (
            pltpu.make_async_copy(x_hbm.at[:, cut], x_out.at[:, cut], sems.at[0, j]),
            pltpu.make_async_copy(a_hbm.at[:, cut], a_out.at[:, cut], sems.at[1, j]),
        )

    def begin(j):
        for copy in pair(j):
            copy.start()

    dual = pltpu.make_async_copy(u_hbm, u_out, sems.at[2, 0])
    for j in range(min(AHEAD, steps)):
        begin(j)
    acc[...] = jnp.zeros_like(acc)

    @pl.loop(0, steps)
    def _(j):
        for copy in pair(j):
            copy.wait()

        @pl.when(j + AHEAD < steps)
        def _():
            begin(j + AHEAD)

        @pl.when(j == max(steps - AHEAD, 0))
        def _():
            dual.start()

        cut = columns(j * STEP, STEP)
        acc[...] += nt(x_out[:, cut].astype(BF16), a_out[:, cut])

    m_out[...] = acc[...].astype(BF16)
    dual.wait()
    half = width // 2
    mine = columns(side[0] * half, half)
    other = columns((1 - side[0]) * half, half)
    mine_out[...] = x_out[:, mine] + u_out[:, mine]
    other_out[...] = x_out[:, other] + u_out[:, other]


def load(side, x, u, design):
    tasks, width = x.shape
    samples = design.shape[0]
    full = pltpu.VMEM((tasks, width), F32)
    half = pltpu.VMEM((tasks, width // 2), F32)
    return call(
        load_kernel,
        "load_and_margins",
        [SMEM] + [HBM] * 3,
        (pltpu.VMEM((tasks, samples), BF16), pltpu.VMEM(design.shape, BF16), full, full, half, half),
        [VMEM] * 6,
        [pltpu.VMEM((tasks, samples), F32), pltpu.SemaphoreType.DMA((3, width // STEP))],
    )(side, *pin(pltpu.HBM, x, u, design))


def rest_kernel(blocks_count, z_hbm, sign_hbm, eta_hbm, rho_hbm, lam_hbm, *refs):
    z_out, sign_out, scale_out, eta_row, rho_row, lam_row, sems = refs
    pairs = ((eta_hbm, eta_row), (rho_hbm, rho_row), (lam_hbm, lam_row), (z_hbm, z_out), (sign_hbm, sign_out))
    copies = [pltpu.make_async_copy(a, b, sems.at[k]) for k, (a, b) in enumerate(pairs)]
    for copy in copies:
        copy.start()
    for copy in copies[:3]:
        copy.wait()
    tasks = z_out.shape[0]
    one = lax.broadcasted_iota(jnp.int32, (tasks, tasks), 0) == lax.broadcasted_iota(jnp.int32, (tasks, tasks), 1)
    eta, rho, lam = eta_row[...], rho_row[...], lam_row[...]
    for k, row in enumerate((eta, eta * rho, lam / (rho * blocks_count))):
        upright = jnp.where(one, jnp.broadcast_to(row, (tasks, tasks)), 0.0)
        scale_out[:, k : k + 1] = jnp.sum(upright, axis=1, keepdims=True)
    for copy in copies[3:]:
        copy.wait()


def load_rest(z, sign, step_size, rho, penalty, blocks_count):
    tasks, width = z.shape
    rows = [v.reshape(1, tasks) for v in (step_size, rho, penalty)]
    return call(
        functools.partial(rest_kernel, blocks_count),
        "load_rest",
        [HBM] * 5,
        (pltpu.VMEM((tasks, width), F32), pltpu.VMEM(sign.shape, jnp.int32), pltpu.VMEM((tasks, 128), F32)),
        [VMEM] * 3,
        [pltpu.VMEM((1, tasks), F32)] * 3 + [pltpu.SemaphoreType.DMA((5,))],
    )(*pin(pltpu.HBM, z, sign, *rows))


def residual(sign, *terms):
    margin = sum(t.astype(F32) for t in terms)
    sign = sign.astype(F32)
    return (sign * jax.nn.sigmoid(-sign * margin)).astype(BF16)


def turn_kernel(sign, scale, x_ref, u_ref, z_ref, a_ref, *refs):
    *terms, q_out, m_out, resid, new_x, acc = refs
    resid[...] = residual(sign[...], *(t[...] for t in terms))
    eta, pull = scale[:, 0:1], scale[:, 1:2]
    width = x_ref.shape[1]

    @pl.loop(0, width // STEP)
    def _(j):
        at = columns(j * STEP, STEP)
        push = eta * jnp.dot(resid[...], a_ref[:, at], preferred_element_type=F32)
        x = x_ref[:, at]
        new_x[:, at] = (x - pull * (x - z_ref[:, at] + u_ref[:, at]) + push).astype(BF16)
        q_out[:, at] = (1.0 - pull) * push

    wide = math.gcd(WIDE, width)
    for j in range(width // wide):
        at = pl.ds(j * wide, wide)
        product = nt(new_x[:, at], a_ref[:, at])
        acc[...] = product if j == 0 else acc[...] + product
    m_out[...] = acc[...].astype(BF16)


def turn(sign, terms, scale, x, u, z, design):
    tasks, width = x.shape
    samples = design.shape[0]
    return call(
        turn_kernel,
        "turn",
        [VMEM] * (6 + len(terms)),
        (pltpu.VMEM((tasks, width), F32), pltpu.VMEM((tasks, samples), BF16)),
        [VMEM] * 2,
        [pltpu.VMEM((tasks, samples), BF16), pltpu.VMEM((tasks, width), BF16), pltpu.VMEM((tasks, samples), F32)],
        work=TURN_BYTES,
    )(*pin(pltpu.VMEM, sign, scale, x, u, z, design, *terms))


def push_kernel(first, mine, begin, offset, size, side, *refs):
    if first:
        scale, q_ref, a_ref, sign, *terms, h_out, sent_out, resid = refs
        resid[...] = residual(sign[...], *(t[...] for t in terms))
    else:
        scale, q_ref, a_ref, resid, *received, h_out, sent_out = refs
    half = q_ref.shape[1] // 2
    eta = scale[:, 0:1]
    base = (side[0] if mine else 1 - side[0]) * half + begin
    step = math.gcd(512, size)
    for j in range(size // step):
        at = columns(base + j * step, step)
        here = pl.ds(j * step, step)
        push = q_ref[:, at] + eta * jnp.dot(resid[...], a_ref[:, at], preferred_element_type=F32)
        h_out[:, here] = push
        if mine:
            push = push + received[0][:, pl.ds(offset + j * step, step)].astype(F32)
        sent_out[:, here] = push.astype(BF16)


def push(side, resid, scale, q, design, received, begin, offset, size):
    tasks = q.shape[0]
    mine = received is not None
    first = isinstance(resid, tuple)
    args = [scale, q, design, *(resid if first else [resid])] + ([received] if mine else [])
    out = [pltpu.VMEM((tasks, size), F32), pltpu.VMEM((tasks, size), BF16)]
    if first:
        out.append(pltpu.VMEM((tasks, design.shape[0]), BF16))
    return call(
        functools.partial(push_kernel, first, mine, begin, offset, size),
        "push_mine" if mine else "push_other",
        [SMEM] + [VMEM] * len(args),
        tuple(out),
        [VMEM] * len(out),
    )(side, *pin(pltpu.VMEM, *args))


def store_kernel(side, scale, x_ref, u_ref, z_ref, *rest):
    *hs, x_out, stage, sems = rest
    half = x_ref.shape[1] // 2
    keep = 1.0 - scale[:, 1:2]
    copies = []
    done = 0
    for c, h_ref in enumerate(hs):
        size = h_ref.shape[1]
        base = (side[0] if done < half else 1 - side[0]) * half + done % half
        done += size
        for j in range(0, size, NARROW):
            at = columns(base + j, NARROW)
            u, z = u_ref[:, at], z_ref[:, at]
            stage[:, at] = z - u + keep * keep * (x_ref[:, at] - z + u) + h_ref[:, pl.ds(j, NARROW)]
        at = columns(base, size)
        copy = pltpu.make_async_copy(stage.at[:, at], x_out.at[:, at], sems.at[c])
        copy.start()
        copies.append(copy)
    for copy in copies:
        copy.wait()


def store_x(side, scale, x, u, z, mines, others):
    tasks, width = x.shape
    args = [scale, x, u, z, *mines, *others]
    return call(
        store_kernel,
        "store_x",
        [SMEM] + [VMEM] * len(args),
        pltpu.HBM((tasks, width), F32),
        HBM,
        [pltpu.VMEM((tasks, width), F32), pltpu.SemaphoreType.DMA((len(mines) + len(others),))],
    )(side, *pin(pltpu.VMEM, *args))


def final_kernel(blocks_count, pieces, buffered, side, scale, x_ref, u_ref, z_ref, *refs):
    outs = refs[3 * len(pieces) + 2 * buffered :][:2]
    stage, sems = refs[-2:]
    half = x_ref.shape[1] // 2
    pull, limit = scale[:, 1:2], scale[:, 2:3]
    keep = 1.0 - pull
    copies, filled = [], 0
    for k, (mine, begin, offset, size) in enumerate(pieces):
        start, h, pushed = refs[3 * k : 3 * k + 3]
        base = (side[0] if mine else 1 - side[0]) * half + begin
        for j in range(0, size, NARROW):
            cut, here = columns(base + j, NARROW), pl.ds(filled + j, NARROW)
            z = z_ref[:, cut]
            total = keep * keep * start[:, pl.ds(begin + j, NARROW)] + pushed[:, pl.ds(j, NARROW)].astype(F32)
            mean = total * (1.0 / blocks_count) + pull * (1.0 + keep) * z
            new_z = mean - jnp.clip(mean, -limit, limit)
            moved = z + keep * keep * (x_ref[:, cut] - z + u_ref[:, cut]) + h[:, pl.ds(offset + j, NARROW)]
            stage[0, :, here] = new_z
            stage[1, :, here] = moved - new_z
        cut, here = columns(base, size), pl.ds(filled, size)
        for o in range(2):
            copy = pltpu.make_async_copy(stage.at[o, :, here], outs[o].at[:, cut], sems.at[k, o])
            copy.start()
            copies.append(copy)
        filled += size
    for copy in copies:
        copy.wait()


def final(side, scale, x, u, z, pieces, buffers, blocks_count):
    tasks, width = x.shape
    buffered = buffers is not None
    args = pin(pltpu.VMEM, scale, x, u, z, *(v for piece in pieces for v in piece[3:]))
    vmem = len(args)
    places = [(*piece[:3], piece[5].shape[1]) for piece in pieces]
    out = pltpu.HBM((tasks, width), F32)
    aliases = {}
    if buffered:
        aliases = {1 + vmem + o: o for o in range(2)}
        args += pin(pltpu.HBM, *buffers)
    return call(
        functools.partial(final_kernel, blocks_count, places, buffered),
        "final",
        [SMEM] + [VMEM] * vmem + [HBM] * (2 * buffered),
        (out, out),
        [HBM] * 2,
        [pltpu.VMEM((2, tasks, sum(p[3] for p in places)), F32), pltpu.SemaphoreType.DMA((len(pieces), 2))],
        aliases,
    )(side, *args)


def tie(value, *after):
    return lax.optimization_barrier((value, after))[0]


def per_device(design, labels, local_x, dual_u, consensus_z, step_size, rho, penalty):
    tasks, width = consensus_z.shape
    half = width // 2
    blocks_count = lax.axis_size("rows")
    side = (lax.axis_index("rows") & 1).astype(jnp.int32)[None]

    margin1, design, x0, dual, start_mine, start_other = load(side, local_x[0], dual_u[0], design)
    terms = doubling(margin1, "feat")
    start_mine = start_mine + exchange(start_other, "rows", 1)
    z, sign, scale = load_rest(consensus_z, labels, tie(step_size, terms[0]), rho, penalty, blocks_count)
    terms = tie(terms, start_mine)

    carried, margin2 = turn(sign, terms, scale, x0, dual, z, design)
    terms = square_sum(margin2, "feat")
    mask = 2
    while mask < blocks_count:
        start_mine = start_mine + exchange(start_mine, "rows", mask)
        mask *= 2
    terms = tie(terms, start_mine)

    sizes = [half * part // sum(MINE) for part in MINE]
    begins = [sum(sizes[:c]) for c in range(len(sizes))]
    other_sizes = [half * part // sum(OTHER) for part in OTHER]
    other_begins = [sum(other_sizes[:c]) for c in range(len(other_sizes))]
    count = len(sizes)
    others, received = [], []
    resid = (sign, *terms)
    for begin, size in zip(other_begins, other_sizes):
        value, other, *made = push(side, resid, scale, carried, design, None, begin, 0, size)
        resid = made[0] if made else resid
        others.append(value)
        received.append(exchange(other, "rows", 1))
    mines, sums, places = [], [], []
    token = tie(side, others[-1])
    for begin, size in zip(begins, sizes):
        source = max(k for k, b in enumerate(other_begins) if b <= begin)
        places.append((source, begin - other_begins[source]))
        value, sent = push(token, resid, scale, carried, design, received[source], begin, places[-1][1], size)
        mines.append(value)
        sums.append(doubling(sent, "rows", 2))
        token = tie(side, sent)
    new_x = store_x(side, scale, x0, dual, z, mines, others)

    start_theirs = exchange(tie(start_mine, mines[0]), "rows", 1)

    waiting, results = [], None
    for c, (a, b) in enumerate(sums):
        b = tie(b, new_x, results)
        piece = (a.astype(F32) + b.astype(F32)).astype(BF16)
        source, offset = places[c]
        back = exchange(piece, "rows", 1)
        ready = waiting + [(True, begins[c], 0, start_mine, mines[c], piece)]
        results = final(side, scale, x0, dual, z, ready, results, blocks_count)
        waiting = [(False, begins[c], offset, start_theirs, others[source], back)]
    results = final(side, scale, x0, dual, z, waiting, results, blocks_count)
    new_z, new_u = results
    return (new_x[None], new_z, new_u[None])


def solution(mesh):
    in_specs = (
        P("rows", "feat"),
        P(None, "rows"),
        P("rows", None, "feat"),
        P("rows", None, "feat"),
        P(None, "feat"),
        P(),
        P(),
        P(),
    )
    out_specs = (P("rows", None, "feat"), P(None, "feat"), P("rows", None, "feat"))
    return jax.shard_map(
        per_device, mesh=mesh, in_specs=in_specs, out_specs=out_specs, check_vma=False
    )
```

time: 70.7 us -> 67.6 us (0.956)
  Pallas kernels: 29.3 us -> 25.7 us
    pallas_call x11 -> x6, Pallas kernels: 24.6 us -> 19.4 us  [the longest x1 7.2 us: turn(): call(turn_kernel, 'turn', [VMEM] * (6 + len(terms)), (pltpu.VMEM((tasks,...]
    pallas_call x5, Pallas kernels: 1.36 us -> 2.9 us  [push(): call(functools.partial(push_kernel, first, mine, begin, offset, size), 'p...]
    ppermute x23 -> x18, waiting for transfers between devices: 16.9 us -> 17.6 us  [exchange(): return lax.ppermute(value, axis, [(i, i ^ mask) for i in range(n)])]
    ppermute x23 -> x18, starting transfers between devices: 22.9 us -> 22.8 us  [exchange(): return lax.ppermute(value, axis, [(i, i ^ mask) for i in range(n)])]
  transfers between devices with their start and end apart: 23 -> 18, of which waited for: 11 -> 10; matrix products, arithmetic and copies ran while one was open for 1% -> 1% of each run, Pallas kernels for 30% -> 26%
where the time goes in v7:
time: 67.6 us; the launch traced here: 67.4 us
  Pallas kernels  25.7 us (38%)
  starting transfers between devices  22.8 us (34%)
  waiting for transfers between devices  17.6 us (26%)
  between operations  0.81 us (1%)
    ppermute x18, starting transfers between devices, exchange(): return lax.ppermute(value, axis, [(i, i ^ mask) for i in range(n)])  22.8 us
    ppermute x18, waiting for transfers between devices, exchange(): return lax.ppermute(value, axis, [(i, i ^ mask) for i in range(n)])  17.6 us
    pallas_call x1, Pallas kernels, turn(): call(turn_kernel, 'turn', [VMEM] * (6 + len(terms)), (pltpu.VMEM((tasks,...  7.2 us
    pallas_call x1, Pallas kernels, load(): call(load_kernel, 'load_and_margins', [SMEM] + [HBM] * 3, (pltpu.VMEM((ta...  6.75 us
    pallas_call x4, Pallas kernels, final(): call(functools.partial(final_kernel, blocks_count, places, buffered), 'fi...  5.47 us
    pallas_call x5, Pallas kernels, push(): call(functools.partial(push_kernel, first, mine, begin, offset, size), 'p...  2.9 us
    pallas_call x1, Pallas kernels, load_rest(): call(functools.partial(rest_kernel, blocks_count), 'load_rest', [HBM] * 5...  1.68 us
    pallas_call x1, Pallas kernels, store_x(): call(store_kernel, 'store_x', [SMEM] + [VMEM] * len(args), pltpu.HBM((tas...  1.68 us
  transfers between devices with their start and end apart: 18, of which 10 were waited for; matrix products, arithmetic and copies ran while one was open for 1% of the time, Pallas kernels for 26%

profile of v7, /device:TPU:0, one launch (start us, length us, event | category | flops | bytes accessed | tf_op | source)
XLA Modules:
  0.0 67.4 jit_solution(5546280690012697008)
XLA Ops:
  0.6 6.8 %load_and_margins.1 = (bf16[64,768]{1,0:T(8,128)(2,1)S(1)}, bf16[768,8192]{1,0:T(8,128)(2,1)S(1)}, f32[64,8192]{1,0:T(8,128)S(1)}, f32[64,8192]{1,0:T(8,128)S(1)...) custom-call(s32[1]{0:T(128)} %bitcast.side, f32[64,8192]{1,0:T(8,128)} %bitcast.9, f32[64,8192]{1,0:T(8,128)} %bitcast.10, ...), custom_call_target="tpu_custom_call" | custom-call | flops 1000 | bytes 1000 | tf_op jit(solution)/shard_map/load_and_margins/pallas_call | solution.py:130
  7.9 2.6 %collective-permute-start = (bf16[64,768]{1,0:T(8,128)(2,1)S(1)}, bf16[64,768]{1,0:T(8,128)(2,1)S(1)}, u32[]{:S(2)}, u32[]{:S(2)}) collective-permute-start(bf16[64,768]{1,0:T(8,128)(2,1)S(1)} %get-tuple-element.45), channel_id=1, source_target_pairs={{0,1},{1,0},{2,3},{3,2},{4,5},{5,4},{6,7},{7,6},{8,9},{9,8},{10,11... | collective-permute-start | bytes 294920 | tf_op jit(solution)/shard_map/ppermute | solution.py:27
  10.6 2.6 %collective-permute-start.8 = (f32[64,4096]{1,0:T(8,128)S(1)}, f32[64,4096]{1,0:T(8,128)S(1)}, u32[]{:S(2)}, u32[]{:S(2)}) collective-permute-start(f32[64,4096]{1,0:T(8,128)S(1)} %add.32), channel_id=1, source_target_pairs={{0,16},{8,24},{16,0},{24,8},{1,17},{9,25},{17,1},{25,9},{2,18},{10... | collective-permute-start | bytes 3145736 | tf_op jit(solution)/shard_map/ppermute | solution.py:27
  13.9 1.9 %collective-permute-start.1 = (bf16[64,768]{1,0:T(8,128)(2,1)S(1)}, bf16[64,768]{1,0:T(8,128)(2,1)S(1)}, u32[]{:S(2)}, u32[]{:S(2)}) collective-permute-start(bf16[64,768]{1,0:T(8,128)(2,1)S(1)} %add_convert_fusion.5), channel_id=1, source_target_pairs={{0,2},{1,3},{2,0},{3,1},{4,6},{5,7},{6,4},{7,5},{8,10},{9,11},{10,... | collective-permute-start | bytes 294920 | tf_op jit(solution)/shard_map/ppermute | solution.py:27
  15.8 2.8 %collective-permute-done.1 = bf16[64,768]{1,0:T(8,128)(2,1)S(1)} collective-permute-done((bf16[64,768]{1,0:T(8,128)(2,1)S(1)}, bf16[64,768]{1,0:T(8,128)(2,1)S(1)}, u32[]{:S(2)}, u32[]{:S(2)}) %collective-permute-start.1) | collective-permute-done | bytes 98336 | tf_op jit(solution)/shard_map/ppermute | solution.py:27
  18.6 2.9 %collective-permute-start.2 = (bf16[64,768]{1,0:T(8,128)(2,1)S(1)}, bf16[64,768]{1,0:T(8,128)(2,1)S(1)}, u32[]{:S(2)}, u32[]{:S(2)}) collective-permute-start(bf16[64,768]{1,0:T(8,128)(2,1)S(1)} %add_convert_fusion.4.refs_0_), channel_id=1, source_target_pairs={{0,4},{1,5},{2,6},{3,7},{4,0},{5,1},{6,2},{7,3},{8,12},{9,13},{10,... | collective-permute-start | bytes 294920 | tf_op jit(solution)/shard_map/ppermute | solution.py:27
  21.5 1.7 %load_rest.1 = (f32[64,8192]{1,0:T(8,128)S(1)}, s32[64,768]{1,0:T(8,128)S(1)}, f32[64,128]{1,0:T(8,128)S(1)}) custom-call(f32[64,8192]{1,0:T(8,128)} %z_hbm.1, s32[64,768]{1,0:T(8,128)} %sign_hbm.1, f32[1,64]{1,0:T(1,128)} %bitcast.12, f32[1,64]{1,0:T(1,128)} %bitcast.13, f32[1,64]{1,0:T(1,128)} %bitcast.14), custom_call_target="tpu_custom_call" | custom-call | flops 1000 | bytes 1000 | tf_op jit(solution)/shard_map/load_rest/pallas_call | solution.py:161
  23.2 1.1 %collective-permute-done.2.refs_1_ = bf16[64,768]{1,0:T(8,128)(2,1)S(1)} collective-permute-done((bf16[64,768]{1,0:T(8,128)(2,1)S(1)}, bf16[64,768]{1,0:T(8,128)(2,1)S(1)}, u32[]{:S(2)}, u32[]{:S(2)}) %collective-permute-start.2) | collective-permute-done | bytes 98336 | tf_op jit(solution)/shard_map/ppermute | solution.py:27
  24.4 7.2 %turn.1 = (f32[64,8192]{1,0:T(8,128)S(1)}, bf16[64,768]{1,0:T(8,128)(2,1)S(1)}) custom-call(s32[64,768]{1,0:T(8,128)S(1)} %get-tuple-element.51.sign.refs_3_, f32[64,128]{1,0:T(8,128)S(1)} %get-tuple-element.47.scale.refs_0_, f32[64,8192]{1,0:T(8,128)S(1)} %get-tuple-element.48.x_ref, f32[64,8192]{1,0:T(8,128)S(1)} %get-tuple-element.49.u_ref, ...), custom_call_target="tpu_custom_call" | custom-call | flops 1000 | bytes 150000000 | tf_op jit(solution)/shard_map/turn/pallas_call | solution.py:202
  31.6 2.8 %collective-permute-start.6 = (bf16[64,768]{1,0:T(8,128)(2,1)S(1)}, bf16[64,768]{1,0:T(8,128)(2,1)S(1)}, u32[]{:S(2)}, u32[]{:S(2)}) collective-permute-start(bf16[64,768]{1,0:T(8,128)(2,1)S(1)} %get-tuple-element.58), channel_id=1, source_target_pairs={{0,3},{1,2},{2,1},{3,0},{4,7},{5,6},{6,5},{7,4},{8,11},{9,10},{10,... | collective-permute-start | bytes 294920 | tf_op jit(solution)/shard_map/ppermute | solution.py:27
  35.1 2.0 %collective-permute-done.6 = bf16[64,768]{1,0:T(8,128)(2,1)S(1)} collective-permute-done((bf16[64,768]{1,0:T(8,128)(2,1)S(1)}, bf16[64,768]{1,0:T(8,128)(2,1)S(1)}, u32[]{:S(2)}, u32[]{:S(2)}) %collective-permute-start.6) | collective-permute-done | bytes 98336 | tf_op jit(solution)/shard_map/ppermute | solution.py:27
  37.1 1.9 %collective-permute-done.5 = bf16[64,768]{1,0:T(8,128)(2,1)S(1)} collective-permute-done((bf16[64,768]{1,0:T(8,128)(2,1)S(1)}, bf16[64,768]{1,0:T(8,128)(2,1)S(1)}, u32[]{:S(2)}, u32[]{:S(2)}) %collective-permute-start.5) | collective-permute-done | bytes 98336 | tf_op jit(solution)/shard_map/ppermute | solution.py:27
  39.4 3.9 %collective-permute-start.7 = (bf16[64,768]{1,0:T(8,128)(2,1)S(1)}, bf16[64,768]{1,0:T(8,128)(2,1)S(1)}, u32[]{:S(2)}, u32[]{:S(2)}) collective-permute-start(bf16[64,768]{1,0:T(8,128)(2,1)S(1)} %add_convert_fusion.3.refs_4_), channel_id=1, source_target_pairs={{0,4},{1,5},{2,6},{3,7},{4,0},{5,1},{6,2},{7,3},{8,12},{9,13},{10,... | collective-permute-start | bytes 294920 | tf_op jit(solution)/shard_map/ppermute | solution.py:27
  43.4 3.5 %collective-permute-done.7.refs_5_ = bf16[64,768]{1,0:T(8,128)(2,1)S(1)} collective-permute-done((bf16[64,768]{1,0:T(8,128)(2,1)S(1)}, bf16[64,768]{1,0:T(8,128)(2,1)S(1)}, u32[]{:S(2)}, u32[]{:S(2)}) %collective-permute-start.7) | collective-permute-done | bytes 98336 | tf_op jit(solution)/shard_map/ppermute | solution.py:27
  49.5 1.5 %collective-permute-start.13 = (bf16[64,1024]{1,0:T(8,128)(2,1)S(1)}, bf16[64,1024]{1,0:T(8,128)(2,1)S(1)}, u32[]{:S(2)}, u32[]{:S(2)}) collective-permute-start(bf16[64,1024]{1,0:T(8,128)(2,1)S(1)} %get-tuple-element.66), channel_id=1, source_target_pairs={{0,16},{8,24},{16,0},{24,8},{1,17},{9,25},{17,1},{25,9},{2,18},{10... | collective-permute-start | bytes 393224 | tf_op jit(solution)/shard_map/ppermute | solution.py:27
  53.0 1.7 %store_x.1 = f32[64,8192]{1,0:T(8,128)} custom-call(s32[1]{0:T(128)} %bitcast.side, f32[64,128]{1,0:T(8,128)S(1)} %get-tuple-element.47.scale.refs_0_, f32[64,8192]{1,0:T(8,128)S(1)} %get-tuple-element.48.x_ref, f32[64,8192]{1,0:T(8,128)S(1)} %get-tuple-element.49.u_ref, f32[64,8192]{1,0:T(8,128)S(1)} %get-tuple-element.50.z_ref, ...), custom_call_target="tpu_custom_call" | custom-call | flops 1000 | bytes 1000 | tf_op jit(solution)/shard_map/store_x/pallas_call | solution.py:275
  54.7 1.1 %collective-permute-done.13 = bf16[64,1024]{1,0:T(8,128)(2,1)S(1)} collective-permute-done((bf16[64,1024]{1,0:T(8,128)(2,1)S(1)}, bf16[64,1024]{1,0:T(8,128)(2,1)S(1)}, u32[]{:S(2)}, u32[]{:S(2)}) %collective-permute-start.13) | collective-permute-done | bytes 131104 | tf_op jit(solution)/shard_map/ppermute | solution.py:27
  55.9 1.0 %final.4 = (f32[64,8192]{1,0:T(8,128)}, f32[64,8192]{1,0:T(8,128)}) custom-call(s32[1]{0:T(128)} %bitcast.side, f32[64,128]{1,0:T(8,128)S(1)} %get-tuple-element.47.scale.refs_0_, f32[64,8192]{1,0:T(8,128)S(1)} %get-tuple-element.48.x_ref, f32[64,8192]{1,0:T(8,128)S(1)} %get-tuple-element.49.u_ref, f32[64,8192]{1,0:T(8,128)S(1)} %get-tuple-element.50.z_ref, ...), custom_call_target="tpu_custom_call" | custom-call | flops 1000 | bytes 1000 | tf_op jit(solution)/shard_map/final/pallas_call | solution.py:325
  57.0 1.6 %collective-permute-start.12 = (bf16[64,1536]{1,0:T(8,128)(2,1)S(1)}, bf16[64,1536]{1,0:T(8,128)(2,1)S(1)}, u32[]{:S(2)}, u32[]{:S(2)}) collective-permute-start(bf16[64,1536]{1,0:T(8,128)(2,1)S(1)} %get-tuple-element.75), channel_id=1, source_target_pairs={{0,16},{8,24},{16,0},{24,8},{1,17},{9,25},{17,1},{25,9},{2,18},{10... | collective-permute-start | bytes 589832 | tf_op jit(solution)/shard_map/ppermute | solution.py:27
  58.5 1.1 %collective-permute-done.15 = bf16[64,1536]{1,0:T(8,128)(2,1)S(1)} collective-permute-done((bf16[64,1536]{1,0:T(8,128)(2,1)S(1)}, bf16[64,1536]{1,0:T(8,128)(2,1)S(1)}, u32[]{:S(2)}, u32[]{:S(2)}) %collective-permute-start.15) | collective-permute-done | bytes 196640 | tf_op jit(solution)/shard_map/ppermute | solution.py:27
  59.7 1.5 %final.5 = (f32[64,8192]{1,0:T(8,128)}, f32[64,8192]{1,0:T(8,128)}) custom-call(s32[1]{0:T(128)} %bitcast.side, f32[64,128]{1,0:T(8,128)S(1)} %get-tuple-element.47.scale.refs_0_, f32[64,8192]{1,0:T(8,128)S(1)} %get-tuple-element.48.x_ref, f32[64,8192]{1,0:T(8,128)S(1)} %get-tuple-element.49.u_ref, ...), custom_call_target="tpu_custom_call", output_to_operand_aliasing={{0}: (11, {}), {1}: (12, {})} | custom-call | flops 1000 | bytes 1000 | tf_op jit(solution)/shard_map/final/pallas_call | solution.py:325
  61.3 3.1 %collective-permute-done.12 = bf16[64,1536]{1,0:T(8,128)(2,1)S(1)} collective-permute-done((bf16[64,1536]{1,0:T(8,128)(2,1)S(1)}, bf16[64,1536]{1,0:T(8,128)(2,1)S(1)}, u32[]{:S(2)}, u32[]{:S(2)}) %collective-permute-start.12) | collective-permute-done | bytes 196640 | tf_op jit(solution)/shard_map/ppermute | solution.py:27
  64.5 1.7 %final.6 = (f32[64,8192]{1,0:T(8,128)}, f32[64,8192]{1,0:T(8,128)}) custom-call(s32[1]{0:T(128)} %bitcast.side, f32[64,128]{1,0:T(8,128)S(1)} %get-tuple-element.47.scale.refs_0_, f32[64,8192]{1,0:T(8,128)S(1)} %get-tuple-element.48.x_ref, f32[64,8192]{1,0:T(8,128)S(1)} %get-tuple-element.49.u_ref, ...), custom_call_target="tpu_custom_call", output_to_operand_aliasing={{0}: (11, {}), {1}: (12, {})} | custom-call | flops 1000 | bytes 1000 | tf_op jit(solution)/shard_map/final/pallas_call | solution.py:325
  66.2 1.2 %final.7 = (f32[64,8192]{1,0:T(8,128)}, f32[64,8192]{1,0:T(8,128)}) custom-call(s32[1]{0:T(128)} %bitcast.side, f32[64,128]{1,0:T(8,128)S(1)} %get-tuple-element.47.scale.refs_0_, f32[64,8192]{1,0:T(8,128)S(1)} %get-tuple-element.48.x_ref, f32[64,8192]{1,0:T(8,128)S(1)} %get-tuple-element.49.u_ref, ...), custom_call_target="tpu_custom_call", output_to_operand_aliasing={{0}: (8, {}), {1}: (9, {})} | custom-call | flops 1000 | bytes 1000 | tf_op jit(solution)/shard_map/final/pallas_call | solution.py:325
  (33 shorter events, 7.4 us)
Async XLA Ops:
  7.4 3.1 %collective-permute-start.3 = (f32[64,4096]{1,0:T(8,128)S(1)}, f32[64,4096]{1,0:T(8,128)S(1)}, u32[]{:S(2)}, u32[]{:S(2)}) collective-permute-start(f32[64,4096]{1,0:T(8,128)S(1)} %get-tuple-element.54), channel_id=1, source_target_pairs={{0,8},{8,0},{16,24},{24,16},{1,9},{9,1},{17,25},{25,17},{2,10},{10... | collective-permute-start | bytes 3145736 | tf_op jit(solution)/shard_map/ppermute | solution.py:27
  7.9 6.0 %collective-permute-start = (bf16[64,768]{1,0:T(8,128)(2,1)S(1)}, bf16[64,768]{1,0:T(8,128)(2,1)S(1)}, u32[]{:S(2)}, u32[]{:S(2)}) collective-permute-start(bf16[64,768]{1,0:T(8,128)(2,1)S(1)} %get-tuple-element.45), channel_id=1, source_target_pairs={{0,1},{1,0},{2,3},{3,2},{4,5},{5,4},{6,7},{7,6},{8,9},{9,8},{10,11... | collective-permute-start | bytes 294920 | tf_op jit(solution)/shard_map/ppermute | solution.py:27
  10.6 32.7 %collective-permute-start.8 = (f32[64,4096]{1,0:T(8,128)S(1)}, f32[64,4096]{1,0:T(8,128)S(1)}, u32[]{:S(2)}, u32[]{:S(2)}) collective-permute-start(f32[64,4096]{1,0:T(8,128)S(1)} %add.32), channel_id=1, source_target_pairs={{0,16},{8,24},{16,0},{24,8},{1,17},{9,25},{17,1},{25,9},{2,18},{10... | collective-permute-start | bytes 3145736 | tf_op jit(solution)/shard_map/ppermute | solution.py:27
  13.9 4.7 %collective-permute-start.1 = (bf16[64,768]{1,0:T(8,128)(2,1)S(1)}, bf16[64,768]{1,0:T(8,128)(2,1)S(1)}, u32[]{:S(2)}, u32[]{:S(2)}) collective-permute-start(bf16[64,768]{1,0:T(8,128)(2,1)S(1)} %add_convert_fusion.5), channel_id=1, source_target_pairs={{0,2},{1,3},{2,0},{3,1},{4,6},{5,7},{6,4},{7,5},{8,10},{9,11},{10,... | collective-permute-start | bytes 294920 | tf_op jit(solution)/shard_map/ppermute | solution.py:27
  18.6 5.7 %collective-permute-start.2 = (bf16[64,768]{1,0:T(8,128)(2,1)S(1)}, bf16[64,768]{1,0:T(8,128)(2,1)S(1)}, u32[]{:S(2)}, u32[]{:S(2)}) collective-permute-start(bf16[64,768]{1,0:T(8,128)(2,1)S(1)} %add_convert_fusion.4.refs_0_), channel_id=1, source_target_pairs={{0,4},{1,5},{2,6},{3,7},{4,0},{5,1},{6,2},{7,3},{8,12},{9,13},{10,... | collective-permute-start | bytes 294920 | tf_op jit(solution)/shard_map/ppermute | solution.py:27
  31.6 5.6 %collective-permute-start.6 = (bf16[64,768]{1,0:T(8,128)(2,1)S(1)}, bf16[64,768]{1,0:T(8,128)(2,1)S(1)}, u32[]{:S(2)}, u32[]{:S(2)}) collective-permute-start(bf16[64,768]{1,0:T(8,128)(2,1)S(1)} %get-tuple-element.58), channel_id=1, source_target_pairs={{0,3},{1,2},{2,1},{3,0},{4,7},{5,6},{6,5},{7,4},{8,11},{9,10},{10,... | collective-permute-start | bytes 294920 | tf_op jit(solution)/shard_map/ppermute | solution.py:27
  34.4 4.6 %collective-permute-start.5 = (bf16[64,768]{1,0:T(8,128)(2,1)S(1)}, bf16[64,768]{1,0:T(8,128)(2,1)S(1)}, u32[]{:S(2)}, u32[]{:S(2)}) collective-permute-start(bf16[64,768]{1,0:T(8,128)(2,1)S(1)} %get-tuple-element.58), channel_id=1, source_target_pairs={{0,2},{1,3},{2,0},{3,1},{4,6},{5,7},{6,4},{7,5},{8,10},{9,11},{10,... | collective-permute-start | bytes 294920 | tf_op jit(solution)/shard_map/ppermute | solution.py:27
  34.7 4.6 %collective-permute-start.4 = (bf16[64,768]{1,0:T(8,128)(2,1)S(1)}, bf16[64,768]{1,0:T(8,128)(2,1)S(1)}, u32[]{:S(2)}, u32[]{:S(2)}) collective-permute-start(bf16[64,768]{1,0:T(8,128)(2,1)S(1)} %get-tuple-element.58), channel_id=1, source_target_pairs={{0,1},{1,0},{2,3},{3,2},{4,5},{5,4},{6,7},{7,6},{8,9},{9,8},{10,11... | collective-permute-start | bytes 294920 | tf_op jit(solution)/shard_map/ppermute | solution.py:27
  39.4 7.5 %collective-permute-start.7 = (bf16[64,768]{1,0:T(8,128)(2,1)S(1)}, bf16[64,768]{1,0:T(8,128)(2,1)S(1)}, u32[]{:S(2)}, u32[]{:S(2)}) collective-permute-start(bf16[64,768]{1,0:T(8,128)(2,1)S(1)} %add_convert_fusion.3.refs_4_), channel_id=1, source_target_pairs={{0,4},{1,5},{2,6},{3,7},{4,0},{5,1},{6,2},{7,3},{8,12},{9,13},{10,... | collective-permute-start | bytes 294920 | tf_op jit(solution)/shard_map/ppermute | solution.py:27
  47.4 1.6 %collective-permute-start.9 = (bf16[64,1024]{1,0:T(8,128)(2,1)S(1)}, bf16[64,1024]{1,0:T(8,128)(2,1)S(1)}, u32[]{:S(2)}, u32[]{:S(2)}) collective-permute-start(bf16[64,1024]{1,0:T(8,128)(2,1)S(1)} %get-tuple-element.64), channel_id=1, source_target_pairs={{0,8},{8,0},{16,24},{24,16},{1,9},{9,1},{17,25},{25,17},{2,10},{10... | collective-permute-start | bytes 393224 | tf_op jit(solution)/shard_map/ppermute | solution.py:27
  48.4 2.6 %collective-permute-start.10 = (bf16[64,3072]{1,0:T(8,128)(2,1)S(1)}, bf16[64,3072]{1,0:T(8,128)(2,1)S(1)}, u32[]{:S(2)}, u32[]{:S(2)}) collective-permute-start(bf16[64,3072]{1,0:T(8,128)(2,1)S(1)} %get-tuple-element.68), channel_id=1, source_target_pairs={{0,8},{8,0},{16,24},{24,16},{1,9},{9,1},{17,25},{25,17},{2,10},{10... | collective-permute-start | bytes 1179656 | tf_op jit(solution)/shard_map/ppermute | solution.py:27
  49.4 10.3 %collective-permute-start.11 = (f32[64,4096]{1,0:T(8,128)S(1)}, f32[64,4096]{1,0:T(8,128)S(1)}, u32[]{:S(2)}, u32[]{:S(2)}) collective-permute-start(f32[64,4096]{1,0:T(8,128)S(1)} %add.36.refs_0_.refs_3_), channel_id=1, source_target_pairs={{0,8},{8,0},{16,24},{24,16},{1,9},{9,1},{17,25},{25,17},{2,10},{10... | collective-permute-start | bytes 3145736 | tf_op jit(solution)/shard_map/ppermute | solution.py:27
  49.5 6.3 %collective-permute-start.13 = (bf16[64,1024]{1,0:T(8,128)(2,1)S(1)}, bf16[64,1024]{1,0:T(8,128)(2,1)S(1)}, u32[]{:S(2)}, u32[]{:S(2)}) collective-permute-start(bf16[64,1024]{1,0:T(8,128)(2,1)S(1)} %get-tuple-element.66), channel_id=1, source_target_pairs={{0,16},{8,24},{16,0},{24,8},{1,17},{9,25},{17,1},{25,9},{2,18},{10... | collective-permute-start | bytes 393224 | tf_op jit(solution)/shard_map/ppermute | solution.py:27
  51.6 8.0 %collective-permute-start.15 = (bf16[64,1536]{1,0:T(8,128)(2,1)S(1)}, bf16[64,1536]{1,0:T(8,128)(2,1)S(1)}, u32[]{:S(2)}, u32[]{:S(2)}) collective-permute-start(bf16[64,1536]{1,0:T(8,128)(2,1)S(1)} %get-tuple-element.70), channel_id=1, source_target_pairs={{0,16},{8,24},{16,0},{24,8},{1,17},{9,25},{17,1},{25,9},{2,18},{10... | collective-permute-start | bytes 589832 | tf_op jit(solution)/shard_map/ppermute | solution.py:27
  55.8 3.9 %collective-permute-start.14 = (bf16[64,1024]{1,0:T(8,128)(2,1)S(1)}, bf16[64,1024]{1,0:T(8,128)(2,1)S(1)}, u32[]{:S(2)}, u32[]{:S(2)}) collective-permute-start(bf16[64,1024]{1,0:T(8,128)(2,1)S(1)} %add_convert_fusion.2.refs_2_), channel_id=1, source_target_pairs={{0,8},{8,0},{16,24},{24,16},{1,9},{9,1},{17,25},{25,17},{2,10},{10... | collective-permute-start | bytes 393224 | tf_op jit(solution)/shard_map/ppermute | solution.py:27
  57.0 7.4 %collective-permute-start.12 = (bf16[64,1536]{1,0:T(8,128)(2,1)S(1)}, bf16[64,1536]{1,0:T(8,128)(2,1)S(1)}, u32[]{:S(2)}, u32[]{:S(2)}) collective-permute-start(bf16[64,1536]{1,0:T(8,128)(2,1)S(1)} %get-tuple-element.75), channel_id=1, source_target_pairs={{0,16},{8,24},{16,0},{24,8},{1,17},{9,25},{17,1},{25,9},{2,18},{10... | collective-permute-start | bytes 589832 | tf_op jit(solution)/shard_map/ppermute | solution.py:27
  59.6 4.8 %collective-permute-start.17 = (bf16[64,1536]{1,0:T(8,128)(2,1)S(1)}, bf16[64,1536]{1,0:T(8,128)(2,1)S(1)}, u32[]{:S(2)}, u32[]{:S(2)}) collective-permute-start(bf16[64,1536]{1,0:T(8,128)(2,1)S(1)} %add_convert_fusion.1.refs_5_), channel_id=1, source_target_pairs={{0,8},{8,0},{16,24},{24,16},{1,9},{9,1},{17,25},{25,17},{2,10},{10... | collective-permute-start | bytes 589832 | tf_op jit(solution)/shard_map/ppermute | solution.py:27
  64.4 1.8 %collective-permute-start.16 = (bf16[64,1536]{1,0:T(8,128)(2,1)S(1)}, bf16[64,1536]{1,0:T(8,128)(2,1)S(1)}, u32[]{:S(2)}, u32[]{:S(2)}) collective-permute-start(bf16[64,1536]{1,0:T(8,128)(2,1)S(1)} %add_convert_fusion.refs_5_), channel_id=1, source_target_pairs={{0,8},{8,0},{16,24},{24,16},{1,9},{9,1},{17,25},{25,17},{2,10},{10... | collective-permute-start | bytes 589832 | tf_op jit(solution)/shard_map/ppermute | solution.py:27

commit v8 on v7

--- a/solution.py
+++ b/solution.py
@@ -16,7 +16,7 @@
 WIDE = 2048
 AHEAD = 4
 NARROW = 256
-TURN_BYTES = 150_000_000
+WAIT_BYTES = 10_000_000
 HBM = pl.BlockSpec(memory_space=pltpu.HBM)
 VMEM = pl.BlockSpec(memory_space=pltpu.VMEM)
 SMEM = pl.BlockSpec(memory_space=pltpu.SMEM)
@@ -137,12 +137,27 @@
     )(side, *pin(pltpu.HBM, x, u, design))
 
 
-def rest_kernel(blocks_count, z_hbm, sign_hbm, eta_hbm, rho_hbm, lam_hbm, *refs):
-    z_out, sign_out, scale_out, eta_row, rho_row, lam_row, sems = refs
+def gram_block(a_ref, row, cols, size, acc, high, low):
+    width = a_ref.shape[1]
+    wide = math.gcd(WIDE, width)
+    for j in range(width // wide):
+        at = pl.ds(j * wide, wide)
+        product = nt(a_ref[pl.ds(row, size), at], a_ref[pl.ds(0, cols), at])
+        acc[:, :cols] = product if j == 0 else acc[:, :cols] + product
+    whole = acc[:, :cols]
+    top = whole.astype(BF16)
+    high[...] = top
+    low[...] = (whole - top.astype(F32)).astype(BF16)
+
+
+def rest_kernel(blocks_count, a_ref, z_hbm, sign_hbm, eta_hbm, rho_hbm, lam_hbm, *refs):
+    z_out, sign_out, scale_out, high, low, eta_row, rho_row, lam_row, acc, sems = refs
     pairs = ((eta_hbm, eta_row), (rho_hbm, rho_row), (lam_hbm, lam_row), (z_hbm, z_out), (sign_hbm, sign_out))
     copies = [pltpu.make_async_copy(a, b, sems.at[k]) for k, (a, b) in enumerate(pairs)]
     for copy in copies:
         copy.start()
+    size, cols = high.shape
+    gram_block(a_ref, cols - size, cols, size, acc, high, low)
     for copy in copies[:3]:
         copy.wait()
     tasks = z_out.shape[0]
@@ -155,17 +170,78 @@
         copy.wait()
 
 
-def load_rest(z, sign, step_size, rho, penalty, blocks_count):
+def gram_shapes(samples, row):
+    size = samples // 3
+    return [pltpu.VMEM((size, (row + 1) * size), BF16)] * 2
+
+
+def load_rest(z, sign, step_size, rho, penalty, design, blocks_count):
     tasks, width = z.shape
+    samples = design.shape[0]
     rows = [v.reshape(1, tasks) for v in (step_size, rho, penalty)]
     return call(
         functools.partial(rest_kernel, blocks_count),
-        "load_rest",
-        [HBM] * 5,
-        (pltpu.VMEM((tasks, width), F32), pltpu.VMEM(sign.shape, jnp.int32), pltpu.VMEM((tasks, 128), F32)),
-        [VMEM] * 3,
-        [pltpu.VMEM((1, tasks), F32)] * 3 + [pltpu.SemaphoreType.DMA((5,))],
-    )(*pin(pltpu.HBM, z, sign, *rows))
+        "load_and_gram",
+        [VMEM] + [HBM] * 5,
+        (
+            pltpu.VMEM((tasks, width), F32), pltpu.VMEM(sign.shape, jnp.int32), pltpu.VMEM((tasks, 128), F32),
+            *gram_shapes(samples, 2),
+        ),
+        [VMEM] * 5,
+        [pltpu.VMEM((1, tasks), F32)] * 3 + [pltpu.VMEM((samples // 3, samples), F32), pltpu.SemaphoreType.DMA((5,))],
+        work=WAIT_BYTES,
+    )(*pin(pltpu.VMEM, design), *pin(pltpu.HBM, z, sign, *rows))
+
+
+def gram_kernel(token, a_ref, *refs):
+    *outs, acc = refs
+    size = outs[0].shape[0]
+    for row in range(2):
+        gram_block(a_ref, row * size, (row + 1) * size, size, acc, outs[2 * row], outs[2 * row + 1])
+
+
+def gram_rows(token, design):
+    samples = design.shape[0]
+    return call(
+        gram_kernel,
+        "gram",
+        [SMEM, VMEM],
+        (*gram_shapes(samples, 0), *gram_shapes(samples, 1)),
+        [VMEM] * 4,
+        [pltpu.VMEM((samples // 3, samples), F32)],
+        work=WAIT_BYTES,
+    )(token, *pin(pltpu.VMEM, design))
+
+
+def pulled_kernel(token, scale, x_ref, u_ref, z_ref, a_ref, out, both, acc):
+    pull = scale[:, 1:2]
+    tasks, width = x_ref.shape
+    wide = math.gcd(WIDE, width)
+    for j in range(width // wide):
+        for k in range(0, wide, 512):
+            at, here = pl.ds(j * wide + k, 512), pl.ds(k, 512)
+            x = x_ref[:, at]
+            v = x - pull * (x - z_ref[:, at] + u_ref[:, at])
+            top = v.astype(BF16)
+            both[:tasks, here] = top
+            both[tasks:, here] = (v - top.astype(F32)).astype(BF16)
+        product = nt(both[...], a_ref[:, pl.ds(j * wide, wide)])
+        acc[...] = product if j == 0 else acc[...] + product
+    out[...] = acc[:tasks] + acc[tasks:]
+
+
+def pulled_margins(token, scale, x, u, z, design):
+    tasks, width = x.shape
+    samples = design.shape[0]
+    return call(
+        pulled_kernel,
+        "pulled_margins",
+        [SMEM] + [VMEM] * 5,
+        pltpu.VMEM((tasks, samples), F32),
+        VMEM,
+        [pltpu.VMEM((2 * tasks, math.gcd(WIDE, width)), BF16), pltpu.VMEM((2 * tasks, samples), F32)],
+        work=WAIT_BYTES,
+    )(token, *pin(pltpu.VMEM, scale, x, u, z, design))
 
 
 def residual(sign, *terms):
@@ -174,70 +250,65 @@
     return (sign * jax.nn.sigmoid(-sign * margin)).astype(BF16)
 
 
-def turn_kernel(sign, scale, x_ref, u_ref, z_ref, a_ref, *refs):
-    *terms, q_out, m_out, resid, new_x, acc = refs
+def turn_kernel(sign, scale, pulled, *refs):
+    *terms, resid, out = refs[6:]
+    grams = refs[:6]
+    size = grams[0].shape[0]
     resid[...] = residual(sign[...], *(t[...] for t in terms))
-    eta, pull = scale[:, 0:1], scale[:, 1:2]
-    width = x_ref.shape[1]
-
-    @pl.loop(0, width // STEP)
-    def _(j):
-        at = columns(j * STEP, STEP)
-        push = eta * jnp.dot(resid[...], a_ref[:, at], preferred_element_type=F32)
-        x = x_ref[:, at]
-        new_x[:, at] = (x - pull * (x - z_ref[:, at] + u_ref[:, at]) + push).astype(BF16)
-        q_out[:, at] = (1.0 - pull) * push
-
-    wide = math.gcd(WIDE, width)
-    for j in range(width // wide):
-        at = pl.ds(j * wide, wide)
-        product = nt(new_x[:, at], a_ref[:, at])
-        acc[...] = product if j == 0 else acc[...] + product
-    m_out[...] = acc[...].astype(BF16)
-
-
-def turn(sign, terms, scale, x, u, z, design):
-    tasks, width = x.shape
-    samples = design.shape[0]
-    return call(
-        turn_kernel,
-        "turn",
-        [VMEM] * (6 + len(terms)),
-        (pltpu.VMEM((tasks, width), F32), pltpu.VMEM((tasks, samples), BF16)),
-        [VMEM] * 2,
-        [pltpu.VMEM((tasks, samples), BF16), pltpu.VMEM((tasks, width), BF16), pltpu.VMEM((tasks, samples), F32)],
-        work=TURN_BYTES,
-    )(*pin(pltpu.VMEM, sign, scale, x, u, z, design, *terms))
+    eta = scale[:, 0:1]
+    r = [resid[:, pl.ds(k * size, size)] for k in range(3)]
+    for col in range(3):
+        total = jnp.zeros((resid.shape[0], size), F32)
+        for row in range(3):
+            for part in range(2):
+                if row >= col:
+                    block = grams[2 * row + part][:, pl.ds(col * size, size)]
+                    total += jnp.dot(r[row], block, preferred_element_type=F32)
+                else:
+                    total += nt(r[row], grams[2 * col + part][:, pl.ds(row * size, size)])
+        here = pl.ds(col * size, size)
+        out[:, here] = (pulled[:, here] + eta * total).astype(BF16)
+
+
+def turn(sign, terms, scale, pulled, grams):
+    tasks, samples = pulled.shape
+    out = pltpu.VMEM((tasks, samples), BF16)
+    args = [sign, scale, pulled, *grams, *terms]
+    return call(turn_kernel, "turn", [VMEM] * len(args), (out, out), [VMEM] * 2)(*pin(pltpu.VMEM, *args))
 
 
 def push_kernel(first, mine, begin, offset, size, side, *refs):
+    tasks = refs[0].shape[0]
     if first:
-        scale, q_ref, a_ref, sign, *terms, h_out, sent_out, resid = refs
-        resid[...] = residual(sign[...], *(t[...] for t in terms))
+        scale, a_ref, resid1, sign, *terms, h_out, sent_out, resid = refs
+        resid[:tasks] = resid1[...]
+        resid[tasks:] = residual(sign[...], *(t[...] for t in terms))
     else:
-        scale, q_ref, a_ref, resid, *received, h_out, sent_out = refs
-    half = q_ref.shape[1] // 2
+        scale, a_ref, resid, *received, h_out, sent_out = refs
+    half = a_ref.shape[1] // 2
     eta = scale[:, 0:1]
+    keep = 1.0 - scale[:, 1:2]
     base = (side[0] if mine else 1 - side[0]) * half + begin
     step = math.gcd(512, size)
     for j in range(size // step):
         at = columns(base + j * step, step)
         here = pl.ds(j * step, step)
-        push = q_ref[:, at] + eta * jnp.dot(resid[...], a_ref[:, at], preferred_element_type=F32)
+        grads = jnp.dot(resid[...], a_ref[:, at], preferred_element_type=F32)
+        push = eta * (keep * grads[:tasks] + grads[tasks:])
         h_out[:, here] = push
         if mine:
             push = push + received[0][:, pl.ds(offset + j * step, step)].astype(F32)
         sent_out[:, here] = push.astype(BF16)
 
 
-def push(side, resid, scale, q, design, received, begin, offset, size):
-    tasks = q.shape[0]
+def push(side, resid, scale, design, received, begin, offset, size):
+    tasks = scale.shape[0]
     mine = received is not None
     first = isinstance(resid, tuple)
-    args = [scale, q, design, *(resid if first else [resid])] + ([received] if mine else [])
+    args = [scale, design, *(resid if first else [resid])] + ([received] if mine else [])
     out = [pltpu.VMEM((tasks, size), F32), pltpu.VMEM((tasks, size), BF16)]
     if first:
-        out.append(pltpu.VMEM((tasks, design.shape[0]), BF16))
+        out.append(pltpu.VMEM((2 * tasks, design.shape[0]), BF16))
     return call(
         functools.partial(push_kernel, first, mine, begin, offset, size),
         "push_mine" if mine else "push_other",
@@ -344,12 +415,30 @@
     side = (lax.axis_index("rows") & 1).astype(jnp.int32)[None]
 
     margin1, design, x0, dual, start_mine, start_other = load(side, local_x[0], dual_u[0], design)
-    terms = doubling(margin1, "feat")
     start_mine = start_mine + exchange(start_other, "rows", 1)
-    z, sign, scale = load_rest(consensus_z, labels, tie(step_size, terms[0]), rho, penalty, blocks_count)
+
+    z, sign, scale, *gram2 = load_rest(consensus_z, labels, step_size, rho, penalty, design, blocks_count)
+    terms, grams, pulled = [margin1], None, None
+    for step in range(lax.axis_size("feat").bit_length() - 1):
+        if step > 0:
+            terms = [sum(t.astype(F32) for t in terms).astype(BF16)]
+        token = tie(side, terms[0])
+        got = exchange(terms[0], "feat", 1 << step)
+        if step == 0:
+            got = tie(got, scale)
+        if step == 1:
+            grams = gram_rows(token, design)
+            got = tie(got, grams[0])
+        if step == 2:
+            pulled = pulled_margins(token, scale, x0, dual, z, design)
+        terms.append(got)
+    if grams is None:
+        grams = gram_rows(side, design)
+    if pulled is None:
+        pulled = pulled_margins(side, scale, x0, dual, z, design)
     terms = tie(terms, start_mine)
 
-    carried, margin2 = turn(sign, terms, scale, x0, dual, z, design)
+    resid1, margin2 = turn(sign, terms, scale, pulled, [*grams, *gram2])
     terms = square_sum(margin2, "feat")
     mask = 2
     while mask < blocks_count:
@@ -363,9 +452,9 @@
     other_begins = [sum(other_sizes[:c]) for c in range(len(other_sizes))]
     count = len(sizes)
     others, received = [], []
-    resid = (sign, *terms)
+    resid = (resid1, sign, *terms)
     for begin, size in zip(other_begins, other_sizes):
-        value, other, *made = push(side, resid, scale, carried, design, None, begin, 0, size)
+        value, other, *made = push(side, resid, scale, design, None, begin, 0, size)
         resid = made[0] if made else resid
         others.append(value)
         received.append(exchange(other, "rows", 1))
@@ -374,7 +463,7 @@
     for begin, size in zip(begins, sizes):
         source = max(k for k, b in enumerate(other_begins) if b <= begin)
         places.append((source, begin - other_begins[source]))
-        value, sent = push(token, resid, scale, carried, design, received[source], begin, places[-1][1], size)
+        value, sent = push(token, resid, scale, design, received[source], begin, places[-1][1], size)
         mines.append(value)
         sums.append(doubling(sent, "rows", 2))
         token = tie(side, sent)

time: 67.6 us -> 65.1 us (0.963)
  starting transfers between devices: 22.8 us -> 16.3 us
  Pallas kernels: 25.7 us -> 30.2 us
  waiting for transfers between devices: 17.6 us -> 16.9 us
    ppermute x18, starting transfers between devices: 22.8 us -> 16.3 us  [exchange(): return lax.ppermute(value, axis, [(i, i ^ mask) for i in range(n)])]
    pallas_call x2 -> x4, Pallas kernels: 8.88 us -> 13.3 us  [the longest x1 4.92 us: load_rest(): call(functools.partial(rest_kernel, blocks_count), 'load_and_gram', [VMEM...]
    ppermute x18, waiting for transfers between devices: 17.6 us -> 16.9 us  [exchange(): return lax.ppermute(value, axis, [(i, i ^ mask) for i in range(n)])]
  transfers between devices with their start and end apart: 18 -> 18, of which waited for: 10 -> 10; matrix products, arithmetic and copies ran while one was open for 1% -> 1% of each run, Pallas kernels for 26% -> 34%
where the time goes in v8:
time: 65.1 us; the launch traced here: 64.9 us
  Pallas kernels  30.2 us (46%)
  waiting for transfers between devices  16.9 us (26%)
  starting transfers between devices  16.3 us (25%)
  between operations  1.04 us (2%)
    ppermute x18, waiting for transfers between devices, exchange(): return lax.ppermute(value, axis, [(i, i ^ mask) for i in range(n)])  16.9 us
    ppermute x18, starting transfers between devices, exchange(): return lax.ppermute(value, axis, [(i, i ^ mask) for i in range(n)])  16.3 us
    pallas_call x1, Pallas kernels, load(): call(load_kernel, 'load_and_margins', [SMEM] + [HBM] * 3, (pltpu.VMEM((ta...  6.79 us
    pallas_call x4, Pallas kernels, final(): call(functools.partial(final_kernel, blocks_count, places, buffered), 'fi...  5.5 us
    pallas_call x1, Pallas kernels, load_rest(): call(functools.partial(rest_kernel, blocks_count), 'load_and_gram', [VMEM...  4.92 us
    pallas_call x1, Pallas kernels, pulled_margins(): call(pulled_kernel, 'pulled_margins', [SMEM] + [VMEM] * 5, pltpu.VMEM((ta...  4.32 us
    pallas_call x1, Pallas kernels, gram_rows(): call(gram_kernel, 'gram', [SMEM, VMEM], (*gram_shapes(samples, 0), *gram_...  3.45 us
    pallas_call x5, Pallas kernels, push(): call(functools.partial(push_kernel, first, mine, begin, offset, size), 'p...  2.92 us
  transfers between devices with their start and end apart: 18, of which 10 were waited for; matrix products, arithmetic and copies ran while one was open for 1% of the time, Pallas kernels for 34%

profile of v8, /device:TPU:0, one launch (start us, length us, event | category | flops | bytes accessed | tf_op | source)
XLA Modules:
  0.0 64.9 jit_solution(13346907161169900661)
XLA Ops:
  0.6 6.8 %load_and_margins.1 = (bf16[64,768]{1,0:T(8,128)(2,1)S(1)}, bf16[768,8192]{1,0:T(8,128)(2,1)S(1)}, f32[64,8192]{1,0:T(8,128)S(1)}, f32[64,8192]{1,0:T(8,128)S(1)...) custom-call(s32[1]{0:T(128)} %bitcast.side.token, f32[64,8192]{1,0:T(8,128)} %bitcast.9, f32[64,8192]{1,0:T(8,128)} %bitcast.10, ...), custom_call_target="tpu_custom_call" | custom-call | flops 1000 | bytes 1000 | tf_op jit(solution)/shard_map/load_and_margins/pallas_call | solution.py:130
  7.9 2.6 %collective-permute-start = (bf16[64,768]{1,0:T(8,128)(2,1)S(1)}, bf16[64,768]{1,0:T(8,128)(2,1)S(1)}, u32[]{:S(2)}, u32[]{:S(2)}) collective-permute-start(bf16[64,768]{1,0:T(8,128)(2,1)S(1)} %get-tuple-element.60), channel_id=1, source_target_pairs={{0,1},{1,0},{2,3},{3,2},{4,5},{5,4},{6,7},{7,6},{8,9},{9,8},{10,11... | collective-permute-start | bytes 294920 | tf_op jit(solution)/shard_map/ppermute | solution.py:27
  10.5 4.9 %load_and_gram.1 = (f32[64,8192]{1,0:T(8,128)S(1)}, s32[64,768]{1,0:T(8,128)S(1)}, f32[64,128]{1,0:T(8,128)S(1)}, bf16[256,768]{1,0:T(8,128)(2,1)S(1)}, bf16[256,768]{1,0:T(8,128)(2,1)S(1)}) custom-call(bf16[768,8192]{1,0:T(8,128)(2,1)S(1)} %get-tuple-element.54.a_ref.refs_1_, f32[64,8192]{1,0:T(8,128)} %z_hbm.1, s32[64,768]{1,0:T(8,128)} %sign_hbm.1, ...), custom_call_target="tpu_custom_call" | custom-call | flops 1000 | bytes 10000000 | tf_op jit(solution)/shard_map/load_and_gram/pallas_call | solution.py:182
  15.6 1.6 %collective-permute-start.8 = (f32[64,4096]{1,0:T(8,128)S(1)}, f32[64,4096]{1,0:T(8,128)S(1)}, u32[]{:S(2)}, u32[]{:S(2)}) collective-permute-start(f32[64,4096]{1,0:T(8,128)S(1)} %add.32), channel_id=1, source_target_pairs={{0,16},{8,24},{16,0},{24,8},{1,17},{9,25},{17,1},{25,9},{2,18},{10... | collective-permute-start | bytes 3145736 | tf_op jit(solution)/shard_map/ppermute | solution.py:27
  17.2 1.6 %collective-permute-start.1 = (bf16[64,768]{1,0:T(8,128)(2,1)S(1)}, bf16[64,768]{1,0:T(8,128)(2,1)S(1)}, u32[]{:S(2)}, u32[]{:S(2)}) collective-permute-start(bf16[64,768]{1,0:T(8,128)(2,1)S(1)} %add_convert_fusion.5), channel_id=1, source_target_pairs={{0,2},{1,3},{2,0},{3,1},{4,6},{5,7},{6,4},{7,5},{8,10},{9,11},{10,... | collective-permute-start | bytes 294920 | tf_op jit(solution)/shard_map/ppermute | solution.py:27
  18.8 3.4 %gram.1 = (bf16[256,256]{1,0:T(8,128)(2,1)S(1)}, bf16[256,256]{1,0:T(8,128)(2,1)S(1)}, bf16[256,512]{1,0:T(8,128)(2,1)S(1)}, bf16[256,512]{1,0:T(8,128)(2,1)S(1)}) custom-call(s32[1]{0:T(128)} %bitcast.side.token, bf16[768,8192]{1,0:T(8,128)(2,1)S(1)} %get-tuple-element.54.a_ref.refs_1_), custom_call_target="tpu_custom_call" | custom-call | flops 1000 | bytes 10000000 | tf_op jit(solution)/shard_map/gram/pallas_call | solution.py:205
  22.3 2.6 %collective-permute-start.2 = (bf16[64,768]{1,0:T(8,128)(2,1)S(1)}, bf16[64,768]{1,0:T(8,128)(2,1)S(1)}, u32[]{:S(2)}, u32[]{:S(2)}) collective-permute-start(bf16[64,768]{1,0:T(8,128)(2,1)S(1)} %add_convert_fusion.4.refs_6_), channel_id=1, source_target_pairs={{0,4},{1,5},{2,6},{3,7},{4,0},{5,1},{6,2},{7,3},{8,12},{9,13},{10,... | collective-permute-start | bytes 294920 | tf_op jit(solution)/shard_map/ppermute | solution.py:27
  25.0 4.3 %pulled_margins.1.pulled = f32[64,768]{1,0:T(8,128)S(1)} custom-call(s32[1]{0:T(128)} %bitcast.side.token, f32[64,128]{1,0:T(8,128)S(1)} %get-tuple-element.55.scale.refs_0_, f32[64,8192]{1,0:T(8,128)S(1)} %get-tuple-element.56.x_ref, f32[64,8192]{1,0:T(8,128)S(1)} %get-tuple-element.57.u_ref, f32[64,8192]{1,0:T(8,128)S(1)} %get-tuple-element.58.z_ref, ...), custom_call_target="tpu_custom_call" | custom-call | flops 1000 | bytes 10000000 | tf_op jit(solution)/shard_map/pulled_margins/pallas_call | solution.py:236
  31.1 1.3 %collective-permute-start.5 = (bf16[64,768]{1,0:T(8,128)(2,1)S(1)}, bf16[64,768]{1,0:T(8,128)(2,1)S(1)}, u32[]{:S(2)}, u32[]{:S(2)}) collective-permute-start(bf16[64,768]{1,0:T(8,128)(2,1)S(1)} %get-tuple-element.76), channel_id=1, source_target_pairs={{0,2},{1,3},{2,0},{3,1},{4,6},{5,7},{6,4},{7,5},{8,10},{9,11},{10,... | collective-permute-start | bytes 294920 | tf_op jit(solution)/shard_map/ppermute | solution.py:27
  32.4 1.5 %collective-permute-start.4 = (bf16[64,768]{1,0:T(8,128)(2,1)S(1)}, bf16[64,768]{1,0:T(8,128)(2,1)S(1)}, u32[]{:S(2)}, u32[]{:S(2)}) collective-permute-start(bf16[64,768]{1,0:T(8,128)(2,1)S(1)} %get-tuple-element.76), channel_id=1, source_target_pairs={{0,1},{1,0},{2,3},{3,2},{4,5},{5,4},{6,7},{7,6},{8,9},{9,8},{10,11... | collective-permute-start | bytes 294920 | tf_op jit(solution)/shard_map/ppermute | solution.py:27
  33.9 3.0 %collective-permute-done.6 = bf16[64,768]{1,0:T(8,128)(2,1)S(1)} collective-permute-done((bf16[64,768]{1,0:T(8,128)(2,1)S(1)}, bf16[64,768]{1,0:T(8,128)(2,1)S(1)}, u32[]{:S(2)}, u32[]{:S(2)}) %collective-permute-start.6) | collective-permute-done | bytes 98336 | tf_op jit(solution)/shard_map/ppermute | solution.py:27
  37.0 1.0 %collective-permute-done.4 = bf16[64,768]{1,0:T(8,128)(2,1)S(1)} collective-permute-done((bf16[64,768]{1,0:T(8,128)(2,1)S(1)}, bf16[64,768]{1,0:T(8,128)(2,1)S(1)}, u32[]{:S(2)}, u32[]{:S(2)}) %collective-permute-start.4) | collective-permute-done | bytes 98336 | tf_op jit(solution)/shard_map/ppermute | solution.py:27
  38.4 2.5 %collective-permute-done.8 = f32[64,4096]{1,0:T(8,128)S(1)} collective-permute-done((f32[64,4096]{1,0:T(8,128)S(1)}, f32[64,4096]{1,0:T(8,128)S(1)}, u32[]{:S(2)}, u32[]{:S(2)}) %collective-permute-start.8) | collective-permute-done | bytes 1048608 | tf_op jit(solution)/shard_map/ppermute | solution.py:27
  41.0 3.4 %collective-permute-done.7.refs_5_ = bf16[64,768]{1,0:T(8,128)(2,1)S(1)} collective-permute-done((bf16[64,768]{1,0:T(8,128)(2,1)S(1)}, bf16[64,768]{1,0:T(8,128)(2,1)S(1)}, u32[]{:S(2)}, u32[]{:S(2)}) %collective-permute-start.7) | collective-permute-done | bytes 98336 | tf_op jit(solution)/shard_map/ppermute | solution.py:27
  44.9 0.9 %push_other.3 = (f32[64,3072]{1,0:T(8,128)S(1)}, bf16[64,3072]{1,0:T(8,128)(2,1)S(1)}) custom-call(s32[1]{0:T(128)} %bitcast.side.token, f32[64,128]{1,0:T(8,128)S(1)} %get-tuple-element.55.scale.refs_0_, bf16[768,8192]{1,0:T(8,128)(2,1)S(1)} %get-tuple-element.54.a_ref.refs_1_, bf16[128,768]{1,0:T(8,128)(2,1)S(1)} %get-tuple-element.79.refs_2_), custom_call_target="tpu_custom_call" | custom-call | flops 1000 | bytes 1000 | tf_op jit(solution)/shard_map/push_other/pallas_call | solution.py:312
  48.2 1.3 %collective-permute-start.15 = (bf16[64,1536]{1,0:T(8,128)(2,1)S(1)}, bf16[64,1536]{1,0:T(8,128)(2,1)S(1)}, u32[]{:S(2)}, u32[]{:S(2)}) collective-permute-start(bf16[64,1536]{1,0:T(8,128)(2,1)S(1)} %get-tuple-element.88), channel_id=1, source_target_pairs={{0,16},{8,24},{16,0},{24,8},{1,17},{9,25},{17,1},{25,9},{2,18},{10... | collective-permute-start | bytes 589832 | tf_op jit(solution)/shard_map/ppermute | solution.py:27
  50.2 1.7 %store_x.1 = f32[64,8192]{1,0:T(8,128)} custom-call(s32[1]{0:T(128)} %bitcast.side.token, f32[64,128]{1,0:T(8,128)S(1)} %get-tuple-element.55.scale.refs_0_, f32[64,8192]{1,0:T(8,128)S(1)} %get-tuple-element.56.x_ref, f32[64,8192]{1,0:T(8,128)S(1)} %get-tuple-element.57.u_ref, f32[64,8192]{1,0:T(8,128)S(1)} %get-tuple-element.58.z_ref, ...), custom_call_target="tpu_custom_call" | custom-call | flops 1000 | bytes 1000 | tf_op jit(solution)/shard_map/store_x/pallas_call | solution.py:346
  51.9 1.3 %collective-permute-done.13 = bf16[64,1024]{1,0:T(8,128)(2,1)S(1)} collective-permute-done((bf16[64,1024]{1,0:T(8,128)(2,1)S(1)}, bf16[64,1024]{1,0:T(8,128)(2,1)S(1)}, u32[]{:S(2)}, u32[]{:S(2)}) %collective-permute-start.13) | collective-permute-done | bytes 131104 | tf_op jit(solution)/shard_map/ppermute | solution.py:27
  53.3 1.0 %final.4 = (f32[64,8192]{1,0:T(8,128)}, f32[64,8192]{1,0:T(8,128)}) custom-call(s32[1]{0:T(128)} %bitcast.side.token, f32[64,128]{1,0:T(8,128)S(1)} %get-tuple-element.55.scale.refs_0_, f32[64,8192]{1,0:T(8,128)S(1)} %get-tuple-element.56.x_ref, f32[64,8192]{1,0:T(8,128)S(1)} %get-tuple-element.57.u_ref, f32[64,8192]{1,0:T(8,128)S(1)} %get-tuple-element.58.z_ref, ...), custom_call_target="tpu_custom_call" | custom-call | flops 1000 | bytes 1000 | tf_op jit(solution)/shard_map/final/pallas_call | solution.py:396
  54.9 2.0 %collective-permute-done.15 = bf16[64,1536]{1,0:T(8,128)(2,1)S(1)} collective-permute-done((bf16[64,1536]{1,0:T(8,128)(2,1)S(1)}, bf16[64,1536]{1,0:T(8,128)(2,1)S(1)}, u32[]{:S(2)}, u32[]{:S(2)}) %collective-permute-start.15) | collective-permute-done | bytes 196640 | tf_op jit(solution)/shard_map/ppermute | solution.py:27
  57.1 1.5 %final.5 = (f32[64,8192]{1,0:T(8,128)}, f32[64,8192]{1,0:T(8,128)}) custom-call(s32[1]{0:T(128)} %bitcast.side.token, f32[64,128]{1,0:T(8,128)S(1)} %get-tuple-element.55.scale.refs_0_, f32[64,8192]{1,0:T(8,128)S(1)} %get-tuple-element.56.x_ref, f32[64,8192]{1,0:T(8,128)S(1)} %get-tuple-element.57.u_ref, ...), custom_call_target="tpu_custom_call", output_to_operand_aliasing={{0}: (11, {}), {1}: (12, {})} | custom-call | flops 1000 | bytes 1000 | tf_op jit(solution)/shard_map/final/pallas_call | solution.py:396
  58.6 3.1 %collective-permute-done.12 = bf16[64,1536]{1,0:T(8,128)(2,1)S(1)} collective-permute-done((bf16[64,1536]{1,0:T(8,128)(2,1)S(1)}, bf16[64,1536]{1,0:T(8,128)(2,1)S(1)}, u32[]{:S(2)}, u32[]{:S(2)}) %collective-permute-start.12) | collective-permute-done | bytes 196640 | tf_op jit(solution)/shard_map/ppermute | solution.py:27
  61.8 1.7 %final.6 = (f32[64,8192]{1,0:T(8,128)}, f32[64,8192]{1,0:T(8,128)}) custom-call(s32[1]{0:T(128)} %bitcast.side.token, f32[64,128]{1,0:T(8,128)S(1)} %get-tuple-element.55.scale.refs_0_, f32[64,8192]{1,0:T(8,128)S(1)} %get-tuple-element.56.x_ref, f32[64,8192]{1,0:T(8,128)S(1)} %get-tuple-element.57.u_ref, ...), custom_call_target="tpu_custom_call", output_to_operand_aliasing={{0}: (11, {}), {1}: (12, {})} | custom-call | flops 1000 | bytes 1000 | tf_op jit(solution)/shard_map/final/pallas_call | solution.py:396
  63.6 1.2 %final.7 = (f32[64,8192]{1,0:T(8,128)}, f32[64,8192]{1,0:T(8,128)}) custom-call(s32[1]{0:T(128)} %bitcast.side.token, f32[64,128]{1,0:T(8,128)S(1)} %get-tuple-element.55.scale.refs_0_, f32[64,8192]{1,0:T(8,128)S(1)} %get-tuple-element.56.x_ref, f32[64,8192]{1,0:T(8,128)S(1)} %get-tuple-element.57.u_ref, ...), custom_call_target="tpu_custom_call", output_to_operand_aliasing={{0}: (8, {}), {1}: (9, {})} | custom-call | flops 1000 | bytes 1000 | tf_op jit(solution)/shard_map/final/pallas_call | solution.py:396
  (35 shorter events, 7.7 us)
Async XLA Ops:
  7.4 8.1 %collective-permute-start.3 = (f32[64,4096]{1,0:T(8,128)S(1)}, f32[64,4096]{1,0:T(8,128)S(1)}, u32[]{:S(2)}, u32[]{:S(2)}) collective-permute-start(f32[64,4096]{1,0:T(8,128)S(1)} %get-tuple-element.72), channel_id=1, source_target_pairs={{0,8},{8,0},{16,24},{24,16},{1,9},{9,1},{17,25},{25,17},{2,10},{10... | collective-permute-start | bytes 3145736 | tf_op jit(solution)/shard_map/ppermute | solution.py:27
  7.9 7.5 %collective-permute-start = (bf16[64,768]{1,0:T(8,128)(2,1)S(1)}, bf16[64,768]{1,0:T(8,128)(2,1)S(1)}, u32[]{:S(2)}, u32[]{:S(2)}) collective-permute-start(bf16[64,768]{1,0:T(8,128)(2,1)S(1)} %get-tuple-element.60), channel_id=1, source_target_pairs={{0,1},{1,0},{2,3},{3,2},{4,5},{5,4},{6,7},{7,6},{8,9},{9,8},{10,11... | collective-permute-start | bytes 294920 | tf_op jit(solution)/shard_map/ppermute | solution.py:27
  15.6 25.3 %collective-permute-start.8 = (f32[64,4096]{1,0:T(8,128)S(1)}, f32[64,4096]{1,0:T(8,128)S(1)}, u32[]{:S(2)}, u32[]{:S(2)}) collective-permute-start(f32[64,4096]{1,0:T(8,128)S(1)} %add.32), channel_id=1, source_target_pairs={{0,16},{8,24},{16,0},{24,8},{1,17},{9,25},{17,1},{25,9},{2,18},{10... | collective-permute-start | bytes 3145736 | tf_op jit(solution)/shard_map/ppermute | solution.py:27
  17.2 5.1 %collective-permute-start.1 = (bf16[64,768]{1,0:T(8,128)(2,1)S(1)}, bf16[64,768]{1,0:T(8,128)(2,1)S(1)}, u32[]{:S(2)}, u32[]{:S(2)}) collective-permute-start(bf16[64,768]{1,0:T(8,128)(2,1)S(1)} %add_convert_fusion.5), channel_id=1, source_target_pairs={{0,2},{1,3},{2,0},{3,1},{4,6},{5,7},{6,4},{7,5},{8,10},{9,11},{10,... | collective-permute-start | bytes 294920 | tf_op jit(solution)/shard_map/ppermute | solution.py:27
  22.3 7.4 %collective-permute-start.2 = (bf16[64,768]{1,0:T(8,128)(2,1)S(1)}, bf16[64,768]{1,0:T(8,128)(2,1)S(1)}, u32[]{:S(2)}, u32[]{:S(2)}) collective-permute-start(bf16[64,768]{1,0:T(8,128)(2,1)S(1)} %add_convert_fusion.4.refs_6_), channel_id=1, source_target_pairs={{0,4},{1,5},{2,6},{3,7},{4,0},{5,1},{6,2},{7,3},{8,12},{9,13},{10,... | collective-permute-start | bytes 294920 | tf_op jit(solution)/shard_map/ppermute | solution.py:27
  30.3 6.5 %collective-permute-start.6 = (bf16[64,768]{1,0:T(8,128)(2,1)S(1)}, bf16[64,768]{1,0:T(8,128)(2,1)S(1)}, u32[]{:S(2)}, u32[]{:S(2)}) collective-permute-start(bf16[64,768]{1,0:T(8,128)(2,1)S(1)} %get-tuple-element.76), channel_id=1, source_target_pairs={{0,3},{1,2},{2,1},{3,0},{4,7},{5,6},{6,5},{7,4},{8,11},{9,10},{10,... | collective-permute-start | bytes 294920 | tf_op jit(solution)/shard_map/ppermute | solution.py:27
  31.1 5.8 %collective-permute-start.5 = (bf16[64,768]{1,0:T(8,128)(2,1)S(1)}, bf16[64,768]{1,0:T(8,128)(2,1)S(1)}, u32[]{:S(2)}, u32[]{:S(2)}) collective-permute-start(bf16[64,768]{1,0:T(8,128)(2,1)S(1)} %get-tuple-element.76), channel_id=1, source_target_pairs={{0,2},{1,3},{2,0},{3,1},{4,6},{5,7},{6,4},{7,5},{8,10},{9,11},{10,... | collective-permute-start | bytes 294920 | tf_op jit(solution)/shard_map/ppermute | solution.py:27
  32.4 5.5 %collective-permute-start.4 = (bf16[64,768]{1,0:T(8,128)(2,1)S(1)}, bf16[64,768]{1,0:T(8,128)(2,1)S(1)}, u32[]{:S(2)}, u32[]{:S(2)}) collective-permute-start(bf16[64,768]{1,0:T(8,128)(2,1)S(1)} %get-tuple-element.76), channel_id=1, source_target_pairs={{0,1},{1,0},{2,3},{3,2},{4,5},{5,4},{6,7},{7,6},{8,9},{9,8},{10,11... | collective-permute-start | bytes 294920 | tf_op jit(solution)/shard_map/ppermute | solution.py:27
  38.0 6.4 %collective-permute-start.7 = (bf16[64,768]{1,0:T(8,128)(2,1)S(1)}, bf16[64,768]{1,0:T(8,128)(2,1)S(1)}, u32[]{:S(2)}, u32[]{:S(2)}) collective-permute-start(bf16[64,768]{1,0:T(8,128)(2,1)S(1)} %add_convert_fusion.3.refs_4_), channel_id=1, source_target_pairs={{0,4},{1,5},{2,6},{3,7},{4,0},{5,1},{6,2},{7,3},{8,12},{9,13},{10,... | collective-permute-start | bytes 294920 | tf_op jit(solution)/shard_map/ppermute | solution.py:27
  44.8 1.5 %collective-permute-start.9 = (bf16[64,1024]{1,0:T(8,128)(2,1)S(1)}, bf16[64,1024]{1,0:T(8,128)(2,1)S(1)}, u32[]{:S(2)}, u32[]{:S(2)}) collective-permute-start(bf16[64,1024]{1,0:T(8,128)(2,1)S(1)} %get-tuple-element.82), channel_id=1, source_target_pairs={{0,8},{8,0},{16,24},{24,16},{1,9},{9,1},{17,25},{25,17},{2,10},{10... | collective-permute-start | bytes 393224 | tf_op jit(solution)/shard_map/ppermute | solution.py:27
  45.8 1.9 %collective-permute-start.10 = (bf16[64,3072]{1,0:T(8,128)(2,1)S(1)}, bf16[64,3072]{1,0:T(8,128)(2,1)S(1)}, u32[]{:S(2)}, u32[]{:S(2)}) collective-permute-start(bf16[64,3072]{1,0:T(8,128)(2,1)S(1)} %get-tuple-element.86), channel_id=1, source_target_pairs={{0,8},{8,0},{16,24},{24,16},{1,9},{9,1},{17,25},{25,17},{2,10},{10... | collective-permute-start | bytes 1179656 | tf_op jit(solution)/shard_map/ppermute | solution.py:27
  46.7 10.3 %collective-permute-start.11 = (f32[64,4096]{1,0:T(8,128)S(1)}, f32[64,4096]{1,0:T(8,128)S(1)}, u32[]{:S(2)}, u32[]{:S(2)}) collective-permute-start(f32[64,4096]{1,0:T(8,128)S(1)} %add.36.refs_0_.refs_3_), channel_id=1, source_target_pairs={{0,8},{8,0},{16,24},{24,16},{1,9},{9,1},{17,25},{25,17},{2,10},{10... | collective-permute-start | bytes 3145736 | tf_op jit(solution)/shard_map/ppermute | solution.py:27
  46.8 6.3 %collective-permute-start.13 = (bf16[64,1024]{1,0:T(8,128)(2,1)S(1)}, bf16[64,1024]{1,0:T(8,128)(2,1)S(1)}, u32[]{:S(2)}, u32[]{:S(2)}) collective-permute-start(bf16[64,1024]{1,0:T(8,128)(2,1)S(1)} %get-tuple-element.84), channel_id=1, source_target_pairs={{0,16},{8,24},{16,0},{24,8},{1,17},{9,25},{17,1},{25,9},{2,18},{10... | collective-permute-start | bytes 393224 | tf_op jit(solution)/shard_map/ppermute | solution.py:27
  48.2 8.7 %collective-permute-start.15 = (bf16[64,1536]{1,0:T(8,128)(2,1)S(1)}, bf16[64,1536]{1,0:T(8,128)(2,1)S(1)}, u32[]{:S(2)}, u32[]{:S(2)}) collective-permute-start(bf16[64,1536]{1,0:T(8,128)(2,1)S(1)} %get-tuple-element.88), channel_id=1, source_target_pairs={{0,16},{8,24},{16,0},{24,8},{1,17},{9,25},{17,1},{25,9},{2,18},{10... | collective-permute-start | bytes 589832 | tf_op jit(solution)/shard_map/ppermute | solution.py:27
  53.2 3.9 %collective-permute-start.14 = (bf16[64,1024]{1,0:T(8,128)(2,1)S(1)}, bf16[64,1024]{1,0:T(8,128)(2,1)S(1)}, u32[]{:S(2)}, u32[]{:S(2)}) collective-permute-start(bf16[64,1024]{1,0:T(8,128)(2,1)S(1)} %add_convert_fusion.2.refs_2_), channel_id=1, source_target_pairs={{0,8},{8,0},{16,24},{24,16},{1,9},{9,1},{17,25},{25,17},{2,10},{10... | collective-permute-start | bytes 393224 | tf_op jit(solution)/shard_map/ppermute | solution.py:27
  54.3 7.4 %collective-permute-start.12 = (bf16[64,1536]{1,0:T(8,128)(2,1)S(1)}, bf16[64,1536]{1,0:T(8,128)(2,1)S(1)}, u32[]{:S(2)}, u32[]{:S(2)}) collective-permute-start(bf16[64,1536]{1,0:T(8,128)(2,1)S(1)} %get-tuple-element.93), channel_id=1, source_target_pairs={{0,16},{8,24},{16,0},{24,8},{1,17},{9,25},{17,1},{25,9},{2,18},{10... | collective-permute-start | bytes 589832 | tf_op jit(solution)/shard_map/ppermute | solution.py:27
  57.0 4.8 %collective-permute-start.17 = (bf16[64,1536]{1,0:T(8,128)(2,1)S(1)}, bf16[64,1536]{1,0:T(8,128)(2,1)S(1)}, u32[]{:S(2)}, u32[]{:S(2)}) collective-permute-start(bf16[64,1536]{1,0:T(8,128)(2,1)S(1)} %add_convert_fusion.1.refs_5_), channel_id=1, source_target_pairs={{0,8},{8,0},{16,24},{24,16},{1,9},{9,1},{17,25},{25,17},{2,10},{10... | collective-permute-start | bytes 589832 | tf_op jit(solution)/shard_map/ppermute | solution.py:27
  61.7 1.8 %collective-permute-start.16 = (bf16[64,1536]{1,0:T(8,128)(2,1)S(1)}, bf16[64,1536]{1,0:T(8,128)(2,1)S(1)}, u32[]{:S(2)}, u32[]{:S(2)}) collective-permute-start(bf16[64,1536]{1,0:T(8,128)(2,1)S(1)} %add_convert_fusion.refs_5_), channel_id=1, source_target_pairs={{0,8},{8,0},{16,24},{24,16},{1,9},{9,1},{17,25},{25,17},{2,10},{10... | collective-permute-start | bytes 589832 | tf_op jit(solution)/shard_map/ppermute | solution.py:27

commit v9 on v8

--- a/solution.py
+++ b/solution.py
@@ -17,6 +17,7 @@
 AHEAD = 4
 NARROW = 256
 WAIT_BYTES = 10_000_000
+GRAM_ORDER = (0, 1, 2)
 HBM = pl.BlockSpec(memory_space=pltpu.HBM)
 VMEM = pl.BlockSpec(memory_space=pltpu.VMEM)
 SMEM = pl.BlockSpec(memory_space=pltpu.SMEM)
@@ -77,29 +78,39 @@
     return pl.ds(pl.multiple_of(start, 128), size)
 
 
-def load_kernel(side, x_hbm, u_hbm, a_hbm, m_out, a_out, x_out, u_out, mine_out, other_out, acc, sems):
-    width = x_hbm.shape[1]
+def load_kernel(blocks_count, side, x_hbm, u_hbm, z_hbm, a_hbm, sign_hbm, eta_hbm, rho_hbm, lam_hbm, *refs):
+    outs, (eta_row, rho_row, lam_row, both, acc, sems) = refs[:10], refs[10:]
+    m_out, pulled_out, a_out, x_out, u_out, z_out, sign_out, scale, mine_out, other_out = outs
+    tasks, width = x_hbm.shape
     steps = width // STEP
-
-    def pair(j):
-        cut = columns(j * STEP, STEP)
-        return (
-            pltpu.make_async_copy(x_hbm.at[:, cut], x_out.at[:, cut], sems.at[0, j]),
-            pltpu.make_async_copy(a_hbm.at[:, cut], a_out.at[:, cut], sems.at[1, j]),
-        )
+    rows = ((eta_hbm, eta_row), (rho_hbm, rho_row), (lam_hbm, lam_row), (sign_hbm, sign_out))
+    small = [pltpu.make_async_copy(a, b, sems.at[4, k]) for k, (a, b) in enumerate(rows)]
+
+    def chunk(j):
+        at = columns(j * STEP, STEP)
+        pairs = ((x_hbm, x_out), (u_hbm, u_out), (z_hbm, z_out), (a_hbm, a_out))
+        return [pltpu.make_async_copy(a.at[:, at], b.at[:, at], sems.at[k, j]) for k, (a, b) in enumerate(pairs)]
 
     def begin(j):
-        for copy in pair(j):
+        for copy in chunk(j):
             copy.start()
 
-    dual = pltpu.make_async_copy(u_hbm, u_out, sems.at[2, 0])
+    for copy in small[:3]:
+        copy.start()
     for j in range(min(AHEAD, steps)):
         begin(j)
+    for copy in small[:3]:
+        copy.wait()
+    one = lax.broadcasted_iota(jnp.int32, (tasks, tasks), 0) == lax.broadcasted_iota(jnp.int32, (tasks, tasks), 1)
+    eta, rho, lam = eta_row[...], rho_row[...], lam_row[...]
+    for k, row in enumerate((eta, eta * rho, lam / (rho * blocks_count))):
+        upright = jnp.where(one, jnp.broadcast_to(row, (tasks, tasks)), 0.0)
+        scale[:, k : k + 1] = jnp.sum(upright, axis=1, keepdims=True)
     acc[...] = jnp.zeros_like(acc)
 
     @pl.loop(0, steps)
     def _(j):
-        for copy in pair(j):
+        for copy in chunk(j):
             copy.wait()
 
         @pl.when(j + AHEAD < steps)
@@ -108,33 +119,50 @@
 
         @pl.when(j == max(steps - AHEAD, 0))
         def _():
-            dual.start()
-
-        cut = columns(j * STEP, STEP)
-        acc[...] += nt(x_out[:, cut].astype(BF16), a_out[:, cut])
-
-    m_out[...] = acc[...].astype(BF16)
-    dual.wait()
+            small[3].start()
+
+        pull = scale[:, 1:2]
+        for k in range(0, STEP, NARROW):
+            at, here = columns(j * STEP + k, NARROW), pl.ds(k, NARROW)
+            x = x_out[:, at]
+            v = x - pull * (x - z_out[:, at] + u_out[:, at])
+            top = v.astype(BF16)
+            both[:tasks, here] = x.astype(BF16)
+            both[tasks : 2 * tasks, here] = top
+            both[2 * tasks :, here] = (v - top.astype(F32)).astype(BF16)
+        acc[...] += nt(both[...], a_out[:, columns(j * STEP, STEP)])
+
+    m_out[...] = acc[:tasks].astype(BF16)
+    pulled_out[...] = acc[tasks : 2 * tasks] + acc[2 * tasks :]
     half = width // 2
     mine = columns(side[0] * half, half)
     other = columns((1 - side[0]) * half, half)
     mine_out[...] = x_out[:, mine] + u_out[:, mine]
     other_out[...] = x_out[:, other] + u_out[:, other]
-
-
-def load(side, x, u, design):
+    small[3].wait()
+
+
+def load(side, x, u, z, design, sign, step_size, rho, penalty, blocks_count):
     tasks, width = x.shape
     samples = design.shape[0]
     full = pltpu.VMEM((tasks, width), F32)
     half = pltpu.VMEM((tasks, width // 2), F32)
+    rows = [v.reshape(1, tasks) for v in (step_size, rho, penalty)]
     return call(
-        load_kernel,
+        functools.partial(load_kernel, blocks_count),
         "load_and_margins",
-        [SMEM] + [HBM] * 3,
-        (pltpu.VMEM((tasks, samples), BF16), pltpu.VMEM(design.shape, BF16), full, full, half, half),
-        [VMEM] * 6,
-        [pltpu.VMEM((tasks, samples), F32), pltpu.SemaphoreType.DMA((3, width // STEP))],
-    )(side, *pin(pltpu.HBM, x, u, design))
+        [SMEM] + [HBM] * 8,
+        (
+            pltpu.VMEM((tasks, samples), BF16), pltpu.VMEM((tasks, samples), F32), pltpu.VMEM(design.shape, BF16),
+            full, full, full, pltpu.VMEM(sign.shape, jnp.int32), pltpu.VMEM((tasks, 128), F32), half, half,
+        ),
+        [VMEM] * 10,
+        [pltpu.VMEM((1, tasks), F32)] * 3
+        + [
+            pltpu.VMEM((3 * tasks, STEP), BF16), pltpu.VMEM((3 * tasks, samples), F32),
+            pltpu.SemaphoreType.DMA((5, max(width // STEP, 4))),
+        ],
+    )(side, *pin(pltpu.HBM, x, u, z, design, sign, *rows))
 
 
 def gram_block(a_ref, row, cols, size, acc, high, low):
@@ -150,98 +178,24 @@
     low[...] = (whole - top.astype(F32)).astype(BF16)
 
 
-def rest_kernel(blocks_count, a_ref, z_hbm, sign_hbm, eta_hbm, rho_hbm, lam_hbm, *refs):
-    z_out, sign_out, scale_out, high, low, eta_row, rho_row, lam_row, acc, sems = refs
-    pairs = ((eta_hbm, eta_row), (rho_hbm, rho_row), (lam_hbm, lam_row), (z_hbm, z_out), (sign_hbm, sign_out))
-    copies = [pltpu.make_async_copy(a, b, sems.at[k]) for k, (a, b) in enumerate(pairs)]
-    for copy in copies:
-        copy.start()
-    size, cols = high.shape
-    gram_block(a_ref, cols - size, cols, size, acc, high, low)
-    for copy in copies[:3]:
-        copy.wait()
-    tasks = z_out.shape[0]
-    one = lax.broadcasted_iota(jnp.int32, (tasks, tasks), 0) == lax.broadcasted_iota(jnp.int32, (tasks, tasks), 1)
-    eta, rho, lam = eta_row[...], rho_row[...], lam_row[...]
-    for k, row in enumerate((eta, eta * rho, lam / (rho * blocks_count))):
-        upright = jnp.where(one, jnp.broadcast_to(row, (tasks, tasks)), 0.0)
-        scale_out[:, k : k + 1] = jnp.sum(upright, axis=1, keepdims=True)
-    for copy in copies[3:]:
-        copy.wait()
-
-
-def gram_shapes(samples, row):
+def gram_kernel(row, token, a_ref, high, low, acc):
+    size = high.shape[0]
+    gram_block(a_ref, row * size, (row + 1) * size, size, acc, high, low)
+
+
+def gram_row(row, token, design):
+    samples = design.shape[0]
     size = samples // 3
-    return [pltpu.VMEM((size, (row + 1) * size), BF16)] * 2
-
-
-def load_rest(z, sign, step_size, rho, penalty, design, blocks_count):
-    tasks, width = z.shape
-    samples = design.shape[0]
-    rows = [v.reshape(1, tasks) for v in (step_size, rho, penalty)]
+    out = pltpu.VMEM((size, (row + 1) * size), BF16)
     return call(
-        functools.partial(rest_kernel, blocks_count),
-        "load_and_gram",
-        [VMEM] + [HBM] * 5,
-        (
-            pltpu.VMEM((tasks, width), F32), pltpu.VMEM(sign.shape, jnp.int32), pltpu.VMEM((tasks, 128), F32),
-            *gram_shapes(samples, 2),
-        ),
-        [VMEM] * 5,
-        [pltpu.VMEM((1, tasks), F32)] * 3 + [pltpu.VMEM((samples // 3, samples), F32), pltpu.SemaphoreType.DMA((5,))],
-        work=WAIT_BYTES,
-    )(*pin(pltpu.VMEM, design), *pin(pltpu.HBM, z, sign, *rows))
-
-
-def gram_kernel(token, a_ref, *refs):
-    *outs, acc = refs
-    size = outs[0].shape[0]
-    for row in range(2):
-        gram_block(a_ref, row * size, (row + 1) * size, size, acc, outs[2 * row], outs[2 * row + 1])
-
-
-def gram_rows(token, design):
-    samples = design.shape[0]
-    return call(
-        gram_kernel,
+        functools.partial(gram_kernel, row),
         "gram",
         [SMEM, VMEM],
-        (*gram_shapes(samples, 0), *gram_shapes(samples, 1)),
-        [VMEM] * 4,
-        [pltpu.VMEM((samples // 3, samples), F32)],
-        work=WAIT_BYTES,
+        (out, out),
+        [VMEM] * 2,
+        [pltpu.VMEM((size, (row + 1) * size), F32)],
+        work=WAIT_BYTES * (row + 1) // 3,
     )(token, *pin(pltpu.VMEM, design))
-
-
-def pulled_kernel(token, scale, x_ref, u_ref, z_ref, a_ref, out, both, acc):
-    pull = scale[:, 1:2]
-    tasks, width = x_ref.shape
-    wide = math.gcd(WIDE, width)
-    for j in range(width // wide):
-        for k in range(0, wide, 512):
-            at, here = pl.ds(j * wide + k, 512), pl.ds(k, 512)
-            x = x_ref[:, at]
-            v = x - pull * (x - z_ref[:, at] + u_ref[:, at])
-            top = v.astype(BF16)
-            both[:tasks, here] = top
-            both[tasks:, here] = (v - top.astype(F32)).astype(BF16)
-        product = nt(both[...], a_ref[:, pl.ds(j * wide, wide)])
-        acc[...] = product if j == 0 else acc[...] + product
-    out[...] = acc[:tasks] + acc[tasks:]
-
-
-def pulled_margins(token, scale, x, u, z, design):
-    tasks, width = x.shape
-    samples = design.shape[0]
-    return call(
-        pulled_kernel,
-        "pulled_margins",
-        [SMEM] + [VMEM] * 5,
-        pltpu.VMEM((tasks, samples), F32),
-        VMEM,
-        [pltpu.VMEM((2 * tasks, math.gcd(WIDE, width)), BF16), pltpu.VMEM((2 * tasks, samples), F32)],
-        work=WAIT_BYTES,
-    )(token, *pin(pltpu.VMEM, scale, x, u, z, design))
 
 
 def residual(sign, *terms):
@@ -414,38 +368,28 @@
     blocks_count = lax.axis_size("rows")
     side = (lax.axis_index("rows") & 1).astype(jnp.int32)[None]
 
-    margin1, design, x0, dual, start_mine, start_other = load(side, local_x[0], dual_u[0], design)
+    margin1, pulled, design, x0, dual, z, sign, scale, start_mine, start_other = load(
+        side, local_x[0], dual_u[0], consensus_z, design, labels, step_size, rho, penalty, blocks_count
+    )
     start_mine = start_mine + exchange(start_other, "rows", 1)
 
-    z, sign, scale, *gram2 = load_rest(consensus_z, labels, step_size, rho, penalty, design, blocks_count)
-    terms, grams, pulled = [margin1], None, None
-    for step in range(lax.axis_size("feat").bit_length() - 1):
-        if step > 0:
+    terms, grams = [margin1], []
+    for step in range(max(lax.axis_size("feat").bit_length() - 1, 3)):
+        more = (1 << step) < lax.axis_size("feat")
+        if step > 0 and more:
             terms = [sum(t.astype(F32) for t in terms).astype(BF16)]
-        token = tie(side, terms[0])
-        got = exchange(terms[0], "feat", 1 << step)
-        if step == 0:
-            got = tie(got, scale)
-        if step == 1:
-            grams = gram_rows(token, design)
-            got = tie(got, grams[0])
-        if step == 2:
-            pulled = pulled_margins(token, scale, x0, dual, z, design)
-        terms.append(got)
-    if grams is None:
-        grams = gram_rows(side, design)
-    if pulled is None:
-        pulled = pulled_margins(side, scale, x0, dual, z, design)
-    terms = tie(terms, start_mine)
-
-    resid1, margin2 = turn(sign, terms, scale, pulled, [*grams, *gram2])
+        row = gram_row(GRAM_ORDER[step], tie(side, terms[0]), design) if step < 3 else []
+        grams.append(row)
+        if more:
+            got = exchange(terms[0], "feat", 1 << step)
+            terms.append(tie(got, row[0], start_mine) if step == 0 else tie(got, row[0]) if step == 1 else got)
+
+    resid1, margin2 = turn(sign, terms, scale, pulled, [g for row in range(3) for g in grams[GRAM_ORDER.index(row)]])
     terms = square_sum(margin2, "feat")
     mask = 2
     while mask < blocks_count:
         start_mine = start_mine + exchange(start_mine, "rows", mask)
         mask *= 2
-    terms = tie(terms, start_mine)
-
     sizes = [half * part // sum(MINE) for part in MINE]
     begins = [sum(sizes[:c]) for c in range(len(sizes))]
     other_sizes = [half * part // sum(OTHER) for part in OTHER]

time: 65.1 us -> 60.5 us (0.929)
  Pallas kernels: 30.2 us -> 25.6 us
  starting transfers between devices: 16.3 us -> 20.2 us
  waiting for transfers between devices: 16.9 us -> 13.1 us
    pallas_call x4, Pallas kernels: 19.5 us -> 15.3 us  [the longest x1 8.18 us: load(): call(functools.partial(load_kernel, blocks_count), 'load_and_margins', [S...]
    ppermute x18, starting transfers between devices: 16.3 us -> 20.2 us  [exchange(): return lax.ppermute(value, axis, [(i, i ^ mask) for i in range(n)])]
    ppermute x18, waiting for transfers between devices: 16.9 us -> 13.1 us  [exchange(): return lax.ppermute(value, axis, [(i, i ^ mask) for i in range(n)])]
  transfers between devices with their start and end apart: 18 -> 18, of which waited for: 10 -> 8; matrix products, arithmetic and copies ran while one was open for 1% -> 1% of each run, Pallas kernels for 34% -> 27%
where the time goes in v9:
time: 60.5 us; the launch traced here: 60.3 us
  Pallas kernels  25.6 us (42%)
  starting transfers between devices  20.2 us (33%)
  waiting for transfers between devices  13.1 us (22%)
  between operations  0.89 us (1%)
    ppermute x18, starting transfers between devices, exchange(): return lax.ppermute(value, axis, [(i, i ^ mask) for i in range(n)])  20.2 us
    ppermute x18, waiting for transfers between devices, exchange(): return lax.ppermute(value, axis, [(i, i ^ mask) for i in range(n)])  13.1 us
    pallas_call x1, Pallas kernels, load(): call(functools.partial(load_kernel, blocks_count), 'load_and_margins', [S...  8.18 us
    pallas_call x3, Pallas kernels, gram_row(): call(functools.partial(gram_kernel, row), 'gram', [SMEM, VMEM], (out, out...  7.09 us
    pallas_call x4, Pallas kernels, final(): call(functools.partial(final_kernel, blocks_count, places, buffered), 'fi...  5.41 us
    pallas_call x5, Pallas kernels, push(): call(functools.partial(push_kernel, first, mine, begin, offset, size), 'p...  2.72 us
    pallas_call x1, Pallas kernels, store_x(): call(store_kernel, 'store_x', [SMEM] + [VMEM] * len(args), pltpu.HBM((tas...  1.61 us
  transfers between devices with their start and end apart: 18, of which 8 were waited for; matrix products, arithmetic and copies ran while one was open for 1% of the time, Pallas kernels for 27%

profile of v9, /device:TPU:0, one launch (start us, length us, event | category | flops | bytes accessed | tf_op | source)
XLA Modules:
  0.0 60.3 jit_solution(8759691123492657503)
XLA Ops:
  0.6 8.2 %load_and_margins.1 = (bf16[64,768]{1,0:T(8,128)(2,1)S(1)}, f32[64,768]{1,0:T(8,128)S(1)}, bf16[768,8192]{1,0:T(8,128)(2,1)S(1)}, f32[64,8192]{1,0:T(8,128)S(1)}...) custom-call(s32[1]{0:T(128)} %bitcast.side.token, ...), custom_call_target="tpu_custom_call" | custom-call | flops 1000 | bytes 1000 | tf_op jit(solution)/shard_map/load_and_margins/pallas_call | solution.py:151
  9.3 2.6 %collective-permute-start = (bf16[64,768]{1,0:T(8,128)(2,1)S(1)}, bf16[64,768]{1,0:T(8,128)(2,1)S(1)}, u32[]{:S(2)}, u32[]{:S(2)}) collective-permute-start(bf16[64,768]{1,0:T(8,128)(2,1)S(1)} %get-tuple-element.59), channel_id=1, source_target_pairs={{0,1},{1,0},{2,3},{3,2},{4,5},{5,4},{6,7},{7,6},{8,9},{9,8},{10,11... | collective-permute-start | bytes 294920 | tf_op jit(solution)/shard_map/ppermute | solution.py:28
  11.9 1.3 %gram.3 = (bf16[256,256]{1,0:T(8,128)(2,1)S(1)}, bf16[256,256]{1,0:T(8,128)(2,1)S(1)}) custom-call(s32[1]{0:T(128)} %bitcast.side.token, bf16[768,8192]{1,0:T(8,128)(2,1)S(1)} %get-tuple-element.56.a_ref.refs_1_), custom_call_target="tpu_custom_call" | custom-call | flops 1000 | bytes 3333333 | tf_op jit(solution)/shard_map/gram/pallas_call | solution.py:190
  13.3 1.6 %collective-permute-start.10 = (f32[64,4096]{1,0:T(8,128)S(1)}, f32[64,4096]{1,0:T(8,128)S(1)}, u32[]{:S(2)}, u32[]{:S(2)}) collective-permute-start(f32[64,4096]{1,0:T(8,128)S(1)} %add.30), channel_id=1, source_target_pairs={{0,16},{8,24},{16,0},{24,8},{1,17},{9,25},{17,1},{25,9},{2,18},{10... | collective-permute-start | bytes 3145736 | tf_op jit(solution)/shard_map/ppermute | solution.py:28
  15.4 1.9 %collective-permute-start.2 = (bf16[64,768]{1,0:T(8,128)(2,1)S(1)}, bf16[64,768]{1,0:T(8,128)(2,1)S(1)}, u32[]{:S(2)}, u32[]{:S(2)}) collective-permute-start(bf16[64,768]{1,0:T(8,128)(2,1)S(1)} %add_convert_fusion.5), channel_id=1, source_target_pairs={{0,2},{1,3},{2,0},{3,1},{4,6},{5,7},{6,4},{7,5},{8,10},{9,11},{10,... | collective-permute-start | bytes 294920 | tf_op jit(solution)/shard_map/ppermute | solution.py:28
  17.2 2.4 %gram.4 = (bf16[256,512]{1,0:T(8,128)(2,1)S(1)}, bf16[256,512]{1,0:T(8,128)(2,1)S(1)}) custom-call(s32[1]{0:T(128)} %bitcast.side.token, bf16[768,8192]{1,0:T(8,128)(2,1)S(1)} %get-tuple-element.56.a_ref.refs_1_), custom_call_target="tpu_custom_call" | custom-call | flops 1000 | bytes 6666666 | tf_op jit(solution)/shard_map/gram/pallas_call | solution.py:190
  20.1 2.9 %collective-permute-start.3 = (bf16[64,768]{1,0:T(8,128)(2,1)S(1)}, bf16[64,768]{1,0:T(8,128)(2,1)S(1)}, u32[]{:S(2)}, u32[]{:S(2)}) collective-permute-start(bf16[64,768]{1,0:T(8,128)(2,1)S(1)} %add_convert_fusion.4.refs_6_), channel_id=1, source_target_pairs={{0,4},{1,5},{2,6},{3,7},{4,0},{5,1},{6,2},{7,3},{8,12},{9,13},{10,... | collective-permute-start | bytes 294920 | tf_op jit(solution)/shard_map/ppermute | solution.py:28
  23.0 3.5 %gram.5 = (bf16[256,768]{1,0:T(8,128)(2,1)S(1)}, bf16[256,768]{1,0:T(8,128)(2,1)S(1)}) custom-call(s32[1]{0:T(128)} %bitcast.side.token, bf16[768,8192]{1,0:T(8,128)(2,1)S(1)} %get-tuple-element.56.a_ref.refs_1_), custom_call_target="tpu_custom_call" | custom-call | flops 1000 | bytes 10000000 | tf_op jit(solution)/shard_map/gram/pallas_call | solution.py:190
  27.1 2.6 %collective-permute-start.6 = (bf16[64,768]{1,0:T(8,128)(2,1)S(1)}, bf16[64,768]{1,0:T(8,128)(2,1)S(1)}, u32[]{:S(2)}, u32[]{:S(2)}) collective-permute-start(bf16[64,768]{1,0:T(8,128)(2,1)S(1)} %get-tuple-element.74), channel_id=1, source_target_pairs={{0,3},{1,2},{2,1},{3,0},{4,7},{5,6},{6,5},{7,4},{8,11},{9,10},{10,... | collective-permute-start | bytes 294920 | tf_op jit(solution)/shard_map/ppermute | solution.py:28
  30.6 2.1 %collective-permute-done.6 = bf16[64,768]{1,0:T(8,128)(2,1)S(1)} collective-permute-done((bf16[64,768]{1,0:T(8,128)(2,1)S(1)}, bf16[64,768]{1,0:T(8,128)(2,1)S(1)}, u32[]{:S(2)}, u32[]{:S(2)}) %collective-permute-start.6) | collective-permute-done | bytes 98336 | tf_op jit(solution)/shard_map/ppermute | solution.py:28
  32.8 1.5 %collective-permute-done.5 = bf16[64,768]{1,0:T(8,128)(2,1)S(1)} collective-permute-done((bf16[64,768]{1,0:T(8,128)(2,1)S(1)}, bf16[64,768]{1,0:T(8,128)(2,1)S(1)}, u32[]{:S(2)}, u32[]{:S(2)}) %collective-permute-start.5) | collective-permute-done | bytes 98336 | tf_op jit(solution)/shard_map/ppermute | solution.py:28
  34.8 2.6 %collective-permute-start.7 = (bf16[64,768]{1,0:T(8,128)(2,1)S(1)}, bf16[64,768]{1,0:T(8,128)(2,1)S(1)}, u32[]{:S(2)}, u32[]{:S(2)}) collective-permute-start(bf16[64,768]{1,0:T(8,128)(2,1)S(1)} %add_convert_fusion.3.refs_4_), channel_id=1, source_target_pairs={{0,4},{1,5},{2,6},{3,7},{4,0},{5,1},{6,2},{7,3},{8,12},{9,13},{10,... | collective-permute-start | bytes 294920 | tf_op jit(solution)/shard_map/ppermute | solution.py:28
  37.4 3.0 %collective-permute-done.7.refs_5_ = bf16[64,768]{1,0:T(8,128)(2,1)S(1)} collective-permute-done((bf16[64,768]{1,0:T(8,128)(2,1)S(1)}, bf16[64,768]{1,0:T(8,128)(2,1)S(1)}, u32[]{:S(2)}, u32[]{:S(2)}) %collective-permute-start.7) | collective-permute-done | bytes 98336 | tf_op jit(solution)/shard_map/ppermute | solution.py:28
  40.9 0.9 %push_other.3 = (f32[64,3072]{1,0:T(8,128)S(1)}, bf16[64,3072]{1,0:T(8,128)(2,1)S(1)}) custom-call(s32[1]{0:T(128)} %bitcast.side.token, f32[64,128]{1,0:T(8,128)S(1)} %get-tuple-element.52.scale.refs_0_, bf16[768,8192]{1,0:T(8,128)(2,1)S(1)} %get-tuple-element.56.a_ref.refs_1_, bf16[128,768]{1,0:T(8,128)(2,1)S(1)} %get-tuple-element.75.refs_2_), custom_call_target="tpu_custom_call" | custom-call | flops 1000 | bytes 1000 | tf_op jit(solution)/shard_map/push_other/pallas_call | solution.py:266
  42.9 1.5 %collective-permute-start.13 = (bf16[64,1024]{1,0:T(8,128)(2,1)S(1)}, bf16[64,1024]{1,0:T(8,128)(2,1)S(1)}, u32[]{:S(2)}, u32[]{:S(2)}) collective-permute-start(bf16[64,1024]{1,0:T(8,128)(2,1)S(1)} %get-tuple-element.80), channel_id=1, source_target_pairs={{0,16},{8,24},{16,0},{24,8},{1,17},{9,25},{17,1},{25,9},{2,18},{10... | collective-permute-start | bytes 393224 | tf_op jit(solution)/shard_map/ppermute | solution.py:28
  45.0 0.7 %collective-permute-start.15 = (bf16[64,1536]{1,0:T(8,128)(2,1)S(1)}, bf16[64,1536]{1,0:T(8,128)(2,1)S(1)}, u32[]{:S(2)}, u32[]{:S(2)}) collective-permute-start(bf16[64,1536]{1,0:T(8,128)(2,1)S(1)} %get-tuple-element.84), channel_id=1, source_target_pairs={{0,16},{8,24},{16,0},{24,8},{1,17},{9,25},{17,1},{25,9},{2,18},{10... | collective-permute-start | bytes 589832 | tf_op jit(solution)/shard_map/ppermute | solution.py:28
  46.3 1.4 %collective-permute-start.12 = (bf16[64,1536]{1,0:T(8,128)(2,1)S(1)}, bf16[64,1536]{1,0:T(8,128)(2,1)S(1)}, u32[]{:S(2)}, u32[]{:S(2)}) collective-permute-start(bf16[64,1536]{1,0:T(8,128)(2,1)S(1)} %get-tuple-element.89), channel_id=1, source_target_pairs={{0,16},{8,24},{16,0},{24,8},{1,17},{9,25},{17,1},{25,9},{2,18},{10... | collective-permute-start | bytes 589832 | tf_op jit(solution)/shard_map/ppermute | solution.py:28
  47.7 1.6 %store_x.1 = f32[64,8192]{1,0:T(8,128)} custom-call(s32[1]{0:T(128)} %bitcast.side.token, f32[64,128]{1,0:T(8,128)S(1)} %get-tuple-element.52.scale.refs_0_, f32[64,8192]{1,0:T(8,128)S(1)} %get-tuple-element.53.x_ref, f32[64,8192]{1,0:T(8,128)S(1)} %get-tuple-element.54.u_ref, f32[64,8192]{1,0:T(8,128)S(1)} %get-tuple-element.55.z_ref, ...), custom_call_target="tpu_custom_call" | custom-call | flops 1000 | bytes 1000 | tf_op jit(solution)/shard_map/store_x/pallas_call | solution.py:300
  49.4 1.0 %final.4 = (f32[64,8192]{1,0:T(8,128)}, f32[64,8192]{1,0:T(8,128)}) custom-call(s32[1]{0:T(128)} %bitcast.side.token, f32[64,128]{1,0:T(8,128)S(1)} %get-tuple-element.52.scale.refs_0_, f32[64,8192]{1,0:T(8,128)S(1)} %get-tuple-element.53.x_ref, f32[64,8192]{1,0:T(8,128)S(1)} %get-tuple-element.54.u_ref, f32[64,8192]{1,0:T(8,128)S(1)} %get-tuple-element.55.z_ref, ...), custom_call_target="tpu_custom_call" | custom-call | flops 1000 | bytes 1000 | tf_op jit(solution)/shard_map/final/pallas_call | solution.py:350
  50.5 3.0 %collective-permute-done.15 = bf16[64,1536]{1,0:T(8,128)(2,1)S(1)} collective-permute-done((bf16[64,1536]{1,0:T(8,128)(2,1)S(1)}, bf16[64,1536]{1,0:T(8,128)(2,1)S(1)}, u32[]{:S(2)}, u32[]{:S(2)}) %collective-permute-start.15) | collective-permute-done | bytes 196640 | tf_op jit(solution)/shard_map/ppermute | solution.py:28
  53.6 1.5 %final.5 = (f32[64,8192]{1,0:T(8,128)}, f32[64,8192]{1,0:T(8,128)}) custom-call(s32[1]{0:T(128)} %bitcast.side.token, f32[64,128]{1,0:T(8,128)S(1)} %get-tuple-element.52.scale.refs_0_, f32[64,8192]{1,0:T(8,128)S(1)} %get-tuple-element.53.x_ref, f32[64,8192]{1,0:T(8,128)S(1)} %get-tuple-element.54.u_ref, ...), custom_call_target="tpu_custom_call", output_to_operand_aliasing={{0}: (11, {}), {1}: (12, {})} | custom-call | flops 1000 | bytes 1000 | tf_op jit(solution)/shard_map/final/pallas_call | solution.py:350
  55.2 2.1 %collective-permute-done.12 = bf16[64,1536]{1,0:T(8,128)(2,1)S(1)} collective-permute-done((bf16[64,1536]{1,0:T(8,128)(2,1)S(1)}, bf16[64,1536]{1,0:T(8,128)(2,1)S(1)}, u32[]{:S(2)}, u32[]{:S(2)}) %collective-permute-start.12) | collective-permute-done | bytes 196640 | tf_op jit(solution)/shard_map/ppermute | solution.py:28
  57.4 1.7 %final.6 = (f32[64,8192]{1,0:T(8,128)}, f32[64,8192]{1,0:T(8,128)}) custom-call(s32[1]{0:T(128)} %bitcast.side.token, f32[64,128]{1,0:T(8,128)S(1)} %get-tuple-element.52.scale.refs_0_, f32[64,8192]{1,0:T(8,128)S(1)} %get-tuple-element.53.x_ref, f32[64,8192]{1,0:T(8,128)S(1)} %get-tuple-element.54.u_ref, ...), custom_call_target="tpu_custom_call", output_to_operand_aliasing={{0}: (11, {}), {1}: (12, {})} | custom-call | flops 1000 | bytes 1000 | tf_op jit(solution)/shard_map/final/pallas_call | solution.py:350
  59.1 1.2 %final.7 = (f32[64,8192]{1,0:T(8,128)}, f32[64,8192]{1,0:T(8,128)}) custom-call(s32[1]{0:T(128)} %bitcast.side.token, f32[64,128]{1,0:T(8,128)S(1)} %get-tuple-element.52.scale.refs_0_, f32[64,8192]{1,0:T(8,128)S(1)} %get-tuple-element.53.x_ref, f32[64,8192]{1,0:T(8,128)S(1)} %get-tuple-element.54.u_ref, ...), custom_call_target="tpu_custom_call", output_to_operand_aliasing={{0}: (8, {}), {1}: (9, {})} | custom-call | flops 1000 | bytes 1000 | tf_op jit(solution)/shard_map/final/pallas_call | solution.py:350
  (35 shorter events, 6.7 us)
Async XLA Ops:
  8.8 4.4 %collective-permute-start.1 = (f32[64,4096]{1,0:T(8,128)S(1)}, f32[64,4096]{1,0:T(8,128)S(1)}, u32[]{:S(2)}, u32[]{:S(2)}) collective-permute-start(f32[64,4096]{1,0:T(8,128)S(1)} %get-tuple-element.64), channel_id=1, source_target_pairs={{0,8},{8,0},{16,24},{24,16},{1,9},{9,1},{17,25},{25,17},{2,10},{10... | collective-permute-start | bytes 3145736 | tf_op jit(solution)/shard_map/ppermute | solution.py:28
  9.3 6.0 %collective-permute-start = (bf16[64,768]{1,0:T(8,128)(2,1)S(1)}, bf16[64,768]{1,0:T(8,128)(2,1)S(1)}, u32[]{:S(2)}, u32[]{:S(2)}) collective-permute-start(bf16[64,768]{1,0:T(8,128)(2,1)S(1)} %get-tuple-element.59), channel_id=1, source_target_pairs={{0,1},{1,0},{2,3},{3,2},{4,5},{5,4},{6,7},{7,6},{8,9},{9,8},{10,11... | collective-permute-start | bytes 294920 | tf_op jit(solution)/shard_map/ppermute | solution.py:28
  13.3 29.3 %collective-permute-start.10 = (f32[64,4096]{1,0:T(8,128)S(1)}, f32[64,4096]{1,0:T(8,128)S(1)}, u32[]{:S(2)}, u32[]{:S(2)}) collective-permute-start(f32[64,4096]{1,0:T(8,128)S(1)} %add.30), channel_id=1, source_target_pairs={{0,16},{8,24},{16,0},{24,8},{1,17},{9,25},{17,1},{25,9},{2,18},{10... | collective-permute-start | bytes 3145736 | tf_op jit(solution)/shard_map/ppermute | solution.py:28
  15.4 4.7 %collective-permute-start.2 = (bf16[64,768]{1,0:T(8,128)(2,1)S(1)}, bf16[64,768]{1,0:T(8,128)(2,1)S(1)}, u32[]{:S(2)}, u32[]{:S(2)}) collective-permute-start(bf16[64,768]{1,0:T(8,128)(2,1)S(1)} %add_convert_fusion.5), channel_id=1, source_target_pairs={{0,2},{1,3},{2,0},{3,1},{4,6},{5,7},{6,4},{7,5},{8,10},{9,11},{10,... | collective-permute-start | bytes 294920 | tf_op jit(solution)/shard_map/ppermute | solution.py:28
  20.1 6.4 %collective-permute-start.3 = (bf16[64,768]{1,0:T(8,128)(2,1)S(1)}, bf16[64,768]{1,0:T(8,128)(2,1)S(1)}, u32[]{:S(2)}, u32[]{:S(2)}) collective-permute-start(bf16[64,768]{1,0:T(8,128)(2,1)S(1)} %add_convert_fusion.4.refs_6_), channel_id=1, source_target_pairs={{0,4},{1,5},{2,6},{3,7},{4,0},{5,1},{6,2},{7,3},{8,12},{9,13},{10,... | collective-permute-start | bytes 294920 | tf_op jit(solution)/shard_map/ppermute | solution.py:28
  27.1 5.7 %collective-permute-start.6 = (bf16[64,768]{1,0:T(8,128)(2,1)S(1)}, bf16[64,768]{1,0:T(8,128)(2,1)S(1)}, u32[]{:S(2)}, u32[]{:S(2)}) collective-permute-start(bf16[64,768]{1,0:T(8,128)(2,1)S(1)} %get-tuple-element.74), channel_id=1, source_target_pairs={{0,3},{1,2},{2,1},{3,0},{4,7},{5,6},{6,5},{7,4},{8,11},{9,10},{10,... | collective-permute-start | bytes 294920 | tf_op jit(solution)/shard_map/ppermute | solution.py:28
  29.7 4.6 %collective-permute-start.5 = (bf16[64,768]{1,0:T(8,128)(2,1)S(1)}, bf16[64,768]{1,0:T(8,128)(2,1)S(1)}, u32[]{:S(2)}, u32[]{:S(2)}) collective-permute-start(bf16[64,768]{1,0:T(8,128)(2,1)S(1)} %get-tuple-element.74), channel_id=1, source_target_pairs={{0,2},{1,3},{2,0},{3,1},{4,6},{5,7},{6,4},{7,5},{8,10},{9,11},{10,... | collective-permute-start | bytes 294920 | tf_op jit(solution)/shard_map/ppermute | solution.py:28
  30.1 4.6 %collective-permute-start.4 = (bf16[64,768]{1,0:T(8,128)(2,1)S(1)}, bf16[64,768]{1,0:T(8,128)(2,1)S(1)}, u32[]{:S(2)}, u32[]{:S(2)}) collective-permute-start(bf16[64,768]{1,0:T(8,128)(2,1)S(1)} %get-tuple-element.74), channel_id=1, source_target_pairs={{0,1},{1,0},{2,3},{3,2},{4,5},{5,4},{6,7},{7,6},{8,9},{9,8},{10,11... | collective-permute-start | bytes 294920 | tf_op jit(solution)/shard_map/ppermute | solution.py:28
  34.8 5.6 %collective-permute-start.7 = (bf16[64,768]{1,0:T(8,128)(2,1)S(1)}, bf16[64,768]{1,0:T(8,128)(2,1)S(1)}, u32[]{:S(2)}, u32[]{:S(2)}) collective-permute-start(bf16[64,768]{1,0:T(8,128)(2,1)S(1)} %add_convert_fusion.3.refs_4_), channel_id=1, source_target_pairs={{0,4},{1,5},{2,6},{3,7},{4,0},{5,1},{6,2},{7,3},{8,12},{9,13},{10,... | collective-permute-start | bytes 294920 | tf_op jit(solution)/shard_map/ppermute | solution.py:28
  40.8 1.5 %collective-permute-start.8 = (bf16[64,1024]{1,0:T(8,128)(2,1)S(1)}, bf16[64,1024]{1,0:T(8,128)(2,1)S(1)}, u32[]{:S(2)}, u32[]{:S(2)}) collective-permute-start(bf16[64,1024]{1,0:T(8,128)(2,1)S(1)} %get-tuple-element.78), channel_id=1, source_target_pairs={{0,8},{8,0},{16,24},{24,16},{1,9},{9,1},{17,25},{25,17},{2,10},{10... | collective-permute-start | bytes 393224 | tf_op jit(solution)/shard_map/ppermute | solution.py:28
  41.7 2.7 %collective-permute-start.9 = (bf16[64,3072]{1,0:T(8,128)(2,1)S(1)}, bf16[64,3072]{1,0:T(8,128)(2,1)S(1)}, u32[]{:S(2)}, u32[]{:S(2)}) collective-permute-start(bf16[64,3072]{1,0:T(8,128)(2,1)S(1)} %get-tuple-element.82), channel_id=1, source_target_pairs={{0,8},{8,0},{16,24},{24,16},{1,9},{9,1},{17,25},{25,17},{2,10},{10... | collective-permute-start | bytes 1179656 | tf_op jit(solution)/shard_map/ppermute | solution.py:28
  42.8 10.8 %collective-permute-start.11 = (f32[64,4096]{1,0:T(8,128)S(1)}, f32[64,4096]{1,0:T(8,128)S(1)}, u32[]{:S(2)}, u32[]{:S(2)}) collective-permute-start(f32[64,4096]{1,0:T(8,128)S(1)} %add.36.refs_0_.refs_3_), channel_id=1, source_target_pairs={{0,8},{8,0},{16,24},{24,16},{1,9},{9,1},{17,25},{25,17},{2,10},{10... | collective-permute-start | bytes 3145736 | tf_op jit(solution)/shard_map/ppermute | solution.py:28
  42.9 6.4 %collective-permute-start.13 = (bf16[64,1024]{1,0:T(8,128)(2,1)S(1)}, bf16[64,1024]{1,0:T(8,128)(2,1)S(1)}, u32[]{:S(2)}, u32[]{:S(2)}) collective-permute-start(bf16[64,1024]{1,0:T(8,128)(2,1)S(1)} %get-tuple-element.80), channel_id=1, source_target_pairs={{0,16},{8,24},{16,0},{24,8},{1,17},{9,25},{17,1},{25,9},{2,18},{10... | collective-permute-start | bytes 393224 | tf_op jit(solution)/shard_map/ppermute | solution.py:28
  45.0 8.5 %collective-permute-start.15 = (bf16[64,1536]{1,0:T(8,128)(2,1)S(1)}, bf16[64,1536]{1,0:T(8,128)(2,1)S(1)}, u32[]{:S(2)}, u32[]{:S(2)}) collective-permute-start(bf16[64,1536]{1,0:T(8,128)(2,1)S(1)} %get-tuple-element.84), channel_id=1, source_target_pairs={{0,16},{8,24},{16,0},{24,8},{1,17},{9,25},{17,1},{25,9},{2,18},{10... | collective-permute-start | bytes 589832 | tf_op jit(solution)/shard_map/ppermute | solution.py:28
  46.3 11.0 %collective-permute-start.12 = (bf16[64,1536]{1,0:T(8,128)(2,1)S(1)}, bf16[64,1536]{1,0:T(8,128)(2,1)S(1)}, u32[]{:S(2)}, u32[]{:S(2)}) collective-permute-start(bf16[64,1536]{1,0:T(8,128)(2,1)S(1)} %get-tuple-element.89), channel_id=1, source_target_pairs={{0,16},{8,24},{16,0},{24,8},{1,17},{9,25},{17,1},{25,9},{2,18},{10... | collective-permute-start | bytes 589832 | tf_op jit(solution)/shard_map/ppermute | solution.py:28
  49.4 4.2 %collective-permute-start.14 = (bf16[64,1024]{1,0:T(8,128)(2,1)S(1)}, bf16[64,1024]{1,0:T(8,128)(2,1)S(1)}, u32[]{:S(2)}, u32[]{:S(2)}) collective-permute-start(bf16[64,1024]{1,0:T(8,128)(2,1)S(1)} %add_convert_fusion.2.refs_2_), channel_id=1, source_target_pairs={{0,8},{8,0},{16,24},{24,16},{1,9},{9,1},{17,25},{25,17},{2,10},{10... | collective-permute-start | bytes 393224 | tf_op jit(solution)/shard_map/ppermute | solution.py:28
  53.5 3.8 %collective-permute-start.17 = (bf16[64,1536]{1,0:T(8,128)(2,1)S(1)}, bf16[64,1536]{1,0:T(8,128)(2,1)S(1)}, u32[]{:S(2)}, u32[]{:S(2)}) collective-permute-start(bf16[64,1536]{1,0:T(8,128)(2,1)S(1)} %add_convert_fusion.1.refs_5_), channel_id=1, source_target_pairs={{0,8},{8,0},{16,24},{24,16},{1,9},{9,1},{17,25},{25,17},{2,10},{10... | collective-permute-start | bytes 589832 | tf_op jit(solution)/shard_map/ppermute | solution.py:28
  57.3 1.8 %collective-permute-start.16 = (bf16[64,1536]{1,0:T(8,128)(2,1)S(1)}, bf16[64,1536]{1,0:T(8,128)(2,1)S(1)}, u32[]{:S(2)}, u32[]{:S(2)}) collective-permute-start(bf16[64,1536]{1,0:T(8,128)(2,1)S(1)} %add_convert_fusion.refs_5_), channel_id=1, source_target_pairs={{0,8},{8,0},{16,24},{24,16},{1,9},{9,1},{17,25},{25,17},{2,10},{10... | collective-permute-start | bytes 589832 | tf_op jit(solution)/shard_map/ppermute | solution.py:28

commit v10 on v9

--- a/solution.py
+++ b/solution.py
@@ -10,14 +10,13 @@
 
 BF16 = jnp.bfloat16
 F32 = jnp.float32
-MINE = (2, 3, 3)
-OTHER = (2, 6)
+MINE = (3, 5)
+OTHER = (3, 5)
 STEP = 1024
 WIDE = 2048
 AHEAD = 4
 NARROW = 256
 WAIT_BYTES = 10_000_000
-GRAM_ORDER = (0, 1, 2)
 HBM = pl.BlockSpec(memory_space=pltpu.HBM)
 VMEM = pl.BlockSpec(memory_space=pltpu.VMEM)
 SMEM = pl.BlockSpec(memory_space=pltpu.SMEM)
@@ -39,15 +38,19 @@
     return value, other
 
 
+def sum_terms(terms):
+    return sum(t.astype(F32) for t in terms).astype(BF16)
+
+
+def square_stage(value, axis, mask):
+    steps = [mask, 2 * mask, 3 * mask] if 2 * mask < lax.axis_size(axis) else [mask]
+    return [value] + [exchange(value, axis, step) for step in steps]
+
+
 def square_sum(value, axis):
-    n = lax.axis_size(axis)
-    terms = [value]
-    mask = 1
-    while mask < n:
-        if len(terms) > 1:
-            terms = [sum(t.astype(F32) for t in terms).astype(value.dtype)]
-        steps = [mask, 2 * mask, 3 * mask] if 2 * mask < n else [mask]
-        terms += [exchange(terms[0], axis, step) for step in steps]
+    terms, mask = square_stage(value, axis, 1), 4
+    while mask < lax.axis_size(axis):
+        terms = square_stage(sum_terms(terms), axis, mask)
         mask *= 4
     return terms
 
@@ -373,18 +376,23 @@
     )
     start_mine = start_mine + exchange(start_other, "rows", 1)
 
-    terms, grams = [margin1], []
-    for step in range(max(lax.axis_size("feat").bit_length() - 1, 3)):
-        more = (1 << step) < lax.axis_size("feat")
-        if step > 0 and more:
-            terms = [sum(t.astype(F32) for t in terms).astype(BF16)]
-        row = gram_row(GRAM_ORDER[step], tie(side, terms[0]), design) if step < 3 else []
-        grams.append(row)
-        if more:
-            got = exchange(terms[0], "feat", 1 << step)
-            terms.append(tie(got, row[0], start_mine) if step == 0 else tie(got, row[0]) if step == 1 else got)
-
-    resid1, margin2 = turn(sign, terms, scale, pulled, [g for row in range(3) for g in grams[GRAM_ORDER.index(row)]])
+    half_rows = [gram_row(row, side, design) for row in range(2)]
+    terms = square_stage(margin1, "feat", 1)
+    terms = [terms[0]] + [tie(t, half_rows, start_mine) for t in terms[1:]]
+    stage, mask = terms, 4
+    last_row = None
+    while mask < lax.axis_size("feat"):
+        value = sum_terms(stage)
+        if last_row is None:
+            last_row = gram_row(2, tie(side, value), design)
+        stage = square_stage(value, "feat", mask)
+        mask *= 4
+    terms = stage
+    if last_row is None:
+        last_row = gram_row(2, side, design)
+    grams = [*half_rows[0], *half_rows[1], *last_row]
+
+    resid1, margin2 = turn(sign, terms, scale, pulled, grams)
     terms = square_sum(margin2, "feat")
     mask = 2
     while mask < blocks_count:
@@ -421,10 +429,12 @@
         piece = (a.astype(F32) + b.astype(F32)).astype(BF16)
         source, offset = places[c]
         back = exchange(piece, "rows", 1)
-        ready = waiting + [(True, begins[c], 0, start_mine, mines[c], piece)]
-        results = final(side, scale, x0, dual, z, ready, results, blocks_count)
-        waiting = [(False, begins[c], offset, start_theirs, others[source], back)]
-    results = final(side, scale, x0, dual, z, waiting, results, blocks_count)
+        results = final(
+            side, scale, x0, dual, z, [(True, begins[c], 0, start_mine, mines[c], piece)], results, blocks_count
+        )
+        results = final(
+            side, scale, x0, dual, z, [(False, begins[c], offset, start_theirs, others[source], back)], results, blocks_count
+        )
     new_z, new_u = results
     return (new_x[None], new_z, new_u[None])
 

time: 60.5 us -> 62.7 us (1.036)
  waiting for transfers between devices: 13.1 us -> 16.4 us
  starting transfers between devices: 20.2 us -> 19.3 us
    ppermute x18 -> x17, waiting for transfers between devices: 13.1 us -> 16.4 us  [exchange(): return lax.ppermute(value, axis, [(i, i ^ mask) for i in range(n)])]
    ppermute x18 -> x17, starting transfers between devices: 20.2 us -> 19.3 us  [exchange(): return lax.ppermute(value, axis, [(i, i ^ mask) for i in range(n)])]
    pallas_call x5 -> x4, Pallas kernels: 2.72 us -> 2.56 us  [push(): call(functools.partial(push_kernel, first, mine, begin, offset, size), 'p...]
  transfers between devices with their start and end apart: 18 -> 17, of which waited for: 8 -> 11; matrix products, arithmetic and copies ran while one was open for 1% -> 0% of each run, Pallas kernels for 27% -> 25%
where the time goes in v10:
time: 62.7 us; the launch traced here: 62.5 us
  Pallas kernels  25.5 us (41%)
  starting transfers between devices  19.3 us (31%)
  waiting for transfers between devices  16.4 us (26%)
  between operations  0.83 us (1%)
    ppermute x17, starting transfers between devices, exchange(): return lax.ppermute(value, axis, [(i, i ^ mask) for i in range(n)])  19.3 us
    ppermute x17, waiting for transfers between devices, exchange(): return lax.ppermute(value, axis, [(i, i ^ mask) for i in range(n)])  16.4 us
    pallas_call x1, Pallas kernels, load(): call(functools.partial(load_kernel, blocks_count), 'load_and_margins', [S...  8.18 us
    pallas_call x3, Pallas kernels, gram_row(): call(functools.partial(gram_kernel, row), 'gram', [SMEM, VMEM], (out, out...  7.09 us
    pallas_call x4, Pallas kernels, final(): call(functools.partial(final_kernel, blocks_count, places, buffered), 'fi...  5.44 us
    pallas_call x4, Pallas kernels, push(): call(functools.partial(push_kernel, first, mine, begin, offset, size), 'p...  2.56 us
    pallas_call x1, Pallas kernels, store_x(): call(store_kernel, 'store_x', [SMEM] + [VMEM] * len(args), pltpu.HBM((tas...  1.6 us
  transfers between devices with their start and end apart: 17, of which 11 were waited for; matrix products, arithmetic and copies ran while one was open for 0% of the time, Pallas kernels for 25%

profile of v10, /device:TPU:0, one launch (start us, length us, event | category | flops | bytes accessed | tf_op | source)
XLA Modules:
  0.0 62.5 jit_solution(9912522982478426914)
XLA Ops:
  0.6 8.2 %load_and_margins.1 = (bf16[64,768]{1,0:T(8,128)(2,1)S(1)}, f32[64,768]{1,0:T(8,128)S(1)}, bf16[768,8192]{1,0:T(8,128)(2,1)S(1)}, f32[64,8192]{1,0:T(8,128)S(1)}...) custom-call(s32[1]{0:T(128)} %bitcast.side.token, ...), custom_call_target="tpu_custom_call" | custom-call | flops 1000 | bytes 1000 | tf_op jit(solution)/shard_map/load_and_margins/pallas_call | solution.py:154
  9.3 2.6 %collective-permute-start = (bf16[64,768]{1,0:T(8,128)(2,1)S(1)}, bf16[64,768]{1,0:T(8,128)(2,1)S(1)}, u32[]{:S(2)}, u32[]{:S(2)}) collective-permute-start(bf16[64,768]{1,0:T(8,128)(2,1)S(1)} %get-tuple-element.58), channel_id=1, source_target_pairs={{0,1},{1,0},{2,3},{3,2},{4,5},{5,4},{6,7},{7,6},{8,9},{9,8},{10,11... | collective-permute-start | bytes 294920 | tf_op jit(solution)/shard_map/ppermute | solution.py:27
  11.9 1.6 %collective-permute-start.2 = (bf16[64,768]{1,0:T(8,128)(2,1)S(1)}, bf16[64,768]{1,0:T(8,128)(2,1)S(1)}, u32[]{:S(2)}, u32[]{:S(2)}) collective-permute-start(bf16[64,768]{1,0:T(8,128)(2,1)S(1)} %get-tuple-element.58), channel_id=1, source_target_pairs={{0,2},{1,3},{2,0},{3,1},{4,6},{5,7},{6,4},{7,5},{8,10},{9,11},{10,... | collective-permute-start | bytes 294920 | tf_op jit(solution)/shard_map/ppermute | solution.py:27
  13.6 1.9 %collective-permute-start.11 = (f32[64,4096]{1,0:T(8,128)S(1)}, f32[64,4096]{1,0:T(8,128)S(1)}, u32[]{:S(2)}, u32[]{:S(2)}) collective-permute-start(f32[64,4096]{1,0:T(8,128)S(1)} %add.30), channel_id=1, source_target_pairs={{0,16},{8,24},{16,0},{24,8},{1,17},{9,25},{17,1},{25,9},{2,18},{10... | collective-permute-start | bytes 3145736 | tf_op jit(solution)/shard_map/ppermute | solution.py:27
  15.6 2.4 %gram.4 = (bf16[256,512]{1,0:T(8,128)(2,1)S(1)}, bf16[256,512]{1,0:T(8,128)(2,1)S(1)}) custom-call(s32[1]{0:T(128)} %bitcast.side.token, bf16[768,8192]{1,0:T(8,128)(2,1)S(1)} %get-tuple-element.51.a_ref.refs_1_), custom_call_target="tpu_custom_call" | custom-call | flops 1000 | bytes 6666666 | tf_op jit(solution)/shard_map/gram/pallas_call | solution.py:193
  17.9 1.3 %gram.3 = (bf16[256,256]{1,0:T(8,128)(2,1)S(1)}, bf16[256,256]{1,0:T(8,128)(2,1)S(1)}) custom-call(s32[1]{0:T(128)} %bitcast.side.token, bf16[768,8192]{1,0:T(8,128)(2,1)S(1)} %get-tuple-element.51.a_ref.refs_1_), custom_call_target="tpu_custom_call" | custom-call | flops 1000 | bytes 3333333 | tf_op jit(solution)/shard_map/gram/pallas_call | solution.py:193
  19.3 2.7 %collective-permute-start.4 = (bf16[64,768]{1,0:T(8,128)(2,1)S(1)}, bf16[64,768]{1,0:T(8,128)(2,1)S(1)}, u32[]{:S(2)}, u32[]{:S(2)}) collective-permute-start(bf16[64,768]{1,0:T(8,128)(2,1)S(1)} %add_convert_fusion.3.refs_6_), channel_id=1, source_target_pairs={{0,4},{1,5},{2,6},{3,7},{4,0},{5,1},{6,2},{7,3},{8,12},{9,13},{10,... | collective-permute-start | bytes 294920 | tf_op jit(solution)/shard_map/ppermute | solution.py:27
  22.0 3.5 %gram.5 = (bf16[256,768]{1,0:T(8,128)(2,1)S(1)}, bf16[256,768]{1,0:T(8,128)(2,1)S(1)}) custom-call(s32[1]{0:T(128)} %bitcast.side.token, bf16[768,8192]{1,0:T(8,128)(2,1)S(1)} %get-tuple-element.51.a_ref.refs_1_), custom_call_target="tpu_custom_call" | custom-call | flops 1000 | bytes 10000000 | tf_op jit(solution)/shard_map/gram/pallas_call | solution.py:193
  27.0 1.6 %collective-permute-start.5 = (bf16[64,768]{1,0:T(8,128)(2,1)S(1)}, bf16[64,768]{1,0:T(8,128)(2,1)S(1)}, u32[]{:S(2)}, u32[]{:S(2)}) collective-permute-start(bf16[64,768]{1,0:T(8,128)(2,1)S(1)} %get-tuple-element.68), channel_id=1, source_target_pairs={{0,1},{1,0},{2,3},{3,2},{4,5},{5,4},{6,7},{7,6},{8,9},{9,8},{10,11... | collective-permute-start | bytes 294920 | tf_op jit(solution)/shard_map/ppermute | solution.py:27
  29.3 1.3 %collective-permute-start.7 = (bf16[64,768]{1,0:T(8,128)(2,1)S(1)}, bf16[64,768]{1,0:T(8,128)(2,1)S(1)}, u32[]{:S(2)}, u32[]{:S(2)}) collective-permute-start(bf16[64,768]{1,0:T(8,128)(2,1)S(1)} %get-tuple-element.68), channel_id=1, source_target_pairs={{0,3},{1,2},{2,1},{3,0},{4,7},{5,6},{6,5},{7,4},{8,11},{9,10},{10,... | collective-permute-start | bytes 294920 | tf_op jit(solution)/shard_map/ppermute | solution.py:27
  30.6 2.0 %collective-permute-done.5 = bf16[64,768]{1,0:T(8,128)(2,1)S(1)} collective-permute-done((bf16[64,768]{1,0:T(8,128)(2,1)S(1)}, bf16[64,768]{1,0:T(8,128)(2,1)S(1)}, u32[]{:S(2)}, u32[]{:S(2)}) %collective-permute-start.5) | collective-permute-done | bytes 98336 | tf_op jit(solution)/shard_map/ppermute | solution.py:27
  33.2 1.6 %collective-permute-done.7 = bf16[64,768]{1,0:T(8,128)(2,1)S(1)} collective-permute-done((bf16[64,768]{1,0:T(8,128)(2,1)S(1)}, bf16[64,768]{1,0:T(8,128)(2,1)S(1)}, u32[]{:S(2)}, u32[]{:S(2)}) %collective-permute-start.7) | collective-permute-done | bytes 98336 | tf_op jit(solution)/shard_map/ppermute | solution.py:27
  34.9 3.4 %collective-permute-start.8 = (bf16[64,768]{1,0:T(8,128)(2,1)S(1)}, bf16[64,768]{1,0:T(8,128)(2,1)S(1)}, u32[]{:S(2)}, u32[]{:S(2)}) collective-permute-start(bf16[64,768]{1,0:T(8,128)(2,1)S(1)} %add_convert_fusion.2.refs_4_), channel_id=1, source_target_pairs={{0,4},{1,5},{2,6},{3,7},{4,0},{5,1},{6,2},{7,3},{8,12},{9,13},{10,... | collective-permute-start | bytes 294920 | tf_op jit(solution)/shard_map/ppermute | solution.py:27
  38.3 3.6 %collective-permute-done.8.refs_5_ = bf16[64,768]{1,0:T(8,128)(2,1)S(1)} collective-permute-done((bf16[64,768]{1,0:T(8,128)(2,1)S(1)}, bf16[64,768]{1,0:T(8,128)(2,1)S(1)}, u32[]{:S(2)}, u32[]{:S(2)}) %collective-permute-start.8) | collective-permute-done | bytes 98336 | tf_op jit(solution)/shard_map/ppermute | solution.py:27
  45.2 1.1 %collective-permute-start.14 = (bf16[64,1536]{1,0:T(8,128)(2,1)S(1)}, bf16[64,1536]{1,0:T(8,128)(2,1)S(1)}, u32[]{:S(2)}, u32[]{:S(2)}) collective-permute-start(bf16[64,1536]{1,0:T(8,128)(2,1)S(1)} %get-tuple-element.74), channel_id=1, source_target_pairs={{0,16},{8,24},{16,0},{24,8},{1,17},{9,25},{17,1},{25,9},{2,18},{10... | collective-permute-start | bytes 589832 | tf_op jit(solution)/shard_map/ppermute | solution.py:27
  46.3 1.5 %collective-permute-done.10.refs_3_ = bf16[64,2560]{1,0:T(8,128)(2,1)S(1)} collective-permute-done((bf16[64,2560]{1,0:T(8,128)(2,1)S(1)}, bf16[64,2560]{1,0:T(8,128)(2,1)S(1)}, u32[]{:S(2)}, u32[]{:S(2)}) %collective-permute-start.10) | collective-permute-done | bytes 327712 | tf_op jit(solution)/shard_map/ppermute | solution.py:27
  48.6 1.2 %collective-permute-start.13 = (bf16[64,2560]{1,0:T(8,128)(2,1)S(1)}, bf16[64,2560]{1,0:T(8,128)(2,1)S(1)}, u32[]{:S(2)}, u32[]{:S(2)}) collective-permute-start(bf16[64,2560]{1,0:T(8,128)(2,1)S(1)} %get-tuple-element.80), channel_id=1, source_target_pairs={{0,16},{8,24},{16,0},{24,8},{1,17},{9,25},{17,1},{25,9},{2,18},{10... | collective-permute-start | bytes 983048 | tf_op jit(solution)/shard_map/ppermute | solution.py:27
  49.8 1.6 %store_x.1 = f32[64,8192]{1,0:T(8,128)} custom-call(s32[1]{0:T(128)} %bitcast.side.token, f32[64,128]{1,0:T(8,128)S(1)} %get-tuple-element.47.scale.refs_0_, f32[64,8192]{1,0:T(8,128)S(1)} %get-tuple-element.48.x_ref, f32[64,8192]{1,0:T(8,128)S(1)} %get-tuple-element.49.u_ref, f32[64,8192]{1,0:T(8,128)S(1)} %get-tuple-element.50.z_ref, ...), custom_call_target="tpu_custom_call" | custom-call | flops 1000 | bytes 1000 | tf_op jit(solution)/shard_map/store_x/pallas_call | solution.py:303
  51.4 1.5 %collective-permute-done.14 = bf16[64,1536]{1,0:T(8,128)(2,1)S(1)} collective-permute-done((bf16[64,1536]{1,0:T(8,128)(2,1)S(1)}, bf16[64,1536]{1,0:T(8,128)(2,1)S(1)}, u32[]{:S(2)}, u32[]{:S(2)}) %collective-permute-start.14) | collective-permute-done | bytes 196640 | tf_op jit(solution)/shard_map/ppermute | solution.py:27
  53.0 1.2 %final.4 = (f32[64,8192]{1,0:T(8,128)}, f32[64,8192]{1,0:T(8,128)}) custom-call(s32[1]{0:T(128)} %bitcast.side.token, f32[64,128]{1,0:T(8,128)S(1)} %get-tuple-element.47.scale.refs_0_, f32[64,8192]{1,0:T(8,128)S(1)} %get-tuple-element.48.x_ref, f32[64,8192]{1,0:T(8,128)S(1)} %get-tuple-element.49.u_ref, f32[64,8192]{1,0:T(8,128)S(1)} %get-tuple-element.50.z_ref, ...), custom_call_target="tpu_custom_call" | custom-call | flops 1000 | bytes 1000 | tf_op jit(solution)/shard_map/final/pallas_call | solution.py:353
  54.4 1.2 %final.5 = (f32[64,8192]{1,0:T(8,128)}, f32[64,8192]{1,0:T(8,128)}) custom-call(s32[1]{0:T(128)} %bitcast.side.token, f32[64,128]{1,0:T(8,128)S(1)} %get-tuple-element.47.scale.refs_0_, f32[64,8192]{1,0:T(8,128)S(1)} %get-tuple-element.48.x_ref, f32[64,8192]{1,0:T(8,128)S(1)} %get-tuple-element.49.u_ref, ...), custom_call_target="tpu_custom_call", output_to_operand_aliasing={{0}: (8, {}), {1}: (9, {})} | custom-call | flops 1000 | bytes 1000 | tf_op jit(solution)/shard_map/final/pallas_call | solution.py:353
  55.6 3.6 %collective-permute-done.13 = bf16[64,2560]{1,0:T(8,128)(2,1)S(1)} collective-permute-done((bf16[64,2560]{1,0:T(8,128)(2,1)S(1)}, bf16[64,2560]{1,0:T(8,128)(2,1)S(1)}, u32[]{:S(2)}, u32[]{:S(2)}) %collective-permute-start.13) | collective-permute-done | bytes 327712 | tf_op jit(solution)/shard_map/ppermute | solution.py:27
  59.4 1.5 %final.6 = (f32[64,8192]{1,0:T(8,128)}, f32[64,8192]{1,0:T(8,128)}) custom-call(s32[1]{0:T(128)} %bitcast.side.token, f32[64,128]{1,0:T(8,128)S(1)} %get-tuple-element.47.scale.refs_0_, f32[64,8192]{1,0:T(8,128)S(1)} %get-tuple-element.48.x_ref, f32[64,8192]{1,0:T(8,128)S(1)} %get-tuple-element.49.u_ref, ...), custom_call_target="tpu_custom_call", output_to_operand_aliasing={{0}: (8, {}), {1}: (9, {})} | custom-call | flops 1000 | bytes 1000 | tf_op jit(solution)/shard_map/final/pallas_call | solution.py:353
  61.0 1.5 %final.7 = (f32[64,8192]{1,0:T(8,128)}, f32[64,8192]{1,0:T(8,128)}) custom-call(s32[1]{0:T(128)} %bitcast.side.token, f32[64,128]{1,0:T(8,128)S(1)} %get-tuple-element.47.scale.refs_0_, f32[64,8192]{1,0:T(8,128)S(1)} %get-tuple-element.48.x_ref, f32[64,8192]{1,0:T(8,128)S(1)} %get-tuple-element.49.u_ref, ...), custom_call_target="tpu_custom_call", output_to_operand_aliasing={{0}: (8, {}), {1}: (9, {})} | custom-call | flops 1000 | bytes 1000 | tf_op jit(solution)/shard_map/final/pallas_call | solution.py:353
  (30 shorter events, 8.2 us)
Async XLA Ops:
  8.8 4.7 %collective-permute-start.1 = (f32[64,4096]{1,0:T(8,128)S(1)}, f32[64,4096]{1,0:T(8,128)S(1)}, u32[]{:S(2)}, u32[]{:S(2)}) collective-permute-start(f32[64,4096]{1,0:T(8,128)S(1)} %get-tuple-element.60), channel_id=1, source_target_pairs={{0,8},{8,0},{16,24},{24,16},{1,9},{9,1},{17,25},{25,17},{2,10},{10... | collective-permute-start | bytes 3145736 | tf_op jit(solution)/shard_map/ppermute | solution.py:27
  9.3 9.9 %collective-permute-start = (bf16[64,768]{1,0:T(8,128)(2,1)S(1)}, bf16[64,768]{1,0:T(8,128)(2,1)S(1)}, u32[]{:S(2)}, u32[]{:S(2)}) collective-permute-start(bf16[64,768]{1,0:T(8,128)(2,1)S(1)} %get-tuple-element.58), channel_id=1, source_target_pairs={{0,1},{1,0},{2,3},{3,2},{4,5},{5,4},{6,7},{7,6},{8,9},{9,8},{10,11... | collective-permute-start | bytes 294920 | tf_op jit(solution)/shard_map/ppermute | solution.py:27
  11.9 7.3 %collective-permute-start.2 = (bf16[64,768]{1,0:T(8,128)(2,1)S(1)}, bf16[64,768]{1,0:T(8,128)(2,1)S(1)}, u32[]{:S(2)}, u32[]{:S(2)}) collective-permute-start(bf16[64,768]{1,0:T(8,128)(2,1)S(1)} %get-tuple-element.58), channel_id=1, source_target_pairs={{0,2},{1,3},{2,0},{3,1},{4,6},{5,7},{6,4},{7,5},{8,10},{9,11},{10,... | collective-permute-start | bytes 294920 | tf_op jit(solution)/shard_map/ppermute | solution.py:27
  13.5 5.7 %collective-permute-start.3 = (bf16[64,768]{1,0:T(8,128)(2,1)S(1)}, bf16[64,768]{1,0:T(8,128)(2,1)S(1)}, u32[]{:S(2)}, u32[]{:S(2)}) collective-permute-start(bf16[64,768]{1,0:T(8,128)(2,1)S(1)} %get-tuple-element.58), channel_id=1, source_target_pairs={{0,3},{1,2},{2,1},{3,0},{4,7},{5,6},{6,5},{7,4},{8,11},{9,10},{10,... | collective-permute-start | bytes 294920 | tf_op jit(solution)/shard_map/ppermute | solution.py:27
  13.6 30.9 %collective-permute-start.11 = (f32[64,4096]{1,0:T(8,128)S(1)}, f32[64,4096]{1,0:T(8,128)S(1)}, u32[]{:S(2)}, u32[]{:S(2)}) collective-permute-start(f32[64,4096]{1,0:T(8,128)S(1)} %add.30), channel_id=1, source_target_pairs={{0,16},{8,24},{16,0},{24,8},{1,17},{9,25},{17,1},{25,9},{2,18},{10... | collective-permute-start | bytes 3145736 | tf_op jit(solution)/shard_map/ppermute | solution.py:27
  19.3 7.1 %collective-permute-start.4 = (bf16[64,768]{1,0:T(8,128)(2,1)S(1)}, bf16[64,768]{1,0:T(8,128)(2,1)S(1)}, u32[]{:S(2)}, u32[]{:S(2)}) collective-permute-start(bf16[64,768]{1,0:T(8,128)(2,1)S(1)} %add_convert_fusion.3.refs_6_), channel_id=1, source_target_pairs={{0,4},{1,5},{2,6},{3,7},{4,0},{5,1},{6,2},{7,3},{8,12},{9,13},{10,... | collective-permute-start | bytes 294920 | tf_op jit(solution)/shard_map/ppermute | solution.py:27
  27.0 5.6 %collective-permute-start.5 = (bf16[64,768]{1,0:T(8,128)(2,1)S(1)}, bf16[64,768]{1,0:T(8,128)(2,1)S(1)}, u32[]{:S(2)}, u32[]{:S(2)}) collective-permute-start(bf16[64,768]{1,0:T(8,128)(2,1)S(1)} %get-tuple-element.68), channel_id=1, source_target_pairs={{0,1},{1,0},{2,3},{3,2},{4,5},{5,4},{6,7},{7,6},{8,9},{9,8},{10,11... | collective-permute-start | bytes 294920 | tf_op jit(solution)/shard_map/ppermute | solution.py:27
  28.6 4.6 %collective-permute-start.6 = (bf16[64,768]{1,0:T(8,128)(2,1)S(1)}, bf16[64,768]{1,0:T(8,128)(2,1)S(1)}, u32[]{:S(2)}, u32[]{:S(2)}) collective-permute-start(bf16[64,768]{1,0:T(8,128)(2,1)S(1)} %get-tuple-element.68), channel_id=1, source_target_pairs={{0,2},{1,3},{2,0},{3,1},{4,6},{5,7},{6,4},{7,5},{8,10},{9,11},{10,... | collective-permute-start | bytes 294920 | tf_op jit(solution)/shard_map/ppermute | solution.py:27
  29.3 5.5 %collective-permute-start.7 = (bf16[64,768]{1,0:T(8,128)(2,1)S(1)}, bf16[64,768]{1,0:T(8,128)(2,1)S(1)}, u32[]{:S(2)}, u32[]{:S(2)}) collective-permute-start(bf16[64,768]{1,0:T(8,128)(2,1)S(1)} %get-tuple-element.68), channel_id=1, source_target_pairs={{0,3},{1,2},{2,1},{3,0},{4,7},{5,6},{6,5},{7,4},{8,11},{9,10},{10,... | collective-permute-start | bytes 294920 | tf_op jit(solution)/shard_map/ppermute | solution.py:27
  34.9 7.1 %collective-permute-start.8 = (bf16[64,768]{1,0:T(8,128)(2,1)S(1)}, bf16[64,768]{1,0:T(8,128)(2,1)S(1)}, u32[]{:S(2)}, u32[]{:S(2)}) collective-permute-start(bf16[64,768]{1,0:T(8,128)(2,1)S(1)} %add_convert_fusion.2.refs_4_), channel_id=1, source_target_pairs={{0,4},{1,5},{2,6},{3,7},{4,0},{5,1},{6,2},{7,3},{8,12},{9,13},{10,... | collective-permute-start | bytes 294920 | tf_op jit(solution)/shard_map/ppermute | solution.py:27
  42.5 1.5 %collective-permute-start.9 = (bf16[64,1536]{1,0:T(8,128)(2,1)S(1)}, bf16[64,1536]{1,0:T(8,128)(2,1)S(1)}, u32[]{:S(2)}, u32[]{:S(2)}) collective-permute-start(bf16[64,1536]{1,0:T(8,128)(2,1)S(1)} %get-tuple-element.72), channel_id=1, source_target_pairs={{0,8},{8,0},{16,24},{24,16},{1,9},{9,1},{17,25},{25,17},{2,10},{10... | collective-permute-start | bytes 589832 | tf_op jit(solution)/shard_map/ppermute | solution.py:27
  44.7 9.8 %collective-permute-start.12 = (f32[64,4096]{1,0:T(8,128)S(1)}, f32[64,4096]{1,0:T(8,128)S(1)}, u32[]{:S(2)}, u32[]{:S(2)}) collective-permute-start(f32[64,4096]{1,0:T(8,128)S(1)} %add.37.refs_0_), channel_id=1, source_target_pairs={{0,8},{8,0},{16,24},{24,16},{1,9},{9,1},{17,25},{25,17},{2,10},{10... | collective-permute-start | bytes 3145736 | tf_op jit(solution)/shard_map/ppermute | solution.py:27
  44.9 3.0 %collective-permute-start.10 = (bf16[64,2560]{1,0:T(8,128)(2,1)S(1)}, bf16[64,2560]{1,0:T(8,128)(2,1)S(1)}, u32[]{:S(2)}, u32[]{:S(2)}) collective-permute-start(bf16[64,2560]{1,0:T(8,128)(2,1)S(1)} %get-tuple-element.76), channel_id=1, source_target_pairs={{0,8},{8,0},{16,24},{24,16},{1,9},{9,1},{17,25},{25,17},{2,10},{10... | collective-permute-start | bytes 983048 | tf_op jit(solution)/shard_map/ppermute | solution.py:27
  45.2 7.6 %collective-permute-start.14 = (bf16[64,1536]{1,0:T(8,128)(2,1)S(1)}, bf16[64,1536]{1,0:T(8,128)(2,1)S(1)}, u32[]{:S(2)}, u32[]{:S(2)}) collective-permute-start(bf16[64,1536]{1,0:T(8,128)(2,1)S(1)} %get-tuple-element.74), channel_id=1, source_target_pairs={{0,16},{8,24},{16,0},{24,8},{1,17},{9,25},{17,1},{25,9},{2,18},{10... | collective-permute-start | bytes 589832 | tf_op jit(solution)/shard_map/ppermute | solution.py:27
  48.6 10.6 %collective-permute-start.13 = (bf16[64,2560]{1,0:T(8,128)(2,1)S(1)}, bf16[64,2560]{1,0:T(8,128)(2,1)S(1)}, u32[]{:S(2)}, u32[]{:S(2)}) collective-permute-start(bf16[64,2560]{1,0:T(8,128)(2,1)S(1)} %get-tuple-element.80), channel_id=1, source_target_pairs={{0,16},{8,24},{16,0},{24,8},{1,17},{9,25},{17,1},{25,9},{2,18},{10... | collective-permute-start | bytes 983048 | tf_op jit(solution)/shard_map/ppermute | solution.py:27
  52.9 1.5 %collective-permute-start.15 = (bf16[64,1536]{1,0:T(8,128)(2,1)S(1)}, bf16[64,1536]{1,0:T(8,128)(2,1)S(1)}, u32[]{:S(2)}, u32[]{:S(2)}) collective-permute-start(bf16[64,1536]{1,0:T(8,128)(2,1)S(1)} %add_convert_fusion.1.refs_2_), channel_id=1, source_target_pairs={{0,8},{8,0},{16,24},{24,16},{1,9},{9,1},{17,25},{25,17},{2,10},{10... | collective-permute-start | bytes 589832 | tf_op jit(solution)/shard_map/ppermute | solution.py:27
  59.3 1.7 %collective-permute-start.16 = (bf16[64,2560]{1,0:T(8,128)(2,1)S(1)}, bf16[64,2560]{1,0:T(8,128)(2,1)S(1)}, u32[]{:S(2)}, u32[]{:S(2)}) collective-permute-start(bf16[64,2560]{1,0:T(8,128)(2,1)S(1)} %add_convert_fusion.refs_2_), channel_id=1, source_target_pairs={{0,8},{8,0},{16,24},{24,16},{1,9},{9,1},{17,25},{25,17},{2,10},{10... | collective-permute-start | bytes 983048 | tf_op jit(solution)/shard_map/ppermute | solution.py:27

commit v11 on v9

--- a/solution.py
+++ b/solution.py
@@ -10,11 +10,12 @@
 
 BF16 = jnp.bfloat16
 F32 = jnp.float32
-MINE = (2, 3, 3)
-OTHER = (2, 6)
+PLAN = ((((True, 0),),), (((False, 0), (True, 1)),), (((False, 1), (True, 2)), ((False, 2),)))
+MINE = (3, 3, 2)
+OTHER = (3, 5)
 STEP = 1024
 WIDE = 2048
-AHEAD = 4
+AHEAD = 8
 NARROW = 256
 WAIT_BYTES = 10_000_000
 GRAM_ORDER = (0, 1, 2)
@@ -390,6 +391,7 @@
     while mask < blocks_count:
         start_mine = start_mine + exchange(start_mine, "rows", mask)
         mask *= 2
+    terms = tie(terms, start_mine)
     sizes = [half * part // sum(MINE) for part in MINE]
     begins = [sum(sizes[:c]) for c in range(len(sizes))]
     other_sizes = [half * part // sum(OTHER) for part in OTHER]
@@ -415,16 +417,20 @@
 
     start_theirs = exchange(tie(start_mine, mines[0]), "rows", 1)
 
-    waiting, results = [], None
+    pieces, backs, results = [], [], None
     for c, (a, b) in enumerate(sums):
         b = tie(b, new_x, results)
-        piece = (a.astype(F32) + b.astype(F32)).astype(BF16)
-        source, offset = places[c]
-        back = exchange(piece, "rows", 1)
-        ready = waiting + [(True, begins[c], 0, start_mine, mines[c], piece)]
-        results = final(side, scale, x0, dual, z, ready, results, blocks_count)
-        waiting = [(False, begins[c], offset, start_theirs, others[source], back)]
-    results = final(side, scale, x0, dual, z, waiting, results, blocks_count)
+        pieces.append((a.astype(F32) + b.astype(F32)).astype(BF16))
+        backs.append(exchange(pieces[c], "rows", 1))
+        for group in PLAN[c]:
+            work = []
+            for mine, k in group:
+                source, offset = places[k]
+                if mine:
+                    work.append((True, begins[k], 0, start_mine, mines[k], pieces[k]))
+                else:
+                    work.append((False, begins[k], offset, start_theirs, others[source], backs[k]))
+            results = final(side, scale, x0, dual, z, work, results, blocks_count)
     new_z, new_u = results
     return (new_x[None], new_z, new_u[None])
 

time: 60.5 us -> 60 us (level)
  transfers between devices with their start and end apart: 18 -> 18, of which waited for: 8 -> 11; matrix products, arithmetic and copies ran while one was open for 1% -> 1% of each run, Pallas kernels for 27% -> 27%
where the time goes in v11:
time: 60 us; the launch traced here: 59.9 us
  Pallas kernels  25.5 us (42%)
  starting transfers between devices  20.5 us (34%)
  waiting for transfers between devices  12.6 us (21%)
  between operations  0.85 us (1%)
    ppermute x18, starting transfers between devices, exchange(): return lax.ppermute(value, axis, [(i, i ^ mask) for i in range(n)])  20.5 us
    ppermute x18, waiting for transfers between devices, exchange(): return lax.ppermute(value, axis, [(i, i ^ mask) for i in range(n)])  12.6 us
    pallas_call x1, Pallas kernels, load(): call(functools.partial(load_kernel, blocks_count), 'load_and_margins', [S...  8.09 us
    pallas_call x3, Pallas kernels, gram_row(): call(functools.partial(gram_kernel, row), 'gram', [SMEM, VMEM], (out, out...  7.1 us
    pallas_call x4, Pallas kernels, final(): call(functools.partial(final_kernel, blocks_count, places, buffered), 'fi...  5.41 us
    pallas_call x5, Pallas kernels, push(): call(functools.partial(push_kernel, first, mine, begin, offset, size), 'p...  2.7 us
    pallas_call x1, Pallas kernels, store_x(): call(store_kernel, 'store_x', [SMEM] + [VMEM] * len(args), pltpu.HBM((tas...  1.58 us
  transfers between devices with their start and end apart: 18, of which 11 were waited for; matrix products, arithmetic and copies ran while one was open for 1% of the time, Pallas kernels for 27%

profile of v11, /device:TPU:0, one launch (start us, length us, event | category | flops | bytes accessed | tf_op | source)
XLA Modules:
  0.0 59.9 jit_solution(17527543145648810761)
XLA Ops:
  0.6 8.1 %load_and_margins.1 = (bf16[64,768]{1,0:T(8,128)(2,1)S(1)}, f32[64,768]{1,0:T(8,128)S(1)}, bf16[768,8192]{1,0:T(8,128)(2,1)S(1)}, f32[64,8192]{1,0:T(8,128)S(1)}...) custom-call(s32[1]{0:T(128)} %bitcast.side.token, ...), custom_call_target="tpu_custom_call" | custom-call | flops 1000 | bytes 1000 | tf_op jit(solution)/shard_map/load_and_margins/pallas_call | solution.py:152
  9.2 2.6 %collective-permute-start = (bf16[64,768]{1,0:T(8,128)(2,1)S(1)}, bf16[64,768]{1,0:T(8,128)(2,1)S(1)}, u32[]{:S(2)}, u32[]{:S(2)}) collective-permute-start(bf16[64,768]{1,0:T(8,128)(2,1)S(1)} %get-tuple-element.61), channel_id=1, source_target_pairs={{0,1},{1,0},{2,3},{3,2},{4,5},{5,4},{6,7},{7,6},{8,9},{9,8},{10,11... | collective-permute-start | bytes 294920 | tf_op jit(solution)/shard_map/ppermute | solution.py:29
  11.8 1.3 %gram.3 = (bf16[256,256]{1,0:T(8,128)(2,1)S(1)}, bf16[256,256]{1,0:T(8,128)(2,1)S(1)}) custom-call(s32[1]{0:T(128)} %bitcast.side.token, bf16[768,8192]{1,0:T(8,128)(2,1)S(1)} %get-tuple-element.58.a_ref.refs_1_), custom_call_target="tpu_custom_call" | custom-call | flops 1000 | bytes 3333333 | tf_op jit(solution)/shard_map/gram/pallas_call | solution.py:191
  13.3 1.6 %collective-permute-start.8 = (f32[64,4096]{1,0:T(8,128)S(1)}, f32[64,4096]{1,0:T(8,128)S(1)}, u32[]{:S(2)}, u32[]{:S(2)}) collective-permute-start(f32[64,4096]{1,0:T(8,128)S(1)} %add.30), channel_id=1, source_target_pairs={{0,16},{8,24},{16,0},{24,8},{1,17},{9,25},{17,1},{25,9},{2,18},{10... | collective-permute-start | bytes 3145736 | tf_op jit(solution)/shard_map/ppermute | solution.py:29
  15.3 1.9 %collective-permute-start.2 = (bf16[64,768]{1,0:T(8,128)(2,1)S(1)}, bf16[64,768]{1,0:T(8,128)(2,1)S(1)}, u32[]{:S(2)}, u32[]{:S(2)}) collective-permute-start(bf16[64,768]{1,0:T(8,128)(2,1)S(1)} %add_convert_fusion.5), channel_id=1, source_target_pairs={{0,2},{1,3},{2,0},{3,1},{4,6},{5,7},{6,4},{7,5},{8,10},{9,11},{10,... | collective-permute-start | bytes 294920 | tf_op jit(solution)/shard_map/ppermute | solution.py:29
  17.1 2.4 %gram.4 = (bf16[256,512]{1,0:T(8,128)(2,1)S(1)}, bf16[256,512]{1,0:T(8,128)(2,1)S(1)}) custom-call(s32[1]{0:T(128)} %bitcast.side.token, bf16[768,8192]{1,0:T(8,128)(2,1)S(1)} %get-tuple-element.58.a_ref.refs_1_), custom_call_target="tpu_custom_call" | custom-call | flops 1000 | bytes 6666666 | tf_op jit(solution)/shard_map/gram/pallas_call | solution.py:191
  20.0 2.9 %collective-permute-start.3 = (bf16[64,768]{1,0:T(8,128)(2,1)S(1)}, bf16[64,768]{1,0:T(8,128)(2,1)S(1)}, u32[]{:S(2)}, u32[]{:S(2)}) collective-permute-start(bf16[64,768]{1,0:T(8,128)(2,1)S(1)} %add_convert_fusion.4.refs_6_), channel_id=1, source_target_pairs={{0,4},{1,5},{2,6},{3,7},{4,0},{5,1},{6,2},{7,3},{8,12},{9,13},{10,... | collective-permute-start | bytes 294920 | tf_op jit(solution)/shard_map/ppermute | solution.py:29
  22.9 3.5 %gram.5 = (bf16[256,768]{1,0:T(8,128)(2,1)S(1)}, bf16[256,768]{1,0:T(8,128)(2,1)S(1)}) custom-call(s32[1]{0:T(128)} %bitcast.side.token, bf16[768,8192]{1,0:T(8,128)(2,1)S(1)} %get-tuple-element.58.a_ref.refs_1_), custom_call_target="tpu_custom_call" | custom-call | flops 1000 | bytes 10000000 | tf_op jit(solution)/shard_map/gram/pallas_call | solution.py:191
  27.0 2.6 %collective-permute-start.6 = (bf16[64,768]{1,0:T(8,128)(2,1)S(1)}, bf16[64,768]{1,0:T(8,128)(2,1)S(1)}, u32[]{:S(2)}, u32[]{:S(2)}) collective-permute-start(bf16[64,768]{1,0:T(8,128)(2,1)S(1)} %get-tuple-element.76), channel_id=1, source_target_pairs={{0,3},{1,2},{2,1},{3,0},{4,7},{5,6},{6,5},{7,4},{8,11},{9,10},{10,... | collective-permute-start | bytes 294920 | tf_op jit(solution)/shard_map/ppermute | solution.py:29
  30.5 2.1 %collective-permute-done.6 = bf16[64,768]{1,0:T(8,128)(2,1)S(1)} collective-permute-done((bf16[64,768]{1,0:T(8,128)(2,1)S(1)}, bf16[64,768]{1,0:T(8,128)(2,1)S(1)}, u32[]{:S(2)}, u32[]{:S(2)}) %collective-permute-start.6) | collective-permute-done | bytes 98336 | tf_op jit(solution)/shard_map/ppermute | solution.py:29
  32.7 1.5 %collective-permute-done.5 = bf16[64,768]{1,0:T(8,128)(2,1)S(1)} collective-permute-done((bf16[64,768]{1,0:T(8,128)(2,1)S(1)}, bf16[64,768]{1,0:T(8,128)(2,1)S(1)}, u32[]{:S(2)}, u32[]{:S(2)}) %collective-permute-start.5) | collective-permute-done | bytes 98336 | tf_op jit(solution)/shard_map/ppermute | solution.py:29
  34.7 2.6 %collective-permute-start.7 = (bf16[64,768]{1,0:T(8,128)(2,1)S(1)}, bf16[64,768]{1,0:T(8,128)(2,1)S(1)}, u32[]{:S(2)}, u32[]{:S(2)}) collective-permute-start(bf16[64,768]{1,0:T(8,128)(2,1)S(1)} %add_convert_fusion.3.refs_4_), channel_id=1, source_target_pairs={{0,4},{1,5},{2,6},{3,7},{4,0},{5,1},{6,2},{7,3},{8,12},{9,13},{10,... | collective-permute-start | bytes 294920 | tf_op jit(solution)/shard_map/ppermute | solution.py:29
  37.3 1.3 %collective-permute-done.8 = f32[64,4096]{1,0:T(8,128)S(1)} collective-permute-done((f32[64,4096]{1,0:T(8,128)S(1)}, f32[64,4096]{1,0:T(8,128)S(1)}, u32[]{:S(2)}, u32[]{:S(2)}) %collective-permute-start.8) | collective-permute-done | bytes 1048608 | tf_op jit(solution)/shard_map/ppermute | solution.py:29
  38.7 1.6 %collective-permute-done.7.refs_5_ = bf16[64,768]{1,0:T(8,128)(2,1)S(1)} collective-permute-done((bf16[64,768]{1,0:T(8,128)(2,1)S(1)}, bf16[64,768]{1,0:T(8,128)(2,1)S(1)}, u32[]{:S(2)}, u32[]{:S(2)}) %collective-permute-start.7) | collective-permute-done | bytes 98336 | tf_op jit(solution)/shard_map/ppermute | solution.py:29
  40.9 0.7 %push_other.3 = (f32[64,2560]{1,0:T(8,128)S(1)}, bf16[64,2560]{1,0:T(8,128)(2,1)S(1)}) custom-call(s32[1]{0:T(128)} %bitcast.side.token, f32[64,128]{1,0:T(8,128)S(1)} %get-tuple-element.54.scale.refs_0_, bf16[768,8192]{1,0:T(8,128)(2,1)S(1)} %get-tuple-element.58.a_ref.refs_1_, bf16[128,768]{1,0:T(8,128)(2,1)S(1)} %get-tuple-element.79.refs_2_), custom_call_target="tpu_custom_call" | custom-call | flops 1000 | bytes 1000 | tf_op jit(solution)/shard_map/push_other/pallas_call | solution.py:267
  42.9 1.6 %collective-permute-start.13 = (bf16[64,1536]{1,0:T(8,128)(2,1)S(1)}, bf16[64,1536]{1,0:T(8,128)(2,1)S(1)}, u32[]{:S(2)}, u32[]{:S(2)}) collective-permute-start(bf16[64,1536]{1,0:T(8,128)(2,1)S(1)} %get-tuple-element.84), channel_id=1, source_target_pairs={{0,16},{8,24},{16,0},{24,8},{1,17},{9,25},{17,1},{25,9},{2,18},{10... | collective-permute-start | bytes 589832 | tf_op jit(solution)/shard_map/ppermute | solution.py:29
  46.0 1.6 %collective-permute-start.12 = (bf16[64,1024]{1,0:T(8,128)(2,1)S(1)}, bf16[64,1024]{1,0:T(8,128)(2,1)S(1)}, u32[]{:S(2)}, u32[]{:S(2)}) collective-permute-start(bf16[64,1024]{1,0:T(8,128)(2,1)S(1)} %get-tuple-element.93), channel_id=1, source_target_pairs={{0,16},{8,24},{16,0},{24,8},{1,17},{9,25},{17,1},{25,9},{2,18},{10... | collective-permute-start | bytes 393224 | tf_op jit(solution)/shard_map/ppermute | solution.py:29
  47.5 1.6 %store_x.1 = f32[64,8192]{1,0:T(8,128)} custom-call(s32[1]{0:T(128)} %bitcast.side.token, f32[64,128]{1,0:T(8,128)S(1)} %get-tuple-element.54.scale.refs_0_, f32[64,8192]{1,0:T(8,128)S(1)} %get-tuple-element.55.x_ref, f32[64,8192]{1,0:T(8,128)S(1)} %get-tuple-element.56.u_ref, f32[64,8192]{1,0:T(8,128)S(1)} %get-tuple-element.57.z_ref, ...), custom_call_target="tpu_custom_call" | custom-call | flops 1000 | bytes 1000 | tf_op jit(solution)/shard_map/store_x/pallas_call | solution.py:301
  49.1 1.6 %collective-permute-done.13 = bf16[64,1536]{1,0:T(8,128)(2,1)S(1)} collective-permute-done((bf16[64,1536]{1,0:T(8,128)(2,1)S(1)}, bf16[64,1536]{1,0:T(8,128)(2,1)S(1)}, u32[]{:S(2)}, u32[]{:S(2)}) %collective-permute-start.13) | collective-permute-done | bytes 196640 | tf_op jit(solution)/shard_map/ppermute | solution.py:29
  50.8 1.2 %final.4 = (f32[64,8192]{1,0:T(8,128)}, f32[64,8192]{1,0:T(8,128)}) custom-call(s32[1]{0:T(128)} %bitcast.side.token, f32[64,128]{1,0:T(8,128)S(1)} %get-tuple-element.54.scale.refs_0_, f32[64,8192]{1,0:T(8,128)S(1)} %get-tuple-element.55.x_ref, f32[64,8192]{1,0:T(8,128)S(1)} %get-tuple-element.56.u_ref, f32[64,8192]{1,0:T(8,128)S(1)} %get-tuple-element.57.z_ref, ...), custom_call_target="tpu_custom_call" | custom-call | flops 1000 | bytes 1000 | tf_op jit(solution)/shard_map/final/pallas_call | solution.py:351
  52.0 2.9 %collective-permute-done.15 = bf16[64,1536]{1,0:T(8,128)(2,1)S(1)} collective-permute-done((bf16[64,1536]{1,0:T(8,128)(2,1)S(1)}, bf16[64,1536]{1,0:T(8,128)(2,1)S(1)}, u32[]{:S(2)}, u32[]{:S(2)}) %collective-permute-start.15) | collective-permute-done | bytes 196640 | tf_op jit(solution)/shard_map/ppermute | solution.py:29
  55.0 1.7 %final.5 = (f32[64,8192]{1,0:T(8,128)}, f32[64,8192]{1,0:T(8,128)}) custom-call(s32[1]{0:T(128)} %bitcast.side.token, f32[64,128]{1,0:T(8,128)S(1)} %get-tuple-element.54.scale.refs_0_, f32[64,8192]{1,0:T(8,128)S(1)} %get-tuple-element.55.x_ref, f32[64,8192]{1,0:T(8,128)S(1)} %get-tuple-element.56.u_ref, ...), custom_call_target="tpu_custom_call", output_to_operand_aliasing={{0}: (11, {}), {1}: (12, {})} | custom-call | flops 1000 | bytes 1000 | tf_op jit(solution)/shard_map/final/pallas_call | solution.py:351
  57.3 1.5 %final.6 = (f32[64,8192]{1,0:T(8,128)}, f32[64,8192]{1,0:T(8,128)}) custom-call(s32[1]{0:T(128)} %bitcast.side.token, f32[64,128]{1,0:T(8,128)S(1)} %get-tuple-element.54.scale.refs_0_, f32[64,8192]{1,0:T(8,128)S(1)} %get-tuple-element.55.x_ref, f32[64,8192]{1,0:T(8,128)S(1)} %get-tuple-element.56.u_ref, ...), custom_call_target="tpu_custom_call", output_to_operand_aliasing={{0}: (11, {}), {1}: (12, {})} | custom-call | flops 1000 | bytes 1000 | tf_op jit(solution)/shard_map/final/pallas_call | solution.py:351
  58.9 1.0 %final.7 = (f32[64,8192]{1,0:T(8,128)}, f32[64,8192]{1,0:T(8,128)}) custom-call(s32[1]{0:T(128)} %bitcast.side.token, f32[64,128]{1,0:T(8,128)S(1)} %get-tuple-element.54.scale.refs_0_, f32[64,8192]{1,0:T(8,128)S(1)} %get-tuple-element.55.x_ref, f32[64,8192]{1,0:T(8,128)S(1)} %get-tuple-element.56.u_ref, ...), custom_call_target="tpu_custom_call", output_to_operand_aliasing={{0}: (8, {}), {1}: (9, {})} | custom-call | flops 1000 | bytes 1000 | tf_op jit(solution)/shard_map/final/pallas_call | solution.py:351
  (35 shorter events, 7.9 us)
Async XLA Ops:
  8.7 4.4 %collective-permute-start.1 = (f32[64,4096]{1,0:T(8,128)S(1)}, f32[64,4096]{1,0:T(8,128)S(1)}, u32[]{:S(2)}, u32[]{:S(2)}) collective-permute-start(f32[64,4096]{1,0:T(8,128)S(1)} %get-tuple-element.66), channel_id=1, source_target_pairs={{0,8},{8,0},{16,24},{24,16},{1,9},{9,1},{17,25},{25,17},{2,10},{10... | collective-permute-start | bytes 3145736 | tf_op jit(solution)/shard_map/ppermute | solution.py:29
  9.2 6.0 %collective-permute-start = (bf16[64,768]{1,0:T(8,128)(2,1)S(1)}, bf16[64,768]{1,0:T(8,128)(2,1)S(1)}, u32[]{:S(2)}, u32[]{:S(2)}) collective-permute-start(bf16[64,768]{1,0:T(8,128)(2,1)S(1)} %get-tuple-element.61), channel_id=1, source_target_pairs={{0,1},{1,0},{2,3},{3,2},{4,5},{5,4},{6,7},{7,6},{8,9},{9,8},{10,11... | collective-permute-start | bytes 294920 | tf_op jit(solution)/shard_map/ppermute | solution.py:29
  13.3 25.3 %collective-permute-start.8 = (f32[64,4096]{1,0:T(8,128)S(1)}, f32[64,4096]{1,0:T(8,128)S(1)}, u32[]{:S(2)}, u32[]{:S(2)}) collective-permute-start(f32[64,4096]{1,0:T(8,128)S(1)} %add.30), channel_id=1, source_target_pairs={{0,16},{8,24},{16,0},{24,8},{1,17},{9,25},{17,1},{25,9},{2,18},{10... | collective-permute-start | bytes 3145736 | tf_op jit(solution)/shard_map/ppermute | solution.py:29
  15.3 4.7 %collective-permute-start.2 = (bf16[64,768]{1,0:T(8,128)(2,1)S(1)}, bf16[64,768]{1,0:T(8,128)(2,1)S(1)}, u32[]{:S(2)}, u32[]{:S(2)}) collective-permute-start(bf16[64,768]{1,0:T(8,128)(2,1)S(1)} %add_convert_fusion.5), channel_id=1, source_target_pairs={{0,2},{1,3},{2,0},{3,1},{4,6},{5,7},{6,4},{7,5},{8,10},{9,11},{10,... | collective-permute-start | bytes 294920 | tf_op jit(solution)/shard_map/ppermute | solution.py:29
  20.0 6.4 %collective-permute-start.3 = (bf16[64,768]{1,0:T(8,128)(2,1)S(1)}, bf16[64,768]{1,0:T(8,128)(2,1)S(1)}, u32[]{:S(2)}, u32[]{:S(2)}) collective-permute-start(bf16[64,768]{1,0:T(8,128)(2,1)S(1)} %add_convert_fusion.4.refs_6_), channel_id=1, source_target_pairs={{0,4},{1,5},{2,6},{3,7},{4,0},{5,1},{6,2},{7,3},{8,12},{9,13},{10,... | collective-permute-start | bytes 294920 | tf_op jit(solution)/shard_map/ppermute | solution.py:29
  27.0 5.7 %collective-permute-start.6 = (bf16[64,768]{1,0:T(8,128)(2,1)S(1)}, bf16[64,768]{1,0:T(8,128)(2,1)S(1)}, u32[]{:S(2)}, u32[]{:S(2)}) collective-permute-start(bf16[64,768]{1,0:T(8,128)(2,1)S(1)} %get-tuple-element.76), channel_id=1, source_target_pairs={{0,3},{1,2},{2,1},{3,0},{4,7},{5,6},{6,5},{7,4},{8,11},{9,10},{10,... | collective-permute-start | bytes 294920 | tf_op jit(solution)/shard_map/ppermute | solution.py:29
  29.6 4.6 %collective-permute-start.5 = (bf16[64,768]{1,0:T(8,128)(2,1)S(1)}, bf16[64,768]{1,0:T(8,128)(2,1)S(1)}, u32[]{:S(2)}, u32[]{:S(2)}) collective-permute-start(bf16[64,768]{1,0:T(8,128)(2,1)S(1)} %get-tuple-element.76), channel_id=1, source_target_pairs={{0,2},{1,3},{2,0},{3,1},{4,6},{5,7},{6,4},{7,5},{8,10},{9,11},{10,... | collective-permute-start | bytes 294920 | tf_op jit(solution)/shard_map/ppermute | solution.py:29
  30.0 4.6 %collective-permute-start.4 = (bf16[64,768]{1,0:T(8,128)(2,1)S(1)}, bf16[64,768]{1,0:T(8,128)(2,1)S(1)}, u32[]{:S(2)}, u32[]{:S(2)}) collective-permute-start(bf16[64,768]{1,0:T(8,128)(2,1)S(1)} %get-tuple-element.76), channel_id=1, source_target_pairs={{0,1},{1,0},{2,3},{3,2},{4,5},{5,4},{6,7},{7,6},{8,9},{9,8},{10,11... | collective-permute-start | bytes 294920 | tf_op jit(solution)/shard_map/ppermute | solution.py:29
  34.7 5.6 %collective-permute-start.7 = (bf16[64,768]{1,0:T(8,128)(2,1)S(1)}, bf16[64,768]{1,0:T(8,128)(2,1)S(1)}, u32[]{:S(2)}, u32[]{:S(2)}) collective-permute-start(bf16[64,768]{1,0:T(8,128)(2,1)S(1)} %add_convert_fusion.3.refs_4_), channel_id=1, source_target_pairs={{0,4},{1,5},{2,6},{3,7},{4,0},{5,1},{6,2},{7,3},{8,12},{9,13},{10,... | collective-permute-start | bytes 294920 | tf_op jit(solution)/shard_map/ppermute | solution.py:29
  40.8 1.5 %collective-permute-start.9 = (bf16[64,1536]{1,0:T(8,128)(2,1)S(1)}, bf16[64,1536]{1,0:T(8,128)(2,1)S(1)}, u32[]{:S(2)}, u32[]{:S(2)}) collective-permute-start(bf16[64,1536]{1,0:T(8,128)(2,1)S(1)} %get-tuple-element.82), channel_id=1, source_target_pairs={{0,8},{8,0},{16,24},{24,16},{1,9},{9,1},{17,25},{25,17},{2,10},{10... | collective-permute-start | bytes 589832 | tf_op jit(solution)/shard_map/ppermute | solution.py:29
  41.6 2.8 %collective-permute-start.10 = (bf16[64,2560]{1,0:T(8,128)(2,1)S(1)}, bf16[64,2560]{1,0:T(8,128)(2,1)S(1)}, u32[]{:S(2)}, u32[]{:S(2)}) collective-permute-start(bf16[64,2560]{1,0:T(8,128)(2,1)S(1)} %get-tuple-element.86), channel_id=1, source_target_pairs={{0,8},{8,0},{16,24},{24,16},{1,9},{9,1},{17,25},{25,17},{2,10},{10... | collective-permute-start | bytes 983048 | tf_op jit(solution)/shard_map/ppermute | solution.py:29
  42.9 7.8 %collective-permute-start.13 = (bf16[64,1536]{1,0:T(8,128)(2,1)S(1)}, bf16[64,1536]{1,0:T(8,128)(2,1)S(1)}, u32[]{:S(2)}, u32[]{:S(2)}) collective-permute-start(bf16[64,1536]{1,0:T(8,128)(2,1)S(1)} %get-tuple-element.84), channel_id=1, source_target_pairs={{0,16},{8,24},{16,0},{24,8},{1,17},{9,25},{17,1},{25,9},{2,18},{10... | collective-permute-start | bytes 589832 | tf_op jit(solution)/shard_map/ppermute | solution.py:29
  44.4 10.6 %collective-permute-start.11 = (f32[64,4096]{1,0:T(8,128)S(1)}, f32[64,4096]{1,0:T(8,128)S(1)}, u32[]{:S(2)}, u32[]{:S(2)}) collective-permute-start(f32[64,4096]{1,0:T(8,128)S(1)} %add.36.refs_0_.refs_3_), channel_id=1, source_target_pairs={{0,8},{8,0},{16,24},{24,16},{1,9},{9,1},{17,25},{25,17},{2,10},{10... | collective-permute-start | bytes 3145736 | tf_op jit(solution)/shard_map/ppermute | solution.py:29
  44.9 9.9 %collective-permute-start.15 = (bf16[64,1536]{1,0:T(8,128)(2,1)S(1)}, bf16[64,1536]{1,0:T(8,128)(2,1)S(1)}, u32[]{:S(2)}, u32[]{:S(2)}) collective-permute-start(bf16[64,1536]{1,0:T(8,128)(2,1)S(1)} %get-tuple-element.88), channel_id=1, source_target_pairs={{0,16},{8,24},{16,0},{24,8},{1,17},{9,25},{17,1},{25,9},{2,18},{10... | collective-permute-start | bytes 589832 | tf_op jit(solution)/shard_map/ppermute | solution.py:29
  46.0 10.9 %collective-permute-start.12 = (bf16[64,1024]{1,0:T(8,128)(2,1)S(1)}, bf16[64,1024]{1,0:T(8,128)(2,1)S(1)}, u32[]{:S(2)}, u32[]{:S(2)}) collective-permute-start(bf16[64,1024]{1,0:T(8,128)(2,1)S(1)} %get-tuple-element.93), channel_id=1, source_target_pairs={{0,16},{8,24},{16,0},{24,8},{1,17},{9,25},{17,1},{25,9},{2,18},{10... | collective-permute-start | bytes 393224 | tf_op jit(solution)/shard_map/ppermute | solution.py:29
  50.7 4.3 %collective-permute-start.14 = (bf16[64,1536]{1,0:T(8,128)(2,1)S(1)}, bf16[64,1536]{1,0:T(8,128)(2,1)S(1)}, u32[]{:S(2)}, u32[]{:S(2)}) collective-permute-start(bf16[64,1536]{1,0:T(8,128)(2,1)S(1)} %add_convert_fusion.1.refs_2_), channel_id=1, source_target_pairs={{0,8},{8,0},{16,24},{24,16},{1,9},{9,1},{17,25},{25,17},{2,10},{10... | collective-permute-start | bytes 589832 | tf_op jit(solution)/shard_map/ppermute | solution.py:29
  54.9 2.4 %collective-permute-start.17 = (bf16[64,1536]{1,0:T(8,128)(2,1)S(1)}, bf16[64,1536]{1,0:T(8,128)(2,1)S(1)}, u32[]{:S(2)}, u32[]{:S(2)}) collective-permute-start(bf16[64,1536]{1,0:T(8,128)(2,1)S(1)} %add_convert_fusion.refs_5_), channel_id=1, source_target_pairs={{0,8},{8,0},{16,24},{24,16},{1,9},{9,1},{17,25},{25,17},{2,10},{10... | collective-permute-start | bytes 589832 | tf_op jit(solution)/shard_map/ppermute | solution.py:29
  56.9 1.9 %collective-permute-start.16 = (bf16[64,1024]{1,0:T(8,128)(2,1)S(1)}, bf16[64,1024]{1,0:T(8,128)(2,1)S(1)}, u32[]{:S(2)}, u32[]{:S(2)}) collective-permute-start(bf16[64,1024]{1,0:T(8,128)(2,1)S(1)} %add_convert_fusion.2.refs_5_), channel_id=1, source_target_pairs={{0,8},{8,0},{16,24},{24,16},{1,9},{9,1},{17,25},{25,17},{2,10},{10... | collective-permute-start | bytes 393224 | tf_op jit(solution)/shard_map/ppermute | solution.py:29

commit v12 on v11

--- a/solution.py
+++ b/solution.py
@@ -17,6 +17,7 @@
 WIDE = 2048
 AHEAD = 8
 NARROW = 256
+FINISH = 512
 WAIT_BYTES = 10_000_000
 GRAM_ORDER = (0, 1, 2)
 HBM = pl.BlockSpec(memory_space=pltpu.HBM)
@@ -47,7 +48,7 @@
     while mask < n:
         if len(terms) > 1:
             terms = [sum(t.astype(F32) for t in terms).astype(value.dtype)]
-        steps = [mask, 2 * mask, 3 * mask] if 2 * mask < n else [mask]
+        steps = [3 * mask, 2 * mask, mask] if 2 * mask < n else [mask]
         terms += [exchange(terms[0], axis, step) for step in steps]
         mask *= 4
     return terms
@@ -79,9 +80,15 @@
     return pl.ds(pl.multiple_of(start, 128), size)
 
 
+def split(whole, high, low):
+    top = whole.astype(BF16)
+    high[...] = top
+    low[...] = (whole - top.astype(F32)).astype(BF16)
+
+
 def load_kernel(blocks_count, side, x_hbm, u_hbm, z_hbm, a_hbm, sign_hbm, eta_hbm, rho_hbm, lam_hbm, *refs):
-    outs, (eta_row, rho_row, lam_row, both, acc, sems) = refs[:10], refs[10:]
-    m_out, pulled_out, a_out, x_out, u_out, z_out, sign_out, scale, mine_out, other_out = outs
+    outs, (eta_row, rho_row, lam_row, both, acc, block, sems) = refs[:12], refs[12:]
+    m_out, pulled_out, a_out, x_out, u_out, z_out, sign_out, scale, mine_out, other_out, high, low = outs
     tasks, width = x_hbm.shape
     steps = width // STEP
     rows = ((eta_hbm, eta_row), (rho_hbm, rho_row), (lam_hbm, lam_row), (sign_hbm, sign_out))
@@ -108,6 +115,7 @@
         upright = jnp.where(one, jnp.broadcast_to(row, (tasks, tasks)), 0.0)
         scale[:, k : k + 1] = jnp.sum(upright, axis=1, keepdims=True)
     acc[...] = jnp.zeros_like(acc)
+    block[...] = jnp.zeros_like(block)
 
     @pl.loop(0, steps)
     def _(j):
@@ -131,8 +139,12 @@
             both[:tasks, here] = x.astype(BF16)
             both[tasks : 2 * tasks, here] = top
             both[2 * tasks :, here] = (v - top.astype(F32)).astype(BF16)
-        acc[...] += nt(both[...], a_out[:, columns(j * STEP, STEP)])
-
+        at = columns(j * STEP, STEP)
+        acc[...] += nt(both[...], a_out[:, at])
+        last = a_out[pl.ds(a_out.shape[0] - block.shape[0], block.shape[0]), at]
+        block[...] += nt(last, last)
+
+    split(block[...], high, low)
     m_out[...] = acc[:tasks].astype(BF16)
     pulled_out[...] = acc[tasks : 2 * tasks] + acc[2 * tasks :]
     half = width // 2
@@ -156,45 +168,41 @@
         (
             pltpu.VMEM((tasks, samples), BF16), pltpu.VMEM((tasks, samples), F32), pltpu.VMEM(design.shape, BF16),
             full, full, full, pltpu.VMEM(sign.shape, jnp.int32), pltpu.VMEM((tasks, 128), F32), half, half,
+            *[pltpu.VMEM((samples // 3, samples // 3), BF16)] * 2,
         ),
-        [VMEM] * 10,
+        [VMEM] * 12,
         [pltpu.VMEM((1, tasks), F32)] * 3
         + [
             pltpu.VMEM((3 * tasks, STEP), BF16), pltpu.VMEM((3 * tasks, samples), F32),
+            pltpu.VMEM((samples // 3, samples // 3), F32),
             pltpu.SemaphoreType.DMA((5, max(width // STEP, 4))),
         ],
     )(side, *pin(pltpu.HBM, x, u, z, design, sign, *rows))
 
 
-def gram_block(a_ref, row, cols, size, acc, high, low):
+def gram_kernel(row, token, a_ref, high, low, acc):
+    size, cols = high.shape
     width = a_ref.shape[1]
     wide = math.gcd(WIDE, width)
     for j in range(width // wide):
         at = pl.ds(j * wide, wide)
-        product = nt(a_ref[pl.ds(row, size), at], a_ref[pl.ds(0, cols), at])
-        acc[:, :cols] = product if j == 0 else acc[:, :cols] + product
-    whole = acc[:, :cols]
-    top = whole.astype(BF16)
-    high[...] = top
-    low[...] = (whole - top.astype(F32)).astype(BF16)
-
-
-def gram_kernel(row, token, a_ref, high, low, acc):
-    size = high.shape[0]
-    gram_block(a_ref, row * size, (row + 1) * size, size, acc, high, low)
+        product = nt(a_ref[pl.ds(row * size, size), at], a_ref[pl.ds(0, cols), at])
+        acc[...] = product if j == 0 else acc[...] + product
+    split(acc[...], high, low)
 
 
 def gram_row(row, token, design):
     samples = design.shape[0]
     size = samples // 3
-    out = pltpu.VMEM((size, (row + 1) * size), BF16)
+    cols = min(row + 1, 2) * size
+    out = pltpu.VMEM((size, cols), BF16)
     return call(
         functools.partial(gram_kernel, row),
         "gram",
         [SMEM, VMEM],
         (out, out),
         [VMEM] * 2,
-        [pltpu.VMEM((size, (row + 1) * size), F32)],
+        [pltpu.VMEM((size, cols), F32)],
         work=WAIT_BYTES * (row + 1) // 3,
     )(token, *pin(pltpu.VMEM, design))
 
@@ -206,8 +214,8 @@
 
 
 def turn_kernel(sign, scale, pulled, *refs):
-    *terms, resid, out = refs[6:]
-    grams = refs[:6]
+    *terms, resid, out = refs[8:]
+    grams = refs[:8]
     size = grams[0].shape[0]
     resid[...] = residual(sign[...], *(t[...] for t in terms))
     eta = scale[:, 0:1]
@@ -216,7 +224,9 @@
         total = jnp.zeros((resid.shape[0], size), F32)
         for row in range(3):
             for part in range(2):
-                if row >= col:
+                if row == 2 and col == 2:
+                    total += jnp.dot(r[row], grams[6 + part][...], preferred_element_type=F32)
+                elif row >= col:
                     block = grams[2 * row + part][:, pl.ds(col * size, size)]
                     total += jnp.dot(r[row], block, preferred_element_type=F32)
                 else:
@@ -327,11 +337,13 @@
             moved = z + keep * keep * (x_ref[:, cut] - z + u_ref[:, cut]) + h[:, pl.ds(offset + j, NARROW)]
             stage[0, :, here] = new_z
             stage[1, :, here] = moved - new_z
-        cut, here = columns(base, size), pl.ds(filled, size)
-        for o in range(2):
-            copy = pltpu.make_async_copy(stage.at[o, :, here], outs[o].at[:, cut], sems.at[k, o])
-            copy.start()
-            copies.append(copy)
+            if (j + NARROW) % FINISH == 0 or j + NARROW == size:
+                long = j % FINISH + NARROW
+                cut, here = columns(base + j + NARROW - long, long), pl.ds(filled + j + NARROW - long, long)
+                for o in range(2):
+                    copy = pltpu.make_async_copy(stage.at[o, :, here], outs[o].at[:, cut], sems.at[len(copies) // 2, o])
+                    copy.start()
+                    copies.append(copy)
         filled += size
     for copy in copies:
         copy.wait()
@@ -354,7 +366,7 @@
         [SMEM] + [VMEM] * vmem + [HBM] * (2 * buffered),
         (out, out),
         [HBM] * 2,
-        [pltpu.VMEM((2, tasks, sum(p[3] for p in places)), F32), pltpu.SemaphoreType.DMA((len(pieces), 2))],
+        [pltpu.VMEM((2, tasks, sum(p[3] for p in places)), F32), pltpu.SemaphoreType.DMA((sum(-(-p[3] // FINISH) for p in places), 2))],
         aliases,
     )(side, *args)
 
@@ -369,7 +381,7 @@
     blocks_count = lax.axis_size("rows")
     side = (lax.axis_index("rows") & 1).astype(jnp.int32)[None]
 
-    margin1, pulled, design, x0, dual, z, sign, scale, start_mine, start_other = load(
+    margin1, pulled, design, x0, dual, z, sign, scale, start_mine, start_other, *block = load(
         side, local_x[0], dual_u[0], consensus_z, design, labels, step_size, rho, penalty, blocks_count
     )
     start_mine = start_mine + exchange(start_other, "rows", 1)
@@ -385,7 +397,7 @@
             got = exchange(terms[0], "feat", 1 << step)
             terms.append(tie(got, row[0], start_mine) if step == 0 else tie(got, row[0]) if step == 1 else got)
 
-    resid1, margin2 = turn(sign, terms, scale, pulled, [g for row in range(3) for g in grams[GRAM_ORDER.index(row)]])
+    resid1, margin2 = turn(sign, terms, scale, pulled, [g for row in range(3) for g in grams[GRAM_ORDER.index(row)]] + block)
     terms = square_sum(margin2, "feat")
     mask = 2
     while mask < blocks_count:

time: 60 us -> 62.5 us (1.042)
  starting transfers between devices: 20.5 us -> 21.8 us
  waiting for transfers between devices: 12.6 us -> 13.8 us
    ppermute x18, starting transfers between devices: 20.5 us -> 21.8 us  [exchange(): return lax.ppermute(value, axis, [(i, i ^ mask) for i in range(n)])]
    ppermute x18, waiting for transfers between devices: 12.6 us -> 13.8 us  [exchange(): return lax.ppermute(value, axis, [(i, i ^ mask) for i in range(n)])]
    pallas_call x3, Pallas kernels: 7.1 us -> 5.99 us  [gram_row(): call(functools.partial(gram_kernel, row), 'gram', [SMEM, VMEM], (out, out...]
    pallas_call x1, Pallas kernels: 8.09 us -> 9.05 us  [load(): call(functools.partial(load_kernel, blocks_count), 'load_and_margins', [S...]
  transfers between devices with their start and end apart: 18 -> 18, of which waited for: 11 -> 12; matrix products, arithmetic and copies ran while one was open for 1% -> 1% of each run, Pallas kernels for 27% -> 24%
where the time goes in v12:
time: 62.5 us; the launch traced here: 62.4 us
  Pallas kernels  25.4 us (41%)
  starting transfers between devices  21.8 us (35%)
  waiting for transfers between devices  13.8 us (22%)
  between operations  0.85 us (1%)
    ppermute x18, starting transfers between devices, exchange(): return lax.ppermute(value, axis, [(i, i ^ mask) for i in range(n)])  21.8 us
    ppermute x18, waiting for transfers between devices, exchange(): return lax.ppermute(value, axis, [(i, i ^ mask) for i in range(n)])  13.8 us
    pallas_call x1, Pallas kernels, load(): call(functools.partial(load_kernel, blocks_count), 'load_and_margins', [S...  9.05 us
    pallas_call x3, Pallas kernels, gram_row(): call(functools.partial(gram_kernel, row), 'gram', [SMEM, VMEM], (out, out...  5.99 us
    pallas_call x4, Pallas kernels, final(): call(functools.partial(final_kernel, blocks_count, places, buffered), 'fi...  5.49 us
    pallas_call x5, Pallas kernels, push(): call(functools.partial(push_kernel, first, mine, begin, offset, size), 'p...  2.71 us
    pallas_call x1, Pallas kernels, store_x(): call(store_kernel, 'store_x', [SMEM] + [VMEM] * len(args), pltpu.HBM((tas...  1.58 us
  transfers between devices with their start and end apart: 18, of which 12 were waited for; matrix products, arithmetic and copies ran while one was open for 1% of the time, Pallas kernels for 24%

profile of v12, /device:TPU:0, one launch (start us, length us, event | category | flops | bytes accessed | tf_op | source)
XLA Modules:
  0.0 62.4 jit_solution(14508331506007963856)
XLA Ops:
  0.6 9.1 %load_and_margins.1 = (bf16[64,768]{1,0:T(8,128)(2,1)S(1)}, f32[64,768]{1,0:T(8,128)S(1)}, bf16[768,8192]{1,0:T(8,128)(2,1)S(1)}, f32[64,8192]{1,0:T(8,128)S(1)}...) custom-call(s32[1]{0:T(128)} %bitcast.side.token, ...), custom_call_target="tpu_custom_call" | custom-call | flops 1000 | bytes 1000 | tf_op jit(solution)/shard_map/load_and_margins/pallas_call | solution.py:164
  10.2 2.6 %collective-permute-start = (bf16[64,768]{1,0:T(8,128)(2,1)S(1)}, bf16[64,768]{1,0:T(8,128)(2,1)S(1)}, u32[]{:S(2)}, u32[]{:S(2)}) collective-permute-start(bf16[64,768]{1,0:T(8,128)(2,1)S(1)} %get-tuple-element.63), channel_id=1, source_target_pairs={{0,1},{1,0},{2,3},{3,2},{4,5},{5,4},{6,7},{7,6},{8,9},{9,8},{10,11... | collective-permute-start | bytes 294920 | tf_op jit(solution)/shard_map/ppermute | solution.py:30
  12.8 1.3 %gram.3 = (bf16[256,256]{1,0:T(8,128)(2,1)S(1)}, bf16[256,256]{1,0:T(8,128)(2,1)S(1)}) custom-call(s32[1]{0:T(128)} %bitcast.side.token, bf16[768,8192]{1,0:T(8,128)(2,1)S(1)} %get-tuple-element.60.a_ref.refs_1_), custom_call_target="tpu_custom_call" | custom-call | flops 1000 | bytes 3333333 | tf_op jit(solution)/shard_map/gram/pallas_call | solution.py:199
  14.2 1.6 %collective-permute-start.8 = (f32[64,4096]{1,0:T(8,128)S(1)}, f32[64,4096]{1,0:T(8,128)S(1)}, u32[]{:S(2)}, u32[]{:S(2)}) collective-permute-start(f32[64,4096]{1,0:T(8,128)S(1)} %add.30), channel_id=1, source_target_pairs={{0,16},{8,24},{16,0},{24,8},{1,17},{9,25},{17,1},{25,9},{2,18},{10... | collective-permute-start | bytes 3145736 | tf_op jit(solution)/shard_map/ppermute | solution.py:30
  16.2 1.9 %collective-permute-start.2 = (bf16[64,768]{1,0:T(8,128)(2,1)S(1)}, bf16[64,768]{1,0:T(8,128)(2,1)S(1)}, u32[]{:S(2)}, u32[]{:S(2)}) collective-permute-start(bf16[64,768]{1,0:T(8,128)(2,1)S(1)} %add_convert_fusion.5), channel_id=1, source_target_pairs={{0,2},{1,3},{2,0},{3,1},{4,6},{5,7},{6,4},{7,5},{8,10},{9,11},{10,... | collective-permute-start | bytes 294920 | tf_op jit(solution)/shard_map/ppermute | solution.py:30
  18.1 2.4 %gram.4 = (bf16[256,512]{1,0:T(8,128)(2,1)S(1)}, bf16[256,512]{1,0:T(8,128)(2,1)S(1)}) custom-call(s32[1]{0:T(128)} %bitcast.side.token, bf16[768,8192]{1,0:T(8,128)(2,1)S(1)} %get-tuple-element.60.a_ref.refs_1_), custom_call_target="tpu_custom_call" | custom-call | flops 1000 | bytes 6666666 | tf_op jit(solution)/shard_map/gram/pallas_call | solution.py:199
  20.9 2.9 %collective-permute-start.3 = (bf16[64,768]{1,0:T(8,128)(2,1)S(1)}, bf16[64,768]{1,0:T(8,128)(2,1)S(1)}, u32[]{:S(2)}, u32[]{:S(2)}) collective-permute-start(bf16[64,768]{1,0:T(8,128)(2,1)S(1)} %add_convert_fusion.4.refs_8_), channel_id=1, source_target_pairs={{0,4},{1,5},{2,6},{3,7},{4,0},{5,1},{6,2},{7,3},{8,12},{9,13},{10,... | collective-permute-start | bytes 294920 | tf_op jit(solution)/shard_map/ppermute | solution.py:30
  23.8 2.4 %gram.5 = (bf16[256,512]{1,0:T(8,128)(2,1)S(1)}, bf16[256,512]{1,0:T(8,128)(2,1)S(1)}) custom-call(s32[1]{0:T(128)} %bitcast.side.token, bf16[768,8192]{1,0:T(8,128)(2,1)S(1)} %get-tuple-element.60.a_ref.refs_1_), custom_call_target="tpu_custom_call" | custom-call | flops 1000 | bytes 10000000 | tf_op jit(solution)/shard_map/gram/pallas_call | solution.py:199
  26.7 0.6 %turn.1 = (bf16[64,768]{1,0:T(8,128)(2,1)S(1)}, bf16[64,768]{1,0:T(8,128)(2,1)S(1)}) custom-call(s32[64,768]{1,0:T(8,128)S(1)} %get-tuple-element.61.sign.refs_3_, f32[64,128]{1,0:T(8,128)S(1)} %get-tuple-element.56.scale.refs_0_, f32[64,768]{1,0:T(8,128)S(1)} %get-tuple-element.62.pulled, bf16[256,256]{1,0:T(8,128)(2,1)S(1)} %get-tuple-element.65.refs_0_, ...), custom_call_target="tpu_custom_call" | custom-call | flops 1000 | bytes 1000 | tf_op jit(solution)/shard_map/turn/pallas_call | solution.py:242
  27.3 2.8 %collective-permute-start.4 = (bf16[64,768]{1,0:T(8,128)(2,1)S(1)}, bf16[64,768]{1,0:T(8,128)(2,1)S(1)}, u32[]{:S(2)}, u32[]{:S(2)}) collective-permute-start(bf16[64,768]{1,0:T(8,128)(2,1)S(1)} %get-tuple-element.80), channel_id=1, source_target_pairs={{0,3},{1,2},{2,1},{3,0},{4,7},{5,6},{6,5},{7,4},{8,11},{9,10},{10,... | collective-permute-start | bytes 294920 | tf_op jit(solution)/shard_map/ppermute | solution.py:30
  30.9 2.0 %collective-permute-done.4 = bf16[64,768]{1,0:T(8,128)(2,1)S(1)} collective-permute-done((bf16[64,768]{1,0:T(8,128)(2,1)S(1)}, bf16[64,768]{1,0:T(8,128)(2,1)S(1)}, u32[]{:S(2)}, u32[]{:S(2)}) %collective-permute-start.4) | collective-permute-done | bytes 98336 | tf_op jit(solution)/shard_map/ppermute | solution.py:30
  32.9 1.9 %collective-permute-done.5 = bf16[64,768]{1,0:T(8,128)(2,1)S(1)} collective-permute-done((bf16[64,768]{1,0:T(8,128)(2,1)S(1)}, bf16[64,768]{1,0:T(8,128)(2,1)S(1)}, u32[]{:S(2)}, u32[]{:S(2)}) %collective-permute-start.5) | collective-permute-done | bytes 98336 | tf_op jit(solution)/shard_map/ppermute | solution.py:30
  35.1 3.9 %collective-permute-start.7 = (bf16[64,768]{1,0:T(8,128)(2,1)S(1)}, bf16[64,768]{1,0:T(8,128)(2,1)S(1)}, u32[]{:S(2)}, u32[]{:S(2)}) collective-permute-start(bf16[64,768]{1,0:T(8,128)(2,1)S(1)} %add_convert_fusion.3.refs_4_), channel_id=1, source_target_pairs={{0,4},{1,5},{2,6},{3,7},{4,0},{5,1},{6,2},{7,3},{8,12},{9,13},{10,... | collective-permute-start | bytes 294920 | tf_op jit(solution)/shard_map/ppermute | solution.py:30
  39.6 3.0 %collective-permute-done.7.refs_5_ = bf16[64,768]{1,0:T(8,128)(2,1)S(1)} collective-permute-done((bf16[64,768]{1,0:T(8,128)(2,1)S(1)}, bf16[64,768]{1,0:T(8,128)(2,1)S(1)}, u32[]{:S(2)}, u32[]{:S(2)}) %collective-permute-start.7) | collective-permute-done | bytes 98336 | tf_op jit(solution)/shard_map/ppermute | solution.py:30
  43.3 0.7 %push_other.3 = (f32[64,2560]{1,0:T(8,128)S(1)}, bf16[64,2560]{1,0:T(8,128)(2,1)S(1)}) custom-call(s32[1]{0:T(128)} %bitcast.side.token, f32[64,128]{1,0:T(8,128)S(1)} %get-tuple-element.56.scale.refs_0_, bf16[768,8192]{1,0:T(8,128)(2,1)S(1)} %get-tuple-element.60.a_ref.refs_1_, bf16[128,768]{1,0:T(8,128)(2,1)S(1)} %get-tuple-element.83.refs_2_), custom_call_target="tpu_custom_call" | custom-call | flops 1000 | bytes 1000 | tf_op jit(solution)/shard_map/push_other/pallas_call | solution.py:277
  45.2 1.6 %collective-permute-start.13 = (bf16[64,1536]{1,0:T(8,128)(2,1)S(1)}, bf16[64,1536]{1,0:T(8,128)(2,1)S(1)}, u32[]{:S(2)}, u32[]{:S(2)}) collective-permute-start(bf16[64,1536]{1,0:T(8,128)(2,1)S(1)} %get-tuple-element.88), channel_id=1, source_target_pairs={{0,16},{8,24},{16,0},{24,8},{1,17},{9,25},{17,1},{25,9},{2,18},{10... | collective-permute-start | bytes 589832 | tf_op jit(solution)/shard_map/ppermute | solution.py:30
  48.3 1.6 %store_x.1 = f32[64,8192]{1,0:T(8,128)} custom-call(s32[1]{0:T(128)} %bitcast.side.token, f32[64,128]{1,0:T(8,128)S(1)} %get-tuple-element.56.scale.refs_0_, f32[64,8192]{1,0:T(8,128)S(1)} %get-tuple-element.57.x_ref, f32[64,8192]{1,0:T(8,128)S(1)} %get-tuple-element.58.u_ref, f32[64,8192]{1,0:T(8,128)S(1)} %get-tuple-element.59.z_ref, ...), custom_call_target="tpu_custom_call" | custom-call | flops 1000 | bytes 1000 | tf_op jit(solution)/shard_map/store_x/pallas_call | solution.py:311
  49.9 3.1 %collective-permute-done.13 = bf16[64,1536]{1,0:T(8,128)(2,1)S(1)} collective-permute-done((bf16[64,1536]{1,0:T(8,128)(2,1)S(1)}, bf16[64,1536]{1,0:T(8,128)(2,1)S(1)}, u32[]{:S(2)}, u32[]{:S(2)}) %collective-permute-start.13) | collective-permute-done | bytes 196640 | tf_op jit(solution)/shard_map/ppermute | solution.py:30
  53.1 1.6 %collective-permute-start.12 = (bf16[64,1024]{1,0:T(8,128)(2,1)S(1)}, bf16[64,1024]{1,0:T(8,128)(2,1)S(1)}, u32[]{:S(2)}, u32[]{:S(2)}) collective-permute-start(bf16[64,1024]{1,0:T(8,128)(2,1)S(1)} %get-tuple-element.97), channel_id=1, source_target_pairs={{0,16},{8,24},{16,0},{24,8},{1,17},{9,25},{17,1},{25,9},{2,18},{10... | collective-permute-start | bytes 393224 | tf_op jit(solution)/shard_map/ppermute | solution.py:30
  54.7 1.2 %final.4 = (f32[64,8192]{1,0:T(8,128)}, f32[64,8192]{1,0:T(8,128)}) custom-call(s32[1]{0:T(128)} %bitcast.side.token, f32[64,128]{1,0:T(8,128)S(1)} %get-tuple-element.56.scale.refs_0_, f32[64,8192]{1,0:T(8,128)S(1)} %get-tuple-element.57.x_ref, f32[64,8192]{1,0:T(8,128)S(1)} %get-tuple-element.58.u_ref, f32[64,8192]{1,0:T(8,128)S(1)} %get-tuple-element.59.z_ref, ...), custom_call_target="tpu_custom_call" | custom-call | flops 1000 | bytes 1000 | tf_op jit(solution)/shard_map/final/pallas_call | solution.py:363
  55.9 1.3 %collective-permute-done.15 = bf16[64,1536]{1,0:T(8,128)(2,1)S(1)} collective-permute-done((bf16[64,1536]{1,0:T(8,128)(2,1)S(1)}, bf16[64,1536]{1,0:T(8,128)(2,1)S(1)}, u32[]{:S(2)}, u32[]{:S(2)}) %collective-permute-start.15) | collective-permute-done | bytes 196640 | tf_op jit(solution)/shard_map/ppermute | solution.py:30
  57.4 1.7 %final.5 = (f32[64,8192]{1,0:T(8,128)}, f32[64,8192]{1,0:T(8,128)}) custom-call(s32[1]{0:T(128)} %bitcast.side.token, f32[64,128]{1,0:T(8,128)S(1)} %get-tuple-element.56.scale.refs_0_, f32[64,8192]{1,0:T(8,128)S(1)} %get-tuple-element.57.x_ref, f32[64,8192]{1,0:T(8,128)S(1)} %get-tuple-element.58.u_ref, ...), custom_call_target="tpu_custom_call", output_to_operand_aliasing={{0}: (11, {}), {1}: (12, {})} | custom-call | flops 1000 | bytes 1000 | tf_op jit(solution)/shard_map/final/pallas_call | solution.py:363
  59.8 1.6 %final.6 = (f32[64,8192]{1,0:T(8,128)}, f32[64,8192]{1,0:T(8,128)}) custom-call(s32[1]{0:T(128)} %bitcast.side.token, f32[64,128]{1,0:T(8,128)S(1)} %get-tuple-element.56.scale.refs_0_, f32[64,8192]{1,0:T(8,128)S(1)} %get-tuple-element.57.x_ref, f32[64,8192]{1,0:T(8,128)S(1)} %get-tuple-element.58.u_ref, ...), custom_call_target="tpu_custom_call", output_to_operand_aliasing={{0}: (11, {}), {1}: (12, {})} | custom-call | flops 1000 | bytes 1000 | tf_op jit(solution)/shard_map/final/pallas_call | solution.py:363
  61.3 1.0 %final.7 = (f32[64,8192]{1,0:T(8,128)}, f32[64,8192]{1,0:T(8,128)}) custom-call(s32[1]{0:T(128)} %bitcast.side.token, f32[64,128]{1,0:T(8,128)S(1)} %get-tuple-element.56.scale.refs_0_, f32[64,8192]{1,0:T(8,128)S(1)} %get-tuple-element.57.x_ref, f32[64,8192]{1,0:T(8,128)S(1)} %get-tuple-element.58.u_ref, ...), custom_call_target="tpu_custom_call", output_to_operand_aliasing={{0}: (8, {}), {1}: (9, {})} | custom-call | flops 1000 | bytes 1000 | tf_op jit(solution)/shard_map/final/pallas_call | solution.py:363
  (35 shorter events, 7.8 us)
Async XLA Ops:
  9.7 4.4 %collective-permute-start.1 = (f32[64,4096]{1,0:T(8,128)S(1)}, f32[64,4096]{1,0:T(8,128)S(1)}, u32[]{:S(2)}, u32[]{:S(2)}) collective-permute-start(f32[64,4096]{1,0:T(8,128)S(1)} %get-tuple-element.68), channel_id=1, source_target_pairs={{0,8},{8,0},{16,24},{24,16},{1,9},{9,1},{17,25},{25,17},{2,10},{10... | collective-permute-start | bytes 3145736 | tf_op jit(solution)/shard_map/ppermute | solution.py:30
  10.2 6.0 %collective-permute-start = (bf16[64,768]{1,0:T(8,128)(2,1)S(1)}, bf16[64,768]{1,0:T(8,128)(2,1)S(1)}, u32[]{:S(2)}, u32[]{:S(2)}) collective-permute-start(bf16[64,768]{1,0:T(8,128)(2,1)S(1)} %get-tuple-element.63), channel_id=1, source_target_pairs={{0,1},{1,0},{2,3},{3,2},{4,5},{5,4},{6,7},{7,6},{8,9},{9,8},{10,11... | collective-permute-start | bytes 294920 | tf_op jit(solution)/shard_map/ppermute | solution.py:30
  14.2 25.3 %collective-permute-start.8 = (f32[64,4096]{1,0:T(8,128)S(1)}, f32[64,4096]{1,0:T(8,128)S(1)}, u32[]{:S(2)}, u32[]{:S(2)}) collective-permute-start(f32[64,4096]{1,0:T(8,128)S(1)} %add.30), channel_id=1, source_target_pairs={{0,16},{8,24},{16,0},{24,8},{1,17},{9,25},{17,1},{25,9},{2,18},{10... | collective-permute-start | bytes 3145736 | tf_op jit(solution)/shard_map/ppermute | solution.py:30
  16.2 4.7 %collective-permute-start.2 = (bf16[64,768]{1,0:T(8,128)(2,1)S(1)}, bf16[64,768]{1,0:T(8,128)(2,1)S(1)}, u32[]{:S(2)}, u32[]{:S(2)}) collective-permute-start(bf16[64,768]{1,0:T(8,128)(2,1)S(1)} %add_convert_fusion.5), channel_id=1, source_target_pairs={{0,2},{1,3},{2,0},{3,1},{4,6},{5,7},{6,4},{7,5},{8,10},{9,11},{10,... | collective-permute-start | bytes 294920 | tf_op jit(solution)/shard_map/ppermute | solution.py:30
  20.9 5.7 %collective-permute-start.3 = (bf16[64,768]{1,0:T(8,128)(2,1)S(1)}, bf16[64,768]{1,0:T(8,128)(2,1)S(1)}, u32[]{:S(2)}, u32[]{:S(2)}) collective-permute-start(bf16[64,768]{1,0:T(8,128)(2,1)S(1)} %add_convert_fusion.4.refs_8_), channel_id=1, source_target_pairs={{0,4},{1,5},{2,6},{3,7},{4,0},{5,1},{6,2},{7,3},{8,12},{9,13},{10,... | collective-permute-start | bytes 294920 | tf_op jit(solution)/shard_map/ppermute | solution.py:30
  27.3 5.6 %collective-permute-start.4 = (bf16[64,768]{1,0:T(8,128)(2,1)S(1)}, bf16[64,768]{1,0:T(8,128)(2,1)S(1)}, u32[]{:S(2)}, u32[]{:S(2)}) collective-permute-start(bf16[64,768]{1,0:T(8,128)(2,1)S(1)} %get-tuple-element.80), channel_id=1, source_target_pairs={{0,3},{1,2},{2,1},{3,0},{4,7},{5,6},{6,5},{7,4},{8,11},{9,10},{10,... | collective-permute-start | bytes 294920 | tf_op jit(solution)/shard_map/ppermute | solution.py:30
  30.1 4.6 %collective-permute-start.5 = (bf16[64,768]{1,0:T(8,128)(2,1)S(1)}, bf16[64,768]{1,0:T(8,128)(2,1)S(1)}, u32[]{:S(2)}, u32[]{:S(2)}) collective-permute-start(bf16[64,768]{1,0:T(8,128)(2,1)S(1)} %get-tuple-element.80), channel_id=1, source_target_pairs={{0,2},{1,3},{2,0},{3,1},{4,6},{5,7},{6,4},{7,5},{8,10},{9,11},{10,... | collective-permute-start | bytes 294920 | tf_op jit(solution)/shard_map/ppermute | solution.py:30
  30.5 4.6 %collective-permute-start.6 = (bf16[64,768]{1,0:T(8,128)(2,1)S(1)}, bf16[64,768]{1,0:T(8,128)(2,1)S(1)}, u32[]{:S(2)}, u32[]{:S(2)}) collective-permute-start(bf16[64,768]{1,0:T(8,128)(2,1)S(1)} %get-tuple-element.80), channel_id=1, source_target_pairs={{0,1},{1,0},{2,3},{3,2},{4,5},{5,4},{6,7},{7,6},{8,9},{9,8},{10,11... | collective-permute-start | bytes 294920 | tf_op jit(solution)/shard_map/ppermute | solution.py:30
  35.1 7.5 %collective-permute-start.7 = (bf16[64,768]{1,0:T(8,128)(2,1)S(1)}, bf16[64,768]{1,0:T(8,128)(2,1)S(1)}, u32[]{:S(2)}, u32[]{:S(2)}) collective-permute-start(bf16[64,768]{1,0:T(8,128)(2,1)S(1)} %add_convert_fusion.3.refs_4_), channel_id=1, source_target_pairs={{0,4},{1,5},{2,6},{3,7},{4,0},{5,1},{6,2},{7,3},{8,12},{9,13},{10,... | collective-permute-start | bytes 294920 | tf_op jit(solution)/shard_map/ppermute | solution.py:30
  43.2 1.5 %collective-permute-start.9 = (bf16[64,1536]{1,0:T(8,128)(2,1)S(1)}, bf16[64,1536]{1,0:T(8,128)(2,1)S(1)}, u32[]{:S(2)}, u32[]{:S(2)}) collective-permute-start(bf16[64,1536]{1,0:T(8,128)(2,1)S(1)} %get-tuple-element.86), channel_id=1, source_target_pairs={{0,8},{8,0},{16,24},{24,16},{1,9},{9,1},{17,25},{25,17},{2,10},{10... | collective-permute-start | bytes 589832 | tf_op jit(solution)/shard_map/ppermute | solution.py:30
  44.0 2.8 %collective-permute-start.10 = (bf16[64,2560]{1,0:T(8,128)(2,1)S(1)}, bf16[64,2560]{1,0:T(8,128)(2,1)S(1)}, u32[]{:S(2)}, u32[]{:S(2)}) collective-permute-start(bf16[64,2560]{1,0:T(8,128)(2,1)S(1)} %get-tuple-element.90), channel_id=1, source_target_pairs={{0,8},{8,0},{16,24},{24,16},{1,9},{9,1},{17,25},{25,17},{2,10},{10... | collective-permute-start | bytes 983048 | tf_op jit(solution)/shard_map/ppermute | solution.py:30
  45.2 7.8 %collective-permute-start.13 = (bf16[64,1536]{1,0:T(8,128)(2,1)S(1)}, bf16[64,1536]{1,0:T(8,128)(2,1)S(1)}, u32[]{:S(2)}, u32[]{:S(2)}) collective-permute-start(bf16[64,1536]{1,0:T(8,128)(2,1)S(1)} %get-tuple-element.88), channel_id=1, source_target_pairs={{0,16},{8,24},{16,0},{24,8},{1,17},{9,25},{17,1},{25,9},{2,18},{10... | collective-permute-start | bytes 589832 | tf_op jit(solution)/shard_map/ppermute | solution.py:30
  46.8 10.6 %collective-permute-start.11 = (f32[64,4096]{1,0:T(8,128)S(1)}, f32[64,4096]{1,0:T(8,128)S(1)}, u32[]{:S(2)}, u32[]{:S(2)}) collective-permute-start(f32[64,4096]{1,0:T(8,128)S(1)} %add.36.refs_0_.refs_3_), channel_id=1, source_target_pairs={{0,8},{8,0},{16,24},{24,16},{1,9},{9,1},{17,25},{25,17},{2,10},{10... | collective-permute-start | bytes 3145736 | tf_op jit(solution)/shard_map/ppermute | solution.py:30
  47.3 9.9 %collective-permute-start.15 = (bf16[64,1536]{1,0:T(8,128)(2,1)S(1)}, bf16[64,1536]{1,0:T(8,128)(2,1)S(1)}, u32[]{:S(2)}, u32[]{:S(2)}) collective-permute-start(bf16[64,1536]{1,0:T(8,128)(2,1)S(1)} %get-tuple-element.92), channel_id=1, source_target_pairs={{0,16},{8,24},{16,0},{24,8},{1,17},{9,25},{17,1},{25,9},{2,18},{10... | collective-permute-start | bytes 589832 | tf_op jit(solution)/shard_map/ppermute | solution.py:30
  53.1 6.2 %collective-permute-start.12 = (bf16[64,1024]{1,0:T(8,128)(2,1)S(1)}, bf16[64,1024]{1,0:T(8,128)(2,1)S(1)}, u32[]{:S(2)}, u32[]{:S(2)}) collective-permute-start(bf16[64,1024]{1,0:T(8,128)(2,1)S(1)} %get-tuple-element.97), channel_id=1, source_target_pairs={{0,16},{8,24},{16,0},{24,8},{1,17},{9,25},{17,1},{25,9},{2,18},{10... | collective-permute-start | bytes 393224 | tf_op jit(solution)/shard_map/ppermute | solution.py:30
  55.8 1.6 %collective-permute-start.14 = (bf16[64,1536]{1,0:T(8,128)(2,1)S(1)}, bf16[64,1536]{1,0:T(8,128)(2,1)S(1)}, u32[]{:S(2)}, u32[]{:S(2)}) collective-permute-start(bf16[64,1536]{1,0:T(8,128)(2,1)S(1)} %add_convert_fusion.1.refs_2_), channel_id=1, source_target_pairs={{0,8},{8,0},{16,24},{24,16},{1,9},{9,1},{17,25},{25,17},{2,10},{10... | collective-permute-start | bytes 589832 | tf_op jit(solution)/shard_map/ppermute | solution.py:30
  57.3 2.4 %collective-permute-start.17 = (bf16[64,1536]{1,0:T(8,128)(2,1)S(1)}, bf16[64,1536]{1,0:T(8,128)(2,1)S(1)}, u32[]{:S(2)}, u32[]{:S(2)}) collective-permute-start(bf16[64,1536]{1,0:T(8,128)(2,1)S(1)} %add_convert_fusion.refs_5_), channel_id=1, source_target_pairs={{0,8},{8,0},{16,24},{24,16},{1,9},{9,1},{17,25},{25,17},{2,10},{10... | collective-permute-start | bytes 589832 | tf_op jit(solution)/shard_map/ppermute | solution.py:30
  59.3 2.0 %collective-permute-start.16 = (bf16[64,1024]{1,0:T(8,128)(2,1)S(1)}, bf16[64,1024]{1,0:T(8,128)(2,1)S(1)}, u32[]{:S(2)}, u32[]{:S(2)}) collective-permute-start(bf16[64,1024]{1,0:T(8,128)(2,1)S(1)} %add_convert_fusion.2.refs_5_), channel_id=1, source_target_pairs={{0,8},{8,0},{16,24},{24,16},{1,9},{9,1},{17,25},{25,17},{2,10},{10... | collective-permute-start | bytes 393224 | tf_op jit(solution)/shard_map/ppermute | solution.py:30

commit v13 on v11

--- a/solution.py
+++ b/solution.py
@@ -15,7 +15,6 @@
 OTHER = (3, 5)
 STEP = 1024
 WIDE = 2048
-AHEAD = 8
 NARROW = 256
 WAIT_BYTES = 10_000_000
 GRAM_ORDER = (0, 1, 2)
@@ -80,26 +79,30 @@
 
 
 def load_kernel(blocks_count, side, x_hbm, u_hbm, z_hbm, a_hbm, sign_hbm, eta_hbm, rho_hbm, lam_hbm, *refs):
-    outs, (eta_row, rho_row, lam_row, both, acc, sems) = refs[:10], refs[10:]
+    outs, (eta_row, rho_row, lam_row, *boths, acc, sems) = refs[:10], refs[10:]
     m_out, pulled_out, a_out, x_out, u_out, z_out, sign_out, scale, mine_out, other_out = outs
     tasks, width = x_hbm.shape
     steps = width // STEP
     rows = ((eta_hbm, eta_row), (rho_hbm, rho_row), (lam_hbm, lam_row), (sign_hbm, sign_out))
     small = [pltpu.make_async_copy(a, b, sems.at[4, k]) for k, (a, b) in enumerate(rows)]
 
-    def chunk(j):
-        at = columns(j * STEP, STEP)
-        pairs = ((x_hbm, x_out), (u_hbm, u_out), (z_hbm, z_out), (a_hbm, a_out))
+    def vectors(j):
+        at = pl.ds(j * STEP, STEP)
+        pairs = ((x_hbm, x_out), (u_hbm, u_out), (z_hbm, z_out))
         return [pltpu.make_async_copy(a.at[:, at], b.at[:, at], sems.at[k, j]) for k, (a, b) in enumerate(pairs)]
 
-    def begin(j):
-        for copy in chunk(j):
-            copy.start()
-
-    for copy in small[:3]:
+    def matrix(j):
+        at = pl.ds(j * STEP, STEP)
+        return pltpu.make_async_copy(a_hbm.at[:, at], a_out.at[:, at], sems.at[3, j])
+
+    for copy in small[:3] + vectors(0):
         copy.start()
-    for j in range(min(AHEAD, steps)):
-        begin(j)
+    for j in range(steps):
+        if j + 1 < steps:
+            for copy in vectors(j + 1):
+                copy.start()
+        matrix(j).start()
+    small[3].start()
     for copy in small[:3]:
         copy.wait()
     one = lax.broadcasted_iota(jnp.int32, (tasks, tasks), 0) == lax.broadcasted_iota(jnp.int32, (tasks, tasks), 1)
@@ -107,34 +110,30 @@
     for k, row in enumerate((eta, eta * rho, lam / (rho * blocks_count))):
         upright = jnp.where(one, jnp.broadcast_to(row, (tasks, tasks)), 0.0)
         scale[:, k : k + 1] = jnp.sum(upright, axis=1, keepdims=True)
-    acc[...] = jnp.zeros_like(acc)
-
-    @pl.loop(0, steps)
-    def _(j):
-        for copy in chunk(j):
-            copy.wait()
-
-        @pl.when(j + AHEAD < steps)
-        def _():
-            begin(j + AHEAD)
-
-        @pl.when(j == max(steps - AHEAD, 0))
-        def _():
-            small[3].start()
-
-        pull = scale[:, 1:2]
+    pull = scale[:, 1:2]
+
+    def prepare(j, both):
         for k in range(0, STEP, NARROW):
-            at, here = columns(j * STEP + k, NARROW), pl.ds(k, NARROW)
+            at, here = pl.ds(j * STEP + k, NARROW), pl.ds(k, NARROW)
             x = x_out[:, at]
             v = x - pull * (x - z_out[:, at] + u_out[:, at])
-            top = v.astype(BF16)
             both[:tasks, here] = x.astype(BF16)
-            both[tasks : 2 * tasks, here] = top
-            both[2 * tasks :, here] = (v - top.astype(F32)).astype(BF16)
-        acc[...] += nt(both[...], a_out[:, columns(j * STEP, STEP)])
+            both[tasks:, here] = v.astype(BF16)
+
+    for copy in vectors(0):
+        copy.wait()
+    prepare(0, boths[0])
+    for j in range(steps):
+        matrix(j).wait()
+        if j + 1 < steps:
+            for copy in vectors(j + 1):
+                copy.wait()
+            prepare(j + 1, boths[(j + 1) % 2])
+        product = nt(boths[j % 2][...], a_out[:, pl.ds(j * STEP, STEP)])
+        acc[...] = product if j == 0 else acc[...] + product
 
     m_out[...] = acc[:tasks].astype(BF16)
-    pulled_out[...] = acc[tasks : 2 * tasks] + acc[2 * tasks :]
+    pulled_out[...] = acc[tasks:]
     half = width // 2
     mine = columns(side[0] * half, half)
     other = columns((1 - side[0]) * half, half)
@@ -160,7 +159,7 @@
         [VMEM] * 10,
         [pltpu.VMEM((1, tasks), F32)] * 3
         + [
-            pltpu.VMEM((3 * tasks, STEP), BF16), pltpu.VMEM((3 * tasks, samples), F32),
+            *[pltpu.VMEM((2 * tasks, STEP), BF16)] * 2, pltpu.VMEM((2 * tasks, samples), F32),
             pltpu.SemaphoreType.DMA((5, max(width // STEP, 4))),
         ],
     )(side, *pin(pltpu.HBM, x, u, z, design, sign, *rows))

time: 60 us -> 60.9 us (1.015)
  Pallas kernels: 25.5 us -> 26.4 us
    pallas_call x1, Pallas kernels: 8.09 us -> 8.82 us  [load(): call(functools.partial(load_kernel, blocks_count), 'load_and_margins', [S...]
  transfers between devices with their start and end apart: 18 -> 18, of which waited for: 11 -> 11; matrix products, arithmetic and copies ran while one was open for 1% -> 1% of each run, Pallas kernels for 27% -> 26%
where the time goes in v13:
time: 60.9 us; the launch traced here: 60.8 us
  Pallas kernels  26.4 us (43%)
  starting transfers between devices  20.5 us (34%)
  waiting for transfers between devices  12.4 us (20%)
  between operations  1.01 us (2%)
    ppermute x18, starting transfers between devices, exchange(): return lax.ppermute(value, axis, [(i, i ^ mask) for i in range(n)])  20.5 us
    ppermute x18, waiting for transfers between devices, exchange(): return lax.ppermute(value, axis, [(i, i ^ mask) for i in range(n)])  12.4 us
    pallas_call x1, Pallas kernels, load(): call(functools.partial(load_kernel, blocks_count), 'load_and_margins', [S...  8.82 us
    pallas_call x3, Pallas kernels, gram_row(): call(functools.partial(gram_kernel, row), 'gram', [SMEM, VMEM], (out, out...  7.1 us
    pallas_call x4, Pallas kernels, final(): call(functools.partial(final_kernel, blocks_count, places, buffered), 'fi...  5.41 us
    pallas_call x5, Pallas kernels, push(): call(functools.partial(push_kernel, first, mine, begin, offset, size), 'p...  2.88 us
    pallas_call x1, Pallas kernels, store_x(): call(store_kernel, 'store_x', [SMEM] + [VMEM] * len(args), pltpu.HBM((tas...  1.58 us
  transfers between devices with their start and end apart: 18, of which 11 were waited for; matrix products, arithmetic and copies ran while one was open for 1% of the time, Pallas kernels for 26%

profile of v13, /device:TPU:0, one launch (start us, length us, event | category | flops | bytes accessed | tf_op | source)
XLA Modules:
  0.0 60.8 jit_solution(5134317892827522270)
XLA Ops:
  0.6 8.8 %load_and_margins.1 = (bf16[64,768]{1,0:T(8,128)(2,1)S(1)}, f32[64,768]{1,0:T(8,128)S(1)}, bf16[768,8192]{1,0:T(8,128)(2,1)S(1)}, f32[64,8192]{1,0:T(8,128)S(1)}...) custom-call(s32[1]{0:T(128)} %bitcast.side.token, ...), custom_call_target="tpu_custom_call" | custom-call | flops 1000 | bytes 1000 | tf_op jit(solution)/shard_map/load_and_margins/pallas_call | solution.py:151
  10.0 2.6 %collective-permute-start = (bf16[64,768]{1,0:T(8,128)(2,1)S(1)}, bf16[64,768]{1,0:T(8,128)(2,1)S(1)}, u32[]{:S(2)}, u32[]{:S(2)}) collective-permute-start(bf16[64,768]{1,0:T(8,128)(2,1)S(1)} %get-tuple-element.61), channel_id=1, source_target_pairs={{0,1},{1,0},{2,3},{3,2},{4,5},{5,4},{6,7},{7,6},{8,9},{9,8},{10,11... | collective-permute-start | bytes 294920 | tf_op jit(solution)/shard_map/ppermute | solution.py:28
  12.6 1.3 %gram.3 = (bf16[256,256]{1,0:T(8,128)(2,1)S(1)}, bf16[256,256]{1,0:T(8,128)(2,1)S(1)}) custom-call(s32[1]{0:T(128)} %bitcast.side.token, bf16[768,8192]{1,0:T(8,128)(2,1)S(1)} %get-tuple-element.58.a_ref.refs_1_), custom_call_target="tpu_custom_call" | custom-call | flops 1000 | bytes 3333333 | tf_op jit(solution)/shard_map/gram/pallas_call | solution.py:190
  14.0 1.6 %collective-permute-start.8 = (f32[64,4096]{1,0:T(8,128)S(1)}, f32[64,4096]{1,0:T(8,128)S(1)}, u32[]{:S(2)}, u32[]{:S(2)}) collective-permute-start(f32[64,4096]{1,0:T(8,128)S(1)} %add.30), channel_id=1, source_target_pairs={{0,16},{8,24},{16,0},{24,8},{1,17},{9,25},{17,1},{25,9},{2,18},{10... | collective-permute-start | bytes 3145736 | tf_op jit(solution)/shard_map/ppermute | solution.py:28
  16.0 1.9 %collective-permute-start.2 = (bf16[64,768]{1,0:T(8,128)(2,1)S(1)}, bf16[64,768]{1,0:T(8,128)(2,1)S(1)}, u32[]{:S(2)}, u32[]{:S(2)}) collective-permute-start(bf16[64,768]{1,0:T(8,128)(2,1)S(1)} %add_convert_fusion.5), channel_id=1, source_target_pairs={{0,2},{1,3},{2,0},{3,1},{4,6},{5,7},{6,4},{7,5},{8,10},{9,11},{10,... | collective-permute-start | bytes 294920 | tf_op jit(solution)/shard_map/ppermute | solution.py:28
  17.9 2.4 %gram.4 = (bf16[256,512]{1,0:T(8,128)(2,1)S(1)}, bf16[256,512]{1,0:T(8,128)(2,1)S(1)}) custom-call(s32[1]{0:T(128)} %bitcast.side.token, bf16[768,8192]{1,0:T(8,128)(2,1)S(1)} %get-tuple-element.58.a_ref.refs_1_), custom_call_target="tpu_custom_call" | custom-call | flops 1000 | bytes 6666666 | tf_op jit(solution)/shard_map/gram/pallas_call | solution.py:190
  20.7 2.9 %collective-permute-start.3 = (bf16[64,768]{1,0:T(8,128)(2,1)S(1)}, bf16[64,768]{1,0:T(8,128)(2,1)S(1)}, u32[]{:S(2)}, u32[]{:S(2)}) collective-permute-start(bf16[64,768]{1,0:T(8,128)(2,1)S(1)} %add_convert_fusion.4.refs_6_), channel_id=1, source_target_pairs={{0,4},{1,5},{2,6},{3,7},{4,0},{5,1},{6,2},{7,3},{8,12},{9,13},{10,... | collective-permute-start | bytes 294920 | tf_op jit(solution)/shard_map/ppermute | solution.py:28
  23.6 3.5 %gram.5 = (bf16[256,768]{1,0:T(8,128)(2,1)S(1)}, bf16[256,768]{1,0:T(8,128)(2,1)S(1)}) custom-call(s32[1]{0:T(128)} %bitcast.side.token, bf16[768,8192]{1,0:T(8,128)(2,1)S(1)} %get-tuple-element.58.a_ref.refs_1_), custom_call_target="tpu_custom_call" | custom-call | flops 1000 | bytes 10000000 | tf_op jit(solution)/shard_map/gram/pallas_call | solution.py:190
  27.7 2.6 %collective-permute-start.6 = (bf16[64,768]{1,0:T(8,128)(2,1)S(1)}, bf16[64,768]{1,0:T(8,128)(2,1)S(1)}, u32[]{:S(2)}, u32[]{:S(2)}) collective-permute-start(bf16[64,768]{1,0:T(8,128)(2,1)S(1)} %get-tuple-element.76), channel_id=1, source_target_pairs={{0,3},{1,2},{2,1},{3,0},{4,7},{5,6},{6,5},{7,4},{8,11},{9,10},{10,... | collective-permute-start | bytes 294920 | tf_op jit(solution)/shard_map/ppermute | solution.py:28
  31.3 2.1 %collective-permute-done.6 = bf16[64,768]{1,0:T(8,128)(2,1)S(1)} collective-permute-done((bf16[64,768]{1,0:T(8,128)(2,1)S(1)}, bf16[64,768]{1,0:T(8,128)(2,1)S(1)}, u32[]{:S(2)}, u32[]{:S(2)}) %collective-permute-start.6) | collective-permute-done | bytes 98336 | tf_op jit(solution)/shard_map/ppermute | solution.py:28
  33.4 1.5 %collective-permute-done.5 = bf16[64,768]{1,0:T(8,128)(2,1)S(1)} collective-permute-done((bf16[64,768]{1,0:T(8,128)(2,1)S(1)}, bf16[64,768]{1,0:T(8,128)(2,1)S(1)}, u32[]{:S(2)}, u32[]{:S(2)}) %collective-permute-start.5) | collective-permute-done | bytes 98336 | tf_op jit(solution)/shard_map/ppermute | solution.py:28
  35.4 2.6 %collective-permute-start.7 = (bf16[64,768]{1,0:T(8,128)(2,1)S(1)}, bf16[64,768]{1,0:T(8,128)(2,1)S(1)}, u32[]{:S(2)}, u32[]{:S(2)}) collective-permute-start(bf16[64,768]{1,0:T(8,128)(2,1)S(1)} %add_convert_fusion.3.refs_4_), channel_id=1, source_target_pairs={{0,4},{1,5},{2,6},{3,7},{4,0},{5,1},{6,2},{7,3},{8,12},{9,13},{10,... | collective-permute-start | bytes 294920 | tf_op jit(solution)/shard_map/ppermute | solution.py:28
  38.0 1.3 %collective-permute-done.8 = f32[64,4096]{1,0:T(8,128)S(1)} collective-permute-done((f32[64,4096]{1,0:T(8,128)S(1)}, f32[64,4096]{1,0:T(8,128)S(1)}, u32[]{:S(2)}, u32[]{:S(2)}) %collective-permute-start.8) | collective-permute-done | bytes 1048608 | tf_op jit(solution)/shard_map/ppermute | solution.py:28
  39.4 1.6 %collective-permute-done.7.refs_5_ = bf16[64,768]{1,0:T(8,128)(2,1)S(1)} collective-permute-done((bf16[64,768]{1,0:T(8,128)(2,1)S(1)}, bf16[64,768]{1,0:T(8,128)(2,1)S(1)}, u32[]{:S(2)}, u32[]{:S(2)}) %collective-permute-start.7) | collective-permute-done | bytes 98336 | tf_op jit(solution)/shard_map/ppermute | solution.py:28
  41.6 0.7 %push_other.3 = (f32[64,2560]{1,0:T(8,128)S(1)}, bf16[64,2560]{1,0:T(8,128)(2,1)S(1)}) custom-call(s32[1]{0:T(128)} %bitcast.side.token, f32[64,128]{1,0:T(8,128)S(1)} %get-tuple-element.54.scale.refs_0_, bf16[768,8192]{1,0:T(8,128)(2,1)S(1)} %get-tuple-element.58.a_ref.refs_1_, bf16[128,768]{1,0:T(8,128)(2,1)S(1)} %get-tuple-element.79.refs_2_), custom_call_target="tpu_custom_call" | custom-call | flops 1000 | bytes 1000 | tf_op jit(solution)/shard_map/push_other/pallas_call | solution.py:266
  43.6 1.6 %collective-permute-start.13 = (bf16[64,1536]{1,0:T(8,128)(2,1)S(1)}, bf16[64,1536]{1,0:T(8,128)(2,1)S(1)}, u32[]{:S(2)}, u32[]{:S(2)}) collective-permute-start(bf16[64,1536]{1,0:T(8,128)(2,1)S(1)} %get-tuple-element.84), channel_id=1, source_target_pairs={{0,16},{8,24},{16,0},{24,8},{1,17},{9,25},{17,1},{25,9},{2,18},{10... | collective-permute-start | bytes 589832 | tf_op jit(solution)/shard_map/ppermute | solution.py:28
  46.9 1.6 %collective-permute-start.12 = (bf16[64,1024]{1,0:T(8,128)(2,1)S(1)}, bf16[64,1024]{1,0:T(8,128)(2,1)S(1)}, u32[]{:S(2)}, u32[]{:S(2)}) collective-permute-start(bf16[64,1024]{1,0:T(8,128)(2,1)S(1)} %get-tuple-element.93), channel_id=1, source_target_pairs={{0,16},{8,24},{16,0},{24,8},{1,17},{9,25},{17,1},{25,9},{2,18},{10... | collective-permute-start | bytes 393224 | tf_op jit(solution)/shard_map/ppermute | solution.py:28
  48.4 1.6 %store_x.1 = f32[64,8192]{1,0:T(8,128)} custom-call(s32[1]{0:T(128)} %bitcast.side.token, f32[64,128]{1,0:T(8,128)S(1)} %get-tuple-element.54.scale.refs_0_, f32[64,8192]{1,0:T(8,128)S(1)} %get-tuple-element.55.x_ref, f32[64,8192]{1,0:T(8,128)S(1)} %get-tuple-element.56.u_ref, f32[64,8192]{1,0:T(8,128)S(1)} %get-tuple-element.57.z_ref, ...), custom_call_target="tpu_custom_call" | custom-call | flops 1000 | bytes 1000 | tf_op jit(solution)/shard_map/store_x/pallas_call | solution.py:300
  50.0 1.4 %collective-permute-done.13 = bf16[64,1536]{1,0:T(8,128)(2,1)S(1)} collective-permute-done((bf16[64,1536]{1,0:T(8,128)(2,1)S(1)}, bf16[64,1536]{1,0:T(8,128)(2,1)S(1)}, u32[]{:S(2)}, u32[]{:S(2)}) %collective-permute-start.13) | collective-permute-done | bytes 196640 | tf_op jit(solution)/shard_map/ppermute | solution.py:28
  51.5 1.2 %final.4 = (f32[64,8192]{1,0:T(8,128)}, f32[64,8192]{1,0:T(8,128)}) custom-call(s32[1]{0:T(128)} %bitcast.side.token, f32[64,128]{1,0:T(8,128)S(1)} %get-tuple-element.54.scale.refs_0_, f32[64,8192]{1,0:T(8,128)S(1)} %get-tuple-element.55.x_ref, f32[64,8192]{1,0:T(8,128)S(1)} %get-tuple-element.56.u_ref, f32[64,8192]{1,0:T(8,128)S(1)} %get-tuple-element.57.z_ref, ...), custom_call_target="tpu_custom_call" | custom-call | flops 1000 | bytes 1000 | tf_op jit(solution)/shard_map/final/pallas_call | solution.py:350
  52.7 2.9 %collective-permute-done.15 = bf16[64,1536]{1,0:T(8,128)(2,1)S(1)} collective-permute-done((bf16[64,1536]{1,0:T(8,128)(2,1)S(1)}, bf16[64,1536]{1,0:T(8,128)(2,1)S(1)}, u32[]{:S(2)}, u32[]{:S(2)}) %collective-permute-start.15) | collective-permute-done | bytes 196640 | tf_op jit(solution)/shard_map/ppermute | solution.py:28
  55.8 1.7 %final.5 = (f32[64,8192]{1,0:T(8,128)}, f32[64,8192]{1,0:T(8,128)}) custom-call(s32[1]{0:T(128)} %bitcast.side.token, f32[64,128]{1,0:T(8,128)S(1)} %get-tuple-element.54.scale.refs_0_, f32[64,8192]{1,0:T(8,128)S(1)} %get-tuple-element.55.x_ref, f32[64,8192]{1,0:T(8,128)S(1)} %get-tuple-element.56.u_ref, ...), custom_call_target="tpu_custom_call", output_to_operand_aliasing={{0}: (11, {}), {1}: (12, {})} | custom-call | flops 1000 | bytes 1000 | tf_op jit(solution)/shard_map/final/pallas_call | solution.py:350
  58.1 1.5 %final.6 = (f32[64,8192]{1,0:T(8,128)}, f32[64,8192]{1,0:T(8,128)}) custom-call(s32[1]{0:T(128)} %bitcast.side.token, f32[64,128]{1,0:T(8,128)S(1)} %get-tuple-element.54.scale.refs_0_, f32[64,8192]{1,0:T(8,128)S(1)} %get-tuple-element.55.x_ref, f32[64,8192]{1,0:T(8,128)S(1)} %get-tuple-element.56.u_ref, ...), custom_call_target="tpu_custom_call", output_to_operand_aliasing={{0}: (11, {}), {1}: (12, {})} | custom-call | flops 1000 | bytes 1000 | tf_op jit(solution)/shard_map/final/pallas_call | solution.py:350
  59.6 1.0 %final.7 = (f32[64,8192]{1,0:T(8,128)}, f32[64,8192]{1,0:T(8,128)}) custom-call(s32[1]{0:T(128)} %bitcast.side.token, f32[64,128]{1,0:T(8,128)S(1)} %get-tuple-element.54.scale.refs_0_, f32[64,8192]{1,0:T(8,128)S(1)} %get-tuple-element.55.x_ref, f32[64,8192]{1,0:T(8,128)S(1)} %get-tuple-element.56.u_ref, ...), custom_call_target="tpu_custom_call", output_to_operand_aliasing={{0}: (8, {}), {1}: (9, {})} | custom-call | flops 1000 | bytes 1000 | tf_op jit(solution)/shard_map/final/pallas_call | solution.py:350
  (35 shorter events, 8.1 us)
Async XLA Ops:
  9.5 4.4 %collective-permute-start.1 = (f32[64,4096]{1,0:T(8,128)S(1)}, f32[64,4096]{1,0:T(8,128)S(1)}, u32[]{:S(2)}, u32[]{:S(2)}) collective-permute-start(f32[64,4096]{1,0:T(8,128)S(1)} %get-tuple-element.66), channel_id=1, source_target_pairs={{0,8},{8,0},{16,24},{24,16},{1,9},{9,1},{17,25},{25,17},{2,10},{10... | collective-permute-start | bytes 3145736 | tf_op jit(solution)/shard_map/ppermute | solution.py:28
  10.0 6.0 %collective-permute-start = (bf16[64,768]{1,0:T(8,128)(2,1)S(1)}, bf16[64,768]{1,0:T(8,128)(2,1)S(1)}, u32[]{:S(2)}, u32[]{:S(2)}) collective-permute-start(bf16[64,768]{1,0:T(8,128)(2,1)S(1)} %get-tuple-element.61), channel_id=1, source_target_pairs={{0,1},{1,0},{2,3},{3,2},{4,5},{5,4},{6,7},{7,6},{8,9},{9,8},{10,11... | collective-permute-start | bytes 294920 | tf_op jit(solution)/shard_map/ppermute | solution.py:28
  14.0 25.3 %collective-permute-start.8 = (f32[64,4096]{1,0:T(8,128)S(1)}, f32[64,4096]{1,0:T(8,128)S(1)}, u32[]{:S(2)}, u32[]{:S(2)}) collective-permute-start(f32[64,4096]{1,0:T(8,128)S(1)} %add.30), channel_id=1, source_target_pairs={{0,16},{8,24},{16,0},{24,8},{1,17},{9,25},{17,1},{25,9},{2,18},{10... | collective-permute-start | bytes 3145736 | tf_op jit(solution)/shard_map/ppermute | solution.py:28
  16.0 4.7 %collective-permute-start.2 = (bf16[64,768]{1,0:T(8,128)(2,1)S(1)}, bf16[64,768]{1,0:T(8,128)(2,1)S(1)}, u32[]{:S(2)}, u32[]{:S(2)}) collective-permute-start(bf16[64,768]{1,0:T(8,128)(2,1)S(1)} %add_convert_fusion.5), channel_id=1, source_target_pairs={{0,2},{1,3},{2,0},{3,1},{4,6},{5,7},{6,4},{7,5},{8,10},{9,11},{10,... | collective-permute-start | bytes 294920 | tf_op jit(solution)/shard_map/ppermute | solution.py:28
  20.7 6.4 %collective-permute-start.3 = (bf16[64,768]{1,0:T(8,128)(2,1)S(1)}, bf16[64,768]{1,0:T(8,128)(2,1)S(1)}, u32[]{:S(2)}, u32[]{:S(2)}) collective-permute-start(bf16[64,768]{1,0:T(8,128)(2,1)S(1)} %add_convert_fusion.4.refs_6_), channel_id=1, source_target_pairs={{0,4},{1,5},{2,6},{3,7},{4,0},{5,1},{6,2},{7,3},{8,12},{9,13},{10,... | collective-permute-start | bytes 294920 | tf_op jit(solution)/shard_map/ppermute | solution.py:28
  27.7 5.7 %collective-permute-start.6 = (bf16[64,768]{1,0:T(8,128)(2,1)S(1)}, bf16[64,768]{1,0:T(8,128)(2,1)S(1)}, u32[]{:S(2)}, u32[]{:S(2)}) collective-permute-start(bf16[64,768]{1,0:T(8,128)(2,1)S(1)} %get-tuple-element.76), channel_id=1, source_target_pairs={{0,3},{1,2},{2,1},{3,0},{4,7},{5,6},{6,5},{7,4},{8,11},{9,10},{10,... | collective-permute-start | bytes 294920 | tf_op jit(solution)/shard_map/ppermute | solution.py:28
  30.3 4.6 %collective-permute-start.5 = (bf16[64,768]{1,0:T(8,128)(2,1)S(1)}, bf16[64,768]{1,0:T(8,128)(2,1)S(1)}, u32[]{:S(2)}, u32[]{:S(2)}) collective-permute-start(bf16[64,768]{1,0:T(8,128)(2,1)S(1)} %get-tuple-element.76), channel_id=1, source_target_pairs={{0,2},{1,3},{2,0},{3,1},{4,6},{5,7},{6,4},{7,5},{8,10},{9,11},{10,... | collective-permute-start | bytes 294920 | tf_op jit(solution)/shard_map/ppermute | solution.py:28
  30.8 4.6 %collective-permute-start.4 = (bf16[64,768]{1,0:T(8,128)(2,1)S(1)}, bf16[64,768]{1,0:T(8,128)(2,1)S(1)}, u32[]{:S(2)}, u32[]{:S(2)}) collective-permute-start(bf16[64,768]{1,0:T(8,128)(2,1)S(1)} %get-tuple-element.76), channel_id=1, source_target_pairs={{0,1},{1,0},{2,3},{3,2},{4,5},{5,4},{6,7},{7,6},{8,9},{9,8},{10,11... | collective-permute-start | bytes 294920 | tf_op jit(solution)/shard_map/ppermute | solution.py:28
  35.4 5.6 %collective-permute-start.7 = (bf16[64,768]{1,0:T(8,128)(2,1)S(1)}, bf16[64,768]{1,0:T(8,128)(2,1)S(1)}, u32[]{:S(2)}, u32[]{:S(2)}) collective-permute-start(bf16[64,768]{1,0:T(8,128)(2,1)S(1)} %add_convert_fusion.3.refs_4_), channel_id=1, source_target_pairs={{0,4},{1,5},{2,6},{3,7},{4,0},{5,1},{6,2},{7,3},{8,12},{9,13},{10,... | collective-permute-start | bytes 294920 | tf_op jit(solution)/shard_map/ppermute | solution.py:28
  41.5 1.5 %collective-permute-start.9 = (bf16[64,1536]{1,0:T(8,128)(2,1)S(1)}, bf16[64,1536]{1,0:T(8,128)(2,1)S(1)}, u32[]{:S(2)}, u32[]{:S(2)}) collective-permute-start(bf16[64,1536]{1,0:T(8,128)(2,1)S(1)} %get-tuple-element.82), channel_id=1, source_target_pairs={{0,8},{8,0},{16,24},{24,16},{1,9},{9,1},{17,25},{25,17},{2,10},{10... | collective-permute-start | bytes 589832 | tf_op jit(solution)/shard_map/ppermute | solution.py:28
  42.4 2.8 %collective-permute-start.10 = (bf16[64,2560]{1,0:T(8,128)(2,1)S(1)}, bf16[64,2560]{1,0:T(8,128)(2,1)S(1)}, u32[]{:S(2)}, u32[]{:S(2)}) collective-permute-start(bf16[64,2560]{1,0:T(8,128)(2,1)S(1)} %get-tuple-element.86), channel_id=1, source_target_pairs={{0,8},{8,0},{16,24},{24,16},{1,9},{9,1},{17,25},{25,17},{2,10},{10... | collective-permute-start | bytes 983048 | tf_op jit(solution)/shard_map/ppermute | solution.py:28
  43.6 7.8 %collective-permute-start.13 = (bf16[64,1536]{1,0:T(8,128)(2,1)S(1)}, bf16[64,1536]{1,0:T(8,128)(2,1)S(1)}, u32[]{:S(2)}, u32[]{:S(2)}) collective-permute-start(bf16[64,1536]{1,0:T(8,128)(2,1)S(1)} %get-tuple-element.84), channel_id=1, source_target_pairs={{0,16},{8,24},{16,0},{24,8},{1,17},{9,25},{17,1},{25,9},{2,18},{10... | collective-permute-start | bytes 589832 | tf_op jit(solution)/shard_map/ppermute | solution.py:28
  45.1 10.6 %collective-permute-start.11 = (f32[64,4096]{1,0:T(8,128)S(1)}, f32[64,4096]{1,0:T(8,128)S(1)}, u32[]{:S(2)}, u32[]{:S(2)}) collective-permute-start(f32[64,4096]{1,0:T(8,128)S(1)} %add.36.refs_0_.refs_3_), channel_id=1, source_target_pairs={{0,8},{8,0},{16,24},{24,16},{1,9},{9,1},{17,25},{25,17},{2,10},{10... | collective-permute-start | bytes 3145736 | tf_op jit(solution)/shard_map/ppermute | solution.py:28
  45.9 9.8 %collective-permute-start.15 = (bf16[64,1536]{1,0:T(8,128)(2,1)S(1)}, bf16[64,1536]{1,0:T(8,128)(2,1)S(1)}, u32[]{:S(2)}, u32[]{:S(2)}) collective-permute-start(bf16[64,1536]{1,0:T(8,128)(2,1)S(1)} %get-tuple-element.88), channel_id=1, source_target_pairs={{0,16},{8,24},{16,0},{24,8},{1,17},{9,25},{17,1},{25,9},{2,18},{10... | collective-permute-start | bytes 589832 | tf_op jit(solution)/shard_map/ppermute | solution.py:28
  46.9 10.8 %collective-permute-start.12 = (bf16[64,1024]{1,0:T(8,128)(2,1)S(1)}, bf16[64,1024]{1,0:T(8,128)(2,1)S(1)}, u32[]{:S(2)}, u32[]{:S(2)}) collective-permute-start(bf16[64,1024]{1,0:T(8,128)(2,1)S(1)} %get-tuple-element.93), channel_id=1, source_target_pairs={{0,16},{8,24},{16,0},{24,8},{1,17},{9,25},{17,1},{25,9},{2,18},{10... | collective-permute-start | bytes 393224 | tf_op jit(solution)/shard_map/ppermute | solution.py:28
  51.4 4.3 %collective-permute-start.14 = (bf16[64,1536]{1,0:T(8,128)(2,1)S(1)}, bf16[64,1536]{1,0:T(8,128)(2,1)S(1)}, u32[]{:S(2)}, u32[]{:S(2)}) collective-permute-start(bf16[64,1536]{1,0:T(8,128)(2,1)S(1)} %add_convert_fusion.1.refs_2_), channel_id=1, source_target_pairs={{0,8},{8,0},{16,24},{24,16},{1,9},{9,1},{17,25},{25,17},{2,10},{10... | collective-permute-start | bytes 589832 | tf_op jit(solution)/shard_map/ppermute | solution.py:28
  55.7 2.4 %collective-permute-start.17 = (bf16[64,1536]{1,0:T(8,128)(2,1)S(1)}, bf16[64,1536]{1,0:T(8,128)(2,1)S(1)}, u32[]{:S(2)}, u32[]{:S(2)}) collective-permute-start(bf16[64,1536]{1,0:T(8,128)(2,1)S(1)} %add_convert_fusion.refs_5_), channel_id=1, source_target_pairs={{0,8},{8,0},{16,24},{24,16},{1,9},{9,1},{17,25},{25,17},{2,10},{10... | collective-permute-start | bytes 589832 | tf_op jit(solution)/shard_map/ppermute | solution.py:28
  57.7 1.9 %collective-permute-start.16 = (bf16[64,1024]{1,0:T(8,128)(2,1)S(1)}, bf16[64,1024]{1,0:T(8,128)(2,1)S(1)}, u32[]{:S(2)}, u32[]{:S(2)}) collective-permute-start(bf16[64,1024]{1,0:T(8,128)(2,1)S(1)} %add_convert_fusion.2.refs_5_), channel_id=1, source_target_pairs={{0,8},{8,0},{16,24},{24,16},{1,9},{9,1},{17,25},{25,17},{2,10},{10... | collective-permute-start | bytes 393224 | tf_op jit(solution)/shard_map/ppermute | solution.py:28

commit v14 on v11

--- a/solution.py
+++ b/solution.py
@@ -18,7 +18,6 @@
 AHEAD = 8
 NARROW = 256
 WAIT_BYTES = 10_000_000
-GRAM_ORDER = (0, 1, 2)
 HBM = pl.BlockSpec(memory_space=pltpu.HBM)
 VMEM = pl.BlockSpec(memory_space=pltpu.VMEM)
 SMEM = pl.BlockSpec(memory_space=pltpu.SMEM)
@@ -127,14 +126,12 @@
             at, here = columns(j * STEP + k, NARROW), pl.ds(k, NARROW)
             x = x_out[:, at]
             v = x - pull * (x - z_out[:, at] + u_out[:, at])
-            top = v.astype(BF16)
             both[:tasks, here] = x.astype(BF16)
-            both[tasks : 2 * tasks, here] = top
-            both[2 * tasks :, here] = (v - top.astype(F32)).astype(BF16)
+            both[tasks:, here] = v.astype(BF16)
         acc[...] += nt(both[...], a_out[:, columns(j * STEP, STEP)])
 
     m_out[...] = acc[:tasks].astype(BF16)
-    pulled_out[...] = acc[tasks : 2 * tasks] + acc[2 * tasks :]
+    pulled_out[...] = acc[tasks:]
     half = width // 2
     mine = columns(side[0] * half, half)
     other = columns((1 - side[0]) * half, half)
@@ -160,43 +157,53 @@
         [VMEM] * 10,
         [pltpu.VMEM((1, tasks), F32)] * 3
         + [
-            pltpu.VMEM((3 * tasks, STEP), BF16), pltpu.VMEM((3 * tasks, samples), F32),
+            pltpu.VMEM((2 * tasks, STEP), BF16), pltpu.VMEM((2 * tasks, samples), F32),
             pltpu.SemaphoreType.DMA((5, max(width // STEP, 4))),
         ],
     )(side, *pin(pltpu.HBM, x, u, z, design, sign, *rows))
 
 
-def gram_block(a_ref, row, cols, size, acc, high, low):
+GRAM_STEPS = (((0, 0),), ((1, 0), (1, 1), (2, 2)), ((2, 0), (2, 1)))
+
+
+def gram_kernel(blocks, token, a_ref, *refs):
+    *outs, acc = refs
+    size = outs[0].shape[0]
     width = a_ref.shape[1]
     wide = math.gcd(WIDE, width)
-    for j in range(width // wide):
-        at = pl.ds(j * wide, wide)
-        product = nt(a_ref[pl.ds(row, size), at], a_ref[pl.ds(0, cols), at])
-        acc[:, :cols] = product if j == 0 else acc[:, :cols] + product
-    whole = acc[:, :cols]
-    top = whole.astype(BF16)
-    high[...] = top
-    low[...] = (whole - top.astype(F32)).astype(BF16)
-
-
-def gram_kernel(row, token, a_ref, high, low, acc):
-    size = high.shape[0]
-    gram_block(a_ref, row * size, (row + 1) * size, size, acc, high, low)
-
-
-def gram_row(row, token, design):
+    rows = sorted({row for row, _ in blocks})
+    done = 0
+    for row in rows:
+        cols = [col for r, col in blocks if r == row]
+        span = pl.ds(cols[0] * size, len(cols) * size)
+        here = pl.ds(0, len(cols) * size)
+        for j in range(width // wide):
+            at = pl.ds(j * wide, wide)
+            product = nt(a_ref[pl.ds(row * size, size), at], a_ref[span, at])
+            acc[:, here] = product if j == 0 else acc[:, here] + product
+        for k in range(len(cols)):
+            whole = acc[:, pl.ds(k * size, size)]
+            top = whole.astype(BF16)
+            outs[2 * done][...] = top
+            outs[2 * done + 1][...] = (whole - top.astype(F32)).astype(BF16)
+            done += 1
+
+
+def gram_blocks(step, token, design):
     samples = design.shape[0]
     size = samples // 3
-    out = pltpu.VMEM((size, (row + 1) * size), BF16)
-    return call(
-        functools.partial(gram_kernel, row),
+    blocks = GRAM_STEPS[step]
+    out = pltpu.VMEM((size, size), BF16)
+    parts = call(
+        functools.partial(gram_kernel, blocks),
         "gram",
         [SMEM, VMEM],
-        (out, out),
-        [VMEM] * 2,
-        [pltpu.VMEM((size, (row + 1) * size), F32)],
-        work=WAIT_BYTES * (row + 1) // 3,
+        (out,) * (2 * len(blocks)),
+        [VMEM] * (2 * len(blocks)),
+        [pltpu.VMEM((size, 2 * size), F32)],
+        work=WAIT_BYTES * (step + 1) // 3,
     )(token, *pin(pltpu.VMEM, design))
+    return {block: parts[2 * k : 2 * k + 2] for k, block in enumerate(blocks)}
 
 
 def residual(sign, *terms):
@@ -205,10 +212,13 @@
     return (sign * jax.nn.sigmoid(-sign * margin)).astype(BF16)
 
 
+LOWER = [(row, col) for row in range(3) for col in range(row + 1)]
+
+
 def turn_kernel(sign, scale, pulled, *refs):
-    *terms, resid, out = refs[6:]
-    grams = refs[:6]
-    size = grams[0].shape[0]
+    *terms, resid, out = refs[12:]
+    grams = {block: refs[2 * k : 2 * k + 2] for k, block in enumerate(LOWER)}
+    size = refs[0].shape[0]
     resid[...] = residual(sign[...], *(t[...] for t in terms))
     eta = scale[:, 0:1]
     r = [resid[:, pl.ds(k * size, size)] for k in range(3)]
@@ -217,10 +227,9 @@
         for row in range(3):
             for part in range(2):
                 if row >= col:
-                    block = grams[2 * row + part][:, pl.ds(col * size, size)]
-                    total += jnp.dot(r[row], block, preferred_element_type=F32)
+                    total += jnp.dot(r[row], grams[row, col][part][...], preferred_element_type=F32)
                 else:
-                    total += nt(r[row], grams[2 * col + part][:, pl.ds(row * size, size)])
+                    total += nt(r[row], grams[col, row][part][...])
         here = pl.ds(col * size, size)
         out[:, here] = (pulled[:, here] + eta * total).astype(BF16)
 
@@ -228,7 +237,7 @@
 def turn(sign, terms, scale, pulled, grams):
     tasks, samples = pulled.shape
     out = pltpu.VMEM((tasks, samples), BF16)
-    args = [sign, scale, pulled, *grams, *terms]
+    args = [sign, scale, pulled, *(part for block in LOWER for part in grams[block]), *terms]
     return call(turn_kernel, "turn", [VMEM] * len(args), (out, out), [VMEM] * 2)(*pin(pltpu.VMEM, *args))
 
 
@@ -374,18 +383,18 @@
     )
     start_mine = start_mine + exchange(start_other, "rows", 1)
 
-    terms, grams = [margin1], []
+    terms, grams = [margin1], {}
     for step in range(max(lax.axis_size("feat").bit_length() - 1, 3)):
         more = (1 << step) < lax.axis_size("feat")
         if step > 0 and more:
             terms = [sum(t.astype(F32) for t in terms).astype(BF16)]
-        row = gram_row(GRAM_ORDER[step], tie(side, terms[0]), design) if step < 3 else []
-        grams.append(row)
+        made = gram_blocks(step, tie(side, terms[0]), design) if step < 3 else {}
+        grams.update(made)
         if more:
             got = exchange(terms[0], "feat", 1 << step)
-            terms.append(tie(got, row[0], start_mine) if step == 0 else tie(got, row[0]) if step == 1 else got)
-
-    resid1, margin2 = turn(sign, terms, scale, pulled, [g for row in range(3) for g in grams[GRAM_ORDER.index(row)]])
+            terms.append(tie(got, made, start_mine) if step == 0 else tie(got, made) if step == 1 else got)
+
+    resid1, margin2 = turn(sign, terms, scale, pulled, grams)
     terms = square_sum(margin2, "feat")
     mask = 2
     while mask < blocks_count:

time: 60 us -> 62.1 us (1.035)
  waiting for transfers between devices: 12.6 us -> 16.6 us
  starting transfers between devices: 20.5 us -> 18.8 us
    ppermute x18, waiting for transfers between devices: 12.6 us -> 16.6 us  [exchange(): return lax.ppermute(value, axis, [(i, i ^ mask) for i in range(n)])]
    ppermute x18, starting transfers between devices: 20.5 us -> 18.8 us  [exchange(): return lax.ppermute(value, axis, [(i, i ^ mask) for i in range(n)])]
  transfers between devices with their start and end apart: 18 -> 18, of which waited for: 11 -> 11; matrix products, arithmetic and copies ran while one was open for 1% -> 1% of each run, Pallas kernels for 27% -> 26%
where the time goes in v14:
time: 62.1 us; the launch traced here: 62 us
  Pallas kernels  25.3 us (41%)
  starting transfers between devices  18.8 us (30%)
  waiting for transfers between devices  16.6 us (27%)
  between operations  0.86 us (1%)
    ppermute x18, starting transfers between devices, exchange(): return lax.ppermute(value, axis, [(i, i ^ mask) for i in range(n)])  18.8 us
    ppermute x18, waiting for transfers between devices, exchange(): return lax.ppermute(value, axis, [(i, i ^ mask) for i in range(n)])  16.6 us
    pallas_call x1, Pallas kernels, load(): call(functools.partial(load_kernel, blocks_count), 'load_and_margins', [S...  7.89 us
    pallas_call x3, Pallas kernels, gram_blocks(): call(functools.partial(gram_kernel, blocks), 'gram', [SMEM, VMEM], (out,)...  7.08 us
    pallas_call x4, Pallas kernels, final(): call(functools.partial(final_kernel, blocks_count, places, buffered), 'fi...  5.41 us
    pallas_call x5, Pallas kernels, push(): call(functools.partial(push_kernel, first, mine, begin, offset, size), 'p...  2.7 us
    pallas_call x1, Pallas kernels, store_x(): call(store_kernel, 'store_x', [SMEM] + [VMEM] * len(args), pltpu.HBM((tas...  1.58 us
  transfers between devices with their start and end apart: 18, of which 11 were waited for; matrix products, arithmetic and copies ran while one was open for 1% of the time, Pallas kernels for 26%

profile of v14, /device:TPU:0, one launch (start us, length us, event | category | flops | bytes accessed | tf_op | source)
XLA Modules:
  0.0 62.0 jit_solution(15170488089038998576)
XLA Ops:
  0.6 7.9 %load_and_margins.1 = (bf16[64,768]{1,0:T(8,128)(2,1)S(1)}, f32[64,768]{1,0:T(8,128)S(1)}, bf16[768,8192]{1,0:T(8,128)(2,1)S(1)}, f32[64,8192]{1,0:T(8,128)S(1)}...) custom-call(s32[1]{0:T(128)} %bitcast.side.token, ...), custom_call_target="tpu_custom_call" | custom-call | flops 1000 | bytes 1000 | tf_op jit(solution)/shard_map/load_and_margins/pallas_call | solution.py:149
  9.1 2.6 %collective-permute-start = (bf16[64,768]{1,0:T(8,128)(2,1)S(1)}, bf16[64,768]{1,0:T(8,128)(2,1)S(1)}, u32[]{:S(2)}, u32[]{:S(2)}) collective-permute-start(bf16[64,768]{1,0:T(8,128)(2,1)S(1)} %get-tuple-element.67), channel_id=1, source_target_pairs={{0,1},{1,0},{2,3},{3,2},{4,5},{5,4},{6,7},{7,6},{8,9},{9,8},{10,11... | collective-permute-start | bytes 294920 | tf_op jit(solution)/shard_map/ppermute | solution.py:28
  11.6 1.3 %gram.3 = (bf16[256,256]{1,0:T(8,128)(2,1)S(1)}, bf16[256,256]{1,0:T(8,128)(2,1)S(1)}) custom-call(s32[1]{0:T(128)} %bitcast.side.token, bf16[768,8192]{1,0:T(8,128)(2,1)S(1)} %get-tuple-element.64.a_ref.refs_1_), custom_call_target="tpu_custom_call" | custom-call | flops 1000 | bytes 3333333 | tf_op jit(solution)/shard_map/gram/pallas_call | solution.py:197
  13.1 1.6 %collective-permute-start.8 = (f32[64,4096]{1,0:T(8,128)S(1)}, f32[64,4096]{1,0:T(8,128)S(1)}, u32[]{:S(2)}, u32[]{:S(2)}) collective-permute-start(f32[64,4096]{1,0:T(8,128)S(1)} %add.30), channel_id=1, source_target_pairs={{0,16},{8,24},{16,0},{24,8},{1,17},{9,25},{17,1},{25,9},{2,18},{10... | collective-permute-start | bytes 3145736 | tf_op jit(solution)/shard_map/ppermute | solution.py:28
  15.1 1.9 %collective-permute-start.2 = (bf16[64,768]{1,0:T(8,128)(2,1)S(1)}, bf16[64,768]{1,0:T(8,128)(2,1)S(1)}, u32[]{:S(2)}, u32[]{:S(2)}) collective-permute-start(bf16[64,768]{1,0:T(8,128)(2,1)S(1)} %add_convert_fusion.5), channel_id=1, source_target_pairs={{0,2},{1,3},{2,0},{3,1},{4,6},{5,7},{6,4},{7,5},{8,10},{9,11},{10,... | collective-permute-start | bytes 294920 | tf_op jit(solution)/shard_map/ppermute | solution.py:28
  16.9 3.4 %gram.4 = (bf16[256,256]{1,0:T(8,128)(2,1)S(1)}, bf16[256,256]{1,0:T(8,128)(2,1)S(1)}, bf16[256,256]{1,0:T(8,128)(2,1)S(1)}, bf16[256,256]{1,0:T(8,128)(2,1)S(1)...) custom-call(s32[1]{0:T(128)} %bitcast.side.token, bf16[768,8192]{1,0:T(8,128)(2,1)S(1)} %get-tuple-element.64.a_ref.refs_1_), custom_call_target="tpu_custom_call" | custom-call | flops 1000 | bytes 6666666 | tf_op jit(solution)/shard_map/gram/pallas_call | solution.py:197
  20.4 2.7 %collective-permute-start.3 = (bf16[64,768]{1,0:T(8,128)(2,1)S(1)}, bf16[64,768]{1,0:T(8,128)(2,1)S(1)}, u32[]{:S(2)}, u32[]{:S(2)}) collective-permute-start(bf16[64,768]{1,0:T(8,128)(2,1)S(1)} %add_convert_fusion.4.refs_12_), channel_id=1, source_target_pairs={{0,4},{1,5},{2,6},{3,7},{4,0},{5,1},{6,2},{7,3},{8,12},{9,13},{10,... | collective-permute-start | bytes 294920 | tf_op jit(solution)/shard_map/ppermute | solution.py:28
  23.1 2.4 %gram.5 = (bf16[256,256]{1,0:T(8,128)(2,1)S(1)}, bf16[256,256]{1,0:T(8,128)(2,1)S(1)}, bf16[256,256]{1,0:T(8,128)(2,1)S(1)}, bf16[256,256]{1,0:T(8,128)(2,1)S(1)}) custom-call(s32[1]{0:T(128)} %bitcast.side.token, bf16[768,8192]{1,0:T(8,128)(2,1)S(1)} %get-tuple-element.64.a_ref.refs_1_), custom_call_target="tpu_custom_call" | custom-call | flops 1000 | bytes 10000000 | tf_op jit(solution)/shard_map/gram/pallas_call | solution.py:197
  25.5 2.1 %collective-permute-done.3.refs_13_ = bf16[64,768]{1,0:T(8,128)(2,1)S(1)} collective-permute-done((bf16[64,768]{1,0:T(8,128)(2,1)S(1)}, bf16[64,768]{1,0:T(8,128)(2,1)S(1)}, u32[]{:S(2)}, u32[]{:S(2)}) %collective-permute-start.3) | collective-permute-done | bytes 98336 | tf_op jit(solution)/shard_map/ppermute | solution.py:28
  29.1 2.2 %collective-permute-start.5 = (bf16[64,768]{1,0:T(8,128)(2,1)S(1)}, bf16[64,768]{1,0:T(8,128)(2,1)S(1)}, u32[]{:S(2)}, u32[]{:S(2)}) collective-permute-start(bf16[64,768]{1,0:T(8,128)(2,1)S(1)} %get-tuple-element.88), channel_id=1, source_target_pairs={{0,2},{1,3},{2,0},{3,1},{4,6},{5,7},{6,4},{7,5},{8,10},{9,11},{10,... | collective-permute-start | bytes 294920 | tf_op jit(solution)/shard_map/ppermute | solution.py:28
  31.8 2.8 %collective-permute-done.6 = bf16[64,768]{1,0:T(8,128)(2,1)S(1)} collective-permute-done((bf16[64,768]{1,0:T(8,128)(2,1)S(1)}, bf16[64,768]{1,0:T(8,128)(2,1)S(1)}, u32[]{:S(2)}, u32[]{:S(2)}) %collective-permute-start.6) | collective-permute-done | bytes 98336 | tf_op jit(solution)/shard_map/ppermute | solution.py:28
  34.6 1.0 %collective-permute-done.5 = bf16[64,768]{1,0:T(8,128)(2,1)S(1)} collective-permute-done((bf16[64,768]{1,0:T(8,128)(2,1)S(1)}, bf16[64,768]{1,0:T(8,128)(2,1)S(1)}, u32[]{:S(2)}, u32[]{:S(2)}) %collective-permute-start.5) | collective-permute-done | bytes 98336 | tf_op jit(solution)/shard_map/ppermute | solution.py:28
  36.0 1.2 %collective-permute-start.7 = (bf16[64,768]{1,0:T(8,128)(2,1)S(1)}, bf16[64,768]{1,0:T(8,128)(2,1)S(1)}, u32[]{:S(2)}, u32[]{:S(2)}) collective-permute-start(bf16[64,768]{1,0:T(8,128)(2,1)S(1)} %add_convert_fusion.3.refs_4_), channel_id=1, source_target_pairs={{0,4},{1,5},{2,6},{3,7},{4,0},{5,1},{6,2},{7,3},{8,12},{9,13},{10,... | collective-permute-start | bytes 294920 | tf_op jit(solution)/shard_map/ppermute | solution.py:28
  37.2 1.1 %collective-permute-done.8 = f32[64,4096]{1,0:T(8,128)S(1)} collective-permute-done((f32[64,4096]{1,0:T(8,128)S(1)}, f32[64,4096]{1,0:T(8,128)S(1)}, u32[]{:S(2)}, u32[]{:S(2)}) %collective-permute-start.8) | collective-permute-done | bytes 1048608 | tf_op jit(solution)/shard_map/ppermute | solution.py:28
  38.5 3.9 %collective-permute-done.7.refs_5_ = bf16[64,768]{1,0:T(8,128)(2,1)S(1)} collective-permute-done((bf16[64,768]{1,0:T(8,128)(2,1)S(1)}, bf16[64,768]{1,0:T(8,128)(2,1)S(1)}, u32[]{:S(2)}, u32[]{:S(2)}) %collective-permute-start.7) | collective-permute-done | bytes 98336 | tf_op jit(solution)/shard_map/ppermute | solution.py:28
  44.9 1.6 %collective-permute-start.13 = (bf16[64,1536]{1,0:T(8,128)(2,1)S(1)}, bf16[64,1536]{1,0:T(8,128)(2,1)S(1)}, u32[]{:S(2)}, u32[]{:S(2)}) collective-permute-start(bf16[64,1536]{1,0:T(8,128)(2,1)S(1)} %get-tuple-element.96), channel_id=1, source_target_pairs={{0,16},{8,24},{16,0},{24,8},{1,17},{9,25},{17,1},{25,9},{2,18},{10... | collective-permute-start | bytes 589832 | tf_op jit(solution)/shard_map/ppermute | solution.py:28
  48.0 1.6 %collective-permute-start.12 = (bf16[64,1024]{1,0:T(8,128)(2,1)S(1)}, bf16[64,1024]{1,0:T(8,128)(2,1)S(1)}, u32[]{:S(2)}, u32[]{:S(2)}) collective-permute-start(bf16[64,1024]{1,0:T(8,128)(2,1)S(1)} %get-tuple-element.105), channel_id=1, source_target_pairs={{0,16},{8,24},{16,0},{24,8},{1,17},{9,25},{17,1},{25,9},{2,18},{10... | collective-permute-start | bytes 393224 | tf_op jit(solution)/shard_map/ppermute | solution.py:28
  49.6 1.6 %store_x.1 = f32[64,8192]{1,0:T(8,128)} custom-call(s32[1]{0:T(128)} %bitcast.side.token, f32[64,128]{1,0:T(8,128)S(1)} %get-tuple-element.60.scale.refs_0_, f32[64,8192]{1,0:T(8,128)S(1)} %get-tuple-element.61.x_ref, f32[64,8192]{1,0:T(8,128)S(1)} %get-tuple-element.62.u_ref, f32[64,8192]{1,0:T(8,128)S(1)} %get-tuple-element.63.z_ref, ...), custom_call_target="tpu_custom_call" | custom-call | flops 1000 | bytes 1000 | tf_op jit(solution)/shard_map/store_x/pallas_call | solution.py:310
  51.2 1.6 %collective-permute-done.13 = bf16[64,1536]{1,0:T(8,128)(2,1)S(1)} collective-permute-done((bf16[64,1536]{1,0:T(8,128)(2,1)S(1)}, bf16[64,1536]{1,0:T(8,128)(2,1)S(1)}, u32[]{:S(2)}, u32[]{:S(2)}) %collective-permute-start.13) | collective-permute-done | bytes 196640 | tf_op jit(solution)/shard_map/ppermute | solution.py:28
  52.9 1.2 %final.4 = (f32[64,8192]{1,0:T(8,128)}, f32[64,8192]{1,0:T(8,128)}) custom-call(s32[1]{0:T(128)} %bitcast.side.token, f32[64,128]{1,0:T(8,128)S(1)} %get-tuple-element.60.scale.refs_0_, f32[64,8192]{1,0:T(8,128)S(1)} %get-tuple-element.61.x_ref, f32[64,8192]{1,0:T(8,128)S(1)} %get-tuple-element.62.u_ref, f32[64,8192]{1,0:T(8,128)S(1)} %get-tuple-element.63.z_ref, ...), custom_call_target="tpu_custom_call" | custom-call | flops 1000 | bytes 1000 | tf_op jit(solution)/shard_map/final/pallas_call | solution.py:360
  54.1 2.9 %collective-permute-done.15 = bf16[64,1536]{1,0:T(8,128)(2,1)S(1)} collective-permute-done((bf16[64,1536]{1,0:T(8,128)(2,1)S(1)}, bf16[64,1536]{1,0:T(8,128)(2,1)S(1)}, u32[]{:S(2)}, u32[]{:S(2)}) %collective-permute-start.15) | collective-permute-done | bytes 196640 | tf_op jit(solution)/shard_map/ppermute | solution.py:28
  57.1 1.7 %final.5 = (f32[64,8192]{1,0:T(8,128)}, f32[64,8192]{1,0:T(8,128)}) custom-call(s32[1]{0:T(128)} %bitcast.side.token, f32[64,128]{1,0:T(8,128)S(1)} %get-tuple-element.60.scale.refs_0_, f32[64,8192]{1,0:T(8,128)S(1)} %get-tuple-element.61.x_ref, f32[64,8192]{1,0:T(8,128)S(1)} %get-tuple-element.62.u_ref, ...), custom_call_target="tpu_custom_call", output_to_operand_aliasing={{0}: (11, {}), {1}: (12, {})} | custom-call | flops 1000 | bytes 1000 | tf_op jit(solution)/shard_map/final/pallas_call | solution.py:360
  59.4 1.5 %final.6 = (f32[64,8192]{1,0:T(8,128)}, f32[64,8192]{1,0:T(8,128)}) custom-call(s32[1]{0:T(128)} %bitcast.side.token, f32[64,128]{1,0:T(8,128)S(1)} %get-tuple-element.60.scale.refs_0_, f32[64,8192]{1,0:T(8,128)S(1)} %get-tuple-element.61.x_ref, f32[64,8192]{1,0:T(8,128)S(1)} %get-tuple-element.62.u_ref, ...), custom_call_target="tpu_custom_call", output_to_operand_aliasing={{0}: (11, {}), {1}: (12, {})} | custom-call | flops 1000 | bytes 1000 | tf_op jit(solution)/shard_map/final/pallas_call | solution.py:360
  61.0 1.0 %final.7 = (f32[64,8192]{1,0:T(8,128)}, f32[64,8192]{1,0:T(8,128)}) custom-call(s32[1]{0:T(128)} %bitcast.side.token, f32[64,128]{1,0:T(8,128)S(1)} %get-tuple-element.60.scale.refs_0_, f32[64,8192]{1,0:T(8,128)S(1)} %get-tuple-element.61.x_ref, f32[64,8192]{1,0:T(8,128)S(1)} %get-tuple-element.62.u_ref, ...), custom_call_target="tpu_custom_call", output_to_operand_aliasing={{0}: (8, {}), {1}: (9, {})} | custom-call | flops 1000 | bytes 1000 | tf_op jit(solution)/shard_map/final/pallas_call | solution.py:360
  (35 shorter events, 8.6 us)
Async XLA Ops:
  8.5 4.4 %collective-permute-start.1 = (f32[64,4096]{1,0:T(8,128)S(1)}, f32[64,4096]{1,0:T(8,128)S(1)}, u32[]{:S(2)}, u32[]{:S(2)}) collective-permute-start(f32[64,4096]{1,0:T(8,128)S(1)} %get-tuple-element.72), channel_id=1, source_target_pairs={{0,8},{8,0},{16,24},{24,16},{1,9},{9,1},{17,25},{25,17},{2,10},{10... | collective-permute-start | bytes 3145736 | tf_op jit(solution)/shard_map/ppermute | solution.py:28
  9.1 6.0 %collective-permute-start = (bf16[64,768]{1,0:T(8,128)(2,1)S(1)}, bf16[64,768]{1,0:T(8,128)(2,1)S(1)}, u32[]{:S(2)}, u32[]{:S(2)}) collective-permute-start(bf16[64,768]{1,0:T(8,128)(2,1)S(1)} %get-tuple-element.67), channel_id=1, source_target_pairs={{0,1},{1,0},{2,3},{3,2},{4,5},{5,4},{6,7},{7,6},{8,9},{9,8},{10,11... | collective-permute-start | bytes 294920 | tf_op jit(solution)/shard_map/ppermute | solution.py:28
  13.1 25.3 %collective-permute-start.8 = (f32[64,4096]{1,0:T(8,128)S(1)}, f32[64,4096]{1,0:T(8,128)S(1)}, u32[]{:S(2)}, u32[]{:S(2)}) collective-permute-start(f32[64,4096]{1,0:T(8,128)S(1)} %add.30), channel_id=1, source_target_pairs={{0,16},{8,24},{16,0},{24,8},{1,17},{9,25},{17,1},{25,9},{2,18},{10... | collective-permute-start | bytes 3145736 | tf_op jit(solution)/shard_map/ppermute | solution.py:28
  15.1 5.3 %collective-permute-start.2 = (bf16[64,768]{1,0:T(8,128)(2,1)S(1)}, bf16[64,768]{1,0:T(8,128)(2,1)S(1)}, u32[]{:S(2)}, u32[]{:S(2)}) collective-permute-start(bf16[64,768]{1,0:T(8,128)(2,1)S(1)} %add_convert_fusion.5), channel_id=1, source_target_pairs={{0,2},{1,3},{2,0},{3,1},{4,6},{5,7},{6,4},{7,5},{8,10},{9,11},{10,... | collective-permute-start | bytes 294920 | tf_op jit(solution)/shard_map/ppermute | solution.py:28
  20.4 7.2 %collective-permute-start.3 = (bf16[64,768]{1,0:T(8,128)(2,1)S(1)}, bf16[64,768]{1,0:T(8,128)(2,1)S(1)}, u32[]{:S(2)}, u32[]{:S(2)}) collective-permute-start(bf16[64,768]{1,0:T(8,128)(2,1)S(1)} %add_convert_fusion.4.refs_12_), channel_id=1, source_target_pairs={{0,4},{1,5},{2,6},{3,7},{4,0},{5,1},{6,2},{7,3},{8,12},{9,13},{10,... | collective-permute-start | bytes 294920 | tf_op jit(solution)/shard_map/ppermute | solution.py:28
  28.2 6.3 %collective-permute-start.6 = (bf16[64,768]{1,0:T(8,128)(2,1)S(1)}, bf16[64,768]{1,0:T(8,128)(2,1)S(1)}, u32[]{:S(2)}, u32[]{:S(2)}) collective-permute-start(bf16[64,768]{1,0:T(8,128)(2,1)S(1)} %get-tuple-element.88), channel_id=1, source_target_pairs={{0,3},{1,2},{2,1},{3,0},{4,7},{5,6},{6,5},{7,4},{8,11},{9,10},{10,... | collective-permute-start | bytes 294920 | tf_op jit(solution)/shard_map/ppermute | solution.py:28
  29.1 6.5 %collective-permute-start.5 = (bf16[64,768]{1,0:T(8,128)(2,1)S(1)}, bf16[64,768]{1,0:T(8,128)(2,1)S(1)}, u32[]{:S(2)}, u32[]{:S(2)}) collective-permute-start(bf16[64,768]{1,0:T(8,128)(2,1)S(1)} %get-tuple-element.88), channel_id=1, source_target_pairs={{0,2},{1,3},{2,0},{3,1},{4,6},{5,7},{6,4},{7,5},{8,10},{9,11},{10,... | collective-permute-start | bytes 294920 | tf_op jit(solution)/shard_map/ppermute | solution.py:28
  31.3 4.7 %collective-permute-start.4 = (bf16[64,768]{1,0:T(8,128)(2,1)S(1)}, bf16[64,768]{1,0:T(8,128)(2,1)S(1)}, u32[]{:S(2)}, u32[]{:S(2)}) collective-permute-start(bf16[64,768]{1,0:T(8,128)(2,1)S(1)} %get-tuple-element.88), channel_id=1, source_target_pairs={{0,1},{1,0},{2,3},{3,2},{4,5},{5,4},{6,7},{7,6},{8,9},{9,8},{10,11... | collective-permute-start | bytes 294920 | tf_op jit(solution)/shard_map/ppermute | solution.py:28
  36.0 6.3 %collective-permute-start.7 = (bf16[64,768]{1,0:T(8,128)(2,1)S(1)}, bf16[64,768]{1,0:T(8,128)(2,1)S(1)}, u32[]{:S(2)}, u32[]{:S(2)}) collective-permute-start(bf16[64,768]{1,0:T(8,128)(2,1)S(1)} %add_convert_fusion.3.refs_4_), channel_id=1, source_target_pairs={{0,4},{1,5},{2,6},{3,7},{4,0},{5,1},{6,2},{7,3},{8,12},{9,13},{10,... | collective-permute-start | bytes 294920 | tf_op jit(solution)/shard_map/ppermute | solution.py:28
  42.9 1.5 %collective-permute-start.9 = (bf16[64,1536]{1,0:T(8,128)(2,1)S(1)}, bf16[64,1536]{1,0:T(8,128)(2,1)S(1)}, u32[]{:S(2)}, u32[]{:S(2)}) collective-permute-start(bf16[64,1536]{1,0:T(8,128)(2,1)S(1)} %get-tuple-element.94), channel_id=1, source_target_pairs={{0,8},{8,0},{16,24},{24,16},{1,9},{9,1},{17,25},{25,17},{2,10},{10... | collective-permute-start | bytes 589832 | tf_op jit(solution)/shard_map/ppermute | solution.py:28
  43.7 2.8 %collective-permute-start.10 = (bf16[64,2560]{1,0:T(8,128)(2,1)S(1)}, bf16[64,2560]{1,0:T(8,128)(2,1)S(1)}, u32[]{:S(2)}, u32[]{:S(2)}) collective-permute-start(bf16[64,2560]{1,0:T(8,128)(2,1)S(1)} %get-tuple-element.98), channel_id=1, source_target_pairs={{0,8},{8,0},{16,24},{24,16},{1,9},{9,1},{17,25},{25,17},{2,10},{10... | collective-permute-start | bytes 983048 | tf_op jit(solution)/shard_map/ppermute | solution.py:28
  44.9 7.8 %collective-permute-start.13 = (bf16[64,1536]{1,0:T(8,128)(2,1)S(1)}, bf16[64,1536]{1,0:T(8,128)(2,1)S(1)}, u32[]{:S(2)}, u32[]{:S(2)}) collective-permute-start(bf16[64,1536]{1,0:T(8,128)(2,1)S(1)} %get-tuple-element.96), channel_id=1, source_target_pairs={{0,16},{8,24},{16,0},{24,8},{1,17},{9,25},{17,1},{25,9},{2,18},{10... | collective-permute-start | bytes 589832 | tf_op jit(solution)/shard_map/ppermute | solution.py:28
  46.5 10.6 %collective-permute-start.11 = (f32[64,4096]{1,0:T(8,128)S(1)}, f32[64,4096]{1,0:T(8,128)S(1)}, u32[]{:S(2)}, u32[]{:S(2)}) collective-permute-start(f32[64,4096]{1,0:T(8,128)S(1)} %add.36.refs_0_.refs_3_), channel_id=1, source_target_pairs={{0,8},{8,0},{16,24},{24,16},{1,9},{9,1},{17,25},{25,17},{2,10},{10... | collective-permute-start | bytes 3145736 | tf_op jit(solution)/shard_map/ppermute | solution.py:28
  47.0 9.9 %collective-permute-start.15 = (bf16[64,1536]{1,0:T(8,128)(2,1)S(1)}, bf16[64,1536]{1,0:T(8,128)(2,1)S(1)}, u32[]{:S(2)}, u32[]{:S(2)}) collective-permute-start(bf16[64,1536]{1,0:T(8,128)(2,1)S(1)} %get-tuple-element.100), channel_id=1, source_target_pairs={{0,16},{8,24},{16,0},{24,8},{1,17},{9,25},{17,1},{25,9},{2,18},{10... | collective-permute-start | bytes 589832 | tf_op jit(solution)/shard_map/ppermute | solution.py:28
  48.0 10.9 %collective-permute-start.12 = (bf16[64,1024]{1,0:T(8,128)(2,1)S(1)}, bf16[64,1024]{1,0:T(8,128)(2,1)S(1)}, u32[]{:S(2)}, u32[]{:S(2)}) collective-permute-start(bf16[64,1024]{1,0:T(8,128)(2,1)S(1)} %get-tuple-element.105), channel_id=1, source_target_pairs={{0,16},{8,24},{16,0},{24,8},{1,17},{9,25},{17,1},{25,9},{2,18},{10... | collective-permute-start | bytes 393224 | tf_op jit(solution)/shard_map/ppermute | solution.py:28
  52.8 4.3 %collective-permute-start.14 = (bf16[64,1536]{1,0:T(8,128)(2,1)S(1)}, bf16[64,1536]{1,0:T(8,128)(2,1)S(1)}, u32[]{:S(2)}, u32[]{:S(2)}) collective-permute-start(bf16[64,1536]{1,0:T(8,128)(2,1)S(1)} %add_convert_fusion.1.refs_2_), channel_id=1, source_target_pairs={{0,8},{8,0},{16,24},{24,16},{1,9},{9,1},{17,25},{25,17},{2,10},{10... | collective-permute-start | bytes 589832 | tf_op jit(solution)/shard_map/ppermute | solution.py:28
  57.0 2.4 %collective-permute-start.17 = (bf16[64,1536]{1,0:T(8,128)(2,1)S(1)}, bf16[64,1536]{1,0:T(8,128)(2,1)S(1)}, u32[]{:S(2)}, u32[]{:S(2)}) collective-permute-start(bf16[64,1536]{1,0:T(8,128)(2,1)S(1)} %add_convert_fusion.refs_5_), channel_id=1, source_target_pairs={{0,8},{8,0},{16,24},{24,16},{1,9},{9,1},{17,25},{25,17},{2,10},{10... | collective-permute-start | bytes 589832 | tf_op jit(solution)/shard_map/ppermute | solution.py:28
  59.0 1.9 %collective-permute-start.16 = (bf16[64,1024]{1,0:T(8,128)(2,1)S(1)}, bf16[64,1024]{1,0:T(8,128)(2,1)S(1)}, u32[]{:S(2)}, u32[]{:S(2)}) collective-permute-start(bf16[64,1024]{1,0:T(8,128)(2,1)S(1)} %add_convert_fusion.2.refs_5_), channel_id=1, source_target_pairs={{0,8},{8,0},{16,24},{24,16},{1,9},{9,1},{17,25},{25,17},{2,10},{10... | collective-permute-start | bytes 393224 | tf_op jit(solution)/shard_map/ppermute | solution.py:28

commit v15 on v14

--- a/solution.py
+++ b/solution.py
@@ -46,7 +46,7 @@
     while mask < n:
         if len(terms) > 1:
             terms = [sum(t.astype(F32) for t in terms).astype(value.dtype)]
-        steps = [mask, 2 * mask, 3 * mask] if 2 * mask < n else [mask]
+        steps = [3 * mask, 2 * mask, mask] if 2 * mask < n else [mask]
         terms += [exchange(terms[0], axis, step) for step in steps]
         mask *= 4
     return terms
@@ -163,12 +163,12 @@
     )(side, *pin(pltpu.HBM, x, u, z, design, sign, *rows))
 
 
-GRAM_STEPS = (((0, 0),), ((1, 0), (1, 1), (2, 2)), ((2, 0), (2, 1)))
+GRAM_STEPS = (((0, 0), (2, 2)), ((1, 0), (1, 1)), ((2, 0), (2, 1)))
 
 
 def gram_kernel(blocks, token, a_ref, *refs):
-    *outs, acc = refs
-    size = outs[0].shape[0]
+    high, low, acc = refs
+    size = high.shape[0]
     width = a_ref.shape[1]
     wide = math.gcd(WIDE, width)
     rows = sorted({row for row, _ in blocks})
@@ -181,29 +181,28 @@
             at = pl.ds(j * wide, wide)
             product = nt(a_ref[pl.ds(row * size, size), at], a_ref[span, at])
             acc[:, here] = product if j == 0 else acc[:, here] + product
-        for k in range(len(cols)):
-            whole = acc[:, pl.ds(k * size, size)]
-            top = whole.astype(BF16)
-            outs[2 * done][...] = top
-            outs[2 * done + 1][...] = (whole - top.astype(F32)).astype(BF16)
-            done += 1
+        there = pl.ds(done * size, len(cols) * size)
+        whole = acc[:, here]
+        top = whole.astype(BF16)
+        high[:, there] = top
+        low[:, there] = (whole - top.astype(F32)).astype(BF16)
+        done += len(cols)
 
 
 def gram_blocks(step, token, design):
     samples = design.shape[0]
     size = samples // 3
     blocks = GRAM_STEPS[step]
-    out = pltpu.VMEM((size, size), BF16)
-    parts = call(
+    out = pltpu.VMEM((size, len(blocks) * size), BF16)
+    return call(
         functools.partial(gram_kernel, blocks),
         "gram",
         [SMEM, VMEM],
-        (out,) * (2 * len(blocks)),
-        [VMEM] * (2 * len(blocks)),
+        (out, out),
+        [VMEM] * 2,
         [pltpu.VMEM((size, 2 * size), F32)],
         work=WAIT_BYTES * (step + 1) // 3,
     )(token, *pin(pltpu.VMEM, design))
-    return {block: parts[2 * k : 2 * k + 2] for k, block in enumerate(blocks)}
 
 
 def residual(sign, *terms):
@@ -212,13 +211,13 @@
     return (sign * jax.nn.sigmoid(-sign * margin)).astype(BF16)
 
 
-LOWER = [(row, col) for row in range(3) for col in range(row + 1)]
-
-
 def turn_kernel(sign, scale, pulled, *refs):
-    *terms, resid, out = refs[12:]
-    grams = {block: refs[2 * k : 2 * k + 2] for k, block in enumerate(LOWER)}
+    *terms, resid, out = refs[6:]
     size = refs[0].shape[0]
+    grams = {}
+    for k, blocks in enumerate(GRAM_STEPS):
+        for j, block in enumerate(blocks):
+            grams[block] = [refs[2 * k + part].at[:, pl.ds(j * size, size)] for part in range(2)]
     resid[...] = residual(sign[...], *(t[...] for t in terms))
     eta = scale[:, 0:1]
     r = [resid[:, pl.ds(k * size, size)] for k in range(3)]
@@ -237,7 +236,7 @@
 def turn(sign, terms, scale, pulled, grams):
     tasks, samples = pulled.shape
     out = pltpu.VMEM((tasks, samples), BF16)
-    args = [sign, scale, pulled, *(part for block in LOWER for part in grams[block]), *terms]
+    args = [sign, scale, pulled, *grams, *terms]
     return call(turn_kernel, "turn", [VMEM] * len(args), (out, out), [VMEM] * 2)(*pin(pltpu.VMEM, *args))
 
 
@@ -383,16 +382,16 @@
     )
     start_mine = start_mine + exchange(start_other, "rows", 1)
 
-    terms, grams = [margin1], {}
+    terms, grams = [margin1], []
     for step in range(max(lax.axis_size("feat").bit_length() - 1, 3)):
         more = (1 << step) < lax.axis_size("feat")
         if step > 0 and more:
             terms = [sum(t.astype(F32) for t in terms).astype(BF16)]
-        made = gram_blocks(step, tie(side, terms[0]), design) if step < 3 else {}
-        grams.update(made)
+        made = gram_blocks(step, tie(side, terms[0]), design) if step < 3 else []
+        grams += made
         if more:
             got = exchange(terms[0], "feat", 1 << step)
-            terms.append(tie(got, made, start_mine) if step == 0 else tie(got, made) if step == 1 else got)
+            terms.append(tie(got, made[0], start_mine) if step == 0 else tie(got, made[0]) if step == 1 else got)
 
     resid1, margin2 = turn(sign, terms, scale, pulled, grams)
     terms = square_sum(margin2, "feat")

time: 62.1 us -> 60.9 us (0.981)
  waiting for transfers between devices: 16.6 us -> 12.5 us
  starting transfers between devices: 18.8 us -> 21.6 us
    ppermute x18, waiting for transfers between devices: 16.6 us -> 12.5 us  [exchange(): return lax.ppermute(value, axis, [(i, i ^ mask) for i in range(n)])]
    ppermute x18, starting transfers between devices: 18.8 us -> 21.6 us  [exchange(): return lax.ppermute(value, axis, [(i, i ^ mask) for i in range(n)])]
where the time goes in v15:
time: 60.9 us; the launch traced here: 60.7 us
  Pallas kernels  25.3 us (42%)
  starting transfers between devices  21.6 us (35%)
  waiting for transfers between devices  12.5 us (21%)
  between operations  0.85 us (1%)
    ppermute x18, starting transfers between devices, exchange(): return lax.ppermute(value, axis, [(i, i ^ mask) for i in range(n)])  21.6 us
    ppermute x18, waiting for transfers between devices, exchange(): return lax.ppermute(value, axis, [(i, i ^ mask) for i in range(n)])  12.5 us
    pallas_call x1, Pallas kernels, load(): call(functools.partial(load_kernel, blocks_count), 'load_and_margins', [S...  7.89 us
    pallas_call x3, Pallas kernels, gram_blocks(): call(functools.partial(gram_kernel, blocks), 'gram', [SMEM, VMEM], (out,...  7.07 us
    pallas_call x4, Pallas kernels, final(): call(functools.partial(final_kernel, blocks_count, places, buffered), 'fi...  5.4 us
    pallas_call x5, Pallas kernels, push(): call(functools.partial(push_kernel, first, mine, begin, offset, size), 'p...  2.71 us
    pallas_call x1, Pallas kernels, store_x(): call(store_kernel, 'store_x', [SMEM] + [VMEM] * len(args), pltpu.HBM((tas...  1.58 us
  transfers between devices with their start and end apart: 18, of which 11 were waited for; matrix products, arithmetic and copies ran while one was open for 1% of the time, Pallas kernels for 26%

profile of v15, /device:TPU:0, one launch (start us, length us, event | category | flops | bytes accessed | tf_op | source)
XLA Modules:
  0.0 60.7 jit_solution(18313918606829497434)
XLA Ops:
  0.6 7.9 %load_and_margins.1 = (bf16[64,768]{1,0:T(8,128)(2,1)S(1)}, f32[64,768]{1,0:T(8,128)S(1)}, bf16[768,8192]{1,0:T(8,128)(2,1)S(1)}, f32[64,8192]{1,0:T(8,128)S(1)}...) custom-call(s32[1]{0:T(128)} %bitcast.side.token, ...), custom_call_target="tpu_custom_call" | custom-call | flops 1000 | bytes 1000 | tf_op jit(solution)/shard_map/load_and_margins/pallas_call | solution.py:149
  9.1 2.6 %collective-permute-start = (bf16[64,768]{1,0:T(8,128)(2,1)S(1)}, bf16[64,768]{1,0:T(8,128)(2,1)S(1)}, u32[]{:S(2)}, u32[]{:S(2)}) collective-permute-start(bf16[64,768]{1,0:T(8,128)(2,1)S(1)} %get-tuple-element.61), channel_id=1, source_target_pairs={{0,1},{1,0},{2,3},{3,2},{4,5},{5,4},{6,7},{7,6},{8,9},{9,8},{10,11... | collective-permute-start | bytes 294920 | tf_op jit(solution)/shard_map/ppermute | solution.py:28
  11.6 2.4 %gram.3 = (bf16[256,512]{1,0:T(8,128)(2,1)S(1)}, bf16[256,512]{1,0:T(8,128)(2,1)S(1)}) custom-call(s32[1]{0:T(128)} %bitcast.side.token, bf16[768,8192]{1,0:T(8,128)(2,1)S(1)} %get-tuple-element.58.a_ref.refs_1_), custom_call_target="tpu_custom_call" | custom-call | flops 1000 | bytes 3333333 | tf_op jit(solution)/shard_map/gram/pallas_call | solution.py:197
  14.1 1.6 %collective-permute-start.8 = (f32[64,4096]{1,0:T(8,128)S(1)}, f32[64,4096]{1,0:T(8,128)S(1)}, u32[]{:S(2)}, u32[]{:S(2)}) collective-permute-start(f32[64,4096]{1,0:T(8,128)S(1)} %add.30), channel_id=1, source_target_pairs={{0,16},{8,24},{16,0},{24,8},{1,17},{9,25},{17,1},{25,9},{2,18},{10... | collective-permute-start | bytes 3145736 | tf_op jit(solution)/shard_map/ppermute | solution.py:28
  15.7 1.6 %collective-permute-start.2 = (bf16[64,768]{1,0:T(8,128)(2,1)S(1)}, bf16[64,768]{1,0:T(8,128)(2,1)S(1)}, u32[]{:S(2)}, u32[]{:S(2)}) collective-permute-start(bf16[64,768]{1,0:T(8,128)(2,1)S(1)} %add_convert_fusion.5), channel_id=1, source_target_pairs={{0,2},{1,3},{2,0},{3,1},{4,6},{5,7},{6,4},{7,5},{8,10},{9,11},{10,... | collective-permute-start | bytes 294920 | tf_op jit(solution)/shard_map/ppermute | solution.py:28
  17.4 2.4 %gram.4 = (bf16[256,512]{1,0:T(8,128)(2,1)S(1)}, bf16[256,512]{1,0:T(8,128)(2,1)S(1)}) custom-call(s32[1]{0:T(128)} %bitcast.side.token, bf16[768,8192]{1,0:T(8,128)(2,1)S(1)} %get-tuple-element.58.a_ref.refs_1_), custom_call_target="tpu_custom_call" | custom-call | flops 1000 | bytes 6666666 | tf_op jit(solution)/shard_map/gram/pallas_call | solution.py:197
  20.4 2.6 %collective-permute-start.3 = (bf16[64,768]{1,0:T(8,128)(2,1)S(1)}, bf16[64,768]{1,0:T(8,128)(2,1)S(1)}, u32[]{:S(2)}, u32[]{:S(2)}) collective-permute-start(bf16[64,768]{1,0:T(8,128)(2,1)S(1)} %add_convert_fusion.4.refs_6_), channel_id=1, source_target_pairs={{0,4},{1,5},{2,6},{3,7},{4,0},{5,1},{6,2},{7,3},{8,12},{9,13},{10,... | collective-permute-start | bytes 294920 | tf_op jit(solution)/shard_map/ppermute | solution.py:28
  23.1 2.4 %gram.5 = (bf16[256,512]{1,0:T(8,128)(2,1)S(1)}, bf16[256,512]{1,0:T(8,128)(2,1)S(1)}) custom-call(s32[1]{0:T(128)} %bitcast.side.token, bf16[768,8192]{1,0:T(8,128)(2,1)S(1)} %get-tuple-element.58.a_ref.refs_1_), custom_call_target="tpu_custom_call" | custom-call | flops 1000 | bytes 10000000 | tf_op jit(solution)/shard_map/gram/pallas_call | solution.py:197
  25.5 1.8 %collective-permute-done.3.refs_7_ = bf16[64,768]{1,0:T(8,128)(2,1)S(1)} collective-permute-done((bf16[64,768]{1,0:T(8,128)(2,1)S(1)}, bf16[64,768]{1,0:T(8,128)(2,1)S(1)}, u32[]{:S(2)}, u32[]{:S(2)}) %collective-permute-start.3) | collective-permute-done | bytes 98336 | tf_op jit(solution)/shard_map/ppermute | solution.py:28
  27.9 1.1 %collective-permute-start.4 = (bf16[64,768]{1,0:T(8,128)(2,1)S(1)}, bf16[64,768]{1,0:T(8,128)(2,1)S(1)}, u32[]{:S(2)}, u32[]{:S(2)}) collective-permute-start(bf16[64,768]{1,0:T(8,128)(2,1)S(1)} %get-tuple-element.76), channel_id=1, source_target_pairs={{0,3},{1,2},{2,1},{3,0},{4,7},{5,6},{6,5},{7,4},{8,11},{9,10},{10,... | collective-permute-start | bytes 294920 | tf_op jit(solution)/shard_map/ppermute | solution.py:28
  29.3 2.1 %collective-permute-start.6 = (bf16[64,768]{1,0:T(8,128)(2,1)S(1)}, bf16[64,768]{1,0:T(8,128)(2,1)S(1)}, u32[]{:S(2)}, u32[]{:S(2)}) collective-permute-start(bf16[64,768]{1,0:T(8,128)(2,1)S(1)} %get-tuple-element.76), channel_id=1, source_target_pairs={{0,1},{1,0},{2,3},{3,2},{4,5},{5,4},{6,7},{7,6},{8,9},{9,8},{10,11... | collective-permute-start | bytes 294920 | tf_op jit(solution)/shard_map/ppermute | solution.py:28
  31.4 2.1 %collective-permute-done.4 = bf16[64,768]{1,0:T(8,128)(2,1)S(1)} collective-permute-done((bf16[64,768]{1,0:T(8,128)(2,1)S(1)}, bf16[64,768]{1,0:T(8,128)(2,1)S(1)}, u32[]{:S(2)}, u32[]{:S(2)}) %collective-permute-start.4) | collective-permute-done | bytes 98336 | tf_op jit(solution)/shard_map/ppermute | solution.py:28
  33.6 0.9 %collective-permute-done.6 = bf16[64,768]{1,0:T(8,128)(2,1)S(1)} collective-permute-done((bf16[64,768]{1,0:T(8,128)(2,1)S(1)}, bf16[64,768]{1,0:T(8,128)(2,1)S(1)}, u32[]{:S(2)}, u32[]{:S(2)}) %collective-permute-start.6) | collective-permute-done | bytes 98336 | tf_op jit(solution)/shard_map/ppermute | solution.py:28
  34.6 2.5 %collective-permute-start.7 = (bf16[64,768]{1,0:T(8,128)(2,1)S(1)}, bf16[64,768]{1,0:T(8,128)(2,1)S(1)}, u32[]{:S(2)}, u32[]{:S(2)}) collective-permute-start(bf16[64,768]{1,0:T(8,128)(2,1)S(1)} %add_convert_fusion.3.refs_4_), channel_id=1, source_target_pairs={{0,4},{1,5},{2,6},{3,7},{4,0},{5,1},{6,2},{7,3},{8,12},{9,13},{10,... | collective-permute-start | bytes 294920 | tf_op jit(solution)/shard_map/ppermute | solution.py:28
  37.1 2.3 %collective-permute-done.8 = f32[64,4096]{1,0:T(8,128)S(1)} collective-permute-done((f32[64,4096]{1,0:T(8,128)S(1)}, f32[64,4096]{1,0:T(8,128)S(1)}, u32[]{:S(2)}, u32[]{:S(2)}) %collective-permute-start.8) | collective-permute-done | bytes 1048608 | tf_op jit(solution)/shard_map/ppermute | solution.py:28
  42.7 2.9 %collective-permute-start.13 = (bf16[64,1536]{1,0:T(8,128)(2,1)S(1)}, bf16[64,1536]{1,0:T(8,128)(2,1)S(1)}, u32[]{:S(2)}, u32[]{:S(2)}) collective-permute-start(bf16[64,1536]{1,0:T(8,128)(2,1)S(1)} %get-tuple-element.84), channel_id=1, source_target_pairs={{0,16},{8,24},{16,0},{24,8},{1,17},{9,25},{17,1},{25,9},{2,18},{10... | collective-permute-start | bytes 589832 | tf_op jit(solution)/shard_map/ppermute | solution.py:28
  47.2 1.6 %store_x.1 = f32[64,8192]{1,0:T(8,128)} custom-call(s32[1]{0:T(128)} %bitcast.side.token, f32[64,128]{1,0:T(8,128)S(1)} %get-tuple-element.54.scale.refs_0_, f32[64,8192]{1,0:T(8,128)S(1)} %get-tuple-element.55.x_ref, f32[64,8192]{1,0:T(8,128)S(1)} %get-tuple-element.56.u_ref, f32[64,8192]{1,0:T(8,128)S(1)} %get-tuple-element.57.z_ref, ...), custom_call_target="tpu_custom_call" | custom-call | flops 1000 | bytes 1000 | tf_op jit(solution)/shard_map/store_x/pallas_call | solution.py:309
  48.8 2.6 %collective-permute-done.13 = bf16[64,1536]{1,0:T(8,128)(2,1)S(1)} collective-permute-done((bf16[64,1536]{1,0:T(8,128)(2,1)S(1)}, bf16[64,1536]{1,0:T(8,128)(2,1)S(1)}, u32[]{:S(2)}, u32[]{:S(2)}) %collective-permute-start.13) | collective-permute-done | bytes 196640 | tf_op jit(solution)/shard_map/ppermute | solution.py:28
  51.4 2.1 %collective-permute-start.12 = (bf16[64,1024]{1,0:T(8,128)(2,1)S(1)}, bf16[64,1024]{1,0:T(8,128)(2,1)S(1)}, u32[]{:S(2)}, u32[]{:S(2)}) collective-permute-start(bf16[64,1024]{1,0:T(8,128)(2,1)S(1)} %get-tuple-element.93), channel_id=1, source_target_pairs={{0,16},{8,24},{16,0},{24,8},{1,17},{9,25},{17,1},{25,9},{2,18},{10... | collective-permute-start | bytes 393224 | tf_op jit(solution)/shard_map/ppermute | solution.py:28
  53.5 1.2 %final.4 = (f32[64,8192]{1,0:T(8,128)}, f32[64,8192]{1,0:T(8,128)}) custom-call(s32[1]{0:T(128)} %bitcast.side.token, f32[64,128]{1,0:T(8,128)S(1)} %get-tuple-element.54.scale.refs_0_, f32[64,8192]{1,0:T(8,128)S(1)} %get-tuple-element.55.x_ref, f32[64,8192]{1,0:T(8,128)S(1)} %get-tuple-element.56.u_ref, f32[64,8192]{1,0:T(8,128)S(1)} %get-tuple-element.57.z_ref, ...), custom_call_target="tpu_custom_call" | custom-call | flops 1000 | bytes 1000 | tf_op jit(solution)/shard_map/final/pallas_call | solution.py:359
  54.8 0.8 %collective-permute-done.15 = bf16[64,1536]{1,0:T(8,128)(2,1)S(1)} collective-permute-done((bf16[64,1536]{1,0:T(8,128)(2,1)S(1)}, bf16[64,1536]{1,0:T(8,128)(2,1)S(1)}, u32[]{:S(2)}, u32[]{:S(2)}) %collective-permute-start.15) | collective-permute-done | bytes 196640 | tf_op jit(solution)/shard_map/ppermute | solution.py:28
  56.2 1.7 %final.5 = (f32[64,8192]{1,0:T(8,128)}, f32[64,8192]{1,0:T(8,128)}) custom-call(s32[1]{0:T(128)} %bitcast.side.token, f32[64,128]{1,0:T(8,128)S(1)} %get-tuple-element.54.scale.refs_0_, f32[64,8192]{1,0:T(8,128)S(1)} %get-tuple-element.55.x_ref, f32[64,8192]{1,0:T(8,128)S(1)} %get-tuple-element.56.u_ref, ...), custom_call_target="tpu_custom_call", output_to_operand_aliasing={{0}: (11, {}), {1}: (12, {})} | custom-call | flops 1000 | bytes 1000 | tf_op jit(solution)/shard_map/final/pallas_call | solution.py:359
  58.1 1.5 %final.6 = (f32[64,8192]{1,0:T(8,128)}, f32[64,8192]{1,0:T(8,128)}) custom-call(s32[1]{0:T(128)} %bitcast.side.token, f32[64,128]{1,0:T(8,128)S(1)} %get-tuple-element.54.scale.refs_0_, f32[64,8192]{1,0:T(8,128)S(1)} %get-tuple-element.55.x_ref, f32[64,8192]{1,0:T(8,128)S(1)} %get-tuple-element.56.u_ref, ...), custom_call_target="tpu_custom_call", output_to_operand_aliasing={{0}: (11, {}), {1}: (12, {})} | custom-call | flops 1000 | bytes 1000 | tf_op jit(solution)/shard_map/final/pallas_call | solution.py:359
  59.7 1.0 %final.7 = (f32[64,8192]{1,0:T(8,128)}, f32[64,8192]{1,0:T(8,128)}) custom-call(s32[1]{0:T(128)} %bitcast.side.token, f32[64,128]{1,0:T(8,128)S(1)} %get-tuple-element.54.scale.refs_0_, f32[64,8192]{1,0:T(8,128)S(1)} %get-tuple-element.55.x_ref, f32[64,8192]{1,0:T(8,128)S(1)} %get-tuple-element.56.u_ref, ...), custom_call_target="tpu_custom_call", output_to_operand_aliasing={{0}: (8, {}), {1}: (9, {})} | custom-call | flops 1000 | bytes 1000 | tf_op jit(solution)/shard_map/final/pallas_call | solution.py:359
  (35 shorter events, 8.2 us)
Async XLA Ops:
  8.5 5.5 %collective-permute-start.1 = (f32[64,4096]{1,0:T(8,128)S(1)}, f32[64,4096]{1,0:T(8,128)S(1)}, u32[]{:S(2)}, u32[]{:S(2)}) collective-permute-start(f32[64,4096]{1,0:T(8,128)S(1)} %get-tuple-element.66), channel_id=1, source_target_pairs={{0,8},{8,0},{16,24},{24,16},{1,9},{9,1},{17,25},{25,17},{2,10},{10... | collective-permute-start | bytes 3145736 | tf_op jit(solution)/shard_map/ppermute | solution.py:28
  9.1 6.7 %collective-permute-start = (bf16[64,768]{1,0:T(8,128)(2,1)S(1)}, bf16[64,768]{1,0:T(8,128)(2,1)S(1)}, u32[]{:S(2)}, u32[]{:S(2)}) collective-permute-start(bf16[64,768]{1,0:T(8,128)(2,1)S(1)} %get-tuple-element.61), channel_id=1, source_target_pairs={{0,1},{1,0},{2,3},{3,2},{4,5},{5,4},{6,7},{7,6},{8,9},{9,8},{10,11... | collective-permute-start | bytes 294920 | tf_op jit(solution)/shard_map/ppermute | solution.py:28
  14.1 25.3 %collective-permute-start.8 = (f32[64,4096]{1,0:T(8,128)S(1)}, f32[64,4096]{1,0:T(8,128)S(1)}, u32[]{:S(2)}, u32[]{:S(2)}) collective-permute-start(f32[64,4096]{1,0:T(8,128)S(1)} %add.30), channel_id=1, source_target_pairs={{0,16},{8,24},{16,0},{24,8},{1,17},{9,25},{17,1},{25,9},{2,18},{10... | collective-permute-start | bytes 3145736 | tf_op jit(solution)/shard_map/ppermute | solution.py:28
  15.7 4.7 %collective-permute-start.2 = (bf16[64,768]{1,0:T(8,128)(2,1)S(1)}, bf16[64,768]{1,0:T(8,128)(2,1)S(1)}, u32[]{:S(2)}, u32[]{:S(2)}) collective-permute-start(bf16[64,768]{1,0:T(8,128)(2,1)S(1)} %add_convert_fusion.5), channel_id=1, source_target_pairs={{0,2},{1,3},{2,0},{3,1},{4,6},{5,7},{6,4},{7,5},{8,10},{9,11},{10,... | collective-permute-start | bytes 294920 | tf_op jit(solution)/shard_map/ppermute | solution.py:28
  20.4 6.8 %collective-permute-start.3 = (bf16[64,768]{1,0:T(8,128)(2,1)S(1)}, bf16[64,768]{1,0:T(8,128)(2,1)S(1)}, u32[]{:S(2)}, u32[]{:S(2)}) collective-permute-start(bf16[64,768]{1,0:T(8,128)(2,1)S(1)} %add_convert_fusion.4.refs_6_), channel_id=1, source_target_pairs={{0,4},{1,5},{2,6},{3,7},{4,0},{5,1},{6,2},{7,3},{8,12},{9,13},{10,... | collective-permute-start | bytes 294920 | tf_op jit(solution)/shard_map/ppermute | solution.py:28
  27.9 5.6 %collective-permute-start.4 = (bf16[64,768]{1,0:T(8,128)(2,1)S(1)}, bf16[64,768]{1,0:T(8,128)(2,1)S(1)}, u32[]{:S(2)}, u32[]{:S(2)}) collective-permute-start(bf16[64,768]{1,0:T(8,128)(2,1)S(1)} %get-tuple-element.76), channel_id=1, source_target_pairs={{0,3},{1,2},{2,1},{3,0},{4,7},{5,6},{6,5},{7,4},{8,11},{9,10},{10,... | collective-permute-start | bytes 294920 | tf_op jit(solution)/shard_map/ppermute | solution.py:28
  29.0 4.6 %collective-permute-start.5 = (bf16[64,768]{1,0:T(8,128)(2,1)S(1)}, bf16[64,768]{1,0:T(8,128)(2,1)S(1)}, u32[]{:S(2)}, u32[]{:S(2)}) collective-permute-start(bf16[64,768]{1,0:T(8,128)(2,1)S(1)} %get-tuple-element.76), channel_id=1, source_target_pairs={{0,2},{1,3},{2,0},{3,1},{4,6},{5,7},{6,4},{7,5},{8,10},{9,11},{10,... | collective-permute-start | bytes 294920 | tf_op jit(solution)/shard_map/ppermute | solution.py:28
  29.3 5.2 %collective-permute-start.6 = (bf16[64,768]{1,0:T(8,128)(2,1)S(1)}, bf16[64,768]{1,0:T(8,128)(2,1)S(1)}, u32[]{:S(2)}, u32[]{:S(2)}) collective-permute-start(bf16[64,768]{1,0:T(8,128)(2,1)S(1)} %get-tuple-element.76), channel_id=1, source_target_pairs={{0,1},{1,0},{2,3},{3,2},{4,5},{5,4},{6,7},{7,6},{8,9},{9,8},{10,11... | collective-permute-start | bytes 294920 | tf_op jit(solution)/shard_map/ppermute | solution.py:28
  34.6 5.6 %collective-permute-start.7 = (bf16[64,768]{1,0:T(8,128)(2,1)S(1)}, bf16[64,768]{1,0:T(8,128)(2,1)S(1)}, u32[]{:S(2)}, u32[]{:S(2)}) collective-permute-start(bf16[64,768]{1,0:T(8,128)(2,1)S(1)} %add_convert_fusion.3.refs_4_), channel_id=1, source_target_pairs={{0,4},{1,5},{2,6},{3,7},{4,0},{5,1},{6,2},{7,3},{8,12},{9,13},{10,... | collective-permute-start | bytes 294920 | tf_op jit(solution)/shard_map/ppermute | solution.py:28
  40.7 1.5 %collective-permute-start.9 = (bf16[64,1536]{1,0:T(8,128)(2,1)S(1)}, bf16[64,1536]{1,0:T(8,128)(2,1)S(1)}, u32[]{:S(2)}, u32[]{:S(2)}) collective-permute-start(bf16[64,1536]{1,0:T(8,128)(2,1)S(1)} %get-tuple-element.82), channel_id=1, source_target_pairs={{0,8},{8,0},{16,24},{24,16},{1,9},{9,1},{17,25},{25,17},{2,10},{10... | collective-permute-start | bytes 589832 | tf_op jit(solution)/shard_map/ppermute | solution.py:28
  41.5 4.1 %collective-permute-start.10 = (bf16[64,2560]{1,0:T(8,128)(2,1)S(1)}, bf16[64,2560]{1,0:T(8,128)(2,1)S(1)}, u32[]{:S(2)}, u32[]{:S(2)}) collective-permute-start(bf16[64,2560]{1,0:T(8,128)(2,1)S(1)} %get-tuple-element.86), channel_id=1, source_target_pairs={{0,8},{8,0},{16,24},{24,16},{1,9},{9,1},{17,25},{25,17},{2,10},{10... | collective-permute-start | bytes 983048 | tf_op jit(solution)/shard_map/ppermute | solution.py:28
  42.7 8.6 %collective-permute-start.13 = (bf16[64,1536]{1,0:T(8,128)(2,1)S(1)}, bf16[64,1536]{1,0:T(8,128)(2,1)S(1)}, u32[]{:S(2)}, u32[]{:S(2)}) collective-permute-start(bf16[64,1536]{1,0:T(8,128)(2,1)S(1)} %get-tuple-element.84), channel_id=1, source_target_pairs={{0,16},{8,24},{16,0},{24,8},{1,17},{9,25},{17,1},{25,9},{2,18},{10... | collective-permute-start | bytes 589832 | tf_op jit(solution)/shard_map/ppermute | solution.py:28
  45.6 10.6 %collective-permute-start.11 = (f32[64,4096]{1,0:T(8,128)S(1)}, f32[64,4096]{1,0:T(8,128)S(1)}, u32[]{:S(2)}, u32[]{:S(2)}) collective-permute-start(f32[64,4096]{1,0:T(8,128)S(1)} %add.36.refs_0_.refs_3_), channel_id=1, source_target_pairs={{0,8},{8,0},{16,24},{24,16},{1,9},{9,1},{17,25},{25,17},{2,10},{10... | collective-permute-start | bytes 3145736 | tf_op jit(solution)/shard_map/ppermute | solution.py:28
  46.2 9.4 %collective-permute-start.15 = (bf16[64,1536]{1,0:T(8,128)(2,1)S(1)}, bf16[64,1536]{1,0:T(8,128)(2,1)S(1)}, u32[]{:S(2)}, u32[]{:S(2)}) collective-permute-start(bf16[64,1536]{1,0:T(8,128)(2,1)S(1)} %get-tuple-element.88), channel_id=1, source_target_pairs={{0,16},{8,24},{16,0},{24,8},{1,17},{9,25},{17,1},{25,9},{2,18},{10... | collective-permute-start | bytes 589832 | tf_op jit(solution)/shard_map/ppermute | solution.py:28
  51.4 6.5 %collective-permute-start.12 = (bf16[64,1024]{1,0:T(8,128)(2,1)S(1)}, bf16[64,1024]{1,0:T(8,128)(2,1)S(1)}, u32[]{:S(2)}, u32[]{:S(2)}) collective-permute-start(bf16[64,1024]{1,0:T(8,128)(2,1)S(1)} %get-tuple-element.93), channel_id=1, source_target_pairs={{0,16},{8,24},{16,0},{24,8},{1,17},{9,25},{17,1},{25,9},{2,18},{10... | collective-permute-start | bytes 393224 | tf_op jit(solution)/shard_map/ppermute | solution.py:28
  54.7 1.5 %collective-permute-start.14 = (bf16[64,1536]{1,0:T(8,128)(2,1)S(1)}, bf16[64,1536]{1,0:T(8,128)(2,1)S(1)}, u32[]{:S(2)}, u32[]{:S(2)}) collective-permute-start(bf16[64,1536]{1,0:T(8,128)(2,1)S(1)} %add_convert_fusion.1.refs_2_), channel_id=1, source_target_pairs={{0,8},{8,0},{16,24},{24,16},{1,9},{9,1},{17,25},{25,17},{2,10},{10... | collective-permute-start | bytes 589832 | tf_op jit(solution)/shard_map/ppermute | solution.py:28
  55.6 2.6 %collective-permute-start.17 = (bf16[64,1536]{1,0:T(8,128)(2,1)S(1)}, bf16[64,1536]{1,0:T(8,128)(2,1)S(1)}, u32[]{:S(2)}, u32[]{:S(2)}) collective-permute-start(bf16[64,1536]{1,0:T(8,128)(2,1)S(1)} %add_convert_fusion.refs_5_), channel_id=1, source_target_pairs={{0,8},{8,0},{16,24},{24,16},{1,9},{9,1},{17,25},{25,17},{2,10},{10... | collective-permute-start | bytes 589832 | tf_op jit(solution)/shard_map/ppermute | solution.py:28
  57.9 1.7 %collective-permute-start.16 = (bf16[64,1024]{1,0:T(8,128)(2,1)S(1)}, bf16[64,1024]{1,0:T(8,128)(2,1)S(1)}, u32[]{:S(2)}, u32[]{:S(2)}) collective-permute-start(bf16[64,1024]{1,0:T(8,128)(2,1)S(1)} %add_convert_fusion.2.refs_5_), channel_id=1, source_target_pairs={{0,8},{8,0},{16,24},{24,16},{1,9},{9,1},{17,25},{25,17},{2,10},{10... | collective-permute-start | bytes 393224 | tf_op jit(solution)/shard_map/ppermute | solution.py:28

commit v16 on v15

--- a/solution.py
+++ b/solution.py
@@ -11,8 +11,8 @@
 BF16 = jnp.bfloat16
 F32 = jnp.float32
 PLAN = ((((True, 0),),), (((False, 0), (True, 1)),), (((False, 1), (True, 2)), ((False, 2),)))
-MINE = (3, 3, 2)
-OTHER = (3, 5)
+MINE = (2, 4, 2)
+OTHER = (2, 6)
 STEP = 1024
 WIDE = 2048
 AHEAD = 8

time: 60.9 us -> 61 us (level)
  transfers between devices with their start and end apart: 18 -> 18, of which waited for: 11 -> 10; matrix products, arithmetic and copies ran while one was open for 1% -> 1% of each run, Pallas kernels for 26% -> 26%
where the time goes in v16:
time: 61 us; the launch traced here: 60.8 us
  Pallas kernels  25.4 us (42%)
  starting transfers between devices  21.7 us (36%)
  waiting for transfers between devices  12.4 us (20%)
  between operations  0.86 us (1%)
    ppermute x18, starting transfers between devices, exchange(): return lax.ppermute(value, axis, [(i, i ^ mask) for i in range(n)])  21.7 us
    ppermute x18, waiting for transfers between devices, exchange(): return lax.ppermute(value, axis, [(i, i ^ mask) for i in range(n)])  12.4 us
    pallas_call x1, Pallas kernels, load(): call(functools.partial(load_kernel, blocks_count), 'load_and_margins', [S...  7.89 us
    pallas_call x3, Pallas kernels, gram_blocks(): call(functools.partial(gram_kernel, blocks), 'gram', [SMEM, VMEM], (out,...  7.07 us
    pallas_call x4, Pallas kernels, final(): call(functools.partial(final_kernel, blocks_count, places, buffered), 'fi...  5.43 us
    pallas_call x5, Pallas kernels, push(): call(functools.partial(push_kernel, first, mine, begin, offset, size), 'p...  2.72 us
    pallas_call x1, Pallas kernels, store_x(): call(store_kernel, 'store_x', [SMEM] + [VMEM] * len(args), pltpu.HBM((tas...  1.62 us
  transfers between devices with their start and end apart: 18, of which 10 were waited for; matrix products, arithmetic and copies ran while one was open for 1% of the time, Pallas kernels for 26%

profile of v16, /device:TPU:0, one launch (start us, length us, event | category | flops | bytes accessed | tf_op | source)
XLA Modules:
  0.0 60.8 jit_solution(9788019079901917634)
XLA Ops:
  0.6 7.9 %load_and_margins.1 = (bf16[64,768]{1,0:T(8,128)(2,1)S(1)}, f32[64,768]{1,0:T(8,128)S(1)}, bf16[768,8192]{1,0:T(8,128)(2,1)S(1)}, f32[64,8192]{1,0:T(8,128)S(1)}...) custom-call(s32[1]{0:T(128)} %bitcast.side.token, ...), custom_call_target="tpu_custom_call" | custom-call | flops 1000 | bytes 1000 | tf_op jit(solution)/shard_map/load_and_margins/pallas_call | solution.py:149
  9.1 2.6 %collective-permute-start = (bf16[64,768]{1,0:T(8,128)(2,1)S(1)}, bf16[64,768]{1,0:T(8,128)(2,1)S(1)}, u32[]{:S(2)}, u32[]{:S(2)}) collective-permute-start(bf16[64,768]{1,0:T(8,128)(2,1)S(1)} %get-tuple-element.61), channel_id=1, source_target_pairs={{0,1},{1,0},{2,3},{3,2},{4,5},{5,4},{6,7},{7,6},{8,9},{9,8},{10,11... | collective-permute-start | bytes 294920 | tf_op jit(solution)/shard_map/ppermute | solution.py:28
  11.6 2.4 %gram.3 = (bf16[256,512]{1,0:T(8,128)(2,1)S(1)}, bf16[256,512]{1,0:T(8,128)(2,1)S(1)}) custom-call(s32[1]{0:T(128)} %bitcast.side.token, bf16[768,8192]{1,0:T(8,128)(2,1)S(1)} %get-tuple-element.58.a_ref.refs_1_), custom_call_target="tpu_custom_call" | custom-call | flops 1000 | bytes 3333333 | tf_op jit(solution)/shard_map/gram/pallas_call | solution.py:197
  14.1 1.6 %collective-permute-start.8 = (f32[64,4096]{1,0:T(8,128)S(1)}, f32[64,4096]{1,0:T(8,128)S(1)}, u32[]{:S(2)}, u32[]{:S(2)}) collective-permute-start(f32[64,4096]{1,0:T(8,128)S(1)} %add.30), channel_id=1, source_target_pairs={{0,16},{8,24},{16,0},{24,8},{1,17},{9,25},{17,1},{25,9},{2,18},{10... | collective-permute-start | bytes 3145736 | tf_op jit(solution)/shard_map/ppermute | solution.py:28
  15.7 1.6 %collective-permute-start.2 = (bf16[64,768]{1,0:T(8,128)(2,1)S(1)}, bf16[64,768]{1,0:T(8,128)(2,1)S(1)}, u32[]{:S(2)}, u32[]{:S(2)}) collective-permute-start(bf16[64,768]{1,0:T(8,128)(2,1)S(1)} %add_convert_fusion.5), channel_id=1, source_target_pairs={{0,2},{1,3},{2,0},{3,1},{4,6},{5,7},{6,4},{7,5},{8,10},{9,11},{10,... | collective-permute-start | bytes 294920 | tf_op jit(solution)/shard_map/ppermute | solution.py:28
  17.4 2.4 %gram.4 = (bf16[256,512]{1,0:T(8,128)(2,1)S(1)}, bf16[256,512]{1,0:T(8,128)(2,1)S(1)}) custom-call(s32[1]{0:T(128)} %bitcast.side.token, bf16[768,8192]{1,0:T(8,128)(2,1)S(1)} %get-tuple-element.58.a_ref.refs_1_), custom_call_target="tpu_custom_call" | custom-call | flops 1000 | bytes 6666666 | tf_op jit(solution)/shard_map/gram/pallas_call | solution.py:197
  20.4 2.6 %collective-permute-start.3 = (bf16[64,768]{1,0:T(8,128)(2,1)S(1)}, bf16[64,768]{1,0:T(8,128)(2,1)S(1)}, u32[]{:S(2)}, u32[]{:S(2)}) collective-permute-start(bf16[64,768]{1,0:T(8,128)(2,1)S(1)} %add_convert_fusion.4.refs_6_), channel_id=1, source_target_pairs={{0,4},{1,5},{2,6},{3,7},{4,0},{5,1},{6,2},{7,3},{8,12},{9,13},{10,... | collective-permute-start | bytes 294920 | tf_op jit(solution)/shard_map/ppermute | solution.py:28
  23.1 2.4 %gram.5 = (bf16[256,512]{1,0:T(8,128)(2,1)S(1)}, bf16[256,512]{1,0:T(8,128)(2,1)S(1)}) custom-call(s32[1]{0:T(128)} %bitcast.side.token, bf16[768,8192]{1,0:T(8,128)(2,1)S(1)} %get-tuple-element.58.a_ref.refs_1_), custom_call_target="tpu_custom_call" | custom-call | flops 1000 | bytes 10000000 | tf_op jit(solution)/shard_map/gram/pallas_call | solution.py:197
  25.5 1.8 %collective-permute-done.3.refs_7_ = bf16[64,768]{1,0:T(8,128)(2,1)S(1)} collective-permute-done((bf16[64,768]{1,0:T(8,128)(2,1)S(1)}, bf16[64,768]{1,0:T(8,128)(2,1)S(1)}, u32[]{:S(2)}, u32[]{:S(2)}) %collective-permute-start.3) | collective-permute-done | bytes 98336 | tf_op jit(solution)/shard_map/ppermute | solution.py:28
  27.9 1.1 %collective-permute-start.4 = (bf16[64,768]{1,0:T(8,128)(2,1)S(1)}, bf16[64,768]{1,0:T(8,128)(2,1)S(1)}, u32[]{:S(2)}, u32[]{:S(2)}) collective-permute-start(bf16[64,768]{1,0:T(8,128)(2,1)S(1)} %get-tuple-element.76), channel_id=1, source_target_pairs={{0,3},{1,2},{2,1},{3,0},{4,7},{5,6},{6,5},{7,4},{8,11},{9,10},{10,... | collective-permute-start | bytes 294920 | tf_op jit(solution)/shard_map/ppermute | solution.py:28
  29.3 2.1 %collective-permute-start.6 = (bf16[64,768]{1,0:T(8,128)(2,1)S(1)}, bf16[64,768]{1,0:T(8,128)(2,1)S(1)}, u32[]{:S(2)}, u32[]{:S(2)}) collective-permute-start(bf16[64,768]{1,0:T(8,128)(2,1)S(1)} %get-tuple-element.76), channel_id=1, source_target_pairs={{0,1},{1,0},{2,3},{3,2},{4,5},{5,4},{6,7},{7,6},{8,9},{9,8},{10,11... | collective-permute-start | bytes 294920 | tf_op jit(solution)/shard_map/ppermute | solution.py:28
  31.4 2.1 %collective-permute-done.4 = bf16[64,768]{1,0:T(8,128)(2,1)S(1)} collective-permute-done((bf16[64,768]{1,0:T(8,128)(2,1)S(1)}, bf16[64,768]{1,0:T(8,128)(2,1)S(1)}, u32[]{:S(2)}, u32[]{:S(2)}) %collective-permute-start.4) | collective-permute-done | bytes 98336 | tf_op jit(solution)/shard_map/ppermute | solution.py:28
  33.6 0.9 %collective-permute-done.6 = bf16[64,768]{1,0:T(8,128)(2,1)S(1)} collective-permute-done((bf16[64,768]{1,0:T(8,128)(2,1)S(1)}, bf16[64,768]{1,0:T(8,128)(2,1)S(1)}, u32[]{:S(2)}, u32[]{:S(2)}) %collective-permute-start.6) | collective-permute-done | bytes 98336 | tf_op jit(solution)/shard_map/ppermute | solution.py:28
  34.6 2.5 %collective-permute-start.7 = (bf16[64,768]{1,0:T(8,128)(2,1)S(1)}, bf16[64,768]{1,0:T(8,128)(2,1)S(1)}, u32[]{:S(2)}, u32[]{:S(2)}) collective-permute-start(bf16[64,768]{1,0:T(8,128)(2,1)S(1)} %add_convert_fusion.3.refs_4_), channel_id=1, source_target_pairs={{0,4},{1,5},{2,6},{3,7},{4,0},{5,1},{6,2},{7,3},{8,12},{9,13},{10,... | collective-permute-start | bytes 294920 | tf_op jit(solution)/shard_map/ppermute | solution.py:28
  37.1 2.3 %collective-permute-done.8 = f32[64,4096]{1,0:T(8,128)S(1)} collective-permute-done((f32[64,4096]{1,0:T(8,128)S(1)}, f32[64,4096]{1,0:T(8,128)S(1)}, u32[]{:S(2)}, u32[]{:S(2)}) %collective-permute-start.8) | collective-permute-done | bytes 1048608 | tf_op jit(solution)/shard_map/ppermute | solution.py:28
  42.6 2.9 %collective-permute-start.13 = (bf16[64,1024]{1,0:T(8,128)(2,1)S(1)}, bf16[64,1024]{1,0:T(8,128)(2,1)S(1)}, u32[]{:S(2)}, u32[]{:S(2)}) collective-permute-start(bf16[64,1024]{1,0:T(8,128)(2,1)S(1)} %get-tuple-element.84), channel_id=1, source_target_pairs={{0,16},{8,24},{16,0},{24,8},{1,17},{9,25},{17,1},{25,9},{2,18},{10... | collective-permute-start | bytes 393224 | tf_op jit(solution)/shard_map/ppermute | solution.py:28
  46.1 0.9 %collective-permute-start.15 = (bf16[64,2048]{1,0:T(8,128)(2,1)S(1)}, bf16[64,2048]{1,0:T(8,128)(2,1)S(1)}, u32[]{:S(2)}, u32[]{:S(2)}) collective-permute-start(bf16[64,2048]{1,0:T(8,128)(2,1)S(1)} %get-tuple-element.88), channel_id=1, source_target_pairs={{0,16},{8,24},{16,0},{24,8},{1,17},{9,25},{17,1},{25,9},{2,18},{10... | collective-permute-start | bytes 786440 | tf_op jit(solution)/shard_map/ppermute | solution.py:28
  47.4 1.6 %store_x.1 = f32[64,8192]{1,0:T(8,128)} custom-call(s32[1]{0:T(128)} %bitcast.side.token, f32[64,128]{1,0:T(8,128)S(1)} %get-tuple-element.54.scale.refs_0_, f32[64,8192]{1,0:T(8,128)S(1)} %get-tuple-element.55.x_ref, f32[64,8192]{1,0:T(8,128)S(1)} %get-tuple-element.56.u_ref, f32[64,8192]{1,0:T(8,128)S(1)} %get-tuple-element.57.z_ref, ...), custom_call_target="tpu_custom_call" | custom-call | flops 1000 | bytes 1000 | tf_op jit(solution)/shard_map/store_x/pallas_call | solution.py:309
  49.9 1.0 %final.4 = (f32[64,8192]{1,0:T(8,128)}, f32[64,8192]{1,0:T(8,128)}) custom-call(s32[1]{0:T(128)} %bitcast.side.token, f32[64,128]{1,0:T(8,128)S(1)} %get-tuple-element.54.scale.refs_0_, f32[64,8192]{1,0:T(8,128)S(1)} %get-tuple-element.55.x_ref, f32[64,8192]{1,0:T(8,128)S(1)} %get-tuple-element.56.u_ref, f32[64,8192]{1,0:T(8,128)S(1)} %get-tuple-element.57.z_ref, ...), custom_call_target="tpu_custom_call" | custom-call | flops 1000 | bytes 1000 | tf_op jit(solution)/shard_map/final/pallas_call | solution.py:359
  51.0 2.0 %collective-permute-start.12 = (bf16[64,1024]{1,0:T(8,128)(2,1)S(1)}, bf16[64,1024]{1,0:T(8,128)(2,1)S(1)}, u32[]{:S(2)}, u32[]{:S(2)}) collective-permute-start(bf16[64,1024]{1,0:T(8,128)(2,1)S(1)} %get-tuple-element.93), channel_id=1, source_target_pairs={{0,16},{8,24},{16,0},{24,8},{1,17},{9,25},{17,1},{25,9},{2,18},{10... | collective-permute-start | bytes 393224 | tf_op jit(solution)/shard_map/ppermute | solution.py:28
  53.0 2.5 %collective-permute-done.15 = bf16[64,2048]{1,0:T(8,128)(2,1)S(1)} collective-permute-done((bf16[64,2048]{1,0:T(8,128)(2,1)S(1)}, bf16[64,2048]{1,0:T(8,128)(2,1)S(1)}, u32[]{:S(2)}, u32[]{:S(2)}) %collective-permute-start.15) | collective-permute-done | bytes 262176 | tf_op jit(solution)/shard_map/ppermute | solution.py:28
  55.6 1.7 %final.5 = (f32[64,8192]{1,0:T(8,128)}, f32[64,8192]{1,0:T(8,128)}) custom-call(s32[1]{0:T(128)} %bitcast.side.token, f32[64,128]{1,0:T(8,128)S(1)} %get-tuple-element.54.scale.refs_0_, f32[64,8192]{1,0:T(8,128)S(1)} %get-tuple-element.55.x_ref, f32[64,8192]{1,0:T(8,128)S(1)} %get-tuple-element.56.u_ref, ...), custom_call_target="tpu_custom_call", output_to_operand_aliasing={{0}: (11, {}), {1}: (12, {})} | custom-call | flops 1000 | bytes 1000 | tf_op jit(solution)/shard_map/final/pallas_call | solution.py:359
  58.1 1.7 %final.6 = (f32[64,8192]{1,0:T(8,128)}, f32[64,8192]{1,0:T(8,128)}) custom-call(s32[1]{0:T(128)} %bitcast.side.token, f32[64,128]{1,0:T(8,128)S(1)} %get-tuple-element.54.scale.refs_0_, f32[64,8192]{1,0:T(8,128)S(1)} %get-tuple-element.55.x_ref, f32[64,8192]{1,0:T(8,128)S(1)} %get-tuple-element.56.u_ref, ...), custom_call_target="tpu_custom_call", output_to_operand_aliasing={{0}: (11, {}), {1}: (12, {})} | custom-call | flops 1000 | bytes 1000 | tf_op jit(solution)/shard_map/final/pallas_call | solution.py:359
  59.8 1.0 %final.7 = (f32[64,8192]{1,0:T(8,128)}, f32[64,8192]{1,0:T(8,128)}) custom-call(s32[1]{0:T(128)} %bitcast.side.token, f32[64,128]{1,0:T(8,128)S(1)} %get-tuple-element.54.scale.refs_0_, f32[64,8192]{1,0:T(8,128)S(1)} %get-tuple-element.55.x_ref, f32[64,8192]{1,0:T(8,128)S(1)} %get-tuple-element.56.u_ref, ...), custom_call_target="tpu_custom_call", output_to_operand_aliasing={{0}: (8, {}), {1}: (9, {})} | custom-call | flops 1000 | bytes 1000 | tf_op jit(solution)/shard_map/final/pallas_call | solution.py:359
  (35 shorter events, 8.4 us)
Async XLA Ops:
  8.5 5.5 %collective-permute-start.1 = (f32[64,4096]{1,0:T(8,128)S(1)}, f32[64,4096]{1,0:T(8,128)S(1)}, u32[]{:S(2)}, u32[]{:S(2)}) collective-permute-start(f32[64,4096]{1,0:T(8,128)S(1)} %get-tuple-element.66), channel_id=1, source_target_pairs={{0,8},{8,0},{16,24},{24,16},{1,9},{9,1},{17,25},{25,17},{2,10},{10... | collective-permute-start | bytes 3145736 | tf_op jit(solution)/shard_map/ppermute | solution.py:28
  9.1 6.7 %collective-permute-start = (bf16[64,768]{1,0:T(8,128)(2,1)S(1)}, bf16[64,768]{1,0:T(8,128)(2,1)S(1)}, u32[]{:S(2)}, u32[]{:S(2)}) collective-permute-start(bf16[64,768]{1,0:T(8,128)(2,1)S(1)} %get-tuple-element.61), channel_id=1, source_target_pairs={{0,1},{1,0},{2,3},{3,2},{4,5},{5,4},{6,7},{7,6},{8,9},{9,8},{10,11... | collective-permute-start | bytes 294920 | tf_op jit(solution)/shard_map/ppermute | solution.py:28
  14.1 25.3 %collective-permute-start.8 = (f32[64,4096]{1,0:T(8,128)S(1)}, f32[64,4096]{1,0:T(8,128)S(1)}, u32[]{:S(2)}, u32[]{:S(2)}) collective-permute-start(f32[64,4096]{1,0:T(8,128)S(1)} %add.30), channel_id=1, source_target_pairs={{0,16},{8,24},{16,0},{24,8},{1,17},{9,25},{17,1},{25,9},{2,18},{10... | collective-permute-start | bytes 3145736 | tf_op jit(solution)/shard_map/ppermute | solution.py:28
  15.7 4.7 %collective-permute-start.2 = (bf16[64,768]{1,0:T(8,128)(2,1)S(1)}, bf16[64,768]{1,0:T(8,128)(2,1)S(1)}, u32[]{:S(2)}, u32[]{:S(2)}) collective-permute-start(bf16[64,768]{1,0:T(8,128)(2,1)S(1)} %add_convert_fusion.5), channel_id=1, source_target_pairs={{0,2},{1,3},{2,0},{3,1},{4,6},{5,7},{6,4},{7,5},{8,10},{9,11},{10,... | collective-permute-start | bytes 294920 | tf_op jit(solution)/shard_map/ppermute | solution.py:28
  20.4 6.8 %collective-permute-start.3 = (bf16[64,768]{1,0:T(8,128)(2,1)S(1)}, bf16[64,768]{1,0:T(8,128)(2,1)S(1)}, u32[]{:S(2)}, u32[]{:S(2)}) collective-permute-start(bf16[64,768]{1,0:T(8,128)(2,1)S(1)} %add_convert_fusion.4.refs_6_), channel_id=1, source_target_pairs={{0,4},{1,5},{2,6},{3,7},{4,0},{5,1},{6,2},{7,3},{8,12},{9,13},{10,... | collective-permute-start | bytes 294920 | tf_op jit(solution)/shard_map/ppermute | solution.py:28
  27.9 5.6 %collective-permute-start.4 = (bf16[64,768]{1,0:T(8,128)(2,1)S(1)}, bf16[64,768]{1,0:T(8,128)(2,1)S(1)}, u32[]{:S(2)}, u32[]{:S(2)}) collective-permute-start(bf16[64,768]{1,0:T(8,128)(2,1)S(1)} %get-tuple-element.76), channel_id=1, source_target_pairs={{0,3},{1,2},{2,1},{3,0},{4,7},{5,6},{6,5},{7,4},{8,11},{9,10},{10,... | collective-permute-start | bytes 294920 | tf_op jit(solution)/shard_map/ppermute | solution.py:28
  29.0 4.6 %collective-permute-start.5 = (bf16[64,768]{1,0:T(8,128)(2,1)S(1)}, bf16[64,768]{1,0:T(8,128)(2,1)S(1)}, u32[]{:S(2)}, u32[]{:S(2)}) collective-permute-start(bf16[64,768]{1,0:T(8,128)(2,1)S(1)} %get-tuple-element.76), channel_id=1, source_target_pairs={{0,2},{1,3},{2,0},{3,1},{4,6},{5,7},{6,4},{7,5},{8,10},{9,11},{10,... | collective-permute-start | bytes 294920 | tf_op jit(solution)/shard_map/ppermute | solution.py:28
  29.3 5.2 %collective-permute-start.6 = (bf16[64,768]{1,0:T(8,128)(2,1)S(1)}, bf16[64,768]{1,0:T(8,128)(2,1)S(1)}, u32[]{:S(2)}, u32[]{:S(2)}) collective-permute-start(bf16[64,768]{1,0:T(8,128)(2,1)S(1)} %get-tuple-element.76), channel_id=1, source_target_pairs={{0,1},{1,0},{2,3},{3,2},{4,5},{5,4},{6,7},{7,6},{8,9},{9,8},{10,11... | collective-permute-start | bytes 294920 | tf_op jit(solution)/shard_map/ppermute | solution.py:28
  34.6 5.6 %collective-permute-start.7 = (bf16[64,768]{1,0:T(8,128)(2,1)S(1)}, bf16[64,768]{1,0:T(8,128)(2,1)S(1)}, u32[]{:S(2)}, u32[]{:S(2)}) collective-permute-start(bf16[64,768]{1,0:T(8,128)(2,1)S(1)} %add_convert_fusion.3.refs_4_), channel_id=1, source_target_pairs={{0,4},{1,5},{2,6},{3,7},{4,0},{5,1},{6,2},{7,3},{8,12},{9,13},{10,... | collective-permute-start | bytes 294920 | tf_op jit(solution)/shard_map/ppermute | solution.py:28
  40.6 1.5 %collective-permute-start.9 = (bf16[64,1024]{1,0:T(8,128)(2,1)S(1)}, bf16[64,1024]{1,0:T(8,128)(2,1)S(1)}, u32[]{:S(2)}, u32[]{:S(2)}) collective-permute-start(bf16[64,1024]{1,0:T(8,128)(2,1)S(1)} %get-tuple-element.82), channel_id=1, source_target_pairs={{0,8},{8,0},{16,24},{24,16},{1,9},{9,1},{17,25},{25,17},{2,10},{10... | collective-permute-start | bytes 393224 | tf_op jit(solution)/shard_map/ppermute | solution.py:28
  41.5 3.9 %collective-permute-start.10 = (bf16[64,3072]{1,0:T(8,128)(2,1)S(1)}, bf16[64,3072]{1,0:T(8,128)(2,1)S(1)}, u32[]{:S(2)}, u32[]{:S(2)}) collective-permute-start(bf16[64,3072]{1,0:T(8,128)(2,1)S(1)} %get-tuple-element.86), channel_id=1, source_target_pairs={{0,8},{8,0},{16,24},{24,16},{1,9},{9,1},{17,25},{25,17},{2,10},{10... | collective-permute-start | bytes 1179656 | tf_op jit(solution)/shard_map/ppermute | solution.py:28
  42.5 13.1 %collective-permute-start.11 = (f32[64,4096]{1,0:T(8,128)S(1)}, f32[64,4096]{1,0:T(8,128)S(1)}, u32[]{:S(2)}, u32[]{:S(2)}) collective-permute-start(f32[64,4096]{1,0:T(8,128)S(1)} %add.36.refs_0_.refs_3_), channel_id=1, source_target_pairs={{0,8},{8,0},{16,24},{24,16},{1,9},{9,1},{17,25},{25,17},{2,10},{10... | collective-permute-start | bytes 3145736 | tf_op jit(solution)/shard_map/ppermute | solution.py:28
  42.6 7.2 %collective-permute-start.13 = (bf16[64,1024]{1,0:T(8,128)(2,1)S(1)}, bf16[64,1024]{1,0:T(8,128)(2,1)S(1)}, u32[]{:S(2)}, u32[]{:S(2)}) collective-permute-start(bf16[64,1024]{1,0:T(8,128)(2,1)S(1)} %get-tuple-element.84), channel_id=1, source_target_pairs={{0,16},{8,24},{16,0},{24,8},{1,17},{9,25},{17,1},{25,9},{2,18},{10... | collective-permute-start | bytes 393224 | tf_op jit(solution)/shard_map/ppermute | solution.py:28
  46.1 9.3 %collective-permute-start.15 = (bf16[64,2048]{1,0:T(8,128)(2,1)S(1)}, bf16[64,2048]{1,0:T(8,128)(2,1)S(1)}, u32[]{:S(2)}, u32[]{:S(2)}) collective-permute-start(bf16[64,2048]{1,0:T(8,128)(2,1)S(1)} %get-tuple-element.88), channel_id=1, source_target_pairs={{0,16},{8,24},{16,0},{24,8},{1,17},{9,25},{17,1},{25,9},{2,18},{10... | collective-permute-start | bytes 786440 | tf_op jit(solution)/shard_map/ppermute | solution.py:28
  50.9 4.7 %collective-permute-start.14 = (bf16[64,1024]{1,0:T(8,128)(2,1)S(1)}, bf16[64,1024]{1,0:T(8,128)(2,1)S(1)}, u32[]{:S(2)}, u32[]{:S(2)}) collective-permute-start(bf16[64,1024]{1,0:T(8,128)(2,1)S(1)} %add_convert_fusion.2.refs_2_), channel_id=1, source_target_pairs={{0,8},{8,0},{16,24},{24,16},{1,9},{9,1},{17,25},{25,17},{2,10},{10... | collective-permute-start | bytes 393224 | tf_op jit(solution)/shard_map/ppermute | solution.py:28
  51.0 7.0 %collective-permute-start.12 = (bf16[64,1024]{1,0:T(8,128)(2,1)S(1)}, bf16[64,1024]{1,0:T(8,128)(2,1)S(1)}, u32[]{:S(2)}, u32[]{:S(2)}) collective-permute-start(bf16[64,1024]{1,0:T(8,128)(2,1)S(1)} %get-tuple-element.93), channel_id=1, source_target_pairs={{0,16},{8,24},{16,0},{24,8},{1,17},{9,25},{17,1},{25,9},{2,18},{10... | collective-permute-start | bytes 393224 | tf_op jit(solution)/shard_map/ppermute | solution.py:28
  55.5 2.6 %collective-permute-start.17 = (bf16[64,2048]{1,0:T(8,128)(2,1)S(1)}, bf16[64,2048]{1,0:T(8,128)(2,1)S(1)}, u32[]{:S(2)}, u32[]{:S(2)}) collective-permute-start(bf16[64,2048]{1,0:T(8,128)(2,1)S(1)} %add_convert_fusion.refs_5_), channel_id=1, source_target_pairs={{0,8},{8,0},{16,24},{24,16},{1,9},{9,1},{17,25},{25,17},{2,10},{10... | collective-permute-start | bytes 786440 | tf_op jit(solution)/shard_map/ppermute | solution.py:28
  58.0 1.8 %collective-permute-start.16 = (bf16[64,1024]{1,0:T(8,128)(2,1)S(1)}, bf16[64,1024]{1,0:T(8,128)(2,1)S(1)}, u32[]{:S(2)}, u32[]{:S(2)}) collective-permute-start(bf16[64,1024]{1,0:T(8,128)(2,1)S(1)} %add_convert_fusion.1.refs_5_), channel_id=1, source_target_pairs={{0,8},{8,0},{16,24},{24,16},{1,9},{9,1},{17,25},{25,17},{2,10},{10... | collective-permute-start | bytes 393224 | tf_op jit(solution)/shard_map/ppermute | solution.py:28

commit v17 on v11

--- a/solution.py
+++ b/solution.py
@@ -127,14 +127,12 @@
             at, here = columns(j * STEP + k, NARROW), pl.ds(k, NARROW)
             x = x_out[:, at]
             v = x - pull * (x - z_out[:, at] + u_out[:, at])
-            top = v.astype(BF16)
             both[:tasks, here] = x.astype(BF16)
-            both[tasks : 2 * tasks, here] = top
-            both[2 * tasks :, here] = (v - top.astype(F32)).astype(BF16)
+            both[tasks:, here] = v.astype(BF16)
         acc[...] += nt(both[...], a_out[:, columns(j * STEP, STEP)])
 
     m_out[...] = acc[:tasks].astype(BF16)
-    pulled_out[...] = acc[tasks : 2 * tasks] + acc[2 * tasks :]
+    pulled_out[...] = acc[tasks:]
     half = width // 2
     mine = columns(side[0] * half, half)
     other = columns((1 - side[0]) * half, half)
@@ -160,7 +158,7 @@
         [VMEM] * 10,
         [pltpu.VMEM((1, tasks), F32)] * 3
         + [
-            pltpu.VMEM((3 * tasks, STEP), BF16), pltpu.VMEM((3 * tasks, samples), F32),
+            pltpu.VMEM((2 * tasks, STEP), BF16), pltpu.VMEM((2 * tasks, samples), F32),
             pltpu.SemaphoreType.DMA((5, max(width // STEP, 4))),
         ],
     )(side, *pin(pltpu.HBM, x, u, z, design, sign, *rows))

time: 60 us -> 59.8 us (level)
  no operation moved by 1% of the time
where the time goes in v17:
time: 59.8 us; the launch traced here: 59.7 us
  Pallas kernels  25.3 us (42%)
  starting transfers between devices  20.5 us (34%)
  waiting for transfers between devices  12.6 us (21%)
  between operations  0.85 us (1%)
    ppermute x18, starting transfers between devices, exchange(): return lax.ppermute(value, axis, [(i, i ^ mask) for i in range(n)])  20.5 us
    ppermute x18, waiting for transfers between devices, exchange(): return lax.ppermute(value, axis, [(i, i ^ mask) for i in range(n)])  12.6 us
    pallas_call x1, Pallas kernels, load(): call(functools.partial(load_kernel, blocks_count), 'load_and_margins', [S...  7.89 us
    pallas_call x3, Pallas kernels, gram_row(): call(functools.partial(gram_kernel, row), 'gram', [SMEM, VMEM], (out, out...  7.09 us
    pallas_call x4, Pallas kernels, final(): call(functools.partial(final_kernel, blocks_count, places, buffered), 'fi...  5.41 us
    pallas_call x5, Pallas kernels, push(): call(functools.partial(push_kernel, first, mine, begin, offset, size), 'p...  2.71 us
    pallas_call x1, Pallas kernels, store_x(): call(store_kernel, 'store_x', [SMEM] + [VMEM] * len(args), pltpu.HBM((tas...  1.58 us
  transfers between devices with their start and end apart: 18, of which 11 were waited for; matrix products, arithmetic and copies ran while one was open for 1% of the time, Pallas kernels for 27%

profile of v17, /device:TPU:0, one launch (start us, length us, event | category | flops | bytes accessed | tf_op | source)
XLA Modules:
  0.0 59.7 jit_solution(8929136599754688738)
XLA Ops:
  0.6 7.9 %load_and_margins.1 = (bf16[64,768]{1,0:T(8,128)(2,1)S(1)}, f32[64,768]{1,0:T(8,128)S(1)}, bf16[768,8192]{1,0:T(8,128)(2,1)S(1)}, f32[64,8192]{1,0:T(8,128)S(1)}...) custom-call(s32[1]{0:T(128)} %bitcast.side.token, ...), custom_call_target="tpu_custom_call" | custom-call | flops 1000 | bytes 1000 | tf_op jit(solution)/shard_map/load_and_margins/pallas_call | solution.py:150
  9.1 2.6 %collective-permute-start = (bf16[64,768]{1,0:T(8,128)(2,1)S(1)}, bf16[64,768]{1,0:T(8,128)(2,1)S(1)}, u32[]{:S(2)}, u32[]{:S(2)}) collective-permute-start(bf16[64,768]{1,0:T(8,128)(2,1)S(1)} %get-tuple-element.61), channel_id=1, source_target_pairs={{0,1},{1,0},{2,3},{3,2},{4,5},{5,4},{6,7},{7,6},{8,9},{9,8},{10,11... | collective-permute-start | bytes 294920 | tf_op jit(solution)/shard_map/ppermute | solution.py:29
  11.6 1.3 %gram.3 = (bf16[256,256]{1,0:T(8,128)(2,1)S(1)}, bf16[256,256]{1,0:T(8,128)(2,1)S(1)}) custom-call(s32[1]{0:T(128)} %bitcast.side.token, bf16[768,8192]{1,0:T(8,128)(2,1)S(1)} %get-tuple-element.58.a_ref.refs_1_), custom_call_target="tpu_custom_call" | custom-call | flops 1000 | bytes 3333333 | tf_op jit(solution)/shard_map/gram/pallas_call | solution.py:189
  13.1 1.6 %collective-permute-start.8 = (f32[64,4096]{1,0:T(8,128)S(1)}, f32[64,4096]{1,0:T(8,128)S(1)}, u32[]{:S(2)}, u32[]{:S(2)}) collective-permute-start(f32[64,4096]{1,0:T(8,128)S(1)} %add.30), channel_id=1, source_target_pairs={{0,16},{8,24},{16,0},{24,8},{1,17},{9,25},{17,1},{25,9},{2,18},{10... | collective-permute-start | bytes 3145736 | tf_op jit(solution)/shard_map/ppermute | solution.py:29
  15.1 1.9 %collective-permute-start.2 = (bf16[64,768]{1,0:T(8,128)(2,1)S(1)}, bf16[64,768]{1,0:T(8,128)(2,1)S(1)}, u32[]{:S(2)}, u32[]{:S(2)}) collective-permute-start(bf16[64,768]{1,0:T(8,128)(2,1)S(1)} %add_convert_fusion.5), channel_id=1, source_target_pairs={{0,2},{1,3},{2,0},{3,1},{4,6},{5,7},{6,4},{7,5},{8,10},{9,11},{10,... | collective-permute-start | bytes 294920 | tf_op jit(solution)/shard_map/ppermute | solution.py:29
  16.9 2.4 %gram.4 = (bf16[256,512]{1,0:T(8,128)(2,1)S(1)}, bf16[256,512]{1,0:T(8,128)(2,1)S(1)}) custom-call(s32[1]{0:T(128)} %bitcast.side.token, bf16[768,8192]{1,0:T(8,128)(2,1)S(1)} %get-tuple-element.58.a_ref.refs_1_), custom_call_target="tpu_custom_call" | custom-call | flops 1000 | bytes 6666666 | tf_op jit(solution)/shard_map/gram/pallas_call | solution.py:189
  19.8 2.9 %collective-permute-start.3 = (bf16[64,768]{1,0:T(8,128)(2,1)S(1)}, bf16[64,768]{1,0:T(8,128)(2,1)S(1)}, u32[]{:S(2)}, u32[]{:S(2)}) collective-permute-start(bf16[64,768]{1,0:T(8,128)(2,1)S(1)} %add_convert_fusion.4.refs_6_), channel_id=1, source_target_pairs={{0,4},{1,5},{2,6},{3,7},{4,0},{5,1},{6,2},{7,3},{8,12},{9,13},{10,... | collective-permute-start | bytes 294920 | tf_op jit(solution)/shard_map/ppermute | solution.py:29
  22.7 3.5 %gram.5 = (bf16[256,768]{1,0:T(8,128)(2,1)S(1)}, bf16[256,768]{1,0:T(8,128)(2,1)S(1)}) custom-call(s32[1]{0:T(128)} %bitcast.side.token, bf16[768,8192]{1,0:T(8,128)(2,1)S(1)} %get-tuple-element.58.a_ref.refs_1_), custom_call_target="tpu_custom_call" | custom-call | flops 1000 | bytes 10000000 | tf_op jit(solution)/shard_map/gram/pallas_call | solution.py:189
  26.8 2.6 %collective-permute-start.6 = (bf16[64,768]{1,0:T(8,128)(2,1)S(1)}, bf16[64,768]{1,0:T(8,128)(2,1)S(1)}, u32[]{:S(2)}, u32[]{:S(2)}) collective-permute-start(bf16[64,768]{1,0:T(8,128)(2,1)S(1)} %get-tuple-element.76), channel_id=1, source_target_pairs={{0,3},{1,2},{2,1},{3,0},{4,7},{5,6},{6,5},{7,4},{8,11},{9,10},{10,... | collective-permute-start | bytes 294920 | tf_op jit(solution)/shard_map/ppermute | solution.py:29
  30.3 2.1 %collective-permute-done.6 = bf16[64,768]{1,0:T(8,128)(2,1)S(1)} collective-permute-done((bf16[64,768]{1,0:T(8,128)(2,1)S(1)}, bf16[64,768]{1,0:T(8,128)(2,1)S(1)}, u32[]{:S(2)}, u32[]{:S(2)}) %collective-permute-start.6) | collective-permute-done | bytes 98336 | tf_op jit(solution)/shard_map/ppermute | solution.py:29
  32.5 1.5 %collective-permute-done.5 = bf16[64,768]{1,0:T(8,128)(2,1)S(1)} collective-permute-done((bf16[64,768]{1,0:T(8,128)(2,1)S(1)}, bf16[64,768]{1,0:T(8,128)(2,1)S(1)}, u32[]{:S(2)}, u32[]{:S(2)}) %collective-permute-start.5) | collective-permute-done | bytes 98336 | tf_op jit(solution)/shard_map/ppermute | solution.py:29
  34.5 2.6 %collective-permute-start.7 = (bf16[64,768]{1,0:T(8,128)(2,1)S(1)}, bf16[64,768]{1,0:T(8,128)(2,1)S(1)}, u32[]{:S(2)}, u32[]{:S(2)}) collective-permute-start(bf16[64,768]{1,0:T(8,128)(2,1)S(1)} %add_convert_fusion.3.refs_4_), channel_id=1, source_target_pairs={{0,4},{1,5},{2,6},{3,7},{4,0},{5,1},{6,2},{7,3},{8,12},{9,13},{10,... | collective-permute-start | bytes 294920 | tf_op jit(solution)/shard_map/ppermute | solution.py:29
  37.1 1.3 %collective-permute-done.8 = f32[64,4096]{1,0:T(8,128)S(1)} collective-permute-done((f32[64,4096]{1,0:T(8,128)S(1)}, f32[64,4096]{1,0:T(8,128)S(1)}, u32[]{:S(2)}, u32[]{:S(2)}) %collective-permute-start.8) | collective-permute-done | bytes 1048608 | tf_op jit(solution)/shard_map/ppermute | solution.py:29
  38.5 1.6 %collective-permute-done.7.refs_5_ = bf16[64,768]{1,0:T(8,128)(2,1)S(1)} collective-permute-done((bf16[64,768]{1,0:T(8,128)(2,1)S(1)}, bf16[64,768]{1,0:T(8,128)(2,1)S(1)}, u32[]{:S(2)}, u32[]{:S(2)}) %collective-permute-start.7) | collective-permute-done | bytes 98336 | tf_op jit(solution)/shard_map/ppermute | solution.py:29
  40.7 0.7 %push_other.3 = (f32[64,2560]{1,0:T(8,128)S(1)}, bf16[64,2560]{1,0:T(8,128)(2,1)S(1)}) custom-call(s32[1]{0:T(128)} %bitcast.side.token, f32[64,128]{1,0:T(8,128)S(1)} %get-tuple-element.54.scale.refs_0_, bf16[768,8192]{1,0:T(8,128)(2,1)S(1)} %get-tuple-element.58.a_ref.refs_1_, bf16[128,768]{1,0:T(8,128)(2,1)S(1)} %get-tuple-element.79.refs_2_), custom_call_target="tpu_custom_call" | custom-call | flops 1000 | bytes 1000 | tf_op jit(solution)/shard_map/push_other/pallas_call | solution.py:265
  42.6 1.6 %collective-permute-start.13 = (bf16[64,1536]{1,0:T(8,128)(2,1)S(1)}, bf16[64,1536]{1,0:T(8,128)(2,1)S(1)}, u32[]{:S(2)}, u32[]{:S(2)}) collective-permute-start(bf16[64,1536]{1,0:T(8,128)(2,1)S(1)} %get-tuple-element.84), channel_id=1, source_target_pairs={{0,16},{8,24},{16,0},{24,8},{1,17},{9,25},{17,1},{25,9},{2,18},{10... | collective-permute-start | bytes 589832 | tf_op jit(solution)/shard_map/ppermute | solution.py:29
  45.8 1.6 %collective-permute-start.12 = (bf16[64,1024]{1,0:T(8,128)(2,1)S(1)}, bf16[64,1024]{1,0:T(8,128)(2,1)S(1)}, u32[]{:S(2)}, u32[]{:S(2)}) collective-permute-start(bf16[64,1024]{1,0:T(8,128)(2,1)S(1)} %get-tuple-element.93), channel_id=1, source_target_pairs={{0,16},{8,24},{16,0},{24,8},{1,17},{9,25},{17,1},{25,9},{2,18},{10... | collective-permute-start | bytes 393224 | tf_op jit(solution)/shard_map/ppermute | solution.py:29
  47.3 1.6 %store_x.1 = f32[64,8192]{1,0:T(8,128)} custom-call(s32[1]{0:T(128)} %bitcast.side.token, f32[64,128]{1,0:T(8,128)S(1)} %get-tuple-element.54.scale.refs_0_, f32[64,8192]{1,0:T(8,128)S(1)} %get-tuple-element.55.x_ref, f32[64,8192]{1,0:T(8,128)S(1)} %get-tuple-element.56.u_ref, f32[64,8192]{1,0:T(8,128)S(1)} %get-tuple-element.57.z_ref, ...), custom_call_target="tpu_custom_call" | custom-call | flops 1000 | bytes 1000 | tf_op jit(solution)/shard_map/store_x/pallas_call | solution.py:299
  48.9 1.6 %collective-permute-done.13 = bf16[64,1536]{1,0:T(8,128)(2,1)S(1)} collective-permute-done((bf16[64,1536]{1,0:T(8,128)(2,1)S(1)}, bf16[64,1536]{1,0:T(8,128)(2,1)S(1)}, u32[]{:S(2)}, u32[]{:S(2)}) %collective-permute-start.13) | collective-permute-done | bytes 196640 | tf_op jit(solution)/shard_map/ppermute | solution.py:29
  50.6 1.2 %final.4 = (f32[64,8192]{1,0:T(8,128)}, f32[64,8192]{1,0:T(8,128)}) custom-call(s32[1]{0:T(128)} %bitcast.side.token, f32[64,128]{1,0:T(8,128)S(1)} %get-tuple-element.54.scale.refs_0_, f32[64,8192]{1,0:T(8,128)S(1)} %get-tuple-element.55.x_ref, f32[64,8192]{1,0:T(8,128)S(1)} %get-tuple-element.56.u_ref, f32[64,8192]{1,0:T(8,128)S(1)} %get-tuple-element.57.z_ref, ...), custom_call_target="tpu_custom_call" | custom-call | flops 1000 | bytes 1000 | tf_op jit(solution)/shard_map/final/pallas_call | solution.py:349
  51.8 2.9 %collective-permute-done.15 = bf16[64,1536]{1,0:T(8,128)(2,1)S(1)} collective-permute-done((bf16[64,1536]{1,0:T(8,128)(2,1)S(1)}, bf16[64,1536]{1,0:T(8,128)(2,1)S(1)}, u32[]{:S(2)}, u32[]{:S(2)}) %collective-permute-start.15) | collective-permute-done | bytes 196640 | tf_op jit(solution)/shard_map/ppermute | solution.py:29
  54.8 1.7 %final.5 = (f32[64,8192]{1,0:T(8,128)}, f32[64,8192]{1,0:T(8,128)}) custom-call(s32[1]{0:T(128)} %bitcast.side.token, f32[64,128]{1,0:T(8,128)S(1)} %get-tuple-element.54.scale.refs_0_, f32[64,8192]{1,0:T(8,128)S(1)} %get-tuple-element.55.x_ref, f32[64,8192]{1,0:T(8,128)S(1)} %get-tuple-element.56.u_ref, ...), custom_call_target="tpu_custom_call", output_to_operand_aliasing={{0}: (11, {}), {1}: (12, {})} | custom-call | flops 1000 | bytes 1000 | tf_op jit(solution)/shard_map/final/pallas_call | solution.py:349
  57.1 1.5 %final.6 = (f32[64,8192]{1,0:T(8,128)}, f32[64,8192]{1,0:T(8,128)}) custom-call(s32[1]{0:T(128)} %bitcast.side.token, f32[64,128]{1,0:T(8,128)S(1)} %get-tuple-element.54.scale.refs_0_, f32[64,8192]{1,0:T(8,128)S(1)} %get-tuple-element.55.x_ref, f32[64,8192]{1,0:T(8,128)S(1)} %get-tuple-element.56.u_ref, ...), custom_call_target="tpu_custom_call", output_to_operand_aliasing={{0}: (11, {}), {1}: (12, {})} | custom-call | flops 1000 | bytes 1000 | tf_op jit(solution)/shard_map/final/pallas_call | solution.py:349
  58.7 1.0 %final.7 = (f32[64,8192]{1,0:T(8,128)}, f32[64,8192]{1,0:T(8,128)}) custom-call(s32[1]{0:T(128)} %bitcast.side.token, f32[64,128]{1,0:T(8,128)S(1)} %get-tuple-element.54.scale.refs_0_, f32[64,8192]{1,0:T(8,128)S(1)} %get-tuple-element.55.x_ref, f32[64,8192]{1,0:T(8,128)S(1)} %get-tuple-element.56.u_ref, ...), custom_call_target="tpu_custom_call", output_to_operand_aliasing={{0}: (8, {}), {1}: (9, {})} | custom-call | flops 1000 | bytes 1000 | tf_op jit(solution)/shard_map/final/pallas_call | solution.py:349
  (35 shorter events, 7.9 us)
Async XLA Ops:
  8.5 4.4 %collective-permute-start.1 = (f32[64,4096]{1,0:T(8,128)S(1)}, f32[64,4096]{1,0:T(8,128)S(1)}, u32[]{:S(2)}, u32[]{:S(2)}) collective-permute-start(f32[64,4096]{1,0:T(8,128)S(1)} %get-tuple-element.66), channel_id=1, source_target_pairs={{0,8},{8,0},{16,24},{24,16},{1,9},{9,1},{17,25},{25,17},{2,10},{10... | collective-permute-start | bytes 3145736 | tf_op jit(solution)/shard_map/ppermute | solution.py:29
  9.1 6.0 %collective-permute-start = (bf16[64,768]{1,0:T(8,128)(2,1)S(1)}, bf16[64,768]{1,0:T(8,128)(2,1)S(1)}, u32[]{:S(2)}, u32[]{:S(2)}) collective-permute-start(bf16[64,768]{1,0:T(8,128)(2,1)S(1)} %get-tuple-element.61), channel_id=1, source_target_pairs={{0,1},{1,0},{2,3},{3,2},{4,5},{5,4},{6,7},{7,6},{8,9},{9,8},{10,11... | collective-permute-start | bytes 294920 | tf_op jit(solution)/shard_map/ppermute | solution.py:29
  13.1 25.3 %collective-permute-start.8 = (f32[64,4096]{1,0:T(8,128)S(1)}, f32[64,4096]{1,0:T(8,128)S(1)}, u32[]{:S(2)}, u32[]{:S(2)}) collective-permute-start(f32[64,4096]{1,0:T(8,128)S(1)} %add.30), channel_id=1, source_target_pairs={{0,16},{8,24},{16,0},{24,8},{1,17},{9,25},{17,1},{25,9},{2,18},{10... | collective-permute-start | bytes 3145736 | tf_op jit(solution)/shard_map/ppermute | solution.py:29
  15.1 4.7 %collective-permute-start.2 = (bf16[64,768]{1,0:T(8,128)(2,1)S(1)}, bf16[64,768]{1,0:T(8,128)(2,1)S(1)}, u32[]{:S(2)}, u32[]{:S(2)}) collective-permute-start(bf16[64,768]{1,0:T(8,128)(2,1)S(1)} %add_convert_fusion.5), channel_id=1, source_target_pairs={{0,2},{1,3},{2,0},{3,1},{4,6},{5,7},{6,4},{7,5},{8,10},{9,11},{10,... | collective-permute-start | bytes 294920 | tf_op jit(solution)/shard_map/ppermute | solution.py:29
  19.8 6.4 %collective-permute-start.3 = (bf16[64,768]{1,0:T(8,128)(2,1)S(1)}, bf16[64,768]{1,0:T(8,128)(2,1)S(1)}, u32[]{:S(2)}, u32[]{:S(2)}) collective-permute-start(bf16[64,768]{1,0:T(8,128)(2,1)S(1)} %add_convert_fusion.4.refs_6_), channel_id=1, source_target_pairs={{0,4},{1,5},{2,6},{3,7},{4,0},{5,1},{6,2},{7,3},{8,12},{9,13},{10,... | collective-permute-start | bytes 294920 | tf_op jit(solution)/shard_map/ppermute | solution.py:29
  26.8 5.7 %collective-permute-start.6 = (bf16[64,768]{1,0:T(8,128)(2,1)S(1)}, bf16[64,768]{1,0:T(8,128)(2,1)S(1)}, u32[]{:S(2)}, u32[]{:S(2)}) collective-permute-start(bf16[64,768]{1,0:T(8,128)(2,1)S(1)} %get-tuple-element.76), channel_id=1, source_target_pairs={{0,3},{1,2},{2,1},{3,0},{4,7},{5,6},{6,5},{7,4},{8,11},{9,10},{10,... | collective-permute-start | bytes 294920 | tf_op jit(solution)/shard_map/ppermute | solution.py:29
  29.4 4.6 %collective-permute-start.5 = (bf16[64,768]{1,0:T(8,128)(2,1)S(1)}, bf16[64,768]{1,0:T(8,128)(2,1)S(1)}, u32[]{:S(2)}, u32[]{:S(2)}) collective-permute-start(bf16[64,768]{1,0:T(8,128)(2,1)S(1)} %get-tuple-element.76), channel_id=1, source_target_pairs={{0,2},{1,3},{2,0},{3,1},{4,6},{5,7},{6,4},{7,5},{8,10},{9,11},{10,... | collective-permute-start | bytes 294920 | tf_op jit(solution)/shard_map/ppermute | solution.py:29
  29.8 4.6 %collective-permute-start.4 = (bf16[64,768]{1,0:T(8,128)(2,1)S(1)}, bf16[64,768]{1,0:T(8,128)(2,1)S(1)}, u32[]{:S(2)}, u32[]{:S(2)}) collective-permute-start(bf16[64,768]{1,0:T(8,128)(2,1)S(1)} %get-tuple-element.76), channel_id=1, source_target_pairs={{0,1},{1,0},{2,3},{3,2},{4,5},{5,4},{6,7},{7,6},{8,9},{9,8},{10,11... | collective-permute-start | bytes 294920 | tf_op jit(solution)/shard_map/ppermute | solution.py:29
  34.5 5.6 %collective-permute-start.7 = (bf16[64,768]{1,0:T(8,128)(2,1)S(1)}, bf16[64,768]{1,0:T(8,128)(2,1)S(1)}, u32[]{:S(2)}, u32[]{:S(2)}) collective-permute-start(bf16[64,768]{1,0:T(8,128)(2,1)S(1)} %add_convert_fusion.3.refs_4_), channel_id=1, source_target_pairs={{0,4},{1,5},{2,6},{3,7},{4,0},{5,1},{6,2},{7,3},{8,12},{9,13},{10,... | collective-permute-start | bytes 294920 | tf_op jit(solution)/shard_map/ppermute | solution.py:29
  40.6 1.5 %collective-permute-start.9 = (bf16[64,1536]{1,0:T(8,128)(2,1)S(1)}, bf16[64,1536]{1,0:T(8,128)(2,1)S(1)}, u32[]{:S(2)}, u32[]{:S(2)}) collective-permute-start(bf16[64,1536]{1,0:T(8,128)(2,1)S(1)} %get-tuple-element.82), channel_id=1, source_target_pairs={{0,8},{8,0},{16,24},{24,16},{1,9},{9,1},{17,25},{25,17},{2,10},{10... | collective-permute-start | bytes 589832 | tf_op jit(solution)/shard_map/ppermute | solution.py:29
  41.4 2.8 %collective-permute-start.10 = (bf16[64,2560]{1,0:T(8,128)(2,1)S(1)}, bf16[64,2560]{1,0:T(8,128)(2,1)S(1)}, u32[]{:S(2)}, u32[]{:S(2)}) collective-permute-start(bf16[64,2560]{1,0:T(8,128)(2,1)S(1)} %get-tuple-element.86), channel_id=1, source_target_pairs={{0,8},{8,0},{16,24},{24,16},{1,9},{9,1},{17,25},{25,17},{2,10},{10... | collective-permute-start | bytes 983048 | tf_op jit(solution)/shard_map/ppermute | solution.py:29
  42.6 7.8 %collective-permute-start.13 = (bf16[64,1536]{1,0:T(8,128)(2,1)S(1)}, bf16[64,1536]{1,0:T(8,128)(2,1)S(1)}, u32[]{:S(2)}, u32[]{:S(2)}) collective-permute-start(bf16[64,1536]{1,0:T(8,128)(2,1)S(1)} %get-tuple-element.84), channel_id=1, source_target_pairs={{0,16},{8,24},{16,0},{24,8},{1,17},{9,25},{17,1},{25,9},{2,18},{10... | collective-permute-start | bytes 589832 | tf_op jit(solution)/shard_map/ppermute | solution.py:29
  44.2 10.6 %collective-permute-start.11 = (f32[64,4096]{1,0:T(8,128)S(1)}, f32[64,4096]{1,0:T(8,128)S(1)}, u32[]{:S(2)}, u32[]{:S(2)}) collective-permute-start(f32[64,4096]{1,0:T(8,128)S(1)} %add.36.refs_0_.refs_3_), channel_id=1, source_target_pairs={{0,8},{8,0},{16,24},{24,16},{1,9},{9,1},{17,25},{25,17},{2,10},{10... | collective-permute-start | bytes 3145736 | tf_op jit(solution)/shard_map/ppermute | solution.py:29
  44.7 9.9 %collective-permute-start.15 = (bf16[64,1536]{1,0:T(8,128)(2,1)S(1)}, bf16[64,1536]{1,0:T(8,128)(2,1)S(1)}, u32[]{:S(2)}, u32[]{:S(2)}) collective-permute-start(bf16[64,1536]{1,0:T(8,128)(2,1)S(1)} %get-tuple-element.88), channel_id=1, source_target_pairs={{0,16},{8,24},{16,0},{24,8},{1,17},{9,25},{17,1},{25,9},{2,18},{10... | collective-permute-start | bytes 589832 | tf_op jit(solution)/shard_map/ppermute | solution.py:29
  45.8 10.9 %collective-permute-start.12 = (bf16[64,1024]{1,0:T(8,128)(2,1)S(1)}, bf16[64,1024]{1,0:T(8,128)(2,1)S(1)}, u32[]{:S(2)}, u32[]{:S(2)}) collective-permute-start(bf16[64,1024]{1,0:T(8,128)(2,1)S(1)} %get-tuple-element.93), channel_id=1, source_target_pairs={{0,16},{8,24},{16,0},{24,8},{1,17},{9,25},{17,1},{25,9},{2,18},{10... | collective-permute-start | bytes 393224 | tf_op jit(solution)/shard_map/ppermute | solution.py:29
  50.5 4.3 %collective-permute-start.14 = (bf16[64,1536]{1,0:T(8,128)(2,1)S(1)}, bf16[64,1536]{1,0:T(8,128)(2,1)S(1)}, u32[]{:S(2)}, u32[]{:S(2)}) collective-permute-start(bf16[64,1536]{1,0:T(8,128)(2,1)S(1)} %add_convert_fusion.1.refs_2_), channel_id=1, source_target_pairs={{0,8},{8,0},{16,24},{24,16},{1,9},{9,1},{17,25},{25,17},{2,10},{10... | collective-permute-start | bytes 589832 | tf_op jit(solution)/shard_map/ppermute | solution.py:29
  54.7 2.4 %collective-permute-start.17 = (bf16[64,1536]{1,0:T(8,128)(2,1)S(1)}, bf16[64,1536]{1,0:T(8,128)(2,1)S(1)}, u32[]{:S(2)}, u32[]{:S(2)}) collective-permute-start(bf16[64,1536]{1,0:T(8,128)(2,1)S(1)} %add_convert_fusion.refs_5_), channel_id=1, source_target_pairs={{0,8},{8,0},{16,24},{24,16},{1,9},{9,1},{17,25},{25,17},{2,10},{10... | collective-permute-start | bytes 589832 | tf_op jit(solution)/shard_map/ppermute | solution.py:29
  56.7 1.9 %collective-permute-start.16 = (bf16[64,1024]{1,0:T(8,128)(2,1)S(1)}, bf16[64,1024]{1,0:T(8,128)(2,1)S(1)}, u32[]{:S(2)}, u32[]{:S(2)}) collective-permute-start(bf16[64,1024]{1,0:T(8,128)(2,1)S(1)} %add_convert_fusion.2.refs_5_), channel_id=1, source_target_pairs={{0,8},{8,0},{16,24},{24,16},{1,9},{9,1},{17,25},{25,17},{2,10},{10... | collective-permute-start | bytes 393224 | tf_op jit(solution)/shard_map/ppermute | solution.py:29

commit v18 on v17

--- a/solution.py
+++ b/solution.py
@@ -13,7 +13,7 @@
 PLAN = ((((True, 0),),), (((False, 0), (True, 1)),), (((False, 1), (True, 2)), ((False, 2),)))
 MINE = (3, 3, 2)
 OTHER = (3, 5)
-STEP = 1024
+STEP = 512
 WIDE = 2048
 AHEAD = 8
 NARROW = 256

time: 59.8 us -> 60.9 us (1.018)
  Pallas kernels: 25.3 us -> 26.3 us
    pallas_call x1, Pallas kernels: 7.89 us -> 8.92 us  [load(): call(functools.partial(load_kernel, blocks_count), 'load_and_margins', [S...]
  transfers between devices with their start and end apart: 18 -> 18, of which waited for: 11 -> 11; matrix products, arithmetic and copies ran while one was open for 1% -> 1% of each run, Pallas kernels for 27% -> 26%
where the time goes in v18:
time: 60.9 us; the launch traced here: 60.7 us
  Pallas kernels  26.3 us (43%)
  starting transfers between devices  20.5 us (34%)
  waiting for transfers between devices  12.6 us (21%)
  between operations  0.85 us (1%)
    ppermute x18, starting transfers between devices, exchange(): return lax.ppermute(value, axis, [(i, i ^ mask) for i in range(n)])  20.5 us
    ppermute x18, waiting for transfers between devices, exchange(): return lax.ppermute(value, axis, [(i, i ^ mask) for i in range(n)])  12.6 us
    pallas_call x1, Pallas kernels, load(): call(functools.partial(load_kernel, blocks_count), 'load_and_margins', [S...  8.92 us
    pallas_call x3, Pallas kernels, gram_row(): call(functools.partial(gram_kernel, row), 'gram', [SMEM, VMEM], (out, out...  7.1 us
    pallas_call x4, Pallas kernels, final(): call(functools.partial(final_kernel, blocks_count, places, buffered), 'fi...  5.41 us
    pallas_call x5, Pallas kernels, push(): call(functools.partial(push_kernel, first, mine, begin, offset, size), 'p...  2.71 us
    pallas_call x1, Pallas kernels, store_x(): call(store_kernel, 'store_x', [SMEM] + [VMEM] * len(args), pltpu.HBM((tas...  1.58 us
  transfers between devices with their start and end apart: 18, of which 11 were waited for; matrix products, arithmetic and copies ran while one was open for 1% of the time, Pallas kernels for 26%

profile of v18, /device:TPU:0, one launch (start us, length us, event | category | flops | bytes accessed | tf_op | source)
XLA Modules:
  0.0 60.7 jit_solution(5832412748095941033)
XLA Ops:
  0.6 8.9 %load_and_margins.1 = (bf16[64,768]{1,0:T(8,128)(2,1)S(1)}, f32[64,768]{1,0:T(8,128)S(1)}, bf16[768,8192]{1,0:T(8,128)(2,1)S(1)}, f32[64,8192]{1,0:T(8,128)S(1)}...) custom-call(s32[1]{0:T(128)} %bitcast.side.token, ...), custom_call_target="tpu_custom_call" | custom-call | flops 1000 | bytes 1000 | tf_op jit(solution)/shard_map/load_and_margins/pallas_call | solution.py:150
  10.1 2.6 %collective-permute-start = (bf16[64,768]{1,0:T(8,128)(2,1)S(1)}, bf16[64,768]{1,0:T(8,128)(2,1)S(1)}, u32[]{:S(2)}, u32[]{:S(2)}) collective-permute-start(bf16[64,768]{1,0:T(8,128)(2,1)S(1)} %get-tuple-element.61), channel_id=1, source_target_pairs={{0,1},{1,0},{2,3},{3,2},{4,5},{5,4},{6,7},{7,6},{8,9},{9,8},{10,11... | collective-permute-start | bytes 294920 | tf_op jit(solution)/shard_map/ppermute | solution.py:29
  12.7 1.3 %gram.3 = (bf16[256,256]{1,0:T(8,128)(2,1)S(1)}, bf16[256,256]{1,0:T(8,128)(2,1)S(1)}) custom-call(s32[1]{0:T(128)} %bitcast.side.token, bf16[768,8192]{1,0:T(8,128)(2,1)S(1)} %get-tuple-element.58.a_ref.refs_1_), custom_call_target="tpu_custom_call" | custom-call | flops 1000 | bytes 3333333 | tf_op jit(solution)/shard_map/gram/pallas_call | solution.py:189
  14.1 1.6 %collective-permute-start.8 = (f32[64,4096]{1,0:T(8,128)S(1)}, f32[64,4096]{1,0:T(8,128)S(1)}, u32[]{:S(2)}, u32[]{:S(2)}) collective-permute-start(f32[64,4096]{1,0:T(8,128)S(1)} %add.30), channel_id=1, source_target_pairs={{0,16},{8,24},{16,0},{24,8},{1,17},{9,25},{17,1},{25,9},{2,18},{10... | collective-permute-start | bytes 3145736 | tf_op jit(solution)/shard_map/ppermute | solution.py:29
  16.1 1.9 %collective-permute-start.2 = (bf16[64,768]{1,0:T(8,128)(2,1)S(1)}, bf16[64,768]{1,0:T(8,128)(2,1)S(1)}, u32[]{:S(2)}, u32[]{:S(2)}) collective-permute-start(bf16[64,768]{1,0:T(8,128)(2,1)S(1)} %add_convert_fusion.5), channel_id=1, source_target_pairs={{0,2},{1,3},{2,0},{3,1},{4,6},{5,7},{6,4},{7,5},{8,10},{9,11},{10,... | collective-permute-start | bytes 294920 | tf_op jit(solution)/shard_map/ppermute | solution.py:29
  18.0 2.4 %gram.4 = (bf16[256,512]{1,0:T(8,128)(2,1)S(1)}, bf16[256,512]{1,0:T(8,128)(2,1)S(1)}) custom-call(s32[1]{0:T(128)} %bitcast.side.token, bf16[768,8192]{1,0:T(8,128)(2,1)S(1)} %get-tuple-element.58.a_ref.refs_1_), custom_call_target="tpu_custom_call" | custom-call | flops 1000 | bytes 6666666 | tf_op jit(solution)/shard_map/gram/pallas_call | solution.py:189
  20.8 2.9 %collective-permute-start.3 = (bf16[64,768]{1,0:T(8,128)(2,1)S(1)}, bf16[64,768]{1,0:T(8,128)(2,1)S(1)}, u32[]{:S(2)}, u32[]{:S(2)}) collective-permute-start(bf16[64,768]{1,0:T(8,128)(2,1)S(1)} %add_convert_fusion.4.refs_6_), channel_id=1, source_target_pairs={{0,4},{1,5},{2,6},{3,7},{4,0},{5,1},{6,2},{7,3},{8,12},{9,13},{10,... | collective-permute-start | bytes 294920 | tf_op jit(solution)/shard_map/ppermute | solution.py:29
  23.7 3.5 %gram.5 = (bf16[256,768]{1,0:T(8,128)(2,1)S(1)}, bf16[256,768]{1,0:T(8,128)(2,1)S(1)}) custom-call(s32[1]{0:T(128)} %bitcast.side.token, bf16[768,8192]{1,0:T(8,128)(2,1)S(1)} %get-tuple-element.58.a_ref.refs_1_), custom_call_target="tpu_custom_call" | custom-call | flops 1000 | bytes 10000000 | tf_op jit(solution)/shard_map/gram/pallas_call | solution.py:189
  27.8 2.6 %collective-permute-start.6 = (bf16[64,768]{1,0:T(8,128)(2,1)S(1)}, bf16[64,768]{1,0:T(8,128)(2,1)S(1)}, u32[]{:S(2)}, u32[]{:S(2)}) collective-permute-start(bf16[64,768]{1,0:T(8,128)(2,1)S(1)} %get-tuple-element.76), channel_id=1, source_target_pairs={{0,3},{1,2},{2,1},{3,0},{4,7},{5,6},{6,5},{7,4},{8,11},{9,10},{10,... | collective-permute-start | bytes 294920 | tf_op jit(solution)/shard_map/ppermute | solution.py:29
  31.4 2.1 %collective-permute-done.6 = bf16[64,768]{1,0:T(8,128)(2,1)S(1)} collective-permute-done((bf16[64,768]{1,0:T(8,128)(2,1)S(1)}, bf16[64,768]{1,0:T(8,128)(2,1)S(1)}, u32[]{:S(2)}, u32[]{:S(2)}) %collective-permute-start.6) | collective-permute-done | bytes 98336 | tf_op jit(solution)/shard_map/ppermute | solution.py:29
  33.5 1.5 %collective-permute-done.5 = bf16[64,768]{1,0:T(8,128)(2,1)S(1)} collective-permute-done((bf16[64,768]{1,0:T(8,128)(2,1)S(1)}, bf16[64,768]{1,0:T(8,128)(2,1)S(1)}, u32[]{:S(2)}, u32[]{:S(2)}) %collective-permute-start.5) | collective-permute-done | bytes 98336 | tf_op jit(solution)/shard_map/ppermute | solution.py:29
  35.5 2.6 %collective-permute-start.7 = (bf16[64,768]{1,0:T(8,128)(2,1)S(1)}, bf16[64,768]{1,0:T(8,128)(2,1)S(1)}, u32[]{:S(2)}, u32[]{:S(2)}) collective-permute-start(bf16[64,768]{1,0:T(8,128)(2,1)S(1)} %add_convert_fusion.3.refs_4_), channel_id=1, source_target_pairs={{0,4},{1,5},{2,6},{3,7},{4,0},{5,1},{6,2},{7,3},{8,12},{9,13},{10,... | collective-permute-start | bytes 294920 | tf_op jit(solution)/shard_map/ppermute | solution.py:29
  38.1 1.3 %collective-permute-done.8 = f32[64,4096]{1,0:T(8,128)S(1)} collective-permute-done((f32[64,4096]{1,0:T(8,128)S(1)}, f32[64,4096]{1,0:T(8,128)S(1)}, u32[]{:S(2)}, u32[]{:S(2)}) %collective-permute-start.8) | collective-permute-done | bytes 1048608 | tf_op jit(solution)/shard_map/ppermute | solution.py:29
  39.5 1.6 %collective-permute-done.7.refs_5_ = bf16[64,768]{1,0:T(8,128)(2,1)S(1)} collective-permute-done((bf16[64,768]{1,0:T(8,128)(2,1)S(1)}, bf16[64,768]{1,0:T(8,128)(2,1)S(1)}, u32[]{:S(2)}, u32[]{:S(2)}) %collective-permute-start.7) | collective-permute-done | bytes 98336 | tf_op jit(solution)/shard_map/ppermute | solution.py:29
  41.7 0.7 %push_other.3 = (f32[64,2560]{1,0:T(8,128)S(1)}, bf16[64,2560]{1,0:T(8,128)(2,1)S(1)}) custom-call(s32[1]{0:T(128)} %bitcast.side.token, f32[64,128]{1,0:T(8,128)S(1)} %get-tuple-element.54.scale.refs_0_, bf16[768,8192]{1,0:T(8,128)(2,1)S(1)} %get-tuple-element.58.a_ref.refs_1_, bf16[128,768]{1,0:T(8,128)(2,1)S(1)} %get-tuple-element.79.refs_2_), custom_call_target="tpu_custom_call" | custom-call | flops 1000 | bytes 1000 | tf_op jit(solution)/shard_map/push_other/pallas_call | solution.py:265
  43.7 1.6 %collective-permute-start.13 = (bf16[64,1536]{1,0:T(8,128)(2,1)S(1)}, bf16[64,1536]{1,0:T(8,128)(2,1)S(1)}, u32[]{:S(2)}, u32[]{:S(2)}) collective-permute-start(bf16[64,1536]{1,0:T(8,128)(2,1)S(1)} %get-tuple-element.84), channel_id=1, source_target_pairs={{0,16},{8,24},{16,0},{24,8},{1,17},{9,25},{17,1},{25,9},{2,18},{10... | collective-permute-start | bytes 589832 | tf_op jit(solution)/shard_map/ppermute | solution.py:29
  46.8 1.6 %collective-permute-start.12 = (bf16[64,1024]{1,0:T(8,128)(2,1)S(1)}, bf16[64,1024]{1,0:T(8,128)(2,1)S(1)}, u32[]{:S(2)}, u32[]{:S(2)}) collective-permute-start(bf16[64,1024]{1,0:T(8,128)(2,1)S(1)} %get-tuple-element.93), channel_id=1, source_target_pairs={{0,16},{8,24},{16,0},{24,8},{1,17},{9,25},{17,1},{25,9},{2,18},{10... | collective-permute-start | bytes 393224 | tf_op jit(solution)/shard_map/ppermute | solution.py:29
  48.3 1.6 %store_x.1 = f32[64,8192]{1,0:T(8,128)} custom-call(s32[1]{0:T(128)} %bitcast.side.token, f32[64,128]{1,0:T(8,128)S(1)} %get-tuple-element.54.scale.refs_0_, f32[64,8192]{1,0:T(8,128)S(1)} %get-tuple-element.55.x_ref, f32[64,8192]{1,0:T(8,128)S(1)} %get-tuple-element.56.u_ref, f32[64,8192]{1,0:T(8,128)S(1)} %get-tuple-element.57.z_ref, ...), custom_call_target="tpu_custom_call" | custom-call | flops 1000 | bytes 1000 | tf_op jit(solution)/shard_map/store_x/pallas_call | solution.py:299
  49.9 1.6 %collective-permute-done.13 = bf16[64,1536]{1,0:T(8,128)(2,1)S(1)} collective-permute-done((bf16[64,1536]{1,0:T(8,128)(2,1)S(1)}, bf16[64,1536]{1,0:T(8,128)(2,1)S(1)}, u32[]{:S(2)}, u32[]{:S(2)}) %collective-permute-start.13) | collective-permute-done | bytes 196640 | tf_op jit(solution)/shard_map/ppermute | solution.py:29
  51.6 1.2 %final.4 = (f32[64,8192]{1,0:T(8,128)}, f32[64,8192]{1,0:T(8,128)}) custom-call(s32[1]{0:T(128)} %bitcast.side.token, f32[64,128]{1,0:T(8,128)S(1)} %get-tuple-element.54.scale.refs_0_, f32[64,8192]{1,0:T(8,128)S(1)} %get-tuple-element.55.x_ref, f32[64,8192]{1,0:T(8,128)S(1)} %get-tuple-element.56.u_ref, f32[64,8192]{1,0:T(8,128)S(1)} %get-tuple-element.57.z_ref, ...), custom_call_target="tpu_custom_call" | custom-call | flops 1000 | bytes 1000 | tf_op jit(solution)/shard_map/final/pallas_call | solution.py:349
  52.8 2.9 %collective-permute-done.15 = bf16[64,1536]{1,0:T(8,128)(2,1)S(1)} collective-permute-done((bf16[64,1536]{1,0:T(8,128)(2,1)S(1)}, bf16[64,1536]{1,0:T(8,128)(2,1)S(1)}, u32[]{:S(2)}, u32[]{:S(2)}) %collective-permute-start.15) | collective-permute-done | bytes 196640 | tf_op jit(solution)/shard_map/ppermute | solution.py:29
  55.9 1.7 %final.5 = (f32[64,8192]{1,0:T(8,128)}, f32[64,8192]{1,0:T(8,128)}) custom-call(s32[1]{0:T(128)} %bitcast.side.token, f32[64,128]{1,0:T(8,128)S(1)} %get-tuple-element.54.scale.refs_0_, f32[64,8192]{1,0:T(8,128)S(1)} %get-tuple-element.55.x_ref, f32[64,8192]{1,0:T(8,128)S(1)} %get-tuple-element.56.u_ref, ...), custom_call_target="tpu_custom_call", output_to_operand_aliasing={{0}: (11, {}), {1}: (12, {})} | custom-call | flops 1000 | bytes 1000 | tf_op jit(solution)/shard_map/final/pallas_call | solution.py:349
  58.2 1.5 %final.6 = (f32[64,8192]{1,0:T(8,128)}, f32[64,8192]{1,0:T(8,128)}) custom-call(s32[1]{0:T(128)} %bitcast.side.token, f32[64,128]{1,0:T(8,128)S(1)} %get-tuple-element.54.scale.refs_0_, f32[64,8192]{1,0:T(8,128)S(1)} %get-tuple-element.55.x_ref, f32[64,8192]{1,0:T(8,128)S(1)} %get-tuple-element.56.u_ref, ...), custom_call_target="tpu_custom_call", output_to_operand_aliasing={{0}: (11, {}), {1}: (12, {})} | custom-call | flops 1000 | bytes 1000 | tf_op jit(solution)/shard_map/final/pallas_call | solution.py:349
  59.7 1.0 %final.7 = (f32[64,8192]{1,0:T(8,128)}, f32[64,8192]{1,0:T(8,128)}) custom-call(s32[1]{0:T(128)} %bitcast.side.token, f32[64,128]{1,0:T(8,128)S(1)} %get-tuple-element.54.scale.refs_0_, f32[64,8192]{1,0:T(8,128)S(1)} %get-tuple-element.55.x_ref, f32[64,8192]{1,0:T(8,128)S(1)} %get-tuple-element.56.u_ref, ...), custom_call_target="tpu_custom_call", output_to_operand_aliasing={{0}: (8, {}), {1}: (9, {})} | custom-call | flops 1000 | bytes 1000 | tf_op jit(solution)/shard_map/final/pallas_call | solution.py:349
  (35 shorter events, 7.9 us)
Async XLA Ops:
  9.6 4.4 %collective-permute-start.1 = (f32[64,4096]{1,0:T(8,128)S(1)}, f32[64,4096]{1,0:T(8,128)S(1)}, u32[]{:S(2)}, u32[]{:S(2)}) collective-permute-start(f32[64,4096]{1,0:T(8,128)S(1)} %get-tuple-element.66), channel_id=1, source_target_pairs={{0,8},{8,0},{16,24},{24,16},{1,9},{9,1},{17,25},{25,17},{2,10},{10... | collective-permute-start | bytes 3145736 | tf_op jit(solution)/shard_map/ppermute | solution.py:29
  10.1 6.0 %collective-permute-start = (bf16[64,768]{1,0:T(8,128)(2,1)S(1)}, bf16[64,768]{1,0:T(8,128)(2,1)S(1)}, u32[]{:S(2)}, u32[]{:S(2)}) collective-permute-start(bf16[64,768]{1,0:T(8,128)(2,1)S(1)} %get-tuple-element.61), channel_id=1, source_target_pairs={{0,1},{1,0},{2,3},{3,2},{4,5},{5,4},{6,7},{7,6},{8,9},{9,8},{10,11... | collective-permute-start | bytes 294920 | tf_op jit(solution)/shard_map/ppermute | solution.py:29
  14.1 25.3 %collective-permute-start.8 = (f32[64,4096]{1,0:T(8,128)S(1)}, f32[64,4096]{1,0:T(8,128)S(1)}, u32[]{:S(2)}, u32[]{:S(2)}) collective-permute-start(f32[64,4096]{1,0:T(8,128)S(1)} %add.30), channel_id=1, source_target_pairs={{0,16},{8,24},{16,0},{24,8},{1,17},{9,25},{17,1},{25,9},{2,18},{10... | collective-permute-start | bytes 3145736 | tf_op jit(solution)/shard_map/ppermute | solution.py:29
  16.1 4.7 %collective-permute-start.2 = (bf16[64,768]{1,0:T(8,128)(2,1)S(1)}, bf16[64,768]{1,0:T(8,128)(2,1)S(1)}, u32[]{:S(2)}, u32[]{:S(2)}) collective-permute-start(bf16[64,768]{1,0:T(8,128)(2,1)S(1)} %add_convert_fusion.5), channel_id=1, source_target_pairs={{0,2},{1,3},{2,0},{3,1},{4,6},{5,7},{6,4},{7,5},{8,10},{9,11},{10,... | collective-permute-start | bytes 294920 | tf_op jit(solution)/shard_map/ppermute | solution.py:29
  20.8 6.4 %collective-permute-start.3 = (bf16[64,768]{1,0:T(8,128)(2,1)S(1)}, bf16[64,768]{1,0:T(8,128)(2,1)S(1)}, u32[]{:S(2)}, u32[]{:S(2)}) collective-permute-start(bf16[64,768]{1,0:T(8,128)(2,1)S(1)} %add_convert_fusion.4.refs_6_), channel_id=1, source_target_pairs={{0,4},{1,5},{2,6},{3,7},{4,0},{5,1},{6,2},{7,3},{8,12},{9,13},{10,... | collective-permute-start | bytes 294920 | tf_op jit(solution)/shard_map/ppermute | solution.py:29
  27.8 5.7 %collective-permute-start.6 = (bf16[64,768]{1,0:T(8,128)(2,1)S(1)}, bf16[64,768]{1,0:T(8,128)(2,1)S(1)}, u32[]{:S(2)}, u32[]{:S(2)}) collective-permute-start(bf16[64,768]{1,0:T(8,128)(2,1)S(1)} %get-tuple-element.76), channel_id=1, source_target_pairs={{0,3},{1,2},{2,1},{3,0},{4,7},{5,6},{6,5},{7,4},{8,11},{9,10},{10,... | collective-permute-start | bytes 294920 | tf_op jit(solution)/shard_map/ppermute | solution.py:29
  30.4 4.6 %collective-permute-start.5 = (bf16[64,768]{1,0:T(8,128)(2,1)S(1)}, bf16[64,768]{1,0:T(8,128)(2,1)S(1)}, u32[]{:S(2)}, u32[]{:S(2)}) collective-permute-start(bf16[64,768]{1,0:T(8,128)(2,1)S(1)} %get-tuple-element.76), channel_id=1, source_target_pairs={{0,2},{1,3},{2,0},{3,1},{4,6},{5,7},{6,4},{7,5},{8,10},{9,11},{10,... | collective-permute-start | bytes 294920 | tf_op jit(solution)/shard_map/ppermute | solution.py:29
  30.9 4.6 %collective-permute-start.4 = (bf16[64,768]{1,0:T(8,128)(2,1)S(1)}, bf16[64,768]{1,0:T(8,128)(2,1)S(1)}, u32[]{:S(2)}, u32[]{:S(2)}) collective-permute-start(bf16[64,768]{1,0:T(8,128)(2,1)S(1)} %get-tuple-element.76), channel_id=1, source_target_pairs={{0,1},{1,0},{2,3},{3,2},{4,5},{5,4},{6,7},{7,6},{8,9},{9,8},{10,11... | collective-permute-start | bytes 294920 | tf_op jit(solution)/shard_map/ppermute | solution.py:29
  35.5 5.6 %collective-permute-start.7 = (bf16[64,768]{1,0:T(8,128)(2,1)S(1)}, bf16[64,768]{1,0:T(8,128)(2,1)S(1)}, u32[]{:S(2)}, u32[]{:S(2)}) collective-permute-start(bf16[64,768]{1,0:T(8,128)(2,1)S(1)} %add_convert_fusion.3.refs_4_), channel_id=1, source_target_pairs={{0,4},{1,5},{2,6},{3,7},{4,0},{5,1},{6,2},{7,3},{8,12},{9,13},{10,... | collective-permute-start | bytes 294920 | tf_op jit(solution)/shard_map/ppermute | solution.py:29
  41.6 1.5 %collective-permute-start.9 = (bf16[64,1536]{1,0:T(8,128)(2,1)S(1)}, bf16[64,1536]{1,0:T(8,128)(2,1)S(1)}, u32[]{:S(2)}, u32[]{:S(2)}) collective-permute-start(bf16[64,1536]{1,0:T(8,128)(2,1)S(1)} %get-tuple-element.82), channel_id=1, source_target_pairs={{0,8},{8,0},{16,24},{24,16},{1,9},{9,1},{17,25},{25,17},{2,10},{10... | collective-permute-start | bytes 589832 | tf_op jit(solution)/shard_map/ppermute | solution.py:29
  42.5 2.8 %collective-permute-start.10 = (bf16[64,2560]{1,0:T(8,128)(2,1)S(1)}, bf16[64,2560]{1,0:T(8,128)(2,1)S(1)}, u32[]{:S(2)}, u32[]{:S(2)}) collective-permute-start(bf16[64,2560]{1,0:T(8,128)(2,1)S(1)} %get-tuple-element.86), channel_id=1, source_target_pairs={{0,8},{8,0},{16,24},{24,16},{1,9},{9,1},{17,25},{25,17},{2,10},{10... | collective-permute-start | bytes 983048 | tf_op jit(solution)/shard_map/ppermute | solution.py:29
  43.7 7.8 %collective-permute-start.13 = (bf16[64,1536]{1,0:T(8,128)(2,1)S(1)}, bf16[64,1536]{1,0:T(8,128)(2,1)S(1)}, u32[]{:S(2)}, u32[]{:S(2)}) collective-permute-start(bf16[64,1536]{1,0:T(8,128)(2,1)S(1)} %get-tuple-element.84), channel_id=1, source_target_pairs={{0,16},{8,24},{16,0},{24,8},{1,17},{9,25},{17,1},{25,9},{2,18},{10... | collective-permute-start | bytes 589832 | tf_op jit(solution)/shard_map/ppermute | solution.py:29
  45.2 10.6 %collective-permute-start.11 = (f32[64,4096]{1,0:T(8,128)S(1)}, f32[64,4096]{1,0:T(8,128)S(1)}, u32[]{:S(2)}, u32[]{:S(2)}) collective-permute-start(f32[64,4096]{1,0:T(8,128)S(1)} %add.36.refs_0_.refs_3_), channel_id=1, source_target_pairs={{0,8},{8,0},{16,24},{24,16},{1,9},{9,1},{17,25},{25,17},{2,10},{10... | collective-permute-start | bytes 3145736 | tf_op jit(solution)/shard_map/ppermute | solution.py:29
  45.8 9.9 %collective-permute-start.15 = (bf16[64,1536]{1,0:T(8,128)(2,1)S(1)}, bf16[64,1536]{1,0:T(8,128)(2,1)S(1)}, u32[]{:S(2)}, u32[]{:S(2)}) collective-permute-start(bf16[64,1536]{1,0:T(8,128)(2,1)S(1)} %get-tuple-element.88), channel_id=1, source_target_pairs={{0,16},{8,24},{16,0},{24,8},{1,17},{9,25},{17,1},{25,9},{2,18},{10... | collective-permute-start | bytes 589832 | tf_op jit(solution)/shard_map/ppermute | solution.py:29
  46.8 10.9 %collective-permute-start.12 = (bf16[64,1024]{1,0:T(8,128)(2,1)S(1)}, bf16[64,1024]{1,0:T(8,128)(2,1)S(1)}, u32[]{:S(2)}, u32[]{:S(2)}) collective-permute-start(bf16[64,1024]{1,0:T(8,128)(2,1)S(1)} %get-tuple-element.93), channel_id=1, source_target_pairs={{0,16},{8,24},{16,0},{24,8},{1,17},{9,25},{17,1},{25,9},{2,18},{10... | collective-permute-start | bytes 393224 | tf_op jit(solution)/shard_map/ppermute | solution.py:29
  51.6 4.3 %collective-permute-start.14 = (bf16[64,1536]{1,0:T(8,128)(2,1)S(1)}, bf16[64,1536]{1,0:T(8,128)(2,1)S(1)}, u32[]{:S(2)}, u32[]{:S(2)}) collective-permute-start(bf16[64,1536]{1,0:T(8,128)(2,1)S(1)} %add_convert_fusion.1.refs_2_), channel_id=1, source_target_pairs={{0,8},{8,0},{16,24},{24,16},{1,9},{9,1},{17,25},{25,17},{2,10},{10... | collective-permute-start | bytes 589832 | tf_op jit(solution)/shard_map/ppermute | solution.py:29
  55.8 2.4 %collective-permute-start.17 = (bf16[64,1536]{1,0:T(8,128)(2,1)S(1)}, bf16[64,1536]{1,0:T(8,128)(2,1)S(1)}, u32[]{:S(2)}, u32[]{:S(2)}) collective-permute-start(bf16[64,1536]{1,0:T(8,128)(2,1)S(1)} %add_convert_fusion.refs_5_), channel_id=1, source_target_pairs={{0,8},{8,0},{16,24},{24,16},{1,9},{9,1},{17,25},{25,17},{2,10},{10... | collective-permute-start | bytes 589832 | tf_op jit(solution)/shard_map/ppermute | solution.py:29
  57.8 1.9 %collective-permute-start.16 = (bf16[64,1024]{1,0:T(8,128)(2,1)S(1)}, bf16[64,1024]{1,0:T(8,128)(2,1)S(1)}, u32[]{:S(2)}, u32[]{:S(2)}) collective-permute-start(bf16[64,1024]{1,0:T(8,128)(2,1)S(1)} %add_convert_fusion.2.refs_5_), channel_id=1, source_target_pairs={{0,8},{8,0},{16,24},{24,16},{1,9},{9,1},{17,25},{25,17},{2,10},{10... | collective-permute-start | bytes 393224 | tf_op jit(solution)/shard_map/ppermute | solution.py:29
